TPU v7x, 32 devices: a whole 2x2x4 slice. The times are simulated.
32 devices in a mesh: rep: 2 (over x), fsdp: 16 (over z, y, core).
Axes of the slice: x: 2, y: 2, z: 4, core: 2. Of those that a mesh axis runs over, the one named last changes fastest.
Arguments:
- tokens: bfloat16 [32, 1024, 768], P(('rep', 'fsdp')), may hold values from -6 to 6
- cotangent: bfloat16 [32, 1024, 768], P(('rep', 'fsdp')), may hold values from -6 to 6
- image_counts: int32 [32, 3], P(('rep', 'fsdp')), may hold values from 0 to 576, as said below
- patch_rows: int32 [32, 1024], P(('rep', 'fsdp')), may hold values from 0 to 23, as said below
- patch_cols: int32 [32, 1024], P(('rep', 'fsdp')), may hold values from 0 to 23, as said below
- ln1_gain: bfloat16 [768], P('fsdp'), may hold values from 0.099609375 to 1.8984375
- ln1_bias: bfloat16 [768], P('fsdp'), may hold values from -1.5 to 1.5
- qkv_weight: bfloat16 [768, 2304], P('fsdp'), may hold values from -0.21875 to 0.21875
- qkv_bias: bfloat16 [2304], P('fsdp'), may hold values from -1.5 to 1.5
- rope_freqs: bfloat16 [768], P('fsdp'), may hold values from -1 to 1
- out_weight: bfloat16 [768, 768], P('fsdp'), may hold values from -0.875 to 0.875
- out_bias: bfloat16 [768], P('fsdp'), may hold values from -1.5 to 1.5
- ln2_gain: bfloat16 [768], P('fsdp'), may hold values from 0.099609375 to 1.8984375
- ln2_bias: bfloat16 [768], P('fsdp'), may hold values from -1.5 to 1.5
- fc1_weight: bfloat16 [768, 3072], P('fsdp'), may hold values from -0.21875 to 0.21875
- fc1_bias: bfloat16 [3072], P('fsdp'), may hold values from -1.5 to 1.5
- fc2_weight: bfloat16 [3072, 768], P('fsdp'), may hold values from -0.109375 to 0.109375
- fc2_bias: bfloat16 [768], P('fsdp'), may hold values from -1.5 to 1.5
Outputs:
- output_tokens: bfloat16 [32, 1024, 768], P(('rep', 'fsdp'))
- input_grad: bfloat16 [32, 1024, 768], P(('rep', 'fsdp'))
- grad_ln1_gain: float32 [768], P('fsdp')
- grad_ln1_bias: float32 [768], P('fsdp')
- grad_qkv_weight: float32 [768, 2304], P('fsdp')
- grad_qkv_bias: float32 [2304], P('fsdp')
- grad_rope_freqs: float32 [768], P('fsdp')
- grad_out_weight: float32 [768, 768], P('fsdp')
- grad_out_bias: float32 [768], P('fsdp')
- grad_ln2_gain: float32 [768], P('fsdp')
- grad_ln2_bias: float32 [768], P('fsdp')
- grad_fc1_weight: float32 [768, 3072], P('fsdp')
- grad_fc1_bias: float32 [3072], P('fsdp')
- grad_fc2_weight: float32 [3072, 768], P('fsdp')
- grad_fc2_bias: float32 [768], P('fsdp')
Inputs may be any that keep to these rules, and one draw needn't show every extreme that they name: `image_counts`: each row packs whole images from its first slot on; counts are 196, 400 or 576, the first of every row is 576, zeros follow the last image, and a row's counts sum to at most 1024. `patch_rows`: an image's slots run row by row over its square of patches; padding slots hold 0. `patch_cols`: the column within that row; padding slots hold 0.
All inputs are finite; a program needn't handle non-finite values.
Results may differ from a plain program's by a relative error of at most 0.015.
Values may be sent and summed in bfloat16 or wider, within the bound.
No kernel may reach another device: no remote copies, remote signals or barrier semaphores. Data moves between devices by JAX's collectives and lax.ppermute only.
A program may use at most 256 MiB of HBM per device.

v0:
```python
from functools import partial

import jax
import jax.numpy as jnp
from jax import lax
from jax.sharding import PartitionSpec as P

HEADS = 12
HEAD_DIM = 64


def for_sending(value):
    return jax.tree.map(lambda a: a.astype(jnp.bfloat16) if a.dtype == jnp.float32 else a, value)


def layer_norm(vector, gain_vec, shift_vec):
    center = jnp.mean(vector, axis=-1, keepdims=True)
    deviation = vector - center
    spread = jnp.mean(deviation * deviation, axis=-1, keepdims=True)
    return deviation * lax.rsqrt(spread + 1e-06) * gain_vec + shift_vec


def segment_ids(counts, slots):
    ends = jnp.cumsum(counts)
    place = jnp.arange(slots, dtype=jnp.int32)
    inside = jnp.sum((place[:, None] >= ends[None, :]).astype(jnp.int32), axis=1)
    return jnp.where(place < ends[-1], inside, -1)


def rotate(rows_f, cols_f, queries, key_in, freqs):
    heads = queries.shape[1]
    half = queries.shape[2] // 2
    col_freq = freqs[: heads * half].reshape(heads, half)
    row_freq = freqs[heads * half :].reshape(heads, half)
    angle = cols_f[:, None, None] * col_freq[None] + rows_f[:, None, None] * row_freq[None]
    cosine = jnp.cos(angle)
    sine = jnp.sin(angle)

    def turn(values):
        first = values[..., :half]
        second = values[..., half:]
        return jnp.concatenate(
            [first * cosine - second * sine, first * sine + second * cosine], axis=-1
        )

    return (turn(queries), turn(key_in))


def across_rows(left, right):
    return lax.dot_general(
        left, right, (((0,), (0,)), ((), ())), preferred_element_type=jnp.float32
    )


def against_cols(left, right):
    return lax.dot_general(
        left, right, (((1,), (1,)), ((), ())), preferred_element_type=jnp.float32
    )


def block_scores(query_blk, key_b, start, seg, place, block, scale):
    seg_blk = lax.dynamic_slice_in_dim(seg, start, block, 0)
    place_blk = start + jnp.arange(block, dtype=jnp.int32)
    raw = jnp.einsum("qhd,khd->hqk", query_blk, key_b, preferred_element_type=jnp.float32) * scale
    allowed = (seg_blk[:, None] == seg[None, :]) & (seg_blk[:, None] >= 0) | (
        place_blk[:, None] == place[None, :]
    )
    return jnp.where(allowed[None], raw, -1e30)


def attend_forward(query_b, key_b, value_b, seg, block, scale):
    slots = query_b.shape[0]
    place = jnp.arange(slots, dtype=jnp.int32)

    def one_block(block_at):
        start = block_at * block
        query_blk = lax.dynamic_slice_in_dim(query_b, start, block, 0)
        masked = block_scores(query_blk, key_b, start, seg, place, block, scale)
        peak = jnp.max(masked, axis=-1, keepdims=True)
        weights = jnp.exp(masked - peak)
        totals = jnp.sum(weights, axis=-1, keepdims=True)
        prob_b = (weights / totals).astype(jnp.bfloat16)
        mixed = jnp.einsum("hqk,khd->qhd", prob_b, value_b, preferred_element_type=jnp.float32)
        return (mixed, (peak + jnp.log(totals))[..., 0])

    mixed_all, log_totals = lax.map(one_block, jnp.arange(slots // block, dtype=jnp.int32))
    return (mixed_all.reshape(query_b.shape), log_totals)


def attend_backward(query_b, key_b, value_b, grad_mix, log_totals, seg, block, scale):
    slots = query_b.shape[0]
    place = jnp.arange(slots, dtype=jnp.int32)

    def one_block(carry, block_at):
        key_acc, value_acc = carry
        start = block_at * block
        query_blk = lax.dynamic_slice_in_dim(query_b, start, block, 0)
        grad_blk = lax.dynamic_slice_in_dim(grad_mix, start, block, 0)
        masked = block_scores(query_blk, key_b, start, seg, place, block, scale)
        prob = jnp.exp(masked - log_totals[block_at][:, :, None])
        prob_b = prob.astype(jnp.bfloat16)
        value_acc = value_acc + jnp.einsum(
            "hqk,qhd->khd", prob_b, grad_blk, preferred_element_type=jnp.float32
        )
        grad_prob = jnp.einsum(
            "qhd,khd->hqk", grad_blk, value_b, preferred_element_type=jnp.float32
        )
        grad_score = prob * (grad_prob - jnp.sum(prob * grad_prob, axis=-1, keepdims=True))
        score_b = grad_score.astype(jnp.bfloat16)
        query_grad = (
            jnp.einsum("hqk,khd->qhd", score_b, key_b, preferred_element_type=jnp.float32) * scale
        )
        key_acc = (
            key_acc
            + jnp.einsum("hqk,qhd->khd", score_b, query_blk, preferred_element_type=jnp.float32)
            * scale
        )
        return ((key_acc, value_acc), query_grad)

    empty = jnp.zeros(key_b.shape, jnp.float32)
    (key_grad, value_grad), query_grads = lax.scan(
        one_block, (empty, empty), jnp.arange(slots // block, dtype=jnp.int32)
    )
    return (query_grads.reshape(query_b.shape), key_grad, value_grad)


def body(
    tokens,
    cotangent,
    image_counts,
    patch_rows,
    patch_cols,
    ln1_gain,
    ln1_bias,
    qkv_weight,
    qkv_bias,
    rope_freqs,
    out_weight,
    out_bias,
    ln2_gain,
    ln2_bias,
    fc1_weight,
    fc1_bias,
    fc2_weight,
    fc2_bias,
):
    gathered = (
        lax.all_gather(ln1_gain, "fsdp", axis=0, tiled=True),
        lax.all_gather(ln1_bias, "fsdp", axis=0, tiled=True),
        lax.all_gather(qkv_weight, "fsdp", axis=0, tiled=True),
        lax.all_gather(qkv_bias, "fsdp", axis=0, tiled=True),
        lax.all_gather(rope_freqs, "fsdp", axis=0, tiled=True),
        lax.all_gather(out_weight, "fsdp", axis=0, tiled=True),
        lax.all_gather(out_bias, "fsdp", axis=0, tiled=True),
        lax.all_gather(ln2_gain, "fsdp", axis=0, tiled=True),
        lax.all_gather(ln2_bias, "fsdp", axis=0, tiled=True),
        lax.all_gather(fc1_weight, "fsdp", axis=0, tiled=True),
        lax.all_gather(fc1_bias, "fsdp", axis=0, tiled=True),
        lax.all_gather(fc2_weight, "fsdp", axis=0, tiled=True),
        lax.all_gather(fc2_bias, "fsdp", axis=0, tiled=True),
    )
    (
        gain_one,
        shift_one,
        w_qkv,
        b_qkv,
        freqs,
        w_out,
        b_out,
        gain_two,
        shift_two,
        w_up,
        b_up,
        w_down,
        b_down,
    ) = gathered
    width = HEADS * HEAD_DIM
    slots = tokens.shape[1]
    block = min(512, slots)
    scale = HEAD_DIM ** (-0.5)
    seg = segment_ids(image_counts[0], slots)
    rows_f = patch_rows[0].astype(jnp.float32)
    cols_f = patch_cols[0].astype(jnp.float32)
    inputs = tokens[0].astype(jnp.float32)
    normed_one, norm_one_back = jax.vjp(
        layer_norm, inputs, gain_one.astype(jnp.float32), shift_one.astype(jnp.float32)
    )
    normed_b = normed_one.astype(jnp.bfloat16)
    qkv = jnp.dot(normed_b, w_qkv, preferred_element_type=jnp.float32) + b_qkv.astype(jnp.float32)
    queries = qkv[:, :width].reshape(slots, HEADS, HEAD_DIM)
    key_in = qkv[:, width : 2 * width].reshape(slots, HEADS, HEAD_DIM)
    value_b = qkv[:, 2 * width :].reshape(slots, HEADS, HEAD_DIM).astype(jnp.bfloat16)
    (query_rot, key_rot), rope_back = jax.vjp(
        partial(rotate, rows_f, cols_f), queries, key_in, freqs.astype(jnp.float32)
    )
    query_b = query_rot.astype(jnp.bfloat16)
    key_b = key_rot.astype(jnp.bfloat16)
    mixed, log_totals = attend_forward(query_b, key_b, value_b, seg, block, scale)
    mixed_b = mixed.reshape(slots, width).astype(jnp.bfloat16)
    hidden_one = inputs + (
        jnp.dot(mixed_b, w_out, preferred_element_type=jnp.float32) + b_out.astype(jnp.float32)
    )
    normed_two, norm_two_back = jax.vjp(
        layer_norm, hidden_one, gain_two.astype(jnp.float32), shift_two.astype(jnp.float32)
    )
    normed_two_b = normed_two.astype(jnp.bfloat16)
    pre_act = jnp.dot(normed_two_b, w_up, preferred_element_type=jnp.float32) + b_up.astype(
        jnp.float32
    )
    act_out, gelu_back = jax.vjp(jax.nn.gelu, pre_act)
    act_b = act_out.astype(jnp.bfloat16)
    result = hidden_one + (
        jnp.dot(act_b, w_down, preferred_element_type=jnp.float32) + b_down.astype(jnp.float32)
    )
    back_qkv, back_out, back_up, back_down = (
        lax.all_gather(qkv_weight, "fsdp", axis=0, tiled=True),
        lax.all_gather(out_weight, "fsdp", axis=0, tiled=True),
        lax.all_gather(fc1_weight, "fsdp", axis=0, tiled=True),
        lax.all_gather(fc2_weight, "fsdp", axis=0, tiled=True),
    )
    grad_out_b = cotangent[0]
    grad_out_f = grad_out_b.astype(jnp.float32)
    grad_down_w = across_rows(act_b, grad_out_b)
    grad_down_b = jnp.sum(grad_out_f, axis=0)
    grad_act = against_cols(grad_out_b, back_down)
    grad_pre_b = gelu_back(grad_act)[0].astype(jnp.bfloat16)
    grad_up_w = across_rows(normed_two_b, grad_pre_b)
    grad_up_b = jnp.sum(grad_pre_b.astype(jnp.float32), axis=0)
    grad_normed_two = against_cols(grad_pre_b, back_up)
    grad_hidden_part, grad_gain_two, grad_shift_two = norm_two_back(grad_normed_two)
    grad_hidden = grad_out_f + grad_hidden_part
    grad_hidden_b = grad_hidden.astype(jnp.bfloat16)
    grad_out_w = across_rows(mixed_b, grad_hidden_b)
    grad_out_bias = jnp.sum(grad_hidden, axis=0)
    grad_mix = (
        against_cols(grad_hidden_b, back_out).astype(jnp.bfloat16).reshape(slots, HEADS, HEAD_DIM)
    )
    grad_query_rot, grad_key_rot, grad_values = attend_backward(
        query_b, key_b, value_b, grad_mix, log_totals, seg, block, scale
    )
    grad_queries, grad_keys, grad_freqs = rope_back((grad_query_rot, grad_key_rot))
    grad_qkv_b = jnp.concatenate(
        [
            grad_queries.reshape(slots, width),
            grad_keys.reshape(slots, width),
            grad_values.reshape(slots, width),
        ],
        axis=1,
    ).astype(jnp.bfloat16)
    grad_qkv_w = across_rows(normed_b, grad_qkv_b)
    grad_qkv_bias = jnp.sum(grad_qkv_b.astype(jnp.float32), axis=0)
    grad_normed_one = against_cols(grad_qkv_b, back_qkv)
    grad_input_part, grad_gain_one, grad_shift_one = norm_one_back(grad_normed_one)
    grad_input = grad_hidden + grad_input_part
    shard_grads = (
        lax.psum_scatter(grad_gain_one, "fsdp", scatter_dimension=0, tiled=True),
        lax.psum_scatter(grad_shift_one, "fsdp", scatter_dimension=0, tiled=True),
        lax.psum_scatter(grad_qkv_w, "fsdp", scatter_dimension=0, tiled=True),
        lax.psum_scatter(grad_qkv_bias, "fsdp", scatter_dimension=0, tiled=True),
        lax.psum_scatter(grad_freqs, "fsdp", scatter_dimension=0, tiled=True),
        lax.psum_scatter(grad_out_w, "fsdp", scatter_dimension=0, tiled=True),
        lax.psum_scatter(grad_out_bias, "fsdp", scatter_dimension=0, tiled=True),
        lax.psum_scatter(grad_gain_two, "fsdp", scatter_dimension=0, tiled=True),
        lax.psum_scatter(grad_shift_two, "fsdp", scatter_dimension=0, tiled=True),
        lax.psum_scatter(grad_up_w, "fsdp", scatter_dimension=0, tiled=True),
        lax.psum_scatter(grad_up_b, "fsdp", scatter_dimension=0, tiled=True),
        lax.psum_scatter(grad_down_w, "fsdp", scatter_dimension=0, tiled=True),
        lax.psum_scatter(grad_down_b, "fsdp", scatter_dimension=0, tiled=True),
    )
    summed = jax.tree.map(
        lambda part: part.astype(jnp.float32), lax.psum(for_sending(tuple(shard_grads)), "rep")
    )
    return (
        result[None].astype(jnp.bfloat16),
        grad_input[None].astype(jnp.bfloat16),
        summed[0],
        summed[1],
        summed[2],
        summed[3],
        summed[4],
        summed[5],
        summed[6],
        summed[7],
        summed[8],
        summed[9],
        summed[10],
        summed[11],
        summed[12],
    )


def solution(mesh):
    in_specs = (
        P(("rep", "fsdp"), None, None),
        P(("rep", "fsdp"), None, None),
        P(("rep", "fsdp"), None),
        P(("rep", "fsdp"), None),
        P(("rep", "fsdp"), None),
        P("fsdp"),
        P("fsdp"),
        P("fsdp", None),
        P("fsdp"),
        P("fsdp"),
        P("fsdp", None),
        P("fsdp"),
        P("fsdp"),
        P("fsdp"),
        P("fsdp", None),
        P("fsdp"),
        P("fsdp", None),
        P("fsdp"),
    )
    out_specs = (
        P(("rep", "fsdp"), None, None),
        P(("rep", "fsdp"), None, None),
        P("fsdp"),
        P("fsdp"),
        P("fsdp", None),
        P("fsdp"),
        P("fsdp"),
        P("fsdp", None),
        P("fsdp"),
        P("fsdp"),
        P("fsdp"),
        P("fsdp", None),
        P("fsdp"),
        P("fsdp", None),
        P("fsdp"),
    )
    return jax.shard_map(body, mesh=mesh, in_specs=in_specs, out_specs=out_specs, check_vma=False)
```

profile of v0, /device:TPU:0, one launch (start us, length us, event | category | flops | bytes accessed | tf_op | source)
XLA Modules:
  0.0 956.0 jit_solution(2803927958178357300)
XLA Ops:
  23.8 63.6 %all-reduce.25 = (bf16[768]{0:T(1024)(128)(2,1)S(1)}, bf16[2304]{0:T(1024)(128)(2,1)S(1)}, bf16[768]{0:T(1024)(128)(2,1)S(1)}, bf16[768]{0:T(1024)(128)(2,1)S(1)...) all-reduce(bf16[768]{0:T(1024)(128)(2,1)S(1)} %dynamic-update-slice, ...), channel_id=1, replica_groups=mesh['rep'=2,'fsdp'=16] {'fsdp'}, use_global_device_ids=true, to_apply=%add.9 | all-reduce | flops 10752 | bytes 43008
  125.5 78.3 %while.28 = (s32[]{:T(128)}, bf16[2,512,12,64]{1,3,2,0:T(8,128)(2,1)S(1)}, f32[2,12,512]{2,1,0:T(8,128)S(1)}, s32[2]{0:T(128)S(1)}, s32[1024]{0:T(1024)S(1)}, /*...) while((s32[]{:T(128)}, ...), condition=%wide.region_7.8_spmd.clone, body=%wide.region_4.7_spmd.clone.sunk | while | flops 1688202240 | bytes 184016096 | solution.py:86
  127.6 12.1 %fusion.119 = (f32[12,512]{1,0:T(8,128)S(1)}, f32[12,512,1024]{2,1,0:T(8,128)}) fusion(pred[512,1024]{1,0:T(8,128)(4,1)S(1)} %fusion.118, bf16[1024,12,64]{0,2,1:T(8,128)(2,1)S(1)} %get-tuple-element.544, bf16[1024,12,64]{0,2,1:T(8,128)(2,1)} %get-tuple-element.543, s32[]{:T(128)S(6)} %select_n.64), kind=kOutput, calls=%fused_computation.5.clone.1 | convolution fusion | flops 824174592 | bytes 28073988 | tf_op jit(solution)/shard_map/while/body/eval_jaxpr/qhd,khd->hqk/dot_general | solution.py:64
  139.7 12.5 %fusion.120 = f32[12,512]{1,0:T(8,128)S(1)} fusion(f32[12,512,1024]{2,1,0:T(8,128)} %get-tuple-element.497, f32[12,512]{1,0:T(8,128)S(1)} %get-tuple-element.498, pred[512,1024]{1,0:T(8,128)(4,1)S(1)} %fusion.118), kind=kLoop, calls=%fused_computation.6.clone.1 | loop fusion | flops 25159680 | bytes 25739264 | tf_op jit(solution)/shard_map/while/body/eval_jaxpr/reduce_sum | solution.py:81
  166.7 12.0 %fusion.119 = (f32[12,512]{1,0:T(8,128)S(1)}, f32[12,512,1024]{2,1,0:T(8,128)}) fusion(pred[512,1024]{1,0:T(8,128)(4,1)S(1)} %fusion.118, bf16[1024,12,64]{0,2,1:T(8,128)(2,1)S(1)} %get-tuple-element.544, bf16[1024,12,64]{0,2,1:T(8,128)(2,1)} %get-tuple-element.543, s32[]{:T(128)S(6)} %select_n.64), kind=kOutput, calls=%fused_computation.5.clone.1 | convolution fusion | flops 824174592 | bytes 28073988 | tf_op jit(solution)/shard_map/while/body/eval_jaxpr/qhd,khd->hqk/dot_general | solution.py:64
  178.7 12.9 %fusion.120 = f32[12,512]{1,0:T(8,128)S(1)} fusion(f32[12,512,1024]{2,1,0:T(8,128)} %get-tuple-element.497, f32[12,512]{1,0:T(8,128)S(1)} %get-tuple-element.498, pred[512,1024]{1,0:T(8,128)(4,1)S(1)} %fusion.118), kind=kLoop, calls=%fused_computation.6.clone.1 | loop fusion | flops 25159680 | bytes 25739264 | tf_op jit(solution)/shard_map/while/body/eval_jaxpr/reduce_sum | solution.py:81
  226.7 15.5 %convert_reduce_fusion = (f32[3072]{0:T(1024)}, bf16[1024,3072]{1,0:T(8,128)(2,1)S(1)}) fusion(f32[1024,3072]{1,0:T(8,128)} %fusion.70, f32[3072]{0:T(1024)S(1)} %copy-done.58, bf16[3072,768]{1,0:T(8,128)(2,1)} %all-gather.11.cloned.1.call-done, bf16[1,1024,768]{2,1,0:T(8,128)(2,1)S(1)} %copy-done.26), kind=kOutput, calls=%fused_computation.54 | convolution fusion | flops 4904186880 | bytes 25190400 | tf_op jit(solution)/shard_map/dot_general | solution.py:56
  267.9 237.3 %while.29 = (s32[]{:T(128)}, f32[1024,12,64]{0,2,1:T(8,128)}, f32[1024,12,64]{0,2,1:T(8,128)}, f32[2,512,12,64]{1,0,3,2:T(2,128)}, s32[2]{0:T(128)S(1)}, /*index...) while((s32[]{:T(128)}, f32[1024,12,64]{0,2,1:T(8,128)}, ...), condition=%wide.region_14.15_spmd.clone, body=%wide.region_12.14_spmd.clone.sunk | while | flops 4127321088 | bytes 231931216 | solution.py:121
  272.0 11.8 %fusion.130 = f32[12,512,1024]{2,1,0:T(8,128)} fusion(bf16[1024,12,64]{0,2,1:T(8,128)(2,1)S(1)} %get-tuple-element.589, bf16[1024,12,64]{0,2,1:T(8,128)(2,1)} %get-tuple-element.587, s32[]{:T(128)S(6)} %select_n.68), kind=kOutput, calls=%fused_computation.34.clone.1 | convolution fusion | flops 805306368 | bytes 27525124 | tf_op jit(solution)/shard_map/while/body/eval_jaxpr/qhd,khd->hqk/dot_general | solution.py:64
  283.7 13.7 %bitcast_add_fusion.5 = f32[1024,12,64]{0,2,1:T(8,128)} fusion(f32[1024,12,64]{0,2,1:T(8,128)} %get-tuple-element.568, f32[12,512,1024]{2,1,0:T(8,128)} %fusion.130, f32[12,512]{1,0:T(8,128)S(1)} %dynamic-slice_bitcast_fusion.2, pred[512,1024]{1,0:T(8,128)(4,1)S(1)} %fusion.131, pred[]{:T(512)S(6)} %compare.9, ...), kind=kOutput, calls=%fused_computation.25.clone.1 | convolution fusion | flops 832045056 | bytes 32800772 | tf_op jit(solution)/shard_map/while/body/eval_jaxpr/hqk,qhd->khd/dot_general | solution.py:102
  297.4 18.2 %multiply_reduce_fusion.7 = (f32[12,512]{1,0:T(8,128)S(1)}, f32[12,512,1024]{2,1,0:T(8,128)}) fusion(f32[12,512,1024]{2,1,0:T(8,128)} %fusion.130, f32[12,512]{1,0:T(8,128)S(1)} %dynamic-slice_bitcast_fusion.2, pred[512,1024]{1,0:T(8,128)(4,1)S(1)} %fusion.131, bf16[1024,12,64]{0,2,1:T(8,128)(2,1)} %get-tuple-element.592, ...), kind=kOutput, calls=%fused_computation.20.clone.1 | convolution fusion | flops 836757504 | bytes 53264388 | tf_op jit(solution)/shard_map/while/body/eval_jaxpr/qhd,khd->hqk/dot_general | solution.py:105
  315.7 21.4 %multiply_convert_fusion.5 = bf16[12,512,1024]{2,1,0:T(8,128)(2,1)} fusion(f32[12,512,1024]{2,1,0:T(8,128)} %get-tuple-element.512, f32[12,512,1024]{2,1,0:T(8,128)} %fusion.130, f32[12,512]{1,0:T(8,128)S(1)} %get-tuple-element.513, f32[12,512]{1,0:T(8,128)S(1)} %dynamic-slice_bitcast_fusion.2, pred[512,1024]{1,0:T(8,128)(4,1)S(1)} %fusion.131), kind=kLoop, calls=%fused_computation.19.clone.1 | loop fusion | flops 37748736 | bytes 63488000 | tf_op jit(solution)/shard_map/while/body/eval_jaxpr/convert_element_type | solution.py:109
  357.3 28.7 %dynamic_update_slice.21 = f32[2,512,12,64]{1,0,3,2:T(2,128)} dynamic-update-slice(f32[2,512,12,64]{1,0,3,2:T(2,128)} %get-tuple-element.569, f32[1,512,12,64]{1,0,3,2:T(1,128)S(1)} %copy.119, s32[]{:T(128)S(6)} %copy.145, s32[]{:T(128)} %constant.48.clone.1..sunk.1, s32[]{:T(128)} %constant.48.clone.1..sunk.1, s32[]{:T(128)} %constant.48.clone.1..sunk.1) | dynamic-update-slice | bytes 3145732 | tf_op jit(solution)/shard_map/while/body/jit(dynamic_update_index_in_dim)/dynamic_update_slice | solution.py:86
  389.9 11.5 %fusion.130 = f32[12,512,1024]{2,1,0:T(8,128)} fusion(bf16[1024,12,64]{0,2,1:T(8,128)(2,1)S(1)} %get-tuple-element.589, bf16[1024,12,64]{0,2,1:T(8,128)(2,1)} %get-tuple-element.587, s32[]{:T(128)S(6)} %select_n.68), kind=kOutput, calls=%fused_computation.34.clone.1 | convolution fusion | flops 805306368 | bytes 27525124 | tf_op jit(solution)/shard_map/while/body/eval_jaxpr/qhd,khd->hqk/dot_general | solution.py:64
  401.4 14.3 %bitcast_add_fusion.5 = f32[1024,12,64]{0,2,1:T(8,128)} fusion(f32[1024,12,64]{0,2,1:T(8,128)} %get-tuple-element.568, f32[12,512,1024]{2,1,0:T(8,128)} %fusion.130, f32[12,512]{1,0:T(8,128)S(1)} %dynamic-slice_bitcast_fusion.2, pred[512,1024]{1,0:T(8,128)(4,1)S(1)} %fusion.131, pred[]{:T(512)S(6)} %compare.9, ...), kind=kOutput, calls=%fused_computation.25.clone.1 | convolution fusion | flops 832045056 | bytes 32800772 | tf_op jit(solution)/shard_map/while/body/eval_jaxpr/hqk,qhd->khd/dot_general | solution.py:102
  415.7 18.1 %multiply_reduce_fusion.7 = (f32[12,512]{1,0:T(8,128)S(1)}, f32[12,512,1024]{2,1,0:T(8,128)}) fusion(f32[12,512,1024]{2,1,0:T(8,128)} %fusion.130, f32[12,512]{1,0:T(8,128)S(1)} %dynamic-slice_bitcast_fusion.2, pred[512,1024]{1,0:T(8,128)(4,1)S(1)} %fusion.131, bf16[1024,12,64]{0,2,1:T(8,128)(2,1)} %get-tuple-element.592, ...), kind=kOutput, calls=%fused_computation.20.clone.1 | convolution fusion | flops 836757504 | bytes 53264388 | tf_op jit(solution)/shard_map/while/body/eval_jaxpr/qhd,khd->hqk/dot_general | solution.py:105
  433.7 21.3 %multiply_convert_fusion.5 = bf16[12,512,1024]{2,1,0:T(8,128)(2,1)} fusion(f32[12,512,1024]{2,1,0:T(8,128)} %get-tuple-element.512, f32[12,512,1024]{2,1,0:T(8,128)} %fusion.130, f32[12,512]{1,0:T(8,128)S(1)} %get-tuple-element.513, f32[12,512]{1,0:T(8,128)S(1)} %dynamic-slice_bitcast_fusion.2, pred[512,1024]{1,0:T(8,128)(4,1)S(1)} %fusion.131), kind=kLoop, calls=%fused_computation.19.clone.1 | loop fusion | flops 37748736 | bytes 63488000 | tf_op jit(solution)/shard_map/while/body/eval_jaxpr/convert_element_type | solution.py:109
  476.1 28.7 %dynamic_update_slice.21 = f32[2,512,12,64]{1,0,3,2:T(2,128)} dynamic-update-slice(f32[2,512,12,64]{1,0,3,2:T(2,128)} %get-tuple-element.569, f32[1,512,12,64]{1,0,3,2:T(1,128)S(1)} %copy.119, s32[]{:T(128)S(6)} %copy.145, s32[]{:T(128)} %constant.48.clone.1..sunk.1, s32[]{:T(128)} %constant.48.clone.1..sunk.1, s32[]{:T(128)} %constant.48.clone.1..sunk.1) | dynamic-update-slice | bytes 3145732 | tf_op jit(solution)/shard_map/while/body/jit(dynamic_update_index_in_dim)/dynamic_update_slice | solution.py:86
  542.6 13.2 %fusion.53 = f32[3072,768]{1,0:T(8,128)} fusion(bf16[1,1024,768]{2,1,0:T(8,128)(2,1)S(1)} %copy-done.27, f32[1024,3072]{1,0:T(8,128)} %fusion.70, f32[3072]{0:T(1024)S(1)} %copy-done.59), kind=kOutput, calls=%fused_computation.91 | convolution fusion | flops 4863295488 | bytes 23605248 | tf_op jit(solution)/shard_map/dot_general | solution.py:50
  588.7 11.8 %fusion.58 = bf16[1,1024,768]{1,2,0:T(8,128)(2,1)} fusion(f32[1024,768]{0,1:T(8,128)S(1)} %copy-done.8, f32[768]{0:T(1024)S(1)} %convert_element_type.216, bf16[3072,768]{1,0:T(8,128)(2,1)} %all-gather.11.cloned.1.call-done, f32[1024,3072]{1,0:T(8,128)} %fusion.70, f32[3072]{0:T(1024)S(1)} %copy-done.59), kind=kOutput, calls=%fused_computation.108 | convolution fusion | flops 4865654784 | bytes 22035456 | tf_op jit(solution)/shard_map/dot_general | solution.py:213
  602.0 26.6 %reduce-scatter.5.cloned.1.call-done = f32[48,2304]{1,0:T(8,128)} async-done(((f32[768,2304]{1,0:T(8,128)}), f32[48,2304]{1,0:T(8,128)}) %reduce-scatter.5.cloned.1.call-update) | async-done | bytes 442384 | tf_op jit(solution)/shard_map/reduce_scatter | solution.py:258
  630.4 113.3 %reduce-scatter.11.cloned.1.call-done = f32[192,768]{1,0:T(8,128)} async-done(((f32[3072,768]{1,0:T(8,128)}), f32[192,768]{1,0:T(8,128)}) %reduce-scatter.11.cloned.1.call-update) | async-done | bytes 589840 | tf_op jit(solution)/shard_map/reduce_scatter | solution.py:267
  745.5 114.0 %reduce-scatter.9.cloned.1.call-done = f32[48,3072]{1,0:T(8,128)} async-done(((f32[768,3072]{1,0:T(8,128)}), f32[48,3072]{1,0:T(8,128)}) %reduce-scatter.9.cloned.1.call-update) | async-done | bytes 589840 | tf_op jit(solution)/shard_map/reduce_scatter | solution.py:265
  869.0 60.5 %all-reduce.24 = (bf16[768]{0:T(1024)(128)(2,1)S(1)}, bf16[768]{0:T(1024)(128)(2,1)S(1)}, bf16[2304]{0:T(1024)(128)(2,1)S(1)}, bf16[768]{0:T(1024)(128)(2,1)S(1)...) all-reduce(f32[768]{0:T(1024)S(1)} %get-tuple-element.269, ...), channel_id=2, replica_groups=mesh['rep'=2,'fsdp'=16] {'fsdp'}, use_global_device_ids=true, to_apply=%region_18.19.clone | all-reduce | flops 10752 | bytes 64512
  (313 shorter events, 274.3 us)
Async XLA Ops:
  7.2 87.7 %all-gather.5.cloned.1.call-start = ((), (), s32[]{:S(2)}) async-start(), calls=%async_computation.4 | async-start | bytes 3760128 | tf_op jit(solution)/shard_map/all_gather | solution.py:150
  7.9 201.8 %all-gather.7.cloned.1.call-start = ((), (), s32[]{:S(2)}) async-start(), calls=%async_computation.5 | async-start | bytes 1253376 | tf_op jit(solution)/shard_map/all_gather | solution.py:153
  8.7 206.6 %all-gather.9.cloned.1.call-start = ((), (), s32[]{:S(2)}) async-start(), calls=%async_computation.6 | async-start | bytes 5013504 | tf_op jit(solution)/shard_map/all_gather | solution.py:157
  9.4 217.3 %all-gather.11.cloned.1.call-start = ((), (), s32[]{:S(2)}) async-start(), calls=%async_computation.7 | async-start | bytes 5013504 | tf_op jit(solution)/shard_map/all_gather | solution.py:159
  10.0 590.5 %reduce-scatter.7.cloned.1.call-start = ((), (), s32[]{:S(2)}) async-start(), calls=%async_computation.9 | async-start | bytes 2506752 | tf_op jit(solution)/shard_map/reduce_scatter | solution.py:261
  15.6 99.7 %copy-start.45 = (f32[1,1024]{1,0:T(1,128)}, f32[1,1024]{1,0:T(1,128)S(1)}, u32[]{:S(2)}) copy-start(f32[1,1024]{1,0:T(1,128)S(1)} %convert_element_type.205) | copy-start | bytes 12292
  16.3 99.0 %copy-start.47 = (f32[1,1024]{1,0:T(1,128)}, f32[1,1024]{1,0:T(1,128)S(1)}, u32[]{:S(2)}) copy-start(f32[1,1024]{1,0:T(1,128)S(1)} %convert_element_type.202) | copy-start | bytes 12292
  89.3 26.0 %copy-start.39 = (f32[12,32]{1,0:T(8,128)}, f32[12,32]{1,0:T(8,128)S(1)}, u32[]{:S(2)}) copy-start(f32[12,32]{1,0:T(8,128)S(1)} %slice.56) | copy-start | bytes 4612
  89.4 25.9 %copy-start.41 = (f32[12,32]{1,0:T(8,128)}, f32[12,32]{1,0:T(8,128)S(1)}, u32[]{:S(2)}) copy-start(f32[12,32]{1,0:T(8,128)S(1)} %slice.58) | copy-start | bytes 4612
  139.7 15.9 %copy-start = (f32[12,512,1024]{2,1,0:T(8,128)S(1)}, f32[12,512,1024]{2,1,0:T(8,128)}, u32[]{:S(2)}) copy-start(f32[12,512,1024]{2,1,0:T(8,128)} %get-tuple-element.497) | copy-start | bytes 75497472 | tf_op jit(solution)/shard_map/while
  178.7 16.1 %copy-start = (f32[12,512,1024]{2,1,0:T(8,128)S(1)}, f32[12,512,1024]{2,1,0:T(8,128)}, u32[]{:S(2)}) copy-start(f32[12,512,1024]{2,1,0:T(8,128)} %get-tuple-element.497) | copy-start | bytes 75497472 | tf_op jit(solution)/shard_map/while
  213.2 44.5 %copy-start.31 = (f32[1024]{0:T(1024)}, f32[1024]{0:T(1024)S(1)}, u32[]{:S(2)}) copy-start(f32[1024]{0:T(1024)S(1)} %broadcast_multiply_fusion) | copy-start | bytes 12292
  215.2 42.4 %copy-start.35 = (f32[1024]{0:T(1024)}, f32[1024]{0:T(1024)S(1)}, u32[]{:S(2)}) copy-start(f32[1024]{0:T(1024)S(1)} %fusion.64) | copy-start | bytes 12292
  215.2 11.5 %copy-start.26 = (bf16[1,1024,768]{2,1,0:T(8,128)(2,1)S(1)}, bf16[1,1024,768]{2,1,0:T(8,128)(2,1)}, u32[]{:S(2)}) copy-start(bf16[1,1024,768]{2,1,0:T(8,128)(2,1)} %param.23) | copy-start | bytes 4718596
  215.2 11.5 %copy-start.58 = (f32[3072]{0:T(1024)S(1)}, f32[3072]{0:T(1024)}, u32[]{:S(2)}) copy-start(f32[3072]{0:T(1024)} %convert_element_type.214) | copy-start | bytes 36868
  226.7 15.5 %copy-start.24 = (bf16[768,3072]{1,0:T(8,128)(2,1)S(1)}, bf16[768,3072]{1,0:T(8,128)(2,1)}, u32[]{:S(2)}) copy-start(bf16[768,3072]{1,0:T(8,128)(2,1)} %all-gather.9.cloned.1.call-done) | copy-start | bytes 14155780
  264.0 364.6 %reduce-scatter.5.cloned.1.call-start = ((), (), s32[]{:S(2)}) async-start(), calls=%async_computation.8 | async-start | bytes 7520256 | tf_op jit(solution)/shard_map/reduce_scatter | solution.py:258
  271.9 11.8 %copy-start.17 = (bf16[1024,12,64]{0,2,1:T(8,128)(2,1)S(1)}, bf16[1024,12,64]{0,2,1:T(8,128)(2,1)}, u32[]{:S(2)}) copy-start(bf16[1024,12,64]{0,2,1:T(8,128)(2,1)} %get-tuple-element.591) | copy-start | bytes 4718596 | tf_op jit(solution)/shard_map/while
  513.2 18.7 %copy-start.18 = (bf16[1024,12,64]{0,2,1:T(8,128)(2,1)}, bf16[1024,12,64]{0,2,1:T(8,128)(2,1)S(1)}, u32[]{:S(2)}) copy-start(bf16[1024,12,64]{0,2,1:T(8,128)(2,1)S(1)} %convert.34) | copy-start | bytes 4718596
  541.2 202.5 %reduce-scatter.11.cloned.1.call-start = ((), (), s32[]{:S(2)}) async-start(), calls=%async_computation.11 | async-start | bytes 10027008 | tf_op jit(solution)/shard_map/reduce_scatter | solution.py:267
  555.8 303.7 %reduce-scatter.9.cloned.1.call-start = ((), (), s32[]{:S(2)}) async-start(), calls=%async_computation.10 | async-start | bytes 10027008 | tf_op jit(solution)/shard_map/reduce_scatter | solution.py:265
  567.8 374.6 %all-reduce.30.cloned.1.call-start = ((), (), s32[]{:S(2)}) async-start(), calls=%async_computation.12 | async-start | bytes 1769472 | tf_op jit(solution)/shard_map/psum | solution.py:271
  602.0 261.9 %copy-start.16 = (bf16[1,1024,768]{1,2,0:T(8,128)(2,1)S(1)}, bf16[1,1024,768]{1,2,0:T(8,128)(2,1)}, u32[]{:S(2)}) copy-start(bf16[1,1024,768]{1,2,0:T(8,128)(2,1)} %copy.82) | copy-start | bytes 4718596
  602.0 261.9 %copy-start.56 = (f32[1024]{0:T(1024)S(1)}, f32[1024]{0:T(1024)}, u32[]{:S(2)}) copy-start(f32[1024]{0:T(1024)} %copy-done.55) | copy-start | bytes 12292
  (55 other events, 204.7 us)
Sparse Core Ops, SparseCore 0:
  10.3 50.2 all-gather.4
  62.9 37.3 all-gather.6
  102.6 52.2 all-gather.8
  157.0 51.8 all-gather.10
  264.1 60.1 reduce-scatter.6
  541.3 87.2 reduce-scatter.4
  632.7 110.9 reduce-scatter.10
  748.4 111.0 reduce-scatter.8
  863.1 36.7 all-reduce.29
where the time goes:
time: 970 us; the launch traced here: 956 us
  matrix products  270 us (28%)
  waiting for transfers between devices  257 us (26%)
  other arithmetic  142 us (15%)
  local copies, waits for them, and re-layouts  132 us (14%)
  blocking collectives  129 us (13%)
  between operations  18.8 us (2%)
    unnamed x2, blocking collectives  124 us
    reduce_scatter x1, waiting for transfers between devices, body(): lax.psum_scatter(grad_up_w, 'fsdp', scatter_dimension=0, tiled=True)  114 us
    reduce_scatter x1, waiting for transfers between devices, body(): lax.psum_scatter(grad_down_w, 'fsdp', scatter_dimension=0, tiled=True)  113 us
    dynamic_update_slice x4, local copies, waits for them, and re-layouts, attend_forward(): lax.map(one_block, jnp.arange(slots // block, dtype=jnp.int32))  60.5 us
    dot_general x4, matrix products, block_scores(): jnp.einsum('qhd,khd->hqk', query_blk, key_b, preferred_element_type=jnp.f...  47.3 us
    convert_element_type x2, other arithmetic, one_block(): score_b = grad_score.astype(jnp.bfloat16)  42.7 us
    dot_general x2, matrix products, one_block(): jnp.einsum('qhd,khd->hqk', grad_blk, value_b, preferred_element_type=jnp....  36.3 us
    dot_general x4, matrix products, against_cols(): lax.dot_general(left, right, (((1,), (1,)), ((), ())), preferred_element_...  35.1 us
  transfers between devices with their start and end apart: 9, of which 3 were waited for; matrix products, arithmetic and copies ran while one was open for 50% of the time, Pallas kernels for 0%

commit v1 on v0

v1 whole, which is shorter than its diff:
```python
from functools import partial

import jax
import jax.numpy as jnp
from jax import lax
from jax.experimental import pallas as pl
from jax.experimental.pallas import tpu as pltpu
from jax.sharding import PartitionSpec as P

HEADS = 12
HEAD_DIM = 64
HALF = HEAD_DIM // 2
FIRST = 576
CUT = 512
WIDE = 640
NEG = -1e30
EPS = 1e-6
BF = jnp.bfloat16
F32 = jnp.float32
VMEM_LIMIT = 56 * 1024 * 1024
GELU_C = 0.7978845608028654
GELU_A = 0.044715


def nn(a, b):
    return lax.dot_general(a, b, (((1,), (0,)), ((), ())), preferred_element_type=F32)


def nt(a, b):
    return lax.dot_general(a, b, (((1,), (1,)), ((), ())), preferred_element_type=F32)


def tn(a, b):
    return lax.dot_general(a, b, (((0,), (0,)), ((), ())), preferred_element_type=F32)


def params(**kw):
    return pltpu.CompilerParams(vmem_limit_bytes=VMEM_LIMIT, **kw)


def norm_parts(v):
    mean = jnp.mean(v, axis=-1, keepdims=True)
    dev = v - mean
    var = jnp.mean(dev * dev, axis=-1, keepdims=True)
    inv = lax.rsqrt(var + EPS)
    return dev * inv, inv


def lane_partial(v):
    total = v[:, :128]
    for i in range(1, v.shape[1] // 128):
        total = total + v[:, i * 128 : (i + 1) * 128]
    return total


def norm1_kernel(x_ref, gain_ref, shift_ref, a_ref, at_ref):
    xhat, _ = norm_parts(x_ref[...].astype(F32))
    a = (xhat * gain_ref[...] + shift_ref[...]).astype(BF)
    a_ref[...] = a
    at_ref[...] = a.T


def norm1(x, gain, shift):
    slots, width = x.shape
    blk = 256
    return pl.pallas_call(
        norm1_kernel,
        grid=(slots // blk,),
        in_specs=[
            pl.BlockSpec((blk, width), lambda i: (i, 0)),
            pl.BlockSpec((1, width), lambda i: (0, 0)),
            pl.BlockSpec((1, width), lambda i: (0, 0)),
        ],
        out_specs=[
            pl.BlockSpec((blk, width), lambda i: (i, 0)),
            pl.BlockSpec((width, blk), lambda i: (0, i)),
        ],
        out_shape=[
            jax.ShapeDtypeStruct((slots, width), BF),
            jax.ShapeDtypeStruct((width, slots), BF),
        ],
        compiler_params=params(),
        name="norm1",
    )(x, gain, shift)


def qkv_kernel(a_ref, wq_ref, wk_ref, wv_ref, bq_ref, bk_ref, bv_ref, cos_ref, sin_ref, q_ref, k_ref, v_ref):
    heads = wq_ref.shape[1] // HEAD_DIM
    a = a_ref[...]
    cos = cos_ref[...]
    sin = sin_ref[...]
    for w_ref, b_ref, out_ref, scale in ((wq_ref, bq_ref, q_ref, HEAD_DIM**-0.5), (wk_ref, bk_ref, k_ref, 1.0)):
        u = nt(w_ref[...].T, a) + b_ref[...]
        for h in range(heads):
            u1 = u[h * HEAD_DIM : h * HEAD_DIM + HALF]
            u2 = u[h * HEAD_DIM + HALF : (h + 1) * HEAD_DIM]
            c = cos[h * HALF : (h + 1) * HALF]
            s = sin[h * HALF : (h + 1) * HALF]
            out_ref[h * HEAD_DIM : h * HEAD_DIM + HALF, :] = ((u1 * c - u2 * s) * scale).astype(BF)
            out_ref[h * HEAD_DIM + HALF : (h + 1) * HEAD_DIM, :] = ((u1 * s + u2 * c) * scale).astype(BF)
    v_ref[...] = (nt(wv_ref[...].T, a) + bv_ref[...]).astype(BF)


def project(a, w, bias, cos, sin):
    slots, width = a.shape
    cols = 256
    groups = width // cols
    wspec = lambda part: pl.BlockSpec((width, cols), lambda g: (0, part * groups + g))
    bspec = lambda part: pl.BlockSpec((cols, 1), lambda g: (part * groups + g, 0))
    out = pl.BlockSpec((cols, slots), lambda g: (g, 0))
    return pl.pallas_call(
        qkv_kernel,
        grid=(groups,),
        in_specs=[pl.BlockSpec((slots, width), lambda g: (0, 0))]
        + [wspec(i) for i in range(3)]
        + [bspec(i) for i in range(3)]
        + [pl.BlockSpec((cols // 2, slots), lambda g: (g, 0))] * 2,
        out_specs=[out] * 3,
        out_shape=[jax.ShapeDtypeStruct((width, slots), BF)] * 3,
        compiler_params=params(),
        name="qkv",
    )(a, w, w, w, bias, bias, bias, cos, sin)


def second_bias(counts_ref, slots):
    shape = (slots - FIRST, slots - CUT)
    key = lax.broadcasted_iota(jnp.int32, shape, 0) + FIRST
    query = lax.broadcasted_iota(jnp.int32, shape, 1) + CUT
    end0 = counts_ref[0]
    end1 = end0 + counts_ref[1]
    end2 = end1 + counts_ref[2]

    def seg(place):
        return (place >= end0).astype(jnp.int32) + (place >= end1).astype(jnp.int32)

    allowed = ((seg(key) == seg(query)) & (key < end2) & (query < end2)) | (key == query)
    return jnp.where(allowed, 0.0, NEG)


def attend_kernel(counts_ref, q_ref, k_ref, v_ref, o_ref, lse_ref, bias_ref):
    slots = q_ref.shape[1]

    @pl.when(pl.program_id(0) == 0)
    def _():
        bias_ref[...] = second_bias(counts_ref, slots)

    k = k_ref[...].T
    q = q_ref[...]
    v = v_ref[...]

    def part(scores, first, values):
        peak = jnp.max(scores, axis=0, keepdims=True)
        weights = jnp.exp(scores - peak)
        total = jnp.sum(weights, axis=0, keepdims=True)
        wb = weights.astype(BF)
        gap = jnp.zeros((values.shape[1] - wb.shape[0], wb.shape[1]), BF)
        wb = jnp.concatenate([wb, gap] if first else [gap, wb], axis=0)
        mixed = nn(values, wb) * (1.0 / total)
        return mixed, peak + jnp.log(total)

    mixed1, lse1 = part(nn(k[:FIRST], q[:, :WIDE]), True, v[:, :WIDE])
    mixed2, lse2 = part(nn(k[FIRST:], q[:, CUT:]) + bias_ref[...], False, v[:, CUT:])
    edge = lax.broadcasted_iota(jnp.int32, (1, WIDE - CUT), 1) < FIRST - CUT
    for out, one, two in ((o_ref, mixed1, mixed2), (lse_ref.at[0], lse1, lse2)):
        out[:, :CUT] = one[:, :CUT].astype(out.dtype)
        out[:, CUT:WIDE] = jnp.where(edge, one[:, CUT:], two[:, : WIDE - CUT]).astype(out.dtype)
        out[:, WIDE:] = two[:, WIDE - CUT :].astype(out.dtype)


def attend(counts, q, k, v):
    width, slots = q.shape
    head = pl.BlockSpec((HEAD_DIM, slots), lambda h: (h, 0))
    return pl.pallas_call(
        attend_kernel,
        grid=(width // HEAD_DIM,),
        in_specs=[pl.BlockSpec(memory_space=pltpu.SMEM)] + [head] * 3,
        out_specs=[head, pl.BlockSpec((1, 1, slots), lambda h: (h, 0, 0))],
        out_shape=[
            jax.ShapeDtypeStruct((width, slots), BF),
            jax.ShapeDtypeStruct((width // HEAD_DIM, 1, slots), F32),
        ],
        scratch_shapes=[pltpu.VMEM((slots - FIRST, slots - CUT), F32)],
        compiler_params=params(),
        name="attend",
    )(counts, q, k, v)


def attend_back_kernel(
    counts_ref, q_ref, k_ref, v_ref, o_ref, do_ref, lse_ref, cos_ref, sin_ref, place_ref,
    dq_ref, dk_ref, dv_ref, bq_ref, bk_ref, bv_ref, fc_ref, fr_ref, bias_ref,
):
    slots = q_ref.shape[1]

    @pl.when(pl.program_id(0) == 0)
    def _():
        bias_ref[...] = second_bias(counts_ref, slots)

    kt = k_ref[...]
    k = kt.T
    v = v_ref[...].T
    q = q_ref[...]
    do = do_ref[...]
    lse = lse_ref[0]
    delta = jnp.sum(do.astype(F32) * o_ref[...].astype(F32), axis=0, keepdims=True)
    lane1 = lax.broadcasted_iota(jnp.int32, (1, WIDE), 1)
    lane2 = lax.broadcasted_iota(jnp.int32, (1, slots - CUT), 1)
    lse1 = jnp.where(lane1 < FIRST, lse[:, :WIDE], -NEG)
    lse2 = jnp.where(lane2 >= FIRST - CUT, lse[:, CUT:], -NEG)

    def part(scores, grads, queries, outs, keys, delta_row, first):
        prob = jnp.exp(scores)
        ds = (prob * (grads - delta_row)).astype(BF)
        pb = prob.astype(BF)
        gap = jnp.zeros((keys.shape[1] - pb.shape[0], pb.shape[1]), BF)
        pb = jnp.concatenate([pb, gap] if first else [gap, pb], axis=0)
        ds = jnp.concatenate([ds, gap] if first else [gap, ds], axis=0)
        return nn(keys, ds), nt(queries, ds), nt(outs, pb)

    grads1 = part(
        nn(k[:FIRST], q[:, :WIDE]) - lse1, nn(v[:FIRST], do[:, :WIDE]),
        q[:, :WIDE], do[:, :WIDE], kt[:, :WIDE], delta[:, :WIDE], True,
    )
    grads2 = part(
        nn(k[FIRST:], q[:, CUT:]) + bias_ref[...] - lse2, nn(v[FIRST:], do[:, CUT:]),
        q[:, CUT:], do[:, CUT:], kt[:, CUT:], delta[:, CUT:], False,
    )
    dq, dk, dv = (
        jnp.concatenate([one[:, :CUT], one[:, CUT:] + two[:, : WIDE - CUT], two[:, WIDE - CUT :]], axis=1)
        for one, two in zip(grads1, grads2)
    )
    scale = HEAD_DIM**-0.5
    cos = cos_ref[...]
    sin = sin_ref[...]
    dangle = None
    for r, rot, out, bias_out in ((dq * scale, q.astype(F32) * (1.0 / scale), dq_ref, bq_ref), (dk, kt.astype(F32), dk_ref, bk_ref)):
        r1, r2 = r[:HALF], r[HALF:]
        term = r2 * rot[:HALF] - r1 * rot[HALF:]
        dangle = term if dangle is None else dangle + term
        g1 = (r1 * cos + r2 * sin).astype(BF)
        g2 = (r2 * cos - r1 * sin).astype(BF)
        out[:HALF, :] = g1
        out[HALF:, :] = g2
        bias_out[:HALF, :] = lane_partial(g1.astype(F32))
        bias_out[HALF:, :] = lane_partial(g2.astype(F32))
    dvb = dv.astype(BF)
    dv_ref[...] = dvb
    bv_ref[...] = lane_partial(dvb.astype(F32))
    fc_ref[...] = lane_partial(dangle * place_ref[0:1, :])
    fr_ref[...] = lane_partial(dangle * place_ref[1:2, :])


def attend_back(counts, q, k, v, o, do, lse, cos, sin, places):
    width, slots = q.shape
    heads = width // HEAD_DIM
    head = pl.BlockSpec((HEAD_DIM, slots), lambda h: (h, 0))
    half = pl.BlockSpec((HALF, slots), lambda h: (h, 0))
    return pl.pallas_call(
        attend_back_kernel,
        grid=(heads,),
        in_specs=[pl.BlockSpec(memory_space=pltpu.SMEM)]
        + [head] * 5
        + [pl.BlockSpec((1, 1, slots), lambda h: (h, 0, 0)), half, half]
        + [pl.BlockSpec((2, slots), lambda h: (0, 0))],
        out_specs=[head] * 3
        + [pl.BlockSpec((HEAD_DIM, 128), lambda h: (h, 0))] * 3
        + [pl.BlockSpec((HALF, 128), lambda h: (h, 0))] * 2,
        out_shape=[jax.ShapeDtypeStruct((width, slots), BF)] * 3
        + [jax.ShapeDtypeStruct((width, 128), F32)] * 3
        + [jax.ShapeDtypeStruct((width // 2, 128), F32)] * 2,
        scratch_shapes=[pltpu.VMEM((slots - FIRST, slots - CUT), F32)],
        compiler_params=params(),
        name="attend_back",
    )(counts, q, k, v, o, do, lse, cos, sin, places)


def out_kernel(o_ref, x_ref, w_ref, b_ref, gain_ref, shift_ref, h_ref, c_ref, ct_ref):
    h = x_ref[...].astype(F32) + (nn(o_ref[...].T, w_ref[...]) + b_ref[...])
    h_ref[...] = h
    xhat, _ = norm_parts(h)
    c = (xhat * gain_ref[...] + shift_ref[...]).astype(BF)
    c_ref[...] = c
    ct_ref[...] = c.T


def out_project(o, x, w, b, gain, shift):
    slots, width = x.shape
    blk = 256
    row = pl.BlockSpec((1, width), lambda i: (0, 0))
    rows = pl.BlockSpec((blk, width), lambda i: (i, 0))
    cols = pl.BlockSpec((width, blk), lambda i: (0, i))
    return pl.pallas_call(
        out_kernel,
        grid=(slots // blk,),
        in_specs=[cols, rows, pl.BlockSpec((width, width), lambda i: (0, 0)), row, row, row],
        out_specs=[rows, rows, cols],
        out_shape=[
            jax.ShapeDtypeStruct((slots, width), F32),
            jax.ShapeDtypeStruct((slots, width), BF),
            jax.ShapeDtypeStruct((width, slots), BF),
        ],
        compiler_params=params(),
        name="out_project",
    )(o, x, w, b, gain, shift)


def mlp_kernel(c_ref, ct_ref, dy_ref, h_ref, w1_ref, b1_ref, w2_ref, b2_ref, y_ref, dc_ref, g1_ref, g2_ref, gb1_ref, y_acc, hb_scr, dp_scr):
    slots = c_ref.shape[0]
    tile = 256

    @pl.when(pl.program_id(0) == 0)
    def _():
        y_acc[...] = h_ref[...] + b2_ref[...]
        dc_ref[...] = jnp.zeros_like(dc_ref)

    gb1_ref[...] = jnp.zeros_like(gb1_ref)

    def step(i, _):
        rows = pl.ds(pl.multiple_of(i * tile, tile), tile)
        pre = nn(c_ref[rows, :], w1_ref[...]) + b1_ref[...]
        square = pre * pre
        th = jnp.tanh(GELU_C * (pre + GELU_A * (pre * square)))
        cdf = 0.5 * (1.0 + th)
        hb = (pre * cdf).astype(BF)
        slope = cdf + 0.5 * pre * (1.0 - th * th) * (GELU_C * (1.0 + (3.0 * GELU_A) * square))
        hb_scr[rows, :] = hb
        y_acc[rows, :] += nn(hb, w2_ref[...])
        dpre = (nt(dy_ref[rows, :], w2_ref[...]) * slope).astype(BF)
        dp_scr[rows, :] = dpre
        dc_ref[rows, :] += nt(dpre, w1_ref[...])
        gb1_ref[...] += jnp.sum(dpre.astype(F32), axis=0, keepdims=True)
        return 0

    lax.fori_loop(0, slots // tile, step, 0)
    g1_ref[...] = nn(ct_ref[...], dp_scr[...]).astype(g1_ref.dtype)
    g2_ref[...] = tn(hb_scr[...], dy_ref[...]).astype(g2_ref.dtype)

    @pl.when(pl.program_id(0) == pl.num_programs(0) - 1)
    def _():
        y_ref[...] = y_acc[...].astype(BF)


def mlp(c, ct, dy, h, w1, b1, w2, b2):
    slots, width = c.shape
    hidden = w1.shape[1]
    blk = 512
    whole = lambda r, k: pl.BlockSpec((r, k), lambda j: (0, 0))
    return pl.pallas_call(
        mlp_kernel,
        grid=(hidden // blk,),
        in_specs=[
            whole(slots, width),
            whole(width, slots),
            whole(slots, width),
            whole(slots, width),
            pl.BlockSpec((width, blk), lambda j: (0, j)),
            pl.BlockSpec((1, blk), lambda j: (0, j)),
            pl.BlockSpec((blk, width), lambda j: (j, 0)),
            whole(1, width),
        ],
        out_specs=[
            whole(slots, width),
            whole(slots, width),
            pl.BlockSpec((width, blk), lambda j: (0, j)),
            pl.BlockSpec((blk, width), lambda j: (j, 0)),
            pl.BlockSpec((1, blk), lambda j: (0, j)),
        ],
        out_shape=[
            jax.ShapeDtypeStruct((slots, width), BF),
            jax.ShapeDtypeStruct((slots, width), F32),
            jax.ShapeDtypeStruct((width, hidden), BF),
            jax.ShapeDtypeStruct((hidden, width), BF),
            jax.ShapeDtypeStruct((1, hidden), F32),
        ],
        scratch_shapes=[
            pltpu.VMEM((slots, width), F32),
            pltpu.VMEM((slots, blk), BF),
            pltpu.VMEM((slots, blk), BF),
        ],
        compiler_params=params(),
        name="mlp",
    )(c, ct, dy, h, w1, b1, w2, b2)


def norm_back(grad, v, gain):
    xhat, inv = norm_parts(v)
    g = grad * gain
    lead = jnp.mean(g, axis=-1, keepdims=True)
    slope = jnp.mean(g * xhat, axis=-1, keepdims=True)
    return (g - lead - xhat * slope) * inv, jnp.sum(grad * xhat, axis=0, keepdims=True), jnp.sum(grad, axis=0, keepdims=True)


def out_back_kernel(dc_ref, h_ref, dy_ref, o_ref, w_ref, gain_ref, dh_ref, do_ref, gw_ref, sums_ref, acc_ref):
    i = pl.program_id(0)

    @pl.when(i == 0)
    def _():
        acc_ref[...] = jnp.zeros_like(acc_ref)
        sums_ref[...] = jnp.zeros_like(sums_ref)

    dy = dy_ref[...].astype(F32)
    part, dgain, dshift = norm_back(dc_ref[...], h_ref[...], gain_ref[...])
    dh = dy + part
    dh_ref[...] = dh
    dhb = dh.astype(BF)
    do_ref[...] = nt(w_ref[...], dhb).astype(BF)
    acc_ref[...] += nn(o_ref[...], dhb)
    sums_ref[0:1, :] += dgain
    sums_ref[1:2, :] += dshift
    sums_ref[2:3, :] += jnp.sum(dh, axis=0, keepdims=True)
    sums_ref[3:4, :] += jnp.sum(dy, axis=0, keepdims=True)

    @pl.when(i == pl.num_programs(0) - 1)
    def _():
        gw_ref[...] = acc_ref[...].astype(gw_ref.dtype)


def out_back(dc, h, dy, o, w, gain):
    slots, width = h.shape
    blk = 256
    rows = pl.BlockSpec((blk, width), lambda i: (i, 0))
    cols = pl.BlockSpec((width, blk), lambda i: (0, i))
    whole = lambda r, k: pl.BlockSpec((r, k), lambda i: (0, 0))
    return pl.pallas_call(
        out_back_kernel,
        grid=(slots // blk,),
        in_specs=[rows, rows, rows, cols, whole(width, width), whole(1, width)],
        out_specs=[rows, cols, whole(width, width), whole(8, width)],
        out_shape=[
            jax.ShapeDtypeStruct((slots, width), F32),
            jax.ShapeDtypeStruct((width, slots), BF),
            jax.ShapeDtypeStruct((width, width), BF),
            jax.ShapeDtypeStruct((8, width), F32),
        ],
        scratch_shapes=[pltpu.VMEM((width, width), F32)],
        compiler_params=params(),
        name="out_back",
    )(dc, h, dy, o, w, gain)


def qkv_back_kernel(at_ref, dqkv_ref, w_ref, x_ref, dh_ref, gain_ref, gw_ref, dx_ref, sums_ref, acc_ref):
    j = pl.program_id(0)

    @pl.when(j == 0)
    def _():
        acc_ref[...] = jnp.zeros_like(acc_ref)

    d = dqkv_ref[...]
    gw_ref[...] = nt(at_ref[...], d).astype(gw_ref.dtype)
    acc_ref[...] += nn(w_ref[...], d)

    @pl.when(j == pl.num_programs(0) - 1)
    def _():
        sums_ref[...] = jnp.zeros_like(sums_ref)
        tile = 256
        for i in range(x_ref.shape[0] // tile):
            rows = slice(i * tile, (i + 1) * tile)
            da = acc_ref[:, rows].T
            part, dgain, dshift = norm_back(da, x_ref[rows, :].astype(F32), gain_ref[...])
            dx_ref[rows, :] = (dh_ref[rows, :] + part).astype(BF)
            sums_ref[0:1, :] += dgain
            sums_ref[1:2, :] += dshift


def qkv_back(at, dqkv, w, x, dh, gain):
    slots, width = x.shape
    outs = w.shape[1]
    blk = 768
    whole = lambda r, k: pl.BlockSpec((r, k), lambda j: (0, 0))
    return pl.pallas_call(
        qkv_back_kernel,
        grid=(outs // blk,),
        in_specs=[
            whole(width, slots),
            pl.BlockSpec((blk, slots), lambda j: (j, 0)),
            pl.BlockSpec((width, blk), lambda j: (0, j)),
            whole(slots, width),
            whole(slots, width),
            whole(1, width),
        ],
        out_specs=[pl.BlockSpec((width, blk), lambda j: (0, j)), whole(slots, width), whole(8, width)],
        out_shape=[
            jax.ShapeDtypeStruct((width, outs), BF),
            jax.ShapeDtypeStruct((slots, width), BF),
            jax.ShapeDtypeStruct((8, width), F32),
        ],
        scratch_shapes=[pltpu.VMEM((width, slots), F32)],
        compiler_params=params(),
        name="qkv_back",
    )(at, dqkv, w, x, dh, gain)


def body(
    tokens, cotangent, image_counts, patch_rows, patch_cols, ln1_gain, ln1_bias, qkv_weight, qkv_bias, rope_freqs,
    out_weight, out_bias, ln2_gain, ln2_bias, fc1_weight, fc1_bias, fc2_weight, fc2_bias,
):
    x = tokens[0]
    dy = cotangent[0]
    counts = image_counts[0]
    width = x.shape[1]
    small = (ln1_gain, ln1_bias, qkv_bias, rope_freqs, out_bias, ln2_gain, ln2_bias, fc1_bias, fc2_bias)
    sizes = [s.shape[0] for s in small]
    gather = partial(lax.all_gather, axis_name="fsdp", axis=0, tiled=True)
    packed = lax.all_gather(jnp.concatenate(small), "fsdp", axis=0)
    vectors = []
    at = 0
    for size in sizes:
        vectors.append(packed[:, at : at + size].reshape(-1).astype(F32))
        at += size
    gain1, shift1, b_qkv, freqs, b_out, gain2, shift2, b1, b2 = vectors
    w_qkv = gather(qkv_weight)
    w_out = gather(out_weight)
    w1 = gather(fc1_weight)
    w2 = gather(fc2_weight)

    row = lambda v: v[None, :]
    a, a_t = norm1(x, row(gain1), row(shift1))
    places = jnp.concatenate([patch_cols, patch_rows], axis=0).astype(F32)
    half = freqs.shape[0] // 2
    angle = freqs[:half, None] * places[0:1] + freqs[half:, None] * places[1:2]
    cos = jnp.cos(angle)
    sin = jnp.sin(angle)
    q, k, v = project(a, w_qkv, b_qkv[:, None], cos, sin)
    o, lse = attend(counts, q, k, v)
    h, c, c_t = out_project(o, x, w_out, row(b_out), row(gain2), row(shift2))
    y, dc, g_w1, g_w2, g_b1 = mlp(c, c_t, dy, h, w1, row(b1), w2, row(b2))
    dh, do, g_wout, sums2 = out_back(dc, h, dy, o, w_out, row(gain2))
    dq, dk, dv, s_bq, s_bk, s_bv, s_fc, s_fr = attend_back(counts, q, k, v, o, do, lse, cos, sin, places)
    dqkv = jnp.concatenate([dq, dk, dv], axis=0)
    g_wqkv, dx, sums1 = qkv_back(a_t, dqkv, w_qkv, x, dh, row(gain1))

    scatter = partial(lax.psum_scatter, axis_name="fsdp", scatter_dimension=0, tiled=True)
    both = lambda g: lax.psum(scatter(g), "rep").astype(F32)
    g_bqkv = jnp.sum(jnp.concatenate([s_bq, s_bk, s_bv], axis=0), axis=1)
    g_freq = jnp.sum(jnp.concatenate([s_fc, s_fr], axis=0), axis=1)
    small_grads = (sums1[0], sums1[1], g_bqkv, g_freq, sums2[2], sums2[0], sums2[1], g_b1[0], sums2[3])
    shards = mesh_size = packed.shape[0]
    block = jnp.concatenate([g.reshape(shards, -1) for g in small_grads], axis=1)
    total = lax.psum(block, ("rep", "fsdp"))
    mine = lax.dynamic_index_in_dim(total, lax.axis_index("fsdp"), 0, keepdims=False)
    outs = []
    at = 0
    for size in sizes:
        outs.append(mine[at : at + size])
        at += size
    s_gain1, s_shift1, s_bqkv, s_freq, s_bout, s_gain2, s_shift2, s_b1, s_b2 = outs
    return (
        y[None], dx[None], s_gain1, s_shift1, both(g_wqkv), s_bqkv, s_freq, both(g_wout), s_bout,
        s_gain2, s_shift2, both(g_w1), s_b1, both(g_w2), s_b2,
    )


def solution(mesh):
    row = P(("rep", "fsdp"), None)
    rows = P(("rep", "fsdp"), None, None)
    vec = P("fsdp")
    mat = P("fsdp", None)
    in_specs = (rows, rows, row, row, row, vec, vec, mat, vec, vec, mat, vec, vec, vec, mat, vec, mat, vec)
    out_specs = (rows, rows, vec, vec, mat, vec, vec, mat, vec, vec, vec, mat, vec, mat, vec)
    return jax.shard_map(body, mesh=mesh, in_specs=in_specs, out_specs=out_specs, check_vma=False)
```

time: 970 us -> 611 us (0.63); the launches traced: 956 us -> 611 us
  matrix products: 270 us -> 0 us
  Pallas kernels: 0 us -> 138 us
  other arithmetic: 142 us -> 17.6 us
  local copies, waits for them, and re-layouts: 132 us -> 18.1 us
  waiting for transfers between devices: 257 us -> 318 us
  blocking collectives: 129 us -> 104 us
    dot_general x26 -> x0, matrix products: 270 us -> none  [the longest x4 47.3 us: block_scores(): jnp.einsum('qhd,khd->hqk', query_blk, key_b, preferred_element_type=jnp.f...]
    pallas_call x0 -> x8, Pallas kernels: none -> 138 us  [the longest x1 49.1 us: mlp(): pl.pallas_call(mlp_kernel, grid=(hidden // blk,), in_specs=[whole(slots,...]
    all_gather x4, waiting for transfers between devices: 0.04 us -> 77.1 us  [the longest x1 54.1 us: body(): w2 = gather(fc2_weight)]
    dynamic_update_slice x4 -> x0, local copies, waits for them, and re-layouts: 60.5 us -> none  [attend_forward(): lax.map(one_block, jnp.arange(slots // block, dtype=jnp.int32))]
    convert_element_type x30 -> x8, other arithmetic: 65.6 us -> 5.38 us  [the longest x4 5.14 us: body(): both = lambda g: lax.psum(scatter(g), 'rep').astype(F32)]
    unnamed x2 -> x1, blocking collectives: 124 us -> 63.9 us
    reduce_sum x13 -> x2, other arithmetic: 47.7 us -> 0.55 us  [the longest x1 0.38 us: body(): g_bqkv = jnp.sum(jnp.concatenate([s_bq, s_bk, s_bv], axis=0), axis=1)]
    psum x1, blocking collectives: 4.98 us -> 40.3 us  [body(): total = lax.psum(block, ('rep', 'fsdp'))]
  transfers between devices with their start and end apart: 9 -> 9, of which waited for: 3 -> 6; matrix products, arithmetic and copies ran while one was open for 50% -> 5% of each run, Pallas kernels for 0% -> 13%
where the time goes in v1:
time: 611 us
  waiting for transfers between devices  318 us (52%)
  Pallas kernels  138 us (23%)
  blocking collectives  104 us (17%)
  local copies, waits for them, and re-layouts  18.1 us (3%)
  other arithmetic  17.6 us (3%)
  between operations  14.7 us (2%)
    reduce_scatter x4, waiting for transfers between devices, body(): both = lambda g: lax.psum(scatter(g), 'rep').astype(F32)  237 us
    unnamed x1, blocking collectives  63.9 us
    all_gather x1, waiting for transfers between devices, body(): w2 = gather(fc2_weight)  54.1 us
    pallas_call x1, Pallas kernels, mlp(): pl.pallas_call(mlp_kernel, grid=(hidden // blk,), in_specs=[whole(slots,...  49.1 us
    psum x1, blocking collectives, body(): total = lax.psum(block, ('rep', 'fsdp'))  40.3 us
    pallas_call x1, Pallas kernels, attend_back(): pl.pallas_call(attend_back_kernel, grid=(heads,), in_specs=[pl.BlockSpec(...  25.7 us
    all_gather x1, waiting for transfers between devices, body(): w1 = gather(fc1_weight)  23 us
    pallas_call x1, Pallas kernels, qkv_back(): pl.pallas_call(qkv_back_kernel, grid=(outs // blk,), in_specs=[whole(widt...  16.6 us
  transfers between devices with their start and end apart: 9, of which 6 were waited for; matrix products, arithmetic and copies ran while one was open for 5% of the time, Pallas kernels for 13%

profile of v1, /device:TPU:0, one launch (start us, length us, event | category | flops | bytes accessed | tf_op | source)
XLA Modules:
  0.0 610.6 jit_solution(16638454226874715771)
XLA Ops:
  10.0 1.2 dynamic-slice
  11.9 6.1 concatenate.18
  18.3 63.9 %all-reduce = bf16[10752]{0:T(1024)(128)(2,1)S(1)} all-reduce(bf16[10752]{0:T(1024)(128)(2,1)S(1)} %dynamic-update-slice), channel_id=2, replica_groups=mesh['rep'=2,'fsdp'=16] {'fsdp'}, use_global_device_ids=true, to_apply=%add | all-reduce | flops 10752 | bytes 43008
  83.9 1.5 reshape.171.bq_ref.bk_ref.bv_ref
  88.8 4.5 norm1.1
  93.4 7.1 %fusion = (f32[384,1024]{1,0:T(8,128)}, f32[384,1024]{1,0:T(8,128)}) fusion(f32[1024]{0:T(1024)S(1)} %bitcast.30, f32[384]{0:T(512)S(1)} %slice.125, f32[1024]{0:T(1024)S(1)} %bitcast.29, f32[384]{0:T(512)S(1)} %slice.122), kind=kLoop, calls=%fused_computation.2 | loop fusion | flops 1179648 | bytes 3156992 | tf_op jit(solution)/shard_map/sin | solution.py:521
  100.4 8.5 %qkv.1 = (bf16[768,1024]{1,0:T(8,128)(2,1)}, bf16[768,1024]{1,0:T(8,128)(2,1)}, bf16[768,1024]{1,0:T(8,128)(2,1)}) custom-call(bf16[1024,768]{1,0:T(8,128)(2,1)} %get-tuple-element.45.a_ref, bf16[768,2304]{1,0:T(8,128)(2,1)} %all-gather.6.cloned.1.call-done.wq_ref.wk_ref.wv_ref.w_ref, ...), custom_call_target="tpu_custom_call" | custom-call | tf_op jit(solution)/shard_map/qkv/pallas_call | solution.py:111
  108.9 16.4 %attend.1 = (bf16[768,1024]{1,0:T(8,128)(2,1)}, f32[12,1,1024]{2,1,0:T(1,128)}) custom-call(s32[3]{0:T(128)} %bitcast.31, bf16[768,1024]{1,0:T(8,128)(2,1)} %get-tuple-element.46.q_ref, bf16[768,1024]{1,0:T(8,128)(2,1)} %get-tuple-element.47.k_ref, bf16[768,1024]{1,0:T(8,128)(2,1)} %get-tuple-element.48.v_ref), custom_call_target="tpu_custom_call" | custom-call | tf_op jit(solution)/shard_map/attend/pallas_call | solution.py:173
  125.3 6.6 %out_project.1 = (f32[1024,768]{1,0:T(8,128)}, bf16[1024,768]{1,0:T(8,128)(2,1)}, bf16[768,1024]{1,0:T(8,128)(2,1)}) custom-call(bf16[768,1024]{1,0:T(8,128)(2,1)} %get-tuple-element.49.o_ref, bf16[1024,768]{1,0:T(8,128)(2,1)} %bitcast.25, bf16[768,768]{1,0:T(8,128)(2,1)} %all-gather.8.cloned.1.call-done.w_ref, f32[1,768]{1,0:T(1,128)} %reshape.160.b_ref, ...), custom_call_target="tpu_custom_call" | custom-call | tf_op jit(solution)/shard_map/out_project/pallas_call | solution.py:291
  132.0 23.0 %all-gather.10.cloned.1.call-done.w1_ref = bf16[768,3072]{1,0:T(8,128)(2,1)} async-done(((bf16[48,3072]{1,0:T(8,128)(2,1)}), bf16[768,3072]{1,0:T(8,128)(2,1)}) %all-gather.10.cloned.1.call-update) | async-done | bytes 4718608 | tf_op jit(solution)/shard_map/all_gather | solution.py:512
  155.0 54.1 %all-gather.12.cloned.1.call-done.w2_ref = bf16[3072,768]{1,0:T(8,128)(2,1)} async-done(((bf16[192,768]{1,0:T(8,128)(2,1)}), bf16[3072,768]{1,0:T(8,128)(2,1)}) %all-gather.12.cloned.1.call-update) | async-done | bytes 4718608 | tf_op jit(solution)/shard_map/all_gather | solution.py:513
  209.1 49.1 %mlp.1 = (bf16[1024,768]{1,0:T(8,128)(2,1)}, f32[1024,768]{1,0:T(8,128)}, bf16[768,3072]{1,0:T(8,128)(2,1)}, bf16[3072,768]{1,0:T(8,128)(2,1)}, f32[1,3072]{1,0:T(1,128)}) custom-call(bf16[1024,768]{1,0:T(8,128)(2,1)} %get-tuple-element.50.c_ref, bf16[768,1024]{1,0:T(8,128)(2,1)} %get-tuple-element.51.ct_ref, bf16[1024,768]{1,0:T(8,128)(2,1)} %bitcast.27, ...), custom_call_target="tpu_custom_call" | custom-call | tf_op jit(solution)/shard_map/mlp/pallas_call | solution.py:347
  258.2 10.2 %out_back.1 = (f32[1024,768]{1,0:T(8,128)}, bf16[768,1024]{1,0:T(8,128)(2,1)}, bf16[768,768]{1,0:T(8,128)(2,1)}, f32[8,768]{1,0:T(8,128)}) custom-call(f32[1024,768]{1,0:T(8,128)} %get-tuple-element.55.dc_ref, f32[1024,768]{1,0:T(8,128)} %get-tuple-element.52.h_ref, bf16[1024,768]{1,0:T(8,128)(2,1)} %bitcast.28, bf16[768,1024]{1,0:T(8,128)(2,1)} %get-tuple-element.49.o_ref, ...), custom_call_target="tpu_custom_call" | custom-call | tf_op jit(solution)/shard_map/out_back/pallas_call | solution.py:423
  268.7 25.7 %attend_back.1 = (bf16[768,1024]{1,0:T(8,128)(2,1)}, bf16[768,1024]{1,0:T(8,128)(2,1)}, bf16[768,1024]{1,0:T(8,128)(2,1)}, f32[768,128]{1,0:T(8,128)}, f32[768,1...) custom-call(s32[3]{0:T(128)} %bitcast.32, ...), custom_call_target="tpu_custom_call" | custom-call | tf_op jit(solution)/shard_map/attend_back/pallas_call | solution.py:257
  294.4 4.0 pad_maximum_fusion.dqkv_ref
  298.3 16.6 %qkv_back.1 = (bf16[768,2304]{1,0:T(8,128)(2,1)}, bf16[1024,768]{1,0:T(8,128)(2,1)}, f32[8,768]{1,0:T(8,128)}) custom-call(bf16[768,1024]{1,0:T(8,128)(2,1)} %get-tuple-element.54.at_ref, bf16[2304,1024]{1,0:T(8,128)(2,1)} %pad_maximum_fusion.dqkv_ref, bf16[768,2304]{1,0:T(8,128)(2,1)} %all-gather.6.cloned.1.call-done.wq_ref.wk_ref.wv_ref.w_ref, ...), custom_call_target="tpu_custom_call" | custom-call | tf_op jit(solution)/shard_map/qkv_back/pallas_call | solution.py:469
  316.5 8.6 %reduce-scatter.7.cloned.1.call-done = bf16[48,768]{1,0:T(8,128)(2,1)} async-done(((bf16[768,768]{1,0:T(8,128)(2,1)}), bf16[48,768]{1,0:T(8,128)(2,1)}) %reduce-scatter.7.cloned.1.call-update) | async-done | bytes 73744 | tf_op jit(solution)/shard_map/reduce_scatter | solution.py:532
  325.2 70.7 %reduce-scatter.5.cloned.1.call-done = bf16[48,2304]{1,0:T(8,128)(2,1)} async-done(((bf16[768,2304]{1,0:T(8,128)(2,1)}), bf16[48,2304]{1,0:T(8,128)(2,1)}) %reduce-scatter.5.cloned.1.call-update) | async-done | bytes 221200 | tf_op jit(solution)/shard_map/reduce_scatter | solution.py:532
  395.9 78.3 %reduce-scatter.11.cloned.1.call-done = bf16[192,768]{1,0:T(8,128)(2,1)} async-done(((bf16[3072,768]{1,0:T(8,128)(2,1)}), bf16[192,768]{1,0:T(8,128)(2,1)}) %reduce-scatter.11.cloned.1.call-update) | async-done | bytes 294928 | tf_op jit(solution)/shard_map/reduce_scatter | solution.py:532
  474.2 79.0 %reduce-scatter.9.cloned.1.call-done = bf16[48,3072]{1,0:T(8,128)(2,1)} async-done(((bf16[768,3072]{1,0:T(8,128)(2,1)}), bf16[48,3072]{1,0:T(8,128)(2,1)}) %reduce-scatter.9.cloned.1.call-update) | async-done | bytes 294928 | tf_op jit(solution)/shard_map/reduce_scatter | solution.py:532
  554.0 0.8 slice_reduce_fusion.4
  556.8 40.3 %psum.35 = f32[16,672]{1,0:T(8,128)S(1)} all-reduce(f32[16,672]{1,0:T(8,128)S(1)} %concatenate.23), channel_id=1, replica_groups=mesh['rep'=2,'fsdp'=16] {'rep','fsdp'}, use_global_device_ids=true, to_apply=%region_2.0 | all-reduce | flops 10752 | bytes 86016 | tf_op jit(solution)/shard_map/psum | solution.py:538
  598.9 1.9 convert_element_type.143
  600.8 1.8 convert_element_type.144
  (83 shorter events, 15.9 us)
Async XLA Ops:
  7.2 93.2 %all-gather.6.cloned.1.call-start = ((), (), s32[]{:S(2)}) async-start(), calls=%async_computation.4 | async-start | bytes 3760128 | tf_op jit(solution)/shard_map/all_gather | solution.py:510
  7.9 117.4 %all-gather.8.cloned.1.call-start = ((), (), s32[]{:S(2)}) async-start(), calls=%async_computation.5 | async-start | bytes 1253376 | tf_op jit(solution)/shard_map/all_gather | solution.py:511
  8.7 146.3 %all-gather.10.cloned.1.call-start = ((), (), s32[]{:S(2)}) async-start(), calls=%async_computation.6 | async-start | bytes 5013504 | tf_op jit(solution)/shard_map/all_gather | solution.py:512
  9.4 199.7 %all-gather.12.cloned.1.call-start = ((), (), s32[]{:S(2)}) async-start(), calls=%async_computation.7 | async-start | bytes 5013504 | tf_op jit(solution)/shard_map/all_gather | solution.py:513
  10.0 315.2 %reduce-scatter.7.cloned.1.call-start = ((), (), s32[]{:S(2)}) async-start(), calls=%async_computation.9 | async-start | bytes 1253376 | tf_op jit(solution)/shard_map/reduce_scatter | solution.py:532
  18.3 75.0 %copy-start.10 = (s32[1,1024]{1,0:T(1,128)S(1)}, s32[1,1024]{1,0:T(1,128)}, u32[]{:S(2)}) copy-start(s32[1,1024]{1,0:T(1,128)} %param.21) | copy-start | bytes 12292
  18.3 75.0 %copy-start.11 = (s32[1,1024]{1,0:T(1,128)S(1)}, s32[1,1024]{1,0:T(1,128)}, u32[]{:S(2)}) copy-start(s32[1,1024]{1,0:T(1,128)} %param.22) | copy-start | bytes 12292
  93.3 7.1 %copy-start.6 = (f32[2,1024]{1,0:T(2,128)}, f32[2,1024]{1,0:T(2,128)S(1)}, u32[]{:S(2)}) copy-start(f32[2,1024]{1,0:T(2,128)S(1)} %add_convert_fusion.place_ref) | copy-start | bytes 24580
  268.4 127.5 %reduce-scatter.5.cloned.1.call-start = ((), (), s32[]{:S(2)}) async-start(), calls=%async_computation.8 | async-start | bytes 3760128 | tf_op jit(solution)/shard_map/reduce_scatter | solution.py:532
  314.9 159.3 %reduce-scatter.11.cloned.1.call-start = ((), (), s32[]{:S(2)}) async-start(), calls=%async_computation.11 | async-start | bytes 5013504 | tf_op jit(solution)/shard_map/reduce_scatter | solution.py:532
  315.7 237.6 %reduce-scatter.9.cloned.1.call-start = ((), (), s32[]{:S(2)}) async-start(), calls=%async_computation.10 | async-start | bytes 5013504 | tf_op jit(solution)/shard_map/reduce_scatter | solution.py:532
  315.7 237.5 %copy-start.4 = (f32[384,128]{1,0:T(8,128)S(1)}, f32[384,128]{1,0:T(8,128)}, u32[]{:S(2)}) copy-start(f32[384,128]{1,0:T(8,128)} %get-tuple-element.67) | copy-start | bytes 589828
  315.8 237.5 %copy-start.5 = (f32[384,128]{1,0:T(8,128)S(1)}, f32[384,128]{1,0:T(8,128)}, u32[]{:S(2)}) copy-start(f32[384,128]{1,0:T(8,128)} %get-tuple-element.68) | copy-start | bytes 589828
  316.4 237.1 %copy-start = (f32[768,128]{1,0:T(8,128)S(1)}, f32[768,128]{1,0:T(8,128)}, u32[]{:S(2)}) copy-start(f32[768,128]{1,0:T(8,128)} %get-tuple-element.64) | copy-start | bytes 1179652
  316.5 237.1 %copy-start.1 = (f32[768,128]{1,0:T(8,128)S(1)}, f32[768,128]{1,0:T(8,128)}, u32[]{:S(2)}) copy-start(f32[768,128]{1,0:T(8,128)} %get-tuple-element.65) | copy-start | bytes 1179652
  316.5 237.1 %copy-start.2 = (f32[768,128]{1,0:T(8,128)S(1)}, f32[768,128]{1,0:T(8,128)}, u32[]{:S(2)}) copy-start(f32[768,128]{1,0:T(8,128)} %get-tuple-element.66) | copy-start | bytes 1179652
  316.5 238.6 %copy-start.9 = (f32[8,768]{1,0:T(8,128)S(1)}, f32[8,768]{1,0:T(8,128)}, u32[]{:S(2)}) copy-start(f32[8,768]{1,0:T(8,128)} %get-tuple-element.69) | copy-start | bytes 73732
  316.5 239.4 %copy-start.8 = (f32[1,3072]{1,0:T(1,128)S(1)}, f32[1,3072]{1,0:T(1,128)}, u32[]{:S(2)}) copy-start(f32[1,3072]{1,0:T(1,128)} %get-tuple-element.70) | copy-start | bytes 36868
  316.5 282.4 %all-reduce.4.cloned.1.call-start = ((), (), s32[]{:S(2)}) async-start(), calls=%async_computation.12 | async-start | bytes 1769472 | tf_op jit(solution)/shard_map/psum | solution.py:532
  598.9 3.7 copy-start.3
  598.9 4.5 copy-start.7
Sparse Core Ops, SparseCore 0:
  10.3 50.2 all-gather.5
  62.9 37.3 all-gather.7
  102.6 52.3 all-gather.9
  157.1 51.9 all-gather.11
  268.5 56.6 reduce-scatter.6
  328.9 66.9 reduce-scatter.4
  399.8 74.4 reduce-scatter.10
  478.6 74.6 reduce-scatter.8
  555.8 36.7 all-reduce.3

commit v2 on v1

--- a/solution.py
+++ b/solution.py
@@ -17,7 +17,6 @@
 EPS = 1e-6
 BF = jnp.bfloat16
 F32 = jnp.float32
-VMEM_LIMIT = 56 * 1024 * 1024
 GELU_C = 0.7978845608028654
 GELU_A = 0.044715
 
@@ -34,8 +33,12 @@
     return lax.dot_general(a, b, (((0,), (0,)), ((), ())), preferred_element_type=F32)
 
 
-def params(**kw):
-    return pltpu.CompilerParams(vmem_limit_bytes=VMEM_LIMIT, **kw)
+def params(mib=56):
+    return pltpu.CompilerParams(vmem_limit_bytes=mib << 20)
+
+
+def cost(us):
+    return pl.CostEstimate(flops=int(us * 1.1e9), bytes_accessed=1 << 16, transcendentals=0)
 
 
 def norm_parts(v):
@@ -80,6 +83,7 @@
             jax.ShapeDtypeStruct((width, slots), BF),
         ],
         compiler_params=params(),
+        cost_estimate=cost(5),
         name="norm1",
     )(x, gain, shift)
 
@@ -181,6 +185,7 @@
         ],
         scratch_shapes=[pltpu.VMEM((slots - FIRST, slots - CUT), F32)],
         compiler_params=params(),
+        cost_estimate=cost(9),
         name="attend",
     )(counts, q, k, v)
 
@@ -269,6 +274,7 @@
         + [jax.ShapeDtypeStruct((width // 2, 128), F32)] * 2,
         scratch_shapes=[pltpu.VMEM((slots - FIRST, slots - CUT), F32)],
         compiler_params=params(),
+        cost_estimate=cost(14),
         name="attend_back",
     )(counts, q, k, v, o, do, lse, cos, sin, places)
 
@@ -489,7 +495,7 @@
     )(at, dqkv, w, x, dh, gain)
 
 
-def body(
+def body_any(
     tokens, cotangent, image_counts, patch_rows, patch_cols, ln1_gain, ln1_bias, qkv_weight, qkv_bias, rope_freqs,
     out_weight, out_bias, ln2_gain, ln2_bias, fc1_weight, fc1_bias, fc2_weight, fc2_bias,
 ):
@@ -549,6 +555,845 @@
     )
 
 
+SHARDS = 16
+GROUPS = 2
+LEAVING = (0, 8, 4, 12, 2, 10, 6, 14)
+
+
+def swap(v, mask):
+    return lax.ppermute(v, "fsdp", [(i, i ^ mask) for i in range(SHARDS)])
+
+
+def tie(v, *after):
+    return lax.optimization_barrier((v,) + after)[0]
+
+
+class Gather:
+    def __init__(self, mine):
+        self.piece = {0: mine}
+
+    def send(self, source, mask, after):
+        v = self.piece[source]
+        self.piece[source ^ mask] = swap(tie(v, *after) if after else v, mask)
+
+    def stage1(self, *after):
+        for mask in (8, 4, 2):
+            self.send(0, mask, after)
+
+    def stage2(self, *after):
+        self.send(8, 4, after)
+        self.send(4, 2, after)
+        self.send(8, 2, after)
+
+    def stage3(self, *after):
+        self.send(12, 2, after)
+
+    def cores(self, *after):
+        for p in (0, 8, 4, 2, 6, 10, 12, 14):
+            self.send(p, 1, after)
+        return [self.piece[p] for p in range(SHARDS)]
+
+
+class Scatter:
+    def __init__(self, near, far):
+        self.got = [near, swap(far, 1)]
+        self.size = 4
+
+    def total(self, lo, hi):
+        out = self.got[0][lo:hi].astype(F32)
+        for g in self.got[1:]:
+            out = out + g[lo:hi].astype(F32)
+        return out.astype(BF)
+
+    def step(self):
+        lo = self.size
+        sent = self.total(lo, 2 * lo)
+        self.got.append(swap(sent, {4: 2, 2: 4, 1: 8}[lo]))
+        self.size = lo // 2
+        return sent
+
+    def finish(self):
+        mine = self.total(0, 1)[0]
+        return mine, lax.ppermute(mine, "rep", [(0, 1), (1, 0)])
+
+
+def start_all(copies):
+    for copy in copies:
+        copy.start()
+
+
+def wait_all(copies):
+    for copy in copies:
+        copy.wait()
+
+
+def fetch(refs, order_ref, moves, sem):
+    copies = []
+    for p, ref in enumerate(refs):
+        for rows, place in moves:
+            copies.append(pltpu.make_async_copy(ref.at[rows], place(order_ref[p]), sem.at[len(copies)]))
+    return copies
+
+
+ANY = pl.BlockSpec(memory_space=pl.ANY)
+SMEM = pl.BlockSpec(memory_space=pltpu.SMEM)
+VMEM = pl.BlockSpec(memory_space=pltpu.VMEM)
+
+
+def group_piece_kernel(w_ref, o_ref, a_ref, b_ref):
+    rows, cols = w_ref.shape[0], a_ref.shape[1]
+    for i in range(3):
+        for g, out in enumerate((a_ref, b_ref)):
+            out[i * rows : (i + 1) * rows, :] = w_ref[:, (i * GROUPS + g) * cols : (i * GROUPS + g + 1) * cols]
+    for i in range(2):
+        b_ref[(3 + i) * rows : (4 + i) * rows, :] = o_ref[:, i * cols : (i + 1) * cols]
+
+
+def group_pieces(w, w_out):
+    rows, cols = w.shape[0], w_out.shape[1] // 2
+    return pl.pallas_call(
+        group_piece_kernel,
+        in_specs=[VMEM, VMEM],
+        out_specs=[VMEM, VMEM],
+        out_shape=[jax.ShapeDtypeStruct((3 * rows, cols), BF), jax.ShapeDtypeStruct((5 * rows, cols), BF)],
+        compiler_params=params(),
+        cost_estimate=cost(2),
+        name="group_pieces",
+    )(w, w_out)
+
+
+def mlp_piece_kernel(w1_ref, w2_ref, *outs):
+    rows1 = w1_ref.shape[0]
+    own = w2_ref.shape[0] // 2
+    per = SHARDS // 2
+    w1 = w1_ref[...].astype(F32)
+    for i, out in enumerate(outs):
+        for b in range(2):
+            runs = [w1[:, (2 * (b * per + j) + i) * own :][:, :own] for j in range(per)]
+            out[b * rows1 : (b + 1) * rows1, :] = jnp.concatenate(runs, axis=1).astype(BF)
+        out[2 * rows1 :, :] = w2_ref[i * own : (i + 1) * own, :]
+
+
+def mlp_pieces(w1, w2):
+    rows = 2 * w1.shape[0] + w2.shape[0] // 2
+    return pl.pallas_call(
+        mlp_piece_kernel,
+        in_specs=[VMEM, VMEM],
+        out_specs=[VMEM, VMEM],
+        out_shape=[jax.ShapeDtypeStruct((rows, w2.shape[1]), BF)] * 2,
+        compiler_params=params(),
+        cost_estimate=cost(2),
+        name="mlp_pieces",
+    )(w1, w2)
+
+
+def mlp_join_kernel(*refs):
+    ins, (w1_ref, w2_ref) = refs[:4], refs[4:]
+    rows1 = w1_ref.shape[0]
+    own = w2_ref.shape[0] // 2
+    per = SHARDS // 2
+    sums = [ins[2 * i][...].astype(F32) + ins[2 * i + 1][...].astype(F32) for i in range(2)]
+    runs = []
+    for b in range(2):
+        for j in range(per):
+            runs += [m[b * rows1 : (b + 1) * rows1, j * own : (j + 1) * own] for m in sums]
+    w1_ref[...] = jnp.concatenate(runs, axis=1)
+    for i in range(2):
+        w2_ref[i * own : (i + 1) * own, :] = sums[i][2 * rows1 :]
+
+
+def mlp_join(rows1, parts):
+    own = parts[0].shape[0] - 2 * rows1
+    return pl.pallas_call(
+        mlp_join_kernel,
+        in_specs=[VMEM] * 4,
+        out_specs=[VMEM] * 2,
+        out_shape=[
+            jax.ShapeDtypeStruct((rows1, 2 * own * SHARDS), F32),
+            jax.ShapeDtypeStruct((2 * own, parts[0].shape[1]), F32),
+        ],
+        compiler_params=params(),
+        cost_estimate=cost(3),
+        name="mlp_join",
+    )(*parts)
+
+
+def spread(packed, lo, size):
+    return jnp.concatenate([packed[j : j + 1, lo : lo + size] for j in range(packed.shape[0])], axis=1)
+
+
+def column(v):
+    return jnp.broadcast_to(v, (8, v.shape[1])).T[:, 0:1]
+
+
+def look_up(table, places):
+    top = table.astype(BF)
+    rest = table - top.astype(F32)
+    middle = rest.astype(BF)
+    low = (rest - middle.astype(F32)).astype(BF)
+    return nn(top, places) + nn(middle, places) + nn(low, places)
+
+
+def prepare_kernel(sizes, packed_ref, x_ref, cols_ref, rows_ref, a_ref, at_ref, cos_ref, sin_ref, vec_ref, b1_ref, bias_ref, sel_ref):
+    packed = packed_ref[...].astype(F32)
+    starts = [sum(sizes[:i]) for i in range(len(sizes))]
+    gain1, shift1, b_qkv, freqs, b_out, gain2, shift2 = (spread(packed, starts[i], sizes[i]) for i in range(7))
+    b2 = spread(packed, starts[8], sizes[8])
+    for i, v in enumerate((b_out, gain1, gain2, shift2, b2)):
+        vec_ref[i : i + 1, :] = v
+    own = sizes[7] // 2
+    for i in range(2):
+        b1_ref[i : i + 1, :] = spread(packed, starts[7] + i * own, own)
+    bias_ref[...] = column(b_qkv)
+    tile = 256
+    for i in range(x_ref.shape[0] // tile):
+        rows = slice(i * tile, (i + 1) * tile)
+        xhat, _ = norm_parts(x_ref[rows, :].astype(F32))
+        a = (xhat * gain1 + shift1).astype(BF)
+        a_ref[rows, :] = a
+        at_ref[:, rows] = a.T
+    freq = column(freqs)
+    half = freq.shape[0] // 2
+    slots = x_ref.shape[0]
+    spots = lax.broadcasted_iota(jnp.int32, (1, 128), 1).astype(F32)
+    found = []
+    for f, at in ((freq[:half], cols_ref[...]), (freq[half:], rows_ref[...])):
+        angle = f * spots
+        one_hot = jnp.where(lax.broadcasted_iota(jnp.int32, (128, slots), 0) == at, 1.0, 0.0).astype(BF)
+        found.append((look_up(jnp.cos(angle), one_hot), look_up(jnp.sin(angle), one_hot)))
+    (cos_c, sin_c), (cos_r, sin_r) = found
+    cos_ref[...] = cos_c * cos_r - sin_c * sin_r
+    sin_ref[...] = sin_c * cos_r + cos_c * sin_r
+    line = lax.broadcasted_iota(jnp.int32, sel_ref.shape, 0)
+    sel = jnp.where(line == 0, cols_ref[...].astype(F32), rows_ref[...].astype(F32))
+    sel_ref[...] = jnp.where(line < 2, sel, jnp.where(line == 2, 1.0, 0.0)).astype(BF)
+
+
+def prepare(sizes, packed, x, patch_cols, patch_rows):
+    slots, width = x.shape
+    own = sizes[7] // 2
+    shape = jax.ShapeDtypeStruct
+    return pl.pallas_call(
+        partial(prepare_kernel, sizes),
+        in_specs=[VMEM] * 4,
+        out_specs=[VMEM] * 8,
+        out_shape=[
+            shape((slots, width), BF),
+            shape((width, slots), BF),
+            shape((width // 2, slots), F32),
+            shape((width // 2, slots), F32),
+            shape((8, width), F32),
+            shape((2, own * SHARDS), F32),
+            shape((3 * width, 1), F32),
+            shape((16, slots), BF),
+        ],
+        compiler_params=params(40),
+        cost_estimate=cost(9),
+        name="prepare",
+    )(packed, x, patch_cols, patch_rows)
+
+
+def pack_kernel(sums1_ref, sums2_ref, b1a_ref, b1b_ref, *rest):
+    heads, out_ref = rest[:-1], rest[-1]
+    bias = [r[2:3, :] for r in heads[:GROUPS]]
+    freq = [r[...] for r in heads[GROUPS:]]
+    cols = bias[0].shape[1] // 3
+    b_qkv = jnp.concatenate([b[:, i * cols : (i + 1) * cols] for i in range(3) for b in bias], axis=1)
+    g_freq = jnp.concatenate([f[i : i + 1] for i in range(2) for f in freq], axis=1)
+    vectors = (
+        sums1_ref[0:1, :], sums1_ref[1:2, :], b_qkv, g_freq, sums2_ref[2:3, :], sums2_ref[0:1, :], sums2_ref[1:2, :],
+        b1a_ref[...], b1b_ref[...], sums2_ref[3:4, :],
+    )
+    lines = []
+    for j in range(SHARDS):
+        runs = []
+        for v in vectors:
+            n = v.shape[1] // SHARDS
+            runs.append(v[:, j * n : (j + 1) * n])
+        lines.append(jnp.concatenate(runs, axis=1))
+    out_ref[...] = jnp.concatenate(lines, axis=0)
+
+
+def pack(size, *sums):
+    return pl.pallas_call(
+        pack_kernel,
+        in_specs=[VMEM] * len(sums),
+        out_specs=VMEM,
+        out_shape=jax.ShapeDtypeStruct((SHARDS, size), F32),
+        compiler_params=params(16),
+        cost_estimate=cost(3),
+        name="pack",
+    )(*sums)
+
+
+def group_kernel(group, order_ref, a_ref, bias_ref, cos_ref, sin_ref, *rest):
+    pieces, (q_ref, k_ref, v_ref, w_scr, sem) = rest[:SHARDS], rest[SHARDS:]
+    cols = q_ref.shape[0]
+    part = w_scr.shape[1] // 3
+    copies = fetch(pieces, order_ref, [(slice(0, 3 * part), lambda d: w_scr.at[d])], sem)
+    start_all(copies)
+    a = a_ref[...]
+    turn = slice(group * cols // 2, (group + 1) * cols // 2)
+    cos = cos_ref[turn, :]
+    sin = sin_ref[turn, :]
+    wait_all(copies)
+
+    def weight(i):
+        return w_scr[:, i * part : (i + 1) * part, :].reshape(a.shape[1], cols).T
+
+    def bias(i):
+        at = i * a.shape[1] + group * cols
+        return bias_ref[at : at + cols, :]
+
+    for i, out_ref, scale in ((0, q_ref, HEAD_DIM**-0.5), (1, k_ref, 1.0)):
+        u = nt(weight(i), a) + bias(i)
+        for h in range(cols // HEAD_DIM):
+            u1 = u[h * HEAD_DIM : h * HEAD_DIM + HALF]
+            u2 = u[h * HEAD_DIM + HALF : (h + 1) * HEAD_DIM]
+            c = cos[h * HALF : (h + 1) * HALF]
+            s = sin[h * HALF : (h + 1) * HALF]
+            out_ref[h * HEAD_DIM : h * HEAD_DIM + HALF, :] = ((u1 * c - u2 * s) * scale).astype(BF)
+            out_ref[h * HEAD_DIM + HALF : (h + 1) * HEAD_DIM, :] = ((u1 * s + u2 * c) * scale).astype(BF)
+    v_ref[...] = (nt(weight(2), a) + bias(2)).astype(BF)
+
+
+def project_group(group, order, a, bias, cos, sin, pieces):
+    slots, width = a.shape
+    cols = pieces[0].shape[1]
+    return pl.pallas_call(
+        partial(group_kernel, group),
+        in_specs=[SMEM] + [VMEM] * 4 + [ANY] * SHARDS,
+        out_specs=[VMEM] * 3,
+        out_shape=[jax.ShapeDtypeStruct((cols, slots), BF)] * 3,
+        scratch_shapes=[pltpu.VMEM((SHARDS, 3 * width // SHARDS, cols), BF), pltpu.SemaphoreType.DMA((SHARDS,))],
+        compiler_params=params(),
+        cost_estimate=cost(7),
+        name="qkv_group",
+    )(order, a, bias, cos, sin, *pieces)
+
+
+def out_moves(w_scr, start):
+    rows = w_scr.shape[1]
+    half = w_scr.shape[2] // 2
+    return [
+        (slice(start + i * rows, start + (i + 1) * rows), lambda d, i=i: w_scr.at[d, :, pl.ds(i * half, half)])
+        for i in range(2)
+    ]
+
+
+def out_group_kernel(start, order_ref, vec_ref, *rest):
+    o_refs, x_ref, pieces = rest[:GROUPS], rest[GROUPS], rest[GROUPS + 1 : GROUPS + 1 + SHARDS]
+    h_ref, c_ref, ct_ref, w_scr, sem = rest[GROUPS + 1 + SHARDS :]
+
+    @pl.when(pl.program_id(0) == 0)
+    def _():
+        copies = fetch(pieces, order_ref, out_moves(w_scr, start), sem)
+        start_all(copies)
+        wait_all(copies)
+
+    width = x_ref.shape[1]
+    o = jnp.concatenate([r[...].T for r in o_refs], axis=1)
+    h = x_ref[...].astype(F32) + (nn(o, w_scr[...].reshape(width, width)) + vec_ref[0:1, :])
+    h_ref[...] = h
+    xhat, _ = norm_parts(h)
+    c = (xhat * vec_ref[2:3, :] + vec_ref[3:4, :]).astype(BF)
+    c_ref[...] = c
+    ct_ref[...] = c.T
+
+
+def out_project_fast(order, o, x, vec, pieces, start):
+    slots, width = x.shape
+    blk = 256
+    rows = pl.BlockSpec((blk, width), lambda i: (i, 0))
+    cols = pl.BlockSpec((width, blk), lambda i: (0, i))
+    return pl.pallas_call(
+        partial(out_group_kernel, start),
+        grid=(slots // blk,),
+        in_specs=[SMEM, VMEM] + [pl.BlockSpec((width // GROUPS, blk), lambda i: (0, i))] * GROUPS + [rows] + [ANY] * SHARDS,
+        out_specs=[rows, rows, cols],
+        out_shape=[
+            jax.ShapeDtypeStruct((slots, width), F32),
+            jax.ShapeDtypeStruct((slots, width), BF),
+            jax.ShapeDtypeStruct((width, slots), BF),
+        ],
+        scratch_shapes=[pltpu.VMEM((SHARDS, width // SHARDS, width), BF), pltpu.SemaphoreType.DMA((2 * SHARDS,))],
+        compiler_params=params(),
+        cost_estimate=cost(8),
+        name="out_project",
+    )(order, vec, *o, x, *pieces)
+
+
+def mlp_half_kernel(part, first, split, n_in, order_ref, c_ref, ct_ref, dy_ref, b1_ref, vec_ref, *rest):
+    acc_in, rest = (rest[:1], rest[1:]) if first else (rest[:2], rest[2:])
+    pieces, rest = rest[:n_in], rest[n_in:]
+    n_g = 2 if split else 1
+    y_ref, dc_ref = rest[:2]
+    g_refs = rest[2 : 2 + n_g]
+    gb1_ref, w1_scr, w2_scr, g1_scr, g2_scr, hb_scr, dp_scr, y_acc, dc_acc, sem, load_sem = rest[2 + n_g : 13 + n_g]
+    y_out = y_acc if first else rest[13 + n_g]
+    slots, width = c_ref.shape
+    rows1 = w1_scr.shape[2]
+    rows2 = w2_scr.shape[1]
+    blk = w1_scr.shape[3]
+    steps = w1_scr.shape[0]
+    per = blk // rows2
+    tile = 512
+    refs = [pieces[0].at[p] for p in range(SHARDS)] if n_in == 1 else pieces
+    places = range(SHARDS) if n_in == 1 else order_ref
+    loads = [
+        fetch(refs, places, [(slice(j * rows1, (j + 1) * rows1), lambda d, j=j: w1_scr.at[j, d])], sem.at[j])
+        for j in range(steps)
+    ]
+    loads.insert(1, fetch(refs, places, [(slice(steps * rows1, steps * rows1 + rows2), lambda d: w2_scr.at[d])], sem.at[steps]))
+    sums = [pltpu.make_async_copy(src, dst, load_sem.at[i]) for i, (src, dst) in enumerate(zip(acc_in, (y_acc, dc_acc)))]
+    for copies in loads[:2] + [sums] + loads[2:]:
+        start_all(copies)
+    sends = []
+    for j in range(steps):
+        cols = slice(j * blk, (j + 1) * blk)
+        wait_all(loads[0] if j == 0 else loads[1 + j])
+        w1 = w1_scr[j].reshape(width, blk)
+        if j == 0:
+            wait_all(loads[1] + sums)
+        w2 = w2_scr[j * per : (j + 1) * per].reshape(blk, width)
+        total = None
+        for i in range(slots // tile):
+            rows = slice(i * tile, (i + 1) * tile)
+            pre = nn(c_ref[rows, :], w1) + b1_ref[part : part + 1, cols]
+            square = pre * pre
+            th = jnp.tanh(GELU_C * (pre + GELU_A * (pre * square)))
+            cdf = 0.5 * (1.0 + th)
+            hb = (pre * cdf).astype(BF)
+            slope = cdf + 0.5 * pre * (1.0 - th * th) * (GELU_C * (1.0 + (3.0 * GELU_A) * square))
+            hb_scr[rows, :] = hb
+            y = y_acc[rows, :] + nn(hb, w2)
+            if first and j == 0:
+                y = y + vec_ref[4:5, :]
+            dpre = (nt(dy_ref[rows, :], w2) * slope).astype(BF)
+            dp_scr[rows, :] = dpre
+            term = jnp.sum(dpre.astype(F32), axis=0, keepdims=True)
+            total = term if total is None else total + term
+            dc = nt(dpre, w1)
+            if not (first and j == 0):
+                dc = dc + dc_acc[rows, :]
+            dc_acc[rows, :] = dc
+            if j == steps - 1:
+                y_out[rows, :] = y.astype(y_out.dtype)
+                sends += [
+                    pltpu.make_async_copy(y_out.at[rows], y_ref.at[rows], load_sem.at[2 + 2 * i]),
+                    pltpu.make_async_copy(dc_acc.at[rows], dc_ref.at[rows], load_sem.at[3 + 2 * i]),
+                ]
+                start_all(sends[-2:])
+            else:
+                y_acc[rows, :] = y
+        gb1_ref[:, cols] = total
+        g1_scr[j] = nn(ct_ref[...], dp_scr[...]).astype(BF).reshape(SHARDS, rows1, blk)
+        if split:
+            dests = [(g_refs[b].at[i], order_ref[p + b]) for b in range(2) for i, p in enumerate(LEAVING)]
+        else:
+            dests = [(g_refs[0].at[p], p) for p in range(SHARDS)]
+        copies = [
+            pltpu.make_async_copy(g1_scr.at[j, d], dst.at[slice(j * rows1, (j + 1) * rows1)], sem.at[j, n])
+            for n, (dst, d) in enumerate(dests)
+        ]
+        start_all(copies)
+        sends += copies
+        g2_scr[j * per : (j + 1) * per] = tn(hb_scr[...], dy_ref[...]).astype(BF).reshape(per, rows2, width)
+    copies = [
+        pltpu.make_async_copy(g2_scr.at[d], dst.at[slice(steps * rows1, steps * rows1 + rows2)], sem.at[steps, n])
+        for n, (dst, d) in enumerate(dests)
+    ]
+    start_all(copies)
+    wait_all(sends + copies)
+
+
+def mlp_half(part, order, c, ct, dy, b1, vec, sums, pieces, split):
+    slots, width = c.shape
+    rows1 = width // SHARDS
+    rows2 = pieces[0].shape[-2] - 2 * rows1
+    hidden = rows2 * SHARDS
+    steps = 2
+    blk = hidden // steps
+    first = len(sums) == 1
+    block = jax.ShapeDtypeStruct((SHARDS // 2 if split else SHARDS, 2 * rows1 + rows2, width), BF)
+    return pl.pallas_call(
+        partial(mlp_half_kernel, part, first, split, len(pieces)),
+        in_specs=[SMEM] + [VMEM] * 5 + [ANY] * (len(sums) + len(pieces)),
+        out_specs=[ANY, ANY] + [ANY] * (2 if split else 1) + [VMEM],
+        out_shape=[jax.ShapeDtypeStruct((slots, width), F32 if first else BF), jax.ShapeDtypeStruct((slots, width), F32)]
+        + [block] * (2 if split else 1)
+        + [jax.ShapeDtypeStruct((1, hidden), F32)],
+        scratch_shapes=[
+            pltpu.VMEM((steps, SHARDS, rows1, blk), BF),
+            pltpu.VMEM((SHARDS, rows2, width), BF),
+            pltpu.VMEM((steps, SHARDS, rows1, blk), BF),
+            pltpu.VMEM((SHARDS, rows2, width), BF),
+            pltpu.VMEM((slots, blk), BF),
+            pltpu.VMEM((slots, blk), BF),
+            pltpu.VMEM((slots, width), F32),
+            pltpu.VMEM((slots, width), F32),
+            pltpu.SemaphoreType.DMA((steps + 1, SHARDS)),
+            pltpu.SemaphoreType.DMA((8,)),
+        ]
+        + ([] if first else [pltpu.VMEM((slots, width), BF)]),
+        compiler_params=params(56),
+        cost_estimate=cost(23),
+        name="mlp_half",
+    )(order, c, ct, dy, b1, vec, *sums, *pieces)
+
+
+def out_back_fast_kernel(start, order_ref, dc_ref, h_ref, dy_ref, vec_ref, *rest):
+    o_refs, pieces = rest[:GROUPS], rest[GROUPS : GROUPS + SHARDS]
+    dh_ref, do_ref, near_ref, far_ref, sums_ref, acc_ref, g_scr, w_scr, sem = rest[GROUPS + SHARDS :]
+    i = pl.program_id(0)
+    width = h_ref.shape[1]
+    each = width // SHARDS
+    half = width // 2
+
+    @pl.when(i == 0)
+    def _():
+        copies = fetch(pieces, order_ref, out_moves(w_scr, start), sem)
+        start_all(copies)
+        acc_ref[...] = jnp.zeros_like(acc_ref)
+        sums_ref[...] = jnp.zeros_like(sums_ref)
+        wait_all(copies)
+
+    dy = dy_ref[...].astype(F32)
+    part, dgain, dshift = norm_back(dc_ref[...], h_ref[...], vec_ref[2:3, :])
+    dh = dy + part
+    dh_ref[...] = dh
+    dhb = dh.astype(BF)
+    do_ref[...] = nt(w_scr[...].reshape(width, width), dhb).astype(BF)
+    rows = width // GROUPS
+    for g in range(GROUPS):
+        acc_ref[g * rows : (g + 1) * rows, :] += nn(o_refs[g][...], dhb)
+    sums_ref[0:1, :] += dgain
+    sums_ref[1:2, :] += dshift
+    sums_ref[2:3, :] += jnp.sum(dh, axis=0, keepdims=True)
+    sums_ref[3:4, :] += jnp.sum(dy, axis=0, keepdims=True)
+
+    @pl.when(i == pl.num_programs(0) - 1)
+    def _():
+        g_scr[...] = acc_ref[...].astype(BF).reshape(g_scr.shape)
+        copies = []
+        for b, out in enumerate((near_ref, far_ref)):
+            for n, p in enumerate(LEAVING):
+                for k in range(2):
+                    src = g_scr.at[order_ref[p + b], :, pl.ds(k * half, half)]
+                    dst = out.at[n, pl.ds(k * each, each)]
+                    copies.append(pltpu.make_async_copy(src, dst, sem.at[len(copies)]))
+        start_all(copies)
+        wait_all(copies)
+
+
+def out_back_fast(order, dc, h, dy, vec, o, pieces, start):
+    slots, width = h.shape
+    blk = 256
+    rows = pl.BlockSpec((blk, width), lambda i: (i, 0))
+    cols = pl.BlockSpec((width, blk), lambda i: (0, i))
+    whole = lambda r, k: pl.BlockSpec((r, k), lambda i: (0, 0))
+    block = jax.ShapeDtypeStruct((SHARDS // 2, 2 * width // SHARDS, width // 2), BF)
+    return pl.pallas_call(
+        partial(out_back_fast_kernel, start),
+        grid=(slots // blk,),
+        in_specs=[SMEM, rows, rows, rows, VMEM]
+        + [pl.BlockSpec((width // GROUPS, blk), lambda i: (0, i))] * GROUPS
+        + [ANY] * SHARDS,
+        out_specs=[rows, cols, ANY, ANY, whole(8, width)],
+        out_shape=[
+            jax.ShapeDtypeStruct((slots, width), F32),
+            jax.ShapeDtypeStruct((width, slots), BF),
+            block,
+            block,
+            jax.ShapeDtypeStruct((8, width), F32),
+        ],
+        scratch_shapes=[
+            pltpu.VMEM((width, width), F32),
+            pltpu.VMEM((SHARDS, width // SHARDS, width), BF),
+            pltpu.VMEM((SHARDS, width // SHARDS, width), BF),
+            pltpu.SemaphoreType.DMA((2 * SHARDS,)),
+        ],
+        compiler_params=params(),
+        cost_estimate=cost(12),
+        name="out_back",
+    )(order, dc, h, dy, vec, *o, *pieces)
+
+
+def heads_back_kernel(
+    counts_ref, q_ref, k_ref, v_ref, o_ref, do_ref, lse_ref, cos_ref, sin_ref,
+    dq_ref, dk_ref, dv_ref, dangle_ref, bias_ref,
+):
+    slots = q_ref.shape[1]
+
+    @pl.when(pl.program_id(0) == 0)
+    def _():
+        bias_ref[...] = second_bias(counts_ref, slots)
+
+    kt = k_ref[...]
+    k = kt.T
+    v = v_ref[...].T
+    q = q_ref[...]
+    do = do_ref[...]
+    lse = lse_ref[0]
+    delta = jnp.sum(do.astype(F32) * o_ref[...].astype(F32), axis=0, keepdims=True)
+    lane1 = lax.broadcasted_iota(jnp.int32, (1, WIDE), 1)
+    lane2 = lax.broadcasted_iota(jnp.int32, (1, slots - CUT), 1)
+    lse1 = jnp.where(lane1 < FIRST, lse[:, :WIDE], -NEG)
+    lse2 = jnp.where(lane2 >= FIRST - CUT, lse[:, CUT:], -NEG)
+
+    def part(scores, grads, queries, outs, keys, delta_row, first):
+        prob = jnp.exp(scores)
+        ds = (prob * (grads - delta_row)).astype(BF)
+        pb = prob.astype(BF)
+        gap = jnp.zeros((keys.shape[1] - pb.shape[0], pb.shape[1]), BF)
+        pb = jnp.concatenate([pb, gap] if first else [gap, pb], axis=0)
+        ds = jnp.concatenate([ds, gap] if first else [gap, ds], axis=0)
+        return nn(keys, ds), nt(queries, ds), nt(outs, pb)
+
+    grads1 = part(
+        nn(k[:FIRST], q[:, :WIDE]) - lse1, nn(v[:FIRST], do[:, :WIDE]),
+        q[:, :WIDE], do[:, :WIDE], kt[:, :WIDE], delta[:, :WIDE], True,
+    )
+    grads2 = part(
+        nn(k[FIRST:], q[:, CUT:]) + bias_ref[...] - lse2, nn(v[FIRST:], do[:, CUT:]),
+        q[:, CUT:], do[:, CUT:], kt[:, CUT:], delta[:, CUT:], False,
+    )
+    dq, dk, dv = (
+        jnp.concatenate([one[:, :CUT], one[:, CUT:] + two[:, : WIDE - CUT], two[:, WIDE - CUT :]], axis=1)
+        for one, two in zip(grads1, grads2)
+    )
+    scale = HEAD_DIM**-0.5
+    cos = cos_ref[...]
+    sin = sin_ref[...]
+    dangle = None
+    for r, rot, out in ((dq * scale, q.astype(F32) * (1.0 / scale), dq_ref), (dk, kt.astype(F32), dk_ref)):
+        r1, r2 = r[:HALF], r[HALF:]
+        term = r2 * rot[:HALF] - r1 * rot[HALF:]
+        dangle = term if dangle is None else dangle + term
+        g1 = (r1 * cos + r2 * sin).astype(BF)
+        g2 = (r2 * cos - r1 * sin).astype(BF)
+        out[:HALF, :] = g1
+        out[HALF:, :] = g2
+    dv_ref[...] = dv.astype(BF)
+    dangle_ref[...] = dangle.astype(BF)
+
+
+def heads_back(group, counts, q, k, v, o, do, lse, cos, sin):
+    width, slots = q.shape
+    heads = width // HEAD_DIM
+    head = pl.BlockSpec((HEAD_DIM, slots), lambda h: (h, 0))
+    half = pl.BlockSpec((HALF, slots), lambda h: (h, 0))
+    turn = pl.BlockSpec((HALF, slots), lambda h: (group * heads + h, 0))
+    late = pl.BlockSpec((HEAD_DIM, slots), lambda h: (group * heads + h, 0))
+    return pl.pallas_call(
+        heads_back_kernel,
+        grid=(heads,),
+        in_specs=[pl.BlockSpec(memory_space=pltpu.SMEM)]
+        + [head] * 4
+        + [late, pl.BlockSpec((1, 1, slots), lambda h: (h, 0, 0)), turn, turn],
+        out_specs=[head] * 3 + [half],
+        out_shape=[jax.ShapeDtypeStruct((width, slots), BF)] * 3 + [jax.ShapeDtypeStruct((width // 2, slots), BF)],
+        scratch_shapes=[pltpu.VMEM((slots - FIRST, slots - CUT), F32)],
+        compiler_params=params(),
+        cost_estimate=cost(14),
+        name="heads_back",
+    )(counts, q, k, v, o, do, lse, cos, sin)
+
+
+def qkv_grad_kernel(order_ref, at_ref, sel_ref, dangle_ref, dq_ref, dk_ref, dv_ref, *rest):
+    more, (near_ref, far_ref, bias_ref, freq_ref, g_scr, sem, more_sem) = rest[:-7], rest[-7:]
+    part = g_scr.shape[1] // 3
+    outs = (near_ref, far_ref)
+    extra = [
+        pltpu.make_async_copy(ref.at[n], out.at[n, pl.ds(3 * part, ref.shape[1])], more_sem.at[b, n])
+        for b, (ref, out) in enumerate(zip(more, outs))
+        for n in range(SHARDS // 2)
+    ]
+    start_all(extra)
+    at = at_ref[...]
+    for i, ref in enumerate((dq_ref, dk_ref, dv_ref)):
+        g = nt(at, ref[...]).astype(BF)
+        g_scr[:, i * part : (i + 1) * part, :] = g.reshape(SHARDS, part, g.shape[1])
+        bias_ref[:, i * g.shape[1] : (i + 1) * g.shape[1]] = nt(sel_ref[...], ref[...])
+    freq_ref[...] = nt(sel_ref[...], dangle_ref[...])
+    copies = []
+    for b, out in enumerate(outs):
+        for n, p in enumerate(LEAVING):
+            dst = out.at[n, pl.ds(0, 3 * part)]
+            copies.append(pltpu.make_async_copy(g_scr.at[order_ref[p + b]], dst, sem.at[len(copies)]))
+    start_all(copies)
+    wait_all(copies + extra)
+
+
+def qkv_grad(order, at, sel, dangle, dq, dk, dv, *more):
+    width, slots = at.shape
+    cols = dq.shape[0]
+    rows = 3 * width // SHARDS
+    total = rows + (more[0].shape[1] if more else 0)
+    return pl.pallas_call(
+        qkv_grad_kernel,
+        in_specs=[SMEM] + [VMEM] * (6 + len(more)),
+        out_specs=[ANY, ANY, VMEM, VMEM],
+        out_shape=[jax.ShapeDtypeStruct((SHARDS // 2, total, cols), BF)] * 2
+        + [jax.ShapeDtypeStruct((sel.shape[0], 3 * cols), F32), jax.ShapeDtypeStruct((sel.shape[0], cols // 2), F32)],
+        scratch_shapes=[
+            pltpu.VMEM((SHARDS, rows, cols), BF),
+            pltpu.SemaphoreType.DMA((SHARDS,)),
+            pltpu.SemaphoreType.DMA((2, SHARDS // 2)),
+        ],
+        compiler_params=params(),
+        cost_estimate=cost(6),
+        name="qkv_grad",
+    )(order, at, sel, dangle, dq, dk, dv, *more)
+
+
+def input_kernel(order_ref, x_ref, dh_ref, vec_ref, *rest):
+    grads = rest[: 3 * GROUPS]
+    pieces = [rest[3 * GROUPS + g * SHARDS : 3 * GROUPS + (g + 1) * SHARDS] for g in range(GROUPS)]
+    dx_ref, sums_ref, w_scr, sem = rest[3 * GROUPS + GROUPS * SHARDS :]
+    width, blk = x_ref.shape[1], x_ref.shape[0]
+    i = pl.program_id(0)
+    part = width // SHARDS
+
+    @pl.when(i == 0)
+    def _():
+        copies = []
+        for g in range(GROUPS):
+            copies += fetch(pieces[g], order_ref, [(slice(0, 3 * part), lambda d: w_scr.at[g, d])], sem.at[g])
+        start_all(copies)
+        sums_ref[...] = jnp.zeros_like(sums_ref)
+        wait_all(copies)
+
+    da = None
+    for g in range(GROUPS):
+        for n in range(3):
+            w = w_scr[g, :, n * part : (n + 1) * part, :].reshape(width, width // GROUPS)
+            term = nn(w, grads[3 * g + n][...])
+            da = term if da is None else da + term
+    out, dgain, dshift = norm_back(da.T, x_ref[...].astype(F32), vec_ref[1:2, :])
+    dx_ref[...] = (dh_ref[...] + out).astype(BF)
+    sums_ref[0:1, :] += dgain
+    sums_ref[1:2, :] += dshift
+
+
+def input_back(order, x, dh, vec, grads, pieces):
+    slots, width = x.shape
+    blk = 256
+    rows = pl.BlockSpec((blk, width), lambda i: (i, 0))
+    whole = lambda r, k: pl.BlockSpec((r, k), lambda i: (0, 0))
+    return pl.pallas_call(
+        input_kernel,
+        grid=(slots // blk,),
+        in_specs=[SMEM, rows, rows, VMEM]
+        + [pl.BlockSpec((width // GROUPS, blk), lambda i: (0, i))] * (3 * GROUPS)
+        + [ANY] * (GROUPS * SHARDS),
+        out_specs=[rows, whole(8, width)],
+        out_shape=[jax.ShapeDtypeStruct((slots, width), BF), jax.ShapeDtypeStruct((8, width), F32)],
+        scratch_shapes=[
+            pltpu.VMEM((GROUPS, SHARDS, 3 * width // SHARDS, width // GROUPS), BF),
+            pltpu.SemaphoreType.DMA((GROUPS, SHARDS)),
+        ],
+        compiler_params=params(),
+        cost_estimate=cost(12),
+        name="input_back",
+    )(order, x, dh, vec, *grads, *[p for group in pieces for p in group])
+
+
+def body_fast(
+    tokens, cotangent, image_counts, patch_rows, patch_cols, ln1_gain, ln1_bias, qkv_weight, qkv_bias, rope_freqs,
+    out_weight, out_bias, ln2_gain, ln2_bias, fc1_weight, fc1_bias, fc2_weight, fc2_bias,
+):
+    x = tokens[0]
+    dy = cotangent[0]
+    counts = image_counts[0]
+    slots, width = x.shape
+    cols = width // GROUPS
+    half = width // 2
+    order = lax.axis_index("fsdp") ^ jnp.arange(SHARDS, dtype=jnp.int32)
+
+    own = fc2_weight.shape[0] // 2
+    piece_a, piece_b = group_pieces(qkv_weight, out_weight)
+    gather_a = Gather(piece_a)
+    gather_a.stage1()
+    piece_c, piece_d = mlp_pieces(tie(fc1_weight, piece_a), fc2_weight)
+
+    small = (ln1_gain, ln1_bias, qkv_bias, rope_freqs, out_bias, ln2_gain, ln2_bias, fc1_bias, fc2_bias)
+    sizes = [s.shape[0] for s in small]
+    mine = jnp.concatenate(small)
+    packed = lax.all_to_all(jnp.broadcast_to(mine[None], (SHARDS, mine.shape[0])), "fsdp", 0, 0, tiled=True)
+    gather_a.stage2(packed)
+    a, a_t, cos, sin, vec, b1, bias, sel = prepare(sizes, packed, tie(x, gather_a.piece[12]), patch_cols, patch_rows)
+    gather_a.stage3()
+    gather_b = Gather(piece_b)
+    gather_b.stage1(gather_a.piece[12])
+    gather_b.stage2(a)
+    gather_b.stage3()
+    gather_c = Gather(piece_c)
+    gather_c.stage1(a)
+    pieces_a = gather_a.cores()
+    q, k, v = project_group(0, order, a, bias, cos, sin, pieces_a)
+    pieces_d = [lax.all_gather(tie(piece_d, gather_b.piece[12]), "fsdp", axis=0)]
+    heads = [(q, k, v) + tuple(attend(counts, q, k, v))]
+    gather_c.stage2(q)
+    pieces_b = gather_b.cores()
+    q, k, v = project_group(1, order, a, bias, cos, sin, pieces_b)
+    gather_c.stage3(q)
+    heads.append((q, k, v) + tuple(attend(counts, q, k, v)))
+    pieces_c = gather_c.cores()
+    pieces_all = (pieces_a, pieces_b)
+    o = [t[3] for t in heads]
+    at_out = piece_a.shape[0]
+    h, c, c_t = out_project_fast(order, o, x, vec, pieces_b, at_out)
+    y, dc, g_c, g_b1a = mlp_half(0, order, c, c_t, dy, b1, vec, (h,), pieces_c, False)
+    mlp_c = lax.psum_scatter(tie(g_c, *pieces_d), "fsdp", scatter_dimension=0, tiled=True)[0]
+    y, dc, near_d, far_d, g_b1b = mlp_half(1, order, c, c_t, dy, b1, vec, (y, dc), pieces_d, True)
+    scatter_d = Scatter(near_d, far_d)
+    dh, do, near_o, far_o, sums2 = out_back_fast(order, dc, h, dy, vec, o, pieces_b, at_out)
+
+    def back(g, do):
+        q, k, v, og, lse = heads[g]
+        *three, dangle = heads_back(g, counts, q, k, v, og, do, lse, cos, sin)
+        return three, dangle
+
+    sent = scatter_d.step()
+    grads_b, dangle_b = back(1, tie(do, sent))
+    near_b, far_b, bias_b, freq_b = qkv_grad(order, a_t, sel, dangle_b, *grads_b, near_o, far_o)
+    scatter_b = Scatter(near_b, far_b)
+    grads_a, dangle_a = back(0, tie(do, near_b))
+    sent = (scatter_b.step(), scatter_d.step())
+    near_a, far_a, bias_a, freq_a = qkv_grad(order, a_t, sel, tie(dangle_a, *sent), *grads_a)
+    scatter_a = Scatter(near_a, far_a)
+    sent = (scatter_a.step(), scatter_d.step(), scatter_b.step())
+    dx, sums1 = input_back(order, x, tie(dh, *sent), vec, grads_a + grads_b, pieces_all)
+    for _ in range(2):
+        scatter_a.step()
+    scatter_b.step()
+    mlp_d = scatter_d.finish()
+    mine_b = scatter_b.finish()
+    mine_a = scatter_a.finish()
+    other_c = lax.ppermute(mlp_c, "rep", [(0, 1), (1, 0)])
+    s_a = mine_a[0].astype(F32) + mine_a[1].astype(F32)
+    s_b = mine_b[0].astype(F32) + mine_b[1].astype(F32)
+    rows1 = width // SHARDS
+    s_w1, s_w2 = mlp_join(rows1, (mlp_c, other_c) + mlp_d)
+    s_wqkv = jnp.concatenate([s[i * rows1 : (i + 1) * rows1] for i in range(3) for s in (s_a, s_b)], axis=1)
+    s_wout = jnp.concatenate([s_b[3 * rows1 : 4 * rows1], s_b[4 * rows1 :]], axis=1)
+
+    block = pack(sum(sizes), sums1, sums2, g_b1a, g_b1b, bias_a, bias_b, freq_a, freq_b)
+    mine = jnp.sum(lax.all_to_all(block, "fsdp", 0, 0, tiled=True), axis=0)
+    mine = mine + lax.ppermute(mine, "rep", [(0, 1), (1, 0)])
+    outs = []
+    at = 0
+    for size in sizes:
+        outs.append(mine[at : at + size])
+        at += size
+    s_gain1, s_shift1, s_bqkv, s_freq, s_bout, s_gain2, s_shift2, s_b1, s_b2 = outs
+    return (
+        y[None], dx[None], s_gain1, s_shift1, s_wqkv, s_bqkv, s_freq, s_wout, s_bout,
+        s_gain2, s_shift2, s_w1, s_b1, s_w2, s_b2,
+    )
+
+
 def solution(mesh):
     row = P(("rep", "fsdp"), None)
     rows = P(("rep", "fsdp"), None, None)
@@ -556,4 +1401,7 @@
     mat = P("fsdp", None)
     in_specs = (rows, rows, row, row, row, vec, vec, mat, vec, vec, mat, vec, vec, vec, mat, vec, mat, vec)
     out_specs = (rows, rows, vec, vec, mat, vec, vec, mat, vec, vec, vec, mat, vec, mat, vec)
-    return jax.shard_map(body, mesh=mesh, in_specs=in_specs, out_specs=out_specs, check_vma=False)
+    fast = mesh.shape["fsdp"] == SHARDS and mesh.shape["rep"] == 2
+    return jax.shard_map(
+        body_fast if fast else body_any, mesh=mesh, in_specs=in_specs, out_specs=out_specs, check_vma=False
+    )

time: 611 us -> 374 us (0.61)
  waiting for transfers between devices: 318 us -> 92.8 us
  blocking collectives: 104 us -> 10.3 us
  starting transfers between devices: 0.53 us -> 44 us
  Pallas kernels: 138 us -> 172 us
    reduce_scatter x4 -> x1, waiting for transfers between devices: 237 us -> 0.02 us  [body_fast(): lax.psum_scatter(tie(g_c, *pieces_d), 'fsdp', scatter_dimension=0, tiled=...]
    ppermute x0 -> x62, waiting for transfers between devices: none -> 87.7 us  [the longest x57 77.1 us: swap(): return lax.ppermute(v, 'fsdp', [(i, i ^ mask) for i in range(SHARDS)])]
    all_gather x4 -> x1, waiting for transfers between devices: 77.1 us -> 0.02 us  [body_fast(): lax.all_gather(tie(piece_d, gather_b.piece[12]), 'fsdp', axis=0)]
    unnamed x1 -> x0, blocking collectives: 63.9 us -> none
    psum x1 -> x0, blocking collectives: 40.3 us -> none  [body(): total = lax.psum(block, ('rep', 'fsdp'))]
    ppermute x0 -> x62, starting transfers between devices: none -> 39.6 us  [the longest x57 34.4 us: swap(): return lax.ppermute(v, 'fsdp', [(i, i ^ mask) for i in range(SHARDS)])]
    pallas_call x7 -> x16, Pallas kernels: 121 us -> 153 us  [the longest x2 50.8 us: mlp_half(): pl.pallas_call(partial(mlp_half_kernel, part, first, split, len(pieces)),...]
    all_to_all x0 -> x1, blocking collectives: none -> 10.3 us  [body_fast(): lax.all_to_all(jnp.broadcast_to(mine[None], (SHARDS, mine.shape[0])), 'fs...]
  transfers between devices with their start and end apart: 9 -> 65, of which waited for: 6 -> 21; matrix products, arithmetic and copies ran while one was open for 5% -> 6% of each run, Pallas kernels for 13% -> 38%
where the time goes in v2:
time: 374 us; the launch traced here: 368 us
  Pallas kernels  172 us (46%)
  waiting for transfers between devices  92.8 us (25%)
  starting transfers between devices  44 us (12%)
  other arithmetic  20.1 us (5%)
  between operations  15.7 us (4%)
  local copies, waits for them, and re-layouts  13.8 us (4%)
  blocking collectives  10.3 us (3%)
    ppermute x57, waiting for transfers between devices, swap(): return lax.ppermute(v, 'fsdp', [(i, i ^ mask) for i in range(SHARDS)])  77.1 us
    pallas_call x2, Pallas kernels, mlp_half(): pl.pallas_call(partial(mlp_half_kernel, part, first, split, len(pieces)),...  50.8 us
    ppermute x57, starting transfers between devices, swap(): return lax.ppermute(v, 'fsdp', [(i, i ^ mask) for i in range(SHARDS)])  34.4 us
    pallas_call x2, Pallas kernels, heads_back(): pl.pallas_call(heads_back_kernel, grid=(heads,), in_specs=[pl.BlockSpec(m...  27.8 us
    pallas_call x2, Pallas kernels, attend(): pl.pallas_call(attend_kernel, grid=(width // HEAD_DIM,), in_specs=[pl.Blo...  18.3 us
    pallas_call x2, Pallas kernels, qkv_grad(): pl.pallas_call(qkv_grad_kernel, in_specs=[SMEM] + [VMEM] * (6 + len(more)...  15.5 us
    pallas_call x2, Pallas kernels, project_group(): pl.pallas_call(partial(group_kernel, group), in_specs=[SMEM] + [VMEM] * 4...  15 us
    convert_element_type x9, other arithmetic, total(): return out.astype(BF)  12.9 us
  transfers between devices with their start and end apart: 65, of which 21 were waited for; matrix products, arithmetic and copies ran while one was open for 6% of the time, Pallas kernels for 38%

profile of v2, /device:TPU:0, one launch (start us, length us, event | category | flops | bytes accessed | tf_op | source)
XLA Modules:
  0.0 368.3 jit_solution(15392823770846581786)
XLA Ops:
  14.8 10.3 %all_to_all.17 = bf16[16,2,336]{2,1,0:T(2,128)(2,1)S(1)} all-to-all(bf16[16,2,336]{2,1,0:T(2,128)(2,1)S(1)} %reshape.39), channel_id=1, replica_groups=mesh['rep'=2,'fsdp'=16] {'fsdp'}, dimensions={0} | all-to-all | bytes 43008 | tf_op jit(solution)/shard_map/all_to_all | solution.py:1323
  30.8 4.8 %prepare.1 = (bf16[1024,768]{1,0:T(8,128)(2,1)S(1)}, bf16[768,1024]{1,0:T(8,128)(2,1)S(1)}, f32[384,1024]{1,0:T(8,128)S(1)}, f32[384,1024]{1,0:T(8,128)S(1)}, f3...) custom-call(bf16[16,672]{1,0:T(8,128)(2,1)S(1)} %bitcast.18, ...), custom_call_target="tpu_custom_call" | custom-call | flops 9900000256 | bytes 65536 | tf_op jit(solution)/shard_map/prepare/pallas_call | solution.py:776
  57.3 4.8 %collective-permute-done.7.rest_6_.rest_12_ = bf16[144,384]{1,0:T(8,128)(2,1)S(1)} collective-permute-done((bf16[144,384]{1,0:T(8,128)(2,1)S(1)}, bf16[144,384]{1,0:T(8,128)(2,1)S(1)}, u32[]{:S(2)}, u32[]{:S(2)}) %collective-permute-start.7) | collective-permute-done | bytes 110624 | tf_op jit(solution)/shard_map/ppermute | solution.py:564
  80.8 6.5 %collective-permute-done.37.rest_9_ = bf16[192,768]{1,0:T(8,128)(2,1)S(1)} collective-permute-done((bf16[192,768]{1,0:T(8,128)(2,1)}, bf16[192,768]{1,0:T(8,128)(2,1)S(1)}, u32[]{:S(2)}, u32[]{:S(2)}) %collective-permute-start.37) | collective-permute-done | bytes 294944 | tf_op jit(solution)/shard_map/ppermute | solution.py:564
  87.3 5.7 %collective-permute-done.33.rest_5_ = bf16[192,768]{1,0:T(8,128)(2,1)S(1)} collective-permute-done((bf16[192,768]{1,0:T(8,128)(2,1)}, bf16[192,768]{1,0:T(8,128)(2,1)S(1)}, u32[]{:S(2)}, u32[]{:S(2)}) %collective-permute-start.33) | collective-permute-done | bytes 294944 | tf_op jit(solution)/shard_map/ppermute | solution.py:564
  93.9 7.5 %qkv_group.2 = (bf16[384,1024]{1,0:T(8,128)(2,1)}, bf16[384,1024]{1,0:T(8,128)(2,1)}, bf16[384,1024]{1,0:T(8,128)(2,1)}) custom-call(s32[16]{0:T(128)} %iota_xor_fusion.order_ref, bf16[1024,768]{1,0:T(8,128)(2,1)} %copy-done.6, f32[2304,1]{1,0:T(8,128)} %copy-done.7, f32[384,1024]{1,0:T(8,128)} %copy-done.4, f32[384,1024]{1,0:T(8,128)} %copy-done.5, ...), custom_call_target="tpu_custom_call" | custom-call | flops 7699999744 | bytes 65536 | tf_op jit(solution)/shard_map/qkv_group/pallas_call | solution.py:863
  104.8 9.2 %attend.2 = (bf16[384,1024]{1,0:T(8,128)(2,1)}, f32[6,1,1024]{2,1,0:T(1,128)}) custom-call(s32[3]{0:T(128)} %bitcast.28, bf16[384,1024]{1,0:T(8,128)(2,1)} %get-tuple-element.100.q_ref, bf16[384,1024]{1,0:T(8,128)(2,1)} %get-tuple-element.101.k_ref, bf16[384,1024]{1,0:T(8,128)(2,1)} %get-tuple-element.102.v_ref), custom_call_target="tpu_custom_call" | custom-call | flops 9900000256 | bytes 65536 | tf_op jit(solution)/shard_map/attend/pallas_call | solution.py:177
  117.4 7.5 %qkv_group.3 = (bf16[384,1024]{1,0:T(8,128)(2,1)}, bf16[384,1024]{1,0:T(8,128)(2,1)}, bf16[384,1024]{1,0:T(8,128)(2,1)}) custom-call(s32[16]{0:T(128)} %iota_xor_fusion.order_ref, bf16[1024,768]{1,0:T(8,128)(2,1)} %copy-done.6, f32[2304,1]{1,0:T(8,128)} %copy-done.7, f32[384,1024]{1,0:T(8,128)} %copy-done.4, f32[384,1024]{1,0:T(8,128)} %copy-done.5, ...), custom_call_target="tpu_custom_call" | custom-call | flops 7699999744 | bytes 65536 | tf_op jit(solution)/shard_map/qkv_group/pallas_call | solution.py:863
  126.9 9.1 %attend.3 = (bf16[384,1024]{1,0:T(8,128)(2,1)}, f32[6,1,1024]{2,1,0:T(1,128)}) custom-call(s32[3]{0:T(128)} %bitcast.29, bf16[384,1024]{1,0:T(8,128)(2,1)} %get-tuple-element.108.q_ref, bf16[384,1024]{1,0:T(8,128)(2,1)} %get-tuple-element.109.k_ref, bf16[384,1024]{1,0:T(8,128)(2,1)} %get-tuple-element.110.v_ref), custom_call_target="tpu_custom_call" | custom-call | flops 9900000256 | bytes 65536 | tf_op jit(solution)/shard_map/attend/pallas_call | solution.py:177
  137.6 5.0 %collective-permute-done.43.rest_15_ = bf16[192,768]{1,0:T(8,128)(2,1)S(1)} collective-permute-done((bf16[192,768]{1,0:T(8,128)(2,1)S(1)}, bf16[192,768]{1,0:T(8,128)(2,1)S(1)}, u32[]{:S(2)}, u32[]{:S(2)}) %collective-permute-start.43) | collective-permute-done | bytes 294944 | tf_op jit(solution)/shard_map/ppermute | solution.py:564
  142.6 8.0 %out_project.1 = (f32[1024,768]{1,0:T(8,128)}, bf16[1024,768]{1,0:T(8,128)(2,1)}, bf16[768,1024]{1,0:T(8,128)(2,1)}) custom-call(s32[16]{0:T(128)} %iota_xor_fusion.order_ref, f32[8,768]{1,0:T(8,128)} %copy-done.17, bf16[384,1024]{1,0:T(8,128)(2,1)} %get-tuple-element.103.rest_0_.o_ref, bf16[384,1024]{1,0:T(8,128)(2,1)} %get-tuple-element.111.rest_1_.o_ref, ...), custom_call_target="tpu_custom_call" | custom-call | flops 8800000000 | bytes 65536 | tf_op jit(solution)/shard_map/out_project/pallas_call | solution.py:909
  151.8 25.0 %mlp_half.2 = (f32[1024,768]{1,0:T(8,128)}, f32[1024,768]{1,0:T(8,128)}, bf16[16,192,768]{2,1,0:T(8,128)(2,1)}, f32[1,1536]{1,0:T(1,128)}) custom-call(s32[16]{0:T(128)} %iota_xor_fusion.order_ref, bf16[1024,768]{1,0:T(8,128)(2,1)} %get-tuple-element.112.c_ref, bf16[768,1024]{1,0:T(8,128)(2,1)} %get-tuple-element.113.ct_ref, bf16[1024,768]{1,0:T(8,128)(2,1)} %bitcast.23, ...), custom_call_target="tpu_custom_call" | custom-call | flops 25300000768 | bytes 65536 | tf_op jit(solution)/shard_map/mlp_half/pallas_call | solution.py:1019
  176.9 25.8 %mlp_half.3 = (bf16[1024,768]{1,0:T(8,128)(2,1)}, f32[1024,768]{1,0:T(8,128)}, bf16[8,192,768]{2,1,0:T(8,128)(2,1)}, bf16[8,192,768]{2,1,0:T(8,128)(2,1)}, f32[1,1536]{1,0:T(1,128)}) custom-call(s32[16]{0:T(128)} %iota_xor_fusion.order_ref, bf16[1024,768]{1,0:T(8,128)(2,1)} %get-tuple-element.112.c_ref, bf16[768,1024]{1,0:T(8,128)(2,1)} %get-tuple-element.113.ct_ref, ...), custom_call_target="tpu_custom_call" | custom-call | flops 25300000768 | bytes 65536 | tf_op jit(solution)/shard_map/mlp_half/pallas_call | solution.py:1019
  203.2 12.2 %out_back.1 = (f32[1024,768]{1,0:T(8,128)}, bf16[768,1024]{1,0:T(8,128)(2,1)}, bf16[8,96,384]{2,1,0:T(8,128)(2,1)}, bf16[8,96,384]{2,1,0:T(8,128)(2,1)}, f32[8,768]{1,0:T(8,128)}) custom-call(s32[16]{0:T(128)} %iota_xor_fusion.order_ref, f32[1024,768]{1,0:T(8,128)} %get-tuple-element.127.dc_ref, f32[1024,768]{1,0:T(8,128)} %get-tuple-element.115.rest_0_.h_ref, ...), custom_call_target="tpu_custom_call" | custom-call | flops 13200000000 | bytes 65536 | tf_op jit(solution)/shard_map/out_back/pallas_call | solution.py:1096
  217.7 14.1 %heads_back.2 = (bf16[384,1024]{1,0:T(8,128)(2,1)}, bf16[384,1024]{1,0:T(8,128)(2,1)}, bf16[384,1024]{1,0:T(8,128)(2,1)}, bf16[192,1024]{1,0:T(8,128)(2,1)}) custom-call(s32[3]{0:T(128)} %bitcast.30, bf16[384,1024]{1,0:T(8,128)(2,1)} %get-tuple-element.108.q_ref, bf16[384,1024]{1,0:T(8,128)(2,1)} %get-tuple-element.109.k_ref, ...), custom_call_target="tpu_custom_call" | custom-call | flops 15399999488 | bytes 65536 | tf_op jit(solution)/shard_map/heads_back/pallas_call | solution.py:1188
  231.8 8.1 %qkv_grad.2 = (bf16[8,240,384]{2,1,0:T(8,128)(2,1)}, bf16[8,240,384]{2,1,0:T(8,128)(2,1)}, f32[16,1152]{1,0:T(8,128)}, f32[16,192]{1,0:T(8,128)}) custom-call(s32[16]{0:T(128)} %iota_xor_fusion.order_ref, bf16[768,1024]{1,0:T(8,128)(2,1)} %copy-done.3, bf16[16,1024]{1,0:T(8,128)(2,1)} %copy-done.14, bf16[192,1024]{1,0:T(8,128)(2,1)} %get-tuple-element.136.dangle_ref, ...), custom_call_target="tpu_custom_call" | custom-call | flops 6600000000 | bytes 65536 | tf_op jit(solution)/shard_map/qkv_grad/pallas_call | solution.py:1233
  240.1 13.7 %heads_back.3 = (bf16[384,1024]{1,0:T(8,128)(2,1)}, bf16[384,1024]{1,0:T(8,128)(2,1)}, bf16[384,1024]{1,0:T(8,128)(2,1)}, bf16[192,1024]{1,0:T(8,128)(2,1)}) custom-call(s32[3]{0:T(128)} %bitcast.31, bf16[384,1024]{1,0:T(8,128)(2,1)} %get-tuple-element.100.q_ref, bf16[384,1024]{1,0:T(8,128)(2,1)} %get-tuple-element.101.k_ref, ...), custom_call_target="tpu_custom_call" | custom-call | flops 15399999488 | bytes 65536 | tf_op jit(solution)/shard_map/heads_back/pallas_call | solution.py:1188
  261.1 7.4 %qkv_grad.3 = (bf16[8,144,384]{2,1,0:T(8,128)(2,1)}, bf16[8,144,384]{2,1,0:T(8,128)(2,1)}, f32[16,1152]{1,0:T(8,128)}, f32[16,192]{1,0:T(8,128)}) custom-call(s32[16]{0:T(128)} %iota_xor_fusion.order_ref, bf16[768,1024]{1,0:T(8,128)(2,1)} %copy-done.3, bf16[16,1024]{1,0:T(8,128)(2,1)} %copy-done.14, bf16[192,1024]{1,0:T(8,128)(2,1)} %get-tuple-element.147.dangle_ref, ...), custom_call_target="tpu_custom_call" | custom-call | flops 6600000000 | bytes 65536 | tf_op jit(solution)/shard_map/qkv_grad/pallas_call | solution.py:1233
  268.6 10.0 %collective-permute-done.49 = bf16[2,192,768]{2,1,0:T(8,128)(2,1)} collective-permute-done((bf16[2,192,768]{2,1,0:T(8,128)(2,1)}, bf16[2,192,768]{2,1,0:T(8,128)(2,1)}, u32[]{:S(2)}, u32[]{:S(2)}) %collective-permute-start.49) | collective-permute-done | bytes 589856 | tf_op jit(solution)/shard_map/ppermute | solution.py:564
  286.2 12.3 %input_back.1 = (bf16[1024,768]{1,0:T(8,128)(2,1)}, f32[8,768]{1,0:T(8,128)}) custom-call(s32[16]{0:T(128)} %iota_xor_fusion.order_ref, bf16[1024,768]{1,0:T(8,128)(2,1)} %bitcast.20, f32[1024,768]{1,0:T(8,128)} %get-tuple-element.153.dh_ref, f32[8,768]{1,0:T(8,128)} %copy-done.17, bf16[384,1024]{1,0:T(8,128)(2,1)} %get-tuple-element.148.dq_ref.rest_0_, ...), custom_call_target="tpu_custom_call" | custom-call | flops 13200000000 | bytes 65536 | tf_op jit(solution)/shard_map/input_back/pallas_call | solution.py:1284
  306.2 5.0 %all-to-all-done.1 = f32[16,1,672]{2,1,0:T(1,128)} async-done(((f32[16,1,672]{2,1,0:T(1,128)}), f32[16,1,672]{2,1,0:T(1,128)}, u32[]{:S(2)}, u32[]{:S(2)}) %all-to-all-start.1) | async-done | bytes 43040 | tf_op jit(solution)/shard_map/all_to_all | solution.py:1383
  321.3 6.7 %collective-permute-done.56 = bf16[2,240,384]{2,1,0:T(8,128)(2,1)S(1)} collective-permute-done((bf16[2,240,384]{2,1,0:T(8,128)(2,1)}, bf16[2,240,384]{2,1,0:T(8,128)(2,1)S(1)}, u32[]{:S(2)}, u32[]{:S(2)}) %collective-permute-start.56) | collective-permute-done | bytes 368672 | tf_op jit(solution)/shard_map/ppermute | solution.py:564
  333.9 6.9 %collective-permute-done.57 = bf16[1,240,384]{2,1,0:T(8,128)(2,1)S(1)} collective-permute-done((bf16[1,240,384]{2,1,0:T(8,128)(2,1)S(1)}, bf16[1,240,384]{2,1,0:T(8,128)(2,1)S(1)}, u32[]{:S(2)}, u32[]{:S(2)}) %collective-permute-start.57) | collective-permute-done | bytes 184352 | tf_op jit(solution)/shard_map/ppermute | solution.py:564
  352.3 5.4 %collective-permute-done.59.refs_1_ = bf16[192,768]{1,0:T(8,128)(2,1)S(1)} collective-permute-done((bf16[192,768]{1,0:T(8,128)(2,1)}, bf16[192,768]{1,0:T(8,128)(2,1)S(1)}, u32[]{:S(2)}, u32[]{:S(2)}) %collective-permute-start.59) | collective-permute-done | bytes 294944 | tf_op jit(solution)/shard_map/ppermute | solution.py:1374
  (334 shorter events, 121.5 us)
Async XLA Ops:
  7.3 169.6 %all-gather.3.cloned.1.call-start = ((), (), s32[]{:S(2)}) async-start(), calls=%async_computation.4 | async-start | bytes 5013504 | tf_op jit(solution)/shard_map/all_gather | solution.py:1335
  9.2 16.0 %collective-permute-start = (bf16[144,384]{1,0:T(8,128)(2,1)}, bf16[144,384]{1,0:T(8,128)(2,1)S(1)}, u32[]{:S(2)}, u32[]{:S(2)}) collective-permute-start(bf16[144,384]{1,0:T(8,128)(2,1)} %get-tuple-element.91.rest_0_.rest_6_), channel_id=1, source_target_pairs={{0,8},{1,9},{2,10},{3,11},{4,12},{5,13},{6,14},{7,15},{8,0},{9,1},... | collective-permute-start | bytes 331784 | tf_op jit(solution)/shard_map/ppermute | solution.py:564
  48.8 301.9 %reduce-scatter.2.cloned.1.call-start = ((), (), s32[]{:S(2)}) async-start(), calls=%async_computation.3 | async-start | bytes 5013504 | tf_op jit(solution)/shard_map/reduce_scatter | solution.py:1348
  62.1 16.0 %collective-permute-start.18 = (bf16[240,384]{1,0:T(8,128)(2,1)S(1)}, bf16[240,384]{1,0:T(8,128)(2,1)S(1)}, u32[]{:S(2)}, u32[]{:S(2)}) collective-permute-start(bf16[240,384]{1,0:T(8,128)(2,1)S(1)} %copy-done.54), channel_id=1, source_target_pairs={{0,4},{1,5},{2,6},{3,7},{4,0},{5,1},{6,2},{7,3},{8,12},{9,13},{10,... | collective-permute-start | bytes 552968 | tf_op jit(solution)/shard_map/ppermute | solution.py:564
  64.9 22.3 %collective-permute-start.37 = (bf16[192,768]{1,0:T(8,128)(2,1)}, bf16[192,768]{1,0:T(8,128)(2,1)S(1)}, u32[]{:S(2)}, u32[]{:S(2)}) collective-permute-start(bf16[192,768]{1,0:T(8,128)(2,1)} %get-tuple-element.118.rest_1_), channel_id=1, source_target_pairs={{0,8},{1,9},{2,10},{3,11},{4,12},{5,13},{6,14},{7,15},{8,0},{9,1},... | collective-permute-start | bytes 884744 | tf_op jit(solution)/shard_map/ppermute | solution.py:564
  67.2 25.8 %collective-permute-start.33 = (bf16[192,768]{1,0:T(8,128)(2,1)}, bf16[192,768]{1,0:T(8,128)(2,1)S(1)}, u32[]{:S(2)}, u32[]{:S(2)}) collective-permute-start(bf16[192,768]{1,0:T(8,128)(2,1)} %get-tuple-element.118.rest_1_), channel_id=1, source_target_pairs={{0,4},{1,5},{2,6},{3,7},{4,0},{5,1},{6,2},{7,3},{8,12},{9,13},{10,... | collective-permute-start | bytes 884744 | tf_op jit(solution)/shard_map/ppermute | solution.py:564
  78.7 23.5 %collective-permute-start.24 = (bf16[240,384]{1,0:T(8,128)(2,1)S(1)}, bf16[240,384]{1,0:T(8,128)(2,1)S(1)}, u32[]{:S(2)}, u32[]{:S(2)}) collective-permute-start(bf16[240,384]{1,0:T(8,128)(2,1)S(1)} %collective-permute-done.22.rest_8_.rest_11_.rest_10_.rest_30_), channel_id=1, source_target_pairs={{0,2},{1,3},{2,0},{3,1},{4,6},{5,7},{6,4},{7,5},{8,10},{9,11},{10,... | collective-permute-start | bytes 552968 | tf_op jit(solution)/shard_map/ppermute | solution.py:564
  79.2 22.9 %collective-permute-start.20 = (bf16[240,384]{1,0:T(8,128)(2,1)S(1)}, bf16[240,384]{1,0:T(8,128)(2,1)S(1)}, u32[]{:S(2)}, u32[]{:S(2)}) collective-permute-start(bf16[240,384]{1,0:T(8,128)(2,1)S(1)} %collective-permute-done.18.rest_4_.rest_7_.rest_6_.rest_26_), channel_id=1, source_target_pairs={{0,2},{1,3},{2,0},{3,1},{4,6},{5,7},{6,4},{7,5},{8,10},{9,11},{10,... | collective-permute-start | bytes 552968 | tf_op jit(solution)/shard_map/ppermute | solution.py:564
  80.7 20.7 %collective-permute-start.23 = (bf16[240,384]{1,0:T(8,128)(2,1)S(1)}, bf16[240,384]{1,0:T(8,128)(2,1)S(1)}, u32[]{:S(2)}, u32[]{:S(2)}) collective-permute-start(bf16[240,384]{1,0:T(8,128)(2,1)S(1)} %collective-permute-done.22.rest_8_.rest_11_.rest_10_.rest_30_), channel_id=1, source_target_pairs={{0,1},{1,0},{2,3},{3,2},{4,5},{5,4},{6,7},{7,6},{8,9},{9,8},{10,11... | collective-permute-start | bytes 552968 | tf_op jit(solution)/shard_map/ppermute | solution.py:564
  87.3 14.3 %collective-permute-start.19 = (bf16[240,384]{1,0:T(8,128)(2,1)S(1)}, bf16[240,384]{1,0:T(8,128)(2,1)S(1)}, u32[]{:S(2)}, u32[]{:S(2)}) collective-permute-start(bf16[240,384]{1,0:T(8,128)(2,1)S(1)} %collective-permute-done.18.rest_4_.rest_7_.rest_6_.rest_26_), channel_id=1, source_target_pairs={{0,1},{1,0},{2,3},{3,2},{4,5},{5,4},{6,7},{7,6},{8,9},{9,8},{10,11... | collective-permute-start | bytes 552968 | tf_op jit(solution)/shard_map/ppermute | solution.py:564
  101.6 13.6 %collective-permute-start.27 = (bf16[240,384]{1,0:T(8,128)(2,1)S(1)}, bf16[240,384]{1,0:T(8,128)(2,1)S(1)}, u32[]{:S(2)}, u32[]{:S(2)}) collective-permute-start(bf16[240,384]{1,0:T(8,128)(2,1)S(1)} %collective-permute-done.26.rest_12_.rest_15_.rest_14_.rest_34_), channel_id=1, source_target_pairs={{0,1},{1,0},{2,3},{3,2},{4,5},{5,4},{6,7},{7,6},{8,9},{9,8},{10,11... | collective-permute-start | bytes 552968 | tf_op jit(solution)/shard_map/ppermute | solution.py:564
  115.2 21.9 %collective-permute-start.39 = (bf16[192,768]{1,0:T(8,128)(2,1)S(1)}, bf16[192,768]{1,0:T(8,128)(2,1)S(1)}, u32[]{:S(2)}, u32[]{:S(2)}) collective-permute-start(bf16[192,768]{1,0:T(8,128)(2,1)S(1)} %collective-permute-done.37.rest_9_), channel_id=1, source_target_pairs={{0,2},{1,3},{2,0},{3,1},{4,6},{5,7},{6,4},{7,5},{8,10},{9,11},{10,... | collective-permute-start | bytes 884744 | tf_op jit(solution)/shard_map/ppermute | solution.py:564
  116.7 20.4 %collective-permute-start.35 = (bf16[192,768]{1,0:T(8,128)(2,1)S(1)}, bf16[192,768]{1,0:T(8,128)(2,1)S(1)}, u32[]{:S(2)}, u32[]{:S(2)}) collective-permute-start(bf16[192,768]{1,0:T(8,128)(2,1)S(1)} %collective-permute-done.33.rest_5_), channel_id=1, source_target_pairs={{0,2},{1,3},{2,0},{3,1},{4,6},{5,7},{6,4},{7,5},{8,10},{9,11},{10,... | collective-permute-start | bytes 884744 | tf_op jit(solution)/shard_map/ppermute | solution.py:564
  125.5 17.0 %collective-permute-start.43 = (bf16[192,768]{1,0:T(8,128)(2,1)S(1)}, bf16[192,768]{1,0:T(8,128)(2,1)S(1)}, u32[]{:S(2)}, u32[]{:S(2)}) collective-permute-start(bf16[192,768]{1,0:T(8,128)(2,1)S(1)} %collective-permute-done.41.rest_13_), channel_id=1, source_target_pairs={{0,2},{1,3},{2,0},{3,1},{4,6},{5,7},{6,4},{7,5},{8,10},{9,11},{10,... | collective-permute-start | bytes 884744 | tf_op jit(solution)/shard_map/ppermute | solution.py:564
  136.1 14.5 %collective-permute-start.32 = (bf16[192,768]{1,0:T(8,128)(2,1)S(1)}, bf16[192,768]{1,0:T(8,128)(2,1)S(1)}, u32[]{:S(2)}, u32[]{:S(2)}) collective-permute-start(bf16[192,768]{1,0:T(8,128)(2,1)S(1)} %collective-permute-done.31.rest_3_), channel_id=1, source_target_pairs={{0,1},{1,0},{2,3},{3,2},{4,5},{5,4},{6,7},{7,6},{8,9},{9,8},{10,11... | collective-permute-start | bytes 884744 | tf_op jit(solution)/shard_map/ppermute | solution.py:564
  136.2 14.5 %collective-permute-start.42 = (bf16[192,768]{1,0:T(8,128)(2,1)S(1)}, bf16[192,768]{1,0:T(8,128)(2,1)S(1)}, u32[]{:S(2)}, u32[]{:S(2)}) collective-permute-start(bf16[192,768]{1,0:T(8,128)(2,1)S(1)} %collective-permute-done.41.rest_13_), channel_id=1, source_target_pairs={{0,1},{1,0},{2,3},{3,2},{4,5},{5,4},{6,7},{7,6},{8,9},{9,8},{10,11... | collective-permute-start | bytes 884744 | tf_op jit(solution)/shard_map/ppermute | solution.py:564
  217.1 39.8 %collective-permute-start.47 = (bf16[4,192,768]{2,1,0:T(8,128)(2,1)S(1)}, bf16[4,192,768]{2,1,0:T(8,128)(2,1)S(1)}, u32[]{:S(2)}, u32[]{:S(2)}) collective-permute-start(bf16[4,192,768]{2,1,0:T(8,128)(2,1)S(1)} %add_convert_fusion), channel_id=1, source_target_pairs={{0,2},{1,3},{2,0},{3,1},{4,6},{5,7},{6,4},{7,5},{8,10},{9,11},{10,... | collective-permute-start | bytes 3538952 | tf_op jit(solution)/shard_map/ppermute | solution.py:564
  239.9 19.1 %collective-permute-start.46 = (bf16[8,240,384]{2,1,0:T(8,128)(2,1)}, bf16[8,240,384]{2,1,0:T(8,128)(2,1)S(1)}, u32[]{:S(2)}, u32[]{:S(2)}) collective-permute-start(bf16[8,240,384]{2,1,0:T(8,128)(2,1)} %get-tuple-element.146), channel_id=1, source_target_pairs={{0,1},{1,0},{2,3},{3,2},{4,5},{5,4},{6,7},{7,6},{8,9},{9,8},{10,11... | collective-permute-start | bytes 4423688 | tf_op jit(solution)/shard_map/ppermute | solution.py:564
  259.0 19.6 %collective-permute-start.49 = (bf16[2,192,768]{2,1,0:T(8,128)(2,1)}, bf16[2,192,768]{2,1,0:T(8,128)(2,1)}, u32[]{:S(2)}, u32[]{:S(2)}) collective-permute-start(bf16[2,192,768]{2,1,0:T(8,128)(2,1)} %add_convert_fusion.2), channel_id=1, source_target_pairs={{0,4},{1,5},{2,6},{3,7},{4,0},{5,1},{6,2},{7,3},{8,12},{9,13},{10,... | collective-permute-start | bytes 1769480 | tf_op jit(solution)/shard_map/ppermute | solution.py:564
  260.2 23.0 %collective-permute-start.50 = (bf16[4,240,384]{2,1,0:T(8,128)(2,1)}, bf16[4,240,384]{2,1,0:T(8,128)(2,1)}, u32[]{:S(2)}, u32[]{:S(2)}) collective-permute-start(bf16[4,240,384]{2,1,0:T(8,128)(2,1)} %add_convert_fusion.1), channel_id=1, source_target_pairs={{0,2},{1,3},{2,0},{3,1},{4,6},{5,7},{6,4},{7,5},{8,10},{9,11},{10,... | collective-permute-start | bytes 2211848 | tf_op jit(solution)/shard_map/ppermute | solution.py:564
  268.5 16.7 %collective-permute-start.48 = (bf16[8,144,384]{2,1,0:T(8,128)(2,1)}, bf16[8,144,384]{2,1,0:T(8,128)(2,1)S(1)}, u32[]{:S(2)}, u32[]{:S(2)}) collective-permute-start(bf16[8,144,384]{2,1,0:T(8,128)(2,1)} %get-tuple-element.152), channel_id=1, source_target_pairs={{0,1},{1,0},{2,3},{3,2},{4,5},{5,4},{6,7},{7,6},{8,9},{9,8},{10,11... | collective-permute-start | bytes 2654216 | tf_op jit(solution)/shard_map/ppermute | solution.py:564
  280.5 33.2 %collective-permute-start.60 = (bf16[1,192,768]{2,1,0:T(8,128)(2,1)}, bf16[1,192,768]{2,1,0:T(8,128)(2,1)}, u32[]{:S(2)}, u32[]{:S(2)}) collective-permute-start(bf16[1,192,768]{2,1,0:T(8,128)(2,1)} %add_convert_fusion.6), channel_id=1, source_target_pairs={{0,8},{1,9},{2,10},{3,11},{4,12},{5,13},{6,14},{7,15},{8,0},{9,1},... | collective-permute-start | bytes 884744 | tf_op jit(solution)/shard_map/ppermute | solution.py:564
  304.5 13.9 %collective-permute-start.52 = (bf16[4,144,384]{2,1,0:T(8,128)(2,1)}, bf16[4,144,384]{2,1,0:T(8,128)(2,1)}, u32[]{:S(2)}, u32[]{:S(2)}) collective-permute-start(bf16[4,144,384]{2,1,0:T(8,128)(2,1)} %add_convert_fusion.3), channel_id=1, source_target_pairs={{0,2},{1,3},{2,0},{3,1},{4,6},{5,7},{6,4},{7,5},{8,10},{9,11},{10,... | collective-permute-start | bytes 1327112 | tf_op jit(solution)/shard_map/ppermute | solution.py:564
  315.7 36.6 %collective-permute-start.61 = (bf16[192,768]{1,0:T(8,128)(2,1)}, bf16[192,768]{1,0:T(8,128)(2,1)S(1)}, u32[]{:S(2)}, u32[]{:S(2)}) collective-permute-start(bf16[192,768]{1,0:T(8,128)(2,1)} %fusion.refs_2_), channel_id=1, source_target_pairs={{0,16},{16,0},{1,17},{17,1},{2,18},{18,2},{3,19},{19,3},{4,20},{20... | collective-permute-start | bytes 884744 | tf_op jit(solution)/shard_map/ppermute | solution.py:617
  (127 other events, 1568.0 us)
Sparse Core Ops, SparseCore 0:
  48.9 65.7 all-gather.2
  203.3 101.7 reduce-scatter.1

commit v3 on v2

--- a/solution.py
+++ b/solution.py
@@ -148,10 +148,6 @@
     def _():
         bias_ref[...] = second_bias(counts_ref, slots)
 
-    k = k_ref[...].T
-    q = q_ref[...]
-    v = v_ref[...]
-
     def part(scores, first, values):
         peak = jnp.max(scores, axis=0, keepdims=True)
         weights = jnp.exp(scores - peak)
@@ -162,30 +158,34 @@
         mixed = nn(values, wb) * (1.0 / total)
         return mixed, peak + jnp.log(total)
 
-    mixed1, lse1 = part(nn(k[:FIRST], q[:, :WIDE]), True, v[:, :WIDE])
-    mixed2, lse2 = part(nn(k[FIRST:], q[:, CUT:]) + bias_ref[...], False, v[:, CUT:])
     edge = lax.broadcasted_iota(jnp.int32, (1, WIDE - CUT), 1) < FIRST - CUT
-    for out, one, two in ((o_ref, mixed1, mixed2), (lse_ref.at[0], lse1, lse2)):
-        out[:, :CUT] = one[:, :CUT].astype(out.dtype)
-        out[:, CUT:WIDE] = jnp.where(edge, one[:, CUT:], two[:, : WIDE - CUT]).astype(out.dtype)
-        out[:, WIDE:] = two[:, WIDE - CUT :].astype(out.dtype)
+    for h in range(q_ref.shape[0] // HEAD_DIM):
+        rows = slice(h * HEAD_DIM, (h + 1) * HEAD_DIM)
+        k = k_ref[rows, :].T
+        q = q_ref[rows, :]
+        v = v_ref[rows, :]
+        mixed1, lse1 = part(nn(k[:FIRST], q[:, :WIDE]), True, v[:, :WIDE])
+        mixed2, lse2 = part(nn(k[FIRST:], q[:, CUT:]) + bias_ref[...], False, v[:, CUT:])
+        for out, one, two in ((o_ref.at[rows], mixed1, mixed2), (lse_ref.at[h], lse1, lse2)):
+            out[:, :CUT] = one[:, :CUT].astype(out.dtype)
+            out[:, CUT:WIDE] = jnp.where(edge, one[:, CUT:], two[:, : WIDE - CUT]).astype(out.dtype)
+            out[:, WIDE:] = two[:, WIDE - CUT :].astype(out.dtype)
 
 
 def attend(counts, q, k, v):
     width, slots = q.shape
-    head = pl.BlockSpec((HEAD_DIM, slots), lambda h: (h, 0))
+    heads = width // HEAD_DIM
+    each = 2
+    head = pl.BlockSpec((each * HEAD_DIM, slots), lambda h: (h, 0))
     return pl.pallas_call(
         attend_kernel,
-        grid=(width // HEAD_DIM,),
+        grid=(heads // each,),
         in_specs=[pl.BlockSpec(memory_space=pltpu.SMEM)] + [head] * 3,
-        out_specs=[head, pl.BlockSpec((1, 1, slots), lambda h: (h, 0, 0))],
-        out_shape=[
-            jax.ShapeDtypeStruct((width, slots), BF),
-            jax.ShapeDtypeStruct((width // HEAD_DIM, 1, slots), F32),
-        ],
+        out_specs=[head, pl.BlockSpec((each, 1, slots), lambda h: (h, 0, 0))],
+        out_shape=[jax.ShapeDtypeStruct((width, slots), BF), jax.ShapeDtypeStruct((heads, 1, slots), F32)],
         scratch_shapes=[pltpu.VMEM((slots - FIRST, slots - CUT), F32)],
         compiler_params=params(),
-        cost_estimate=cost(9),
+        cost_estimate=cost(8),
         name="attend",
     )(counts, q, k, v)
 
@@ -576,6 +576,10 @@
         v = self.piece[source]
         self.piece[source ^ mask] = swap(tie(v, *after) if after else v, mask)
 
+    def hold(self, sources, after):
+        for p in sources:
+            self.piece[p] = tie(self.piece[p], after)
+
     def stage1(self, *after):
         for mask in (8, 4, 2):
             self.send(0, mask, after)
@@ -604,6 +608,9 @@
         for g in self.got[1:]:
             out = out + g[lo:hi].astype(F32)
         return out.astype(BF)
+
+    def hold(self, after):
+        self.got[-1] = tie(self.got[-1], after)
 
     def step(self):
         lo = self.size
@@ -614,7 +621,23 @@
 
     def finish(self):
         mine = self.total(0, 1)[0]
-        return mine, lax.ppermute(mine, "rep", [(0, 1), (1, 0)])
+        return mine, across(mine)
+
+
+class SplitScatter(Scatter):
+    def __init__(self, near, far):
+        self.start = [near, swap(far, 1)]
+        self.size = 4
+
+    def split(self):
+        sent = (self.start[0][1].astype(F32) + self.start[1][1].astype(F32)).astype(BF)
+        got = across(sent)
+        self.got = [self.start[0][0], self.start[1][0], got]
+        return sent
+
+
+def across(v):
+    return lax.ppermute(v, "rep", [(0, 1), (1, 0)])
 
 
 def start_all(copies):
@@ -640,26 +663,30 @@
 VMEM = pl.BlockSpec(memory_space=pltpu.VMEM)
 
 
-def group_piece_kernel(w_ref, o_ref, a_ref, b_ref):
+LINES = 16
+
+
+def group_piece_kernel(w_ref, o_ref, v_ref, a_ref, b_ref):
     rows, cols = w_ref.shape[0], a_ref.shape[1]
     for i in range(3):
         for g, out in enumerate((a_ref, b_ref)):
             out[i * rows : (i + 1) * rows, :] = w_ref[:, (i * GROUPS + g) * cols : (i * GROUPS + g + 1) * cols]
     for i in range(2):
         b_ref[(3 + i) * rows : (4 + i) * rows, :] = o_ref[:, i * cols : (i + 1) * cols]
-
-
-def group_pieces(w, w_out):
+    a_ref[3 * rows :, :] = jnp.concatenate([v_ref[...], jnp.zeros((LINES - v_ref.shape[0], cols), BF)], axis=0)
+
+
+def group_pieces(w, w_out, vectors):
     rows, cols = w.shape[0], w_out.shape[1] // 2
     return pl.pallas_call(
         group_piece_kernel,
-        in_specs=[VMEM, VMEM],
+        in_specs=[VMEM] * 3,
         out_specs=[VMEM, VMEM],
-        out_shape=[jax.ShapeDtypeStruct((3 * rows, cols), BF), jax.ShapeDtypeStruct((5 * rows, cols), BF)],
+        out_shape=[jax.ShapeDtypeStruct((3 * rows + LINES, cols), BF), jax.ShapeDtypeStruct((5 * rows, cols), BF)],
         compiler_params=params(),
         cost_estimate=cost(2),
         name="group_pieces",
-    )(w, w_out)
+    )(w, w_out, vectors)
 
 
 def mlp_piece_kernel(w1_ref, w2_ref, *outs):
@@ -687,26 +714,29 @@
     )(w1, w2)
 
 
-def mlp_join_kernel(*refs):
-    ins, (w1_ref, w2_ref) = refs[:4], refs[4:]
+def mlp_join_kernel(order_ref, c_ref, c_other_ref, d_ref, d_other_ref, w1_ref, w2_ref):
     rows1 = w1_ref.shape[0]
     own = w2_ref.shape[0] // 2
     per = SHARDS // 2
-    sums = [ins[2 * i][...].astype(F32) + ins[2 * i + 1][...].astype(F32) for i in range(2)]
+    c = c_ref[...].astype(F32) + c_other_ref[...].astype(F32)
+    mine = d_ref[...].astype(F32)
+    other = d_other_ref[...].astype(F32)
+    here = order_ref[SHARDS] == 0
+    d = jnp.where(here, mine, other)
     runs = []
     for b in range(2):
         for j in range(per):
-            runs += [m[b * rows1 : (b + 1) * rows1, j * own : (j + 1) * own] for m in sums]
+            runs += [m[b * rows1 : (b + 1) * rows1, j * own : (j + 1) * own] for m in (c, d)]
     w1_ref[...] = jnp.concatenate(runs, axis=1)
-    for i in range(2):
-        w2_ref[i * own : (i + 1) * own, :] = sums[i][2 * rows1 :]
-
-
-def mlp_join(rows1, parts):
+    w2_ref[:own, :] = c[2 * rows1 :]
+    w2_ref[own:, :] = jnp.where(here, other, mine)
+
+
+def mlp_join(rows1, order, parts):
     own = parts[0].shape[0] - 2 * rows1
     return pl.pallas_call(
         mlp_join_kernel,
-        in_specs=[VMEM] * 4,
+        in_specs=[SMEM] + [VMEM] * 4,
         out_specs=[VMEM] * 2,
         out_shape=[
             jax.ShapeDtypeStruct((rows1, 2 * own * SHARDS), F32),
@@ -715,7 +745,7 @@
         compiler_params=params(),
         cost_estimate=cost(3),
         name="mlp_join",
-    )(*parts)
+    )(order, *parts)
 
 
 def spread(packed, lo, size):
@@ -726,41 +756,43 @@
     return jnp.broadcast_to(v, (8, v.shape[1])).T[:, 0:1]
 
 
-def look_up(table, places):
-    top = table.astype(BF)
-    rest = table - top.astype(F32)
-    middle = rest.astype(BF)
-    low = (rest - middle.astype(F32)).astype(BF)
-    return nn(top, places) + nn(middle, places) + nn(low, places)
-
-
-def prepare_kernel(sizes, packed_ref, x_ref, cols_ref, rows_ref, a_ref, at_ref, cos_ref, sin_ref, vec_ref, b1_ref, bias_ref, sel_ref):
-    packed = packed_ref[...].astype(F32)
-    starts = [sum(sizes[:i]) for i in range(len(sizes))]
-    gain1, shift1, b_qkv, freqs, b_out, gain2, shift2 = (spread(packed, starts[i], sizes[i]) for i in range(7))
-    b2 = spread(packed, starts[8], sizes[8])
-    for i, v in enumerate((b_out, gain1, gain2, shift2, b2)):
-        vec_ref[i : i + 1, :] = v
-    own = sizes[7] // 2
-    for i in range(2):
-        b1_ref[i : i + 1, :] = spread(packed, starts[7] + i * own, own)
-    bias_ref[...] = column(b_qkv)
-    tile = 256
-    for i in range(x_ref.shape[0] // tile):
-        rows = slice(i * tile, (i + 1) * tile)
-        xhat, _ = norm_parts(x_ref[rows, :].astype(F32))
-        a = (xhat * gain1 + shift1).astype(BF)
-        a_ref[rows, :] = a
-        at_ref[:, rows] = a.T
-    freq = column(freqs)
-    half = freq.shape[0] // 2
-    slots = x_ref.shape[0]
-    spots = lax.broadcasted_iota(jnp.int32, (1, 128), 1).astype(F32)
+def prepare_kernel(sizes, order_ref, x_ref, cols_ref, rows_ref, *rest):
+    pieces = rest[:SHARDS]
+    at_ref, cos_ref, sin_ref, vec_ref, b1_ref, bias_ref, sel_ref, line_scr, table_scr, sem = rest[SHARDS:]
+    half = cos_ref.shape[0]
+
+    @pl.when(pl.program_id(0) == 0)
+    def _():
+        last = pieces[0].shape[0]
+        copies = fetch(pieces, order_ref, [(slice(last - LINES, last), lambda d: line_scr.at[d])], sem)
+        start_all(copies)
+        wait_all(copies)
+        packed = jnp.concatenate([line_scr[:, i, :] for i in range(2)], axis=1).astype(F32)
+        starts = [sum(sizes[:i]) for i in range(len(sizes))]
+        gain1, shift1, b_qkv, freqs, b_out, gain2, shift2 = (spread(packed, starts[i], sizes[i]) for i in range(7))
+        b2 = spread(packed, starts[8], sizes[8])
+        for i, v in enumerate((b_out, gain1, gain2, shift2, b2, shift1)):
+            vec_ref[i : i + 1, :] = v
+        own = sizes[7] // 2
+        for i in range(2):
+            b1_ref[i : i + 1, :] = spread(packed, starts[7] + i * own, own)
+        bias_ref[...] = column(b_qkv)
+        freq = column(freqs)
+        spots = lax.broadcasted_iota(jnp.int32, (1, 128), 1).astype(F32)
+        for i in range(2):
+            angle = freq[i * half : (i + 1) * half] * spots
+            for k, table in enumerate((jnp.cos(angle), jnp.sin(angle))):
+                for n in range(3):
+                    term = table.astype(BF)
+                    table_scr[i, k, n] = term
+                    table = table - term.astype(F32)
+
+    xhat, _ = norm_parts(x_ref[...].astype(F32))
+    at_ref[...] = (xhat * vec_ref[1:2, :] + vec_ref[5:6, :]).astype(BF).T
     found = []
-    for f, at in ((freq[:half], cols_ref[...]), (freq[half:], rows_ref[...])):
-        angle = f * spots
-        one_hot = jnp.where(lax.broadcasted_iota(jnp.int32, (128, slots), 0) == at, 1.0, 0.0).astype(BF)
-        found.append((look_up(jnp.cos(angle), one_hot), look_up(jnp.sin(angle), one_hot)))
+    for i, at in enumerate((cols_ref[...], rows_ref[...])):
+        one_hot = jnp.where(lax.broadcasted_iota(jnp.int32, (128, at.shape[1]), 0) == at, 1.0, 0.0).astype(BF)
+        found.append([sum(nn(table_scr[i, k, n], one_hot) for n in range(3)) for k in range(2)])
     (cos_c, sin_c), (cos_r, sin_r) = found
     cos_ref[...] = cos_c * cos_r - sin_c * sin_r
     sin_ref[...] = sin_c * cos_r + cos_c * sin_r
@@ -769,16 +801,22 @@
     sel_ref[...] = jnp.where(line < 2, sel, jnp.where(line == 2, 1.0, 0.0)).astype(BF)
 
 
-def prepare(sizes, packed, x, patch_cols, patch_rows):
+def prepare(sizes, order, x, patch_cols, patch_rows, pieces):
     slots, width = x.shape
     own = sizes[7] // 2
+    blk = 256
     shape = jax.ShapeDtypeStruct
+    tall = lambda n: pl.BlockSpec((n, blk), lambda i: (0, i))
+    whole = lambda r, k: pl.BlockSpec((r, k), lambda i: (0, 0))
     return pl.pallas_call(
         partial(prepare_kernel, sizes),
-        in_specs=[VMEM] * 4,
-        out_specs=[VMEM] * 8,
+        grid=(slots // blk,),
+        in_specs=[SMEM, pl.BlockSpec((blk, width), lambda i: (i, 0)), tall(1), tall(1)] + [ANY] * SHARDS,
+        out_specs=[
+            tall(width), tall(width // 2), tall(width // 2),
+            whole(8, width), whole(2, own * SHARDS), whole(3 * width, 1), tall(16),
+        ],
         out_shape=[
-            shape((slots, width), BF),
             shape((width, slots), BF),
             shape((width // 2, slots), F32),
             shape((width // 2, slots), F32),
@@ -787,10 +825,15 @@
             shape((3 * width, 1), F32),
             shape((16, slots), BF),
         ],
-        compiler_params=params(40),
-        cost_estimate=cost(9),
+        scratch_shapes=[
+            pltpu.VMEM((SHARDS, LINES, width // GROUPS), BF),
+            pltpu.VMEM((2, 2, 3, width // 2, 128), BF),
+            pltpu.SemaphoreType.DMA((SHARDS,)),
+        ],
+        compiler_params=params(),
+        cost_estimate=cost(8),
         name="prepare",
-    )(packed, x, patch_cols, patch_rows)
+    )(order, x, patch_cols, patch_rows, *pieces)
 
 
 def pack_kernel(sums1_ref, sums2_ref, b1a_ref, b1b_ref, *rest):
@@ -820,33 +863,30 @@
         in_specs=[VMEM] * len(sums),
         out_specs=VMEM,
         out_shape=jax.ShapeDtypeStruct((SHARDS, size), F32),
-        compiler_params=params(16),
+        compiler_params=params(),
         cost_estimate=cost(3),
         name="pack",
     )(*sums)
 
 
-def group_kernel(group, order_ref, a_ref, bias_ref, cos_ref, sin_ref, *rest):
-    pieces, (q_ref, k_ref, v_ref, w_scr, sem) = rest[:SHARDS], rest[SHARDS:]
+def group_kernel(order_ref, at_ref, bq_ref, bk_ref, bv_ref, cos_ref, sin_ref, *rest):
+    pieces, (q_ref, k_ref, v_ref, w_scr, wt_scr, sem) = rest[:SHARDS], rest[SHARDS:]
     cols = q_ref.shape[0]
     part = w_scr.shape[1] // 3
-    copies = fetch(pieces, order_ref, [(slice(0, 3 * part), lambda d: w_scr.at[d])], sem)
-    start_all(copies)
-    a = a_ref[...]
-    turn = slice(group * cols // 2, (group + 1) * cols // 2)
-    cos = cos_ref[turn, :]
-    sin = sin_ref[turn, :]
-    wait_all(copies)
-
-    def weight(i):
-        return w_scr[:, i * part : (i + 1) * part, :].reshape(a.shape[1], cols).T
-
-    def bias(i):
-        at = i * a.shape[1] + group * cols
-        return bias_ref[at : at + cols, :]
-
-    for i, out_ref, scale in ((0, q_ref, HEAD_DIM**-0.5), (1, k_ref, 1.0)):
-        u = nt(weight(i), a) + bias(i)
+
+    @pl.when(pl.program_id(0) == 0)
+    def _():
+        copies = fetch(pieces, order_ref, [(slice(0, 3 * part), lambda d: w_scr.at[d])], sem)
+        start_all(copies)
+        wait_all(copies)
+        for i in range(3):
+            wt_scr[i] = w_scr[:, i * part : (i + 1) * part, :].reshape(SHARDS * part, cols).T
+
+    a_t = at_ref[...]
+    cos = cos_ref[...]
+    sin = sin_ref[...]
+    for i, b_ref, out_ref, scale in ((0, bq_ref, q_ref, HEAD_DIM**-0.5), (1, bk_ref, k_ref, 1.0)):
+        u = nn(wt_scr[i], a_t) + b_ref[...]
         for h in range(cols // HEAD_DIM):
             u1 = u[h * HEAD_DIM : h * HEAD_DIM + HALF]
             u2 = u[h * HEAD_DIM + HALF : (h + 1) * HEAD_DIM]
@@ -854,22 +894,32 @@
             s = sin[h * HALF : (h + 1) * HALF]
             out_ref[h * HEAD_DIM : h * HEAD_DIM + HALF, :] = ((u1 * c - u2 * s) * scale).astype(BF)
             out_ref[h * HEAD_DIM + HALF : (h + 1) * HEAD_DIM, :] = ((u1 * s + u2 * c) * scale).astype(BF)
-    v_ref[...] = (nt(weight(2), a) + bias(2)).astype(BF)
-
-
-def project_group(group, order, a, bias, cos, sin, pieces):
-    slots, width = a.shape
+    v_ref[...] = (nn(wt_scr[2], a_t) + bv_ref[...]).astype(BF)
+
+
+def project_group(group, order, a_t, bias, cos, sin, pieces):
+    width, slots = a_t.shape
     cols = pieces[0].shape[1]
-    return pl.pallas_call(
-        partial(group_kernel, group),
-        in_specs=[SMEM] + [VMEM] * 4 + [ANY] * SHARDS,
-        out_specs=[VMEM] * 3,
+    blk = 512
+    tall = lambda n, at: pl.BlockSpec((n, blk), lambda i: (at, i))
+    return pl.pallas_call(
+        group_kernel,
+        grid=(slots // blk,),
+        in_specs=[SMEM, tall(width, 0)]
+        + [pl.BlockSpec((cols, 1), lambda i, n=n: (n * GROUPS + group, 0)) for n in range(3)]
+        + [tall(cols // 2, group)] * 2
+        + [ANY] * SHARDS,
+        out_specs=[tall(cols, 0)] * 3,
         out_shape=[jax.ShapeDtypeStruct((cols, slots), BF)] * 3,
-        scratch_shapes=[pltpu.VMEM((SHARDS, 3 * width // SHARDS, cols), BF), pltpu.SemaphoreType.DMA((SHARDS,))],
+        scratch_shapes=[
+            pltpu.VMEM((SHARDS, 3 * width // SHARDS, cols), BF),
+            pltpu.VMEM((3, cols, width), BF),
+            pltpu.SemaphoreType.DMA((SHARDS,)),
+        ],
         compiler_params=params(),
         cost_estimate=cost(7),
         name="qkv_group",
-    )(order, a, bias, cos, sin, *pieces)
+    )(order, a_t, bias, bias, bias, cos, sin, *pieces)
 
 
 def out_moves(w_scr, start):
@@ -989,19 +1039,22 @@
         gb1_ref[:, cols] = total
         g1_scr[j] = nn(ct_ref[...], dp_scr[...]).astype(BF).reshape(SHARDS, rows1, blk)
         if split:
-            dests = [(g_refs[b].at[i], order_ref[p + b]) for b in range(2) for i, p in enumerate(LEAVING)]
+            mine = order_ref[SHARDS]
+            dests = [(g_refs[b], i, order_ref[p + b]) for b in range(2) for i, p in enumerate(LEAVING)]
+            place = lambda dst, i, lo, n: dst.at[lax.rem(lo // (steps * rows1) + mine, 2), i, pl.ds(lo % (steps * rows1), n)]
         else:
-            dests = [(g_refs[0].at[p], p) for p in range(SHARDS)]
+            dests = [(g_refs[0], p, p) for p in range(SHARDS)]
+            place = lambda dst, i, lo, n: dst.at[i, pl.ds(lo, n)]
         copies = [
-            pltpu.make_async_copy(g1_scr.at[j, d], dst.at[slice(j * rows1, (j + 1) * rows1)], sem.at[j, n])
-            for n, (dst, d) in enumerate(dests)
+            pltpu.make_async_copy(g1_scr.at[j, d], place(dst, i, j * rows1, rows1), sem.at[j, n])
+            for n, (dst, i, d) in enumerate(dests)
         ]
         start_all(copies)
         sends += copies
         g2_scr[j * per : (j + 1) * per] = tn(hb_scr[...], dy_ref[...]).astype(BF).reshape(per, rows2, width)
     copies = [
-        pltpu.make_async_copy(g2_scr.at[d], dst.at[slice(steps * rows1, steps * rows1 + rows2)], sem.at[steps, n])
-        for n, (dst, d) in enumerate(dests)
+        pltpu.make_async_copy(g2_scr.at[d], place(dst, i, steps * rows1, rows2), sem.at[steps, n])
+        for n, (dst, i, d) in enumerate(dests)
     ]
     start_all(copies)
     wait_all(sends + copies)
@@ -1015,7 +1068,9 @@
     steps = 2
     blk = hidden // steps
     first = len(sums) == 1
-    block = jax.ShapeDtypeStruct((SHARDS // 2 if split else SHARDS, 2 * rows1 + rows2, width), BF)
+    block = jax.ShapeDtypeStruct((SHARDS, 2 * rows1 + rows2, width), BF)
+    if split:
+        block = jax.ShapeDtypeStruct((2, SHARDS // 2, rows2, width), BF)
     return pl.pallas_call(
         partial(mlp_half_kernel, part, first, split, len(pieces)),
         in_specs=[SMEM] + [VMEM] * 5 + [ANY] * (len(sums) + len(pieces)),
@@ -1036,7 +1091,7 @@
             pltpu.SemaphoreType.DMA((8,)),
         ]
         + ([] if first else [pltpu.VMEM((slots, width), BF)]),
-        compiler_params=params(56),
+        compiler_params=params(),
         cost_estimate=cost(23),
         name="mlp_half",
     )(order, c, ct, dy, b1, vec, *sums, *pieces)
@@ -1129,17 +1184,9 @@
     def _():
         bias_ref[...] = second_bias(counts_ref, slots)
 
-    kt = k_ref[...]
-    k = kt.T
-    v = v_ref[...].T
-    q = q_ref[...]
-    do = do_ref[...]
-    lse = lse_ref[0]
-    delta = jnp.sum(do.astype(F32) * o_ref[...].astype(F32), axis=0, keepdims=True)
     lane1 = lax.broadcasted_iota(jnp.int32, (1, WIDE), 1)
     lane2 = lax.broadcasted_iota(jnp.int32, (1, slots - CUT), 1)
-    lse1 = jnp.where(lane1 < FIRST, lse[:, :WIDE], -NEG)
-    lse2 = jnp.where(lane2 >= FIRST - CUT, lse[:, CUT:], -NEG)
+    scale = HEAD_DIM**-0.5
 
     def part(scores, grads, queries, outs, keys, delta_row, first):
         prob = jnp.exp(scores)
@@ -1150,52 +1197,61 @@
         ds = jnp.concatenate([ds, gap] if first else [gap, ds], axis=0)
         return nn(keys, ds), nt(queries, ds), nt(outs, pb)
 
-    grads1 = part(
-        nn(k[:FIRST], q[:, :WIDE]) - lse1, nn(v[:FIRST], do[:, :WIDE]),
-        q[:, :WIDE], do[:, :WIDE], kt[:, :WIDE], delta[:, :WIDE], True,
-    )
-    grads2 = part(
-        nn(k[FIRST:], q[:, CUT:]) + bias_ref[...] - lse2, nn(v[FIRST:], do[:, CUT:]),
-        q[:, CUT:], do[:, CUT:], kt[:, CUT:], delta[:, CUT:], False,
-    )
-    dq, dk, dv = (
-        jnp.concatenate([one[:, :CUT], one[:, CUT:] + two[:, : WIDE - CUT], two[:, WIDE - CUT :]], axis=1)
-        for one, two in zip(grads1, grads2)
-    )
-    scale = HEAD_DIM**-0.5
-    cos = cos_ref[...]
-    sin = sin_ref[...]
-    dangle = None
-    for r, rot, out in ((dq * scale, q.astype(F32) * (1.0 / scale), dq_ref), (dk, kt.astype(F32), dk_ref)):
-        r1, r2 = r[:HALF], r[HALF:]
-        term = r2 * rot[:HALF] - r1 * rot[HALF:]
-        dangle = term if dangle is None else dangle + term
-        g1 = (r1 * cos + r2 * sin).astype(BF)
-        g2 = (r2 * cos - r1 * sin).astype(BF)
-        out[:HALF, :] = g1
-        out[HALF:, :] = g2
-    dv_ref[...] = dv.astype(BF)
-    dangle_ref[...] = dangle.astype(BF)
+    for h in range(q_ref.shape[0] // HEAD_DIM):
+        top = h * HEAD_DIM
+        rows = slice(top, top + HEAD_DIM)
+        kt = k_ref[rows, :]
+        k = kt.T
+        v = v_ref[rows, :].T
+        q = q_ref[rows, :]
+        do = do_ref[rows, :]
+        lse = lse_ref[h]
+        delta = jnp.sum(do.astype(F32) * o_ref[rows, :].astype(F32), axis=0, keepdims=True)
+        lse1 = jnp.where(lane1 < FIRST, lse[:, :WIDE], -NEG)
+        lse2 = jnp.where(lane2 >= FIRST - CUT, lse[:, CUT:], -NEG)
+        grads1 = part(
+            nn(k[:FIRST], q[:, :WIDE]) - lse1, nn(v[:FIRST], do[:, :WIDE]),
+            q[:, :WIDE], do[:, :WIDE], kt[:, :WIDE], delta[:, :WIDE], True,
+        )
+        grads2 = part(
+            nn(k[FIRST:], q[:, CUT:]) + bias_ref[...] - lse2, nn(v[FIRST:], do[:, CUT:]),
+            q[:, CUT:], do[:, CUT:], kt[:, CUT:], delta[:, CUT:], False,
+        )
+        dq, dk, dv = (
+            jnp.concatenate([one[:, :CUT], one[:, CUT:] + two[:, : WIDE - CUT], two[:, WIDE - CUT :]], axis=1)
+            for one, two in zip(grads1, grads2)
+        )
+        cos = cos_ref[h * HALF : (h + 1) * HALF, :]
+        sin = sin_ref[h * HALF : (h + 1) * HALF, :]
+        dangle = None
+        for r, rot, out in ((dq * scale, q.astype(F32) * (1.0 / scale), dq_ref), (dk, kt.astype(F32), dk_ref)):
+            r1, r2 = r[:HALF], r[HALF:]
+            term = r2 * rot[:HALF] - r1 * rot[HALF:]
+            dangle = term if dangle is None else dangle + term
+            out[top : top + HALF, :] = (r1 * cos + r2 * sin).astype(BF)
+            out[top + HALF : top + HEAD_DIM, :] = (r2 * cos - r1 * sin).astype(BF)
+        dv_ref[rows, :] = dv.astype(BF)
+        dangle_ref[h * HALF : (h + 1) * HALF, :] = dangle.astype(BF)
 
 
 def heads_back(group, counts, q, k, v, o, do, lse, cos, sin):
     width, slots = q.shape
     heads = width // HEAD_DIM
-    head = pl.BlockSpec((HEAD_DIM, slots), lambda h: (h, 0))
-    half = pl.BlockSpec((HALF, slots), lambda h: (h, 0))
-    turn = pl.BlockSpec((HALF, slots), lambda h: (group * heads + h, 0))
-    late = pl.BlockSpec((HEAD_DIM, slots), lambda h: (group * heads + h, 0))
+    each = 2
+    steps = heads // each
+    head = pl.BlockSpec((each * HEAD_DIM, slots), lambda h: (h, 0))
+    half = pl.BlockSpec((each * HALF, slots), lambda h: (h, 0))
+    turn = pl.BlockSpec((each * HALF, slots), lambda h: (group * steps + h, 0))
+    late = pl.BlockSpec((each * HEAD_DIM, slots), lambda h: (group * steps + h, 0))
     return pl.pallas_call(
         heads_back_kernel,
-        grid=(heads,),
-        in_specs=[pl.BlockSpec(memory_space=pltpu.SMEM)]
-        + [head] * 4
-        + [late, pl.BlockSpec((1, 1, slots), lambda h: (h, 0, 0)), turn, turn],
+        grid=(steps,),
+        in_specs=[SMEM] + [head] * 4 + [late, pl.BlockSpec((each, 1, slots), lambda h: (h, 0, 0)), turn, turn],
         out_specs=[head] * 3 + [half],
         out_shape=[jax.ShapeDtypeStruct((width, slots), BF)] * 3 + [jax.ShapeDtypeStruct((width // 2, slots), BF)],
         scratch_shapes=[pltpu.VMEM((slots - FIRST, slots - CUT), F32)],
         compiler_params=params(),
-        cost_estimate=cost(14),
+        cost_estimate=cost(13),
         name="heads_back",
     )(counts, q, k, v, o, do, lse, cos, sin)
 
@@ -1247,56 +1303,85 @@
     )(order, at, sel, dangle, dq, dk, dv, *more)
 
 
-def input_kernel(order_ref, x_ref, dh_ref, vec_ref, *rest):
-    grads = rest[: 3 * GROUPS]
-    pieces = [rest[3 * GROUPS + g * SHARDS : 3 * GROUPS + (g + 1) * SHARDS] for g in range(GROUPS)]
-    dx_ref, sums_ref, w_scr, sem = rest[3 * GROUPS + GROUPS * SHARDS :]
-    width, blk = x_ref.shape[1], x_ref.shape[0]
-    i = pl.program_id(0)
-    part = width // SHARDS
-
-    @pl.when(i == 0)
+def part_kernel(order_ref, *rest):
+    grads, pieces, (da_ref, w_scr, sem) = rest[:3], rest[3 : 3 + SHARDS], rest[3 + SHARDS :]
+    add_group(order_ref, grads, pieces, da_ref, w_scr, sem)
+
+
+def group_weights(order_ref, pieces, w_scr, sem):
+    rows = w_scr.shape[1]
+    copies = fetch(pieces, order_ref, [(slice(0, rows), lambda d: w_scr.at[d])], sem)
+    start_all(copies)
+    wait_all(copies)
+
+
+def group_product(grads, w_scr):
+    rows = w_scr.shape[1] // 3
+    total = None
+    for n in range(3):
+        w = w_scr[:, n * rows : (n + 1) * rows, :].reshape(SHARDS * rows, w_scr.shape[2])
+        term = nn(w, grads[n][...])
+        total = term if total is None else total + term
+    return total
+
+
+def add_group(order_ref, grads, pieces, da_ref, w_scr, sem):
+    @pl.when(pl.program_id(0) == 0)
     def _():
-        copies = []
-        for g in range(GROUPS):
-            copies += fetch(pieces[g], order_ref, [(slice(0, 3 * part), lambda d: w_scr.at[g, d])], sem.at[g])
-        start_all(copies)
+        group_weights(order_ref, pieces, w_scr, sem)
+
+    da_ref[...] = group_product(grads, w_scr)
+
+
+def input_part(order, grads, pieces, width):
+    cols, slots = grads[0].shape
+    blk = 512
+    return pl.pallas_call(
+        part_kernel,
+        grid=(slots // blk,),
+        in_specs=[SMEM] + [pl.BlockSpec((cols, blk), lambda i: (0, i))] * 3 + [ANY] * SHARDS,
+        out_specs=pl.BlockSpec((width, blk), lambda i: (0, i)),
+        out_shape=jax.ShapeDtypeStruct((width, slots), F32),
+        scratch_shapes=[pltpu.VMEM((SHARDS, 3 * width // SHARDS, cols), BF), pltpu.SemaphoreType.DMA((SHARDS,))],
+        compiler_params=params(),
+        cost_estimate=cost(6),
+        name="input_part",
+    )(order, *grads, *pieces)
+
+
+def input_kernel(order_ref, x_ref, dh_ref, vec_ref, da_ref, *rest):
+    grads, pieces, (dx_ref, sums_ref, w_scr, sem) = rest[:3], rest[3 : 3 + SHARDS], rest[3 + SHARDS :]
+
+    @pl.when(pl.program_id(0) == 0)
+    def _():
+        group_weights(order_ref, pieces, w_scr, sem)
         sums_ref[...] = jnp.zeros_like(sums_ref)
-        wait_all(copies)
-
-    da = None
-    for g in range(GROUPS):
-        for n in range(3):
-            w = w_scr[g, :, n * part : (n + 1) * part, :].reshape(width, width // GROUPS)
-            term = nn(w, grads[3 * g + n][...])
-            da = term if da is None else da + term
+
+    da = da_ref[...] + group_product(grads, w_scr)
     out, dgain, dshift = norm_back(da.T, x_ref[...].astype(F32), vec_ref[1:2, :])
     dx_ref[...] = (dh_ref[...] + out).astype(BF)
     sums_ref[0:1, :] += dgain
     sums_ref[1:2, :] += dshift
 
 
-def input_back(order, x, dh, vec, grads, pieces):
+def input_back(order, x, dh, vec, da, grads, pieces):
     slots, width = x.shape
-    blk = 256
+    cols = grads[0].shape[0]
+    blk = 512
     rows = pl.BlockSpec((blk, width), lambda i: (i, 0))
-    whole = lambda r, k: pl.BlockSpec((r, k), lambda i: (0, 0))
     return pl.pallas_call(
         input_kernel,
         grid=(slots // blk,),
-        in_specs=[SMEM, rows, rows, VMEM]
-        + [pl.BlockSpec((width // GROUPS, blk), lambda i: (0, i))] * (3 * GROUPS)
-        + [ANY] * (GROUPS * SHARDS),
-        out_specs=[rows, whole(8, width)],
+        in_specs=[SMEM, rows, rows, VMEM, pl.BlockSpec((width, blk), lambda i: (0, i))]
+        + [pl.BlockSpec((cols, blk), lambda i: (0, i))] * 3
+        + [ANY] * SHARDS,
+        out_specs=[rows, pl.BlockSpec((8, width), lambda i: (0, 0))],
         out_shape=[jax.ShapeDtypeStruct((slots, width), BF), jax.ShapeDtypeStruct((8, width), F32)],
-        scratch_shapes=[
-            pltpu.VMEM((GROUPS, SHARDS, 3 * width // SHARDS, width // GROUPS), BF),
-            pltpu.SemaphoreType.DMA((GROUPS, SHARDS)),
-        ],
-        compiler_params=params(),
-        cost_estimate=cost(12),
+        scratch_shapes=[pltpu.VMEM((SHARDS, 3 * width // SHARDS, cols), BF), pltpu.SemaphoreType.DMA((SHARDS,))],
+        compiler_params=params(),
+        cost_estimate=cost(10),
         name="input_back",
-    )(order, x, dh, vec, *grads, *[p for group in pieces for p in group])
+    )(order, x, dh, vec, da, *grads, *pieces)
 
 
 def body_fast(
@@ -1310,44 +1395,42 @@
     cols = width // GROUPS
     half = width // 2
     order = lax.axis_index("fsdp") ^ jnp.arange(SHARDS, dtype=jnp.int32)
+    order = jnp.concatenate([order, lax.axis_index("rep")[None].astype(jnp.int32)])
 
     own = fc2_weight.shape[0] // 2
-    piece_a, piece_b = group_pieces(qkv_weight, out_weight)
+    small = (ln1_gain, ln1_bias, qkv_bias, rope_freqs, out_bias, ln2_gain, ln2_bias, fc1_bias, fc2_bias)
+    sizes = [s.shape[0] for s in small]
+    vectors = jnp.concatenate(small + (jnp.zeros((2 * cols - sum(sizes),), BF),)).reshape(2, cols)
+    piece_c, piece_d = mlp_pieces(fc1_weight, fc2_weight)
+    piece_a, piece_b = group_pieces(qkv_weight, out_weight, vectors)
+    pieces_c = [lax.all_gather(piece_c, "fsdp", axis=0)]
+    pieces_d = [lax.all_gather(piece_d, "fsdp", axis=0)]
+    first = lambda g: (g.piece[8], g.piece[4], g.piece[2])
+    second = lambda g: (g.piece[12], g.piece[6], g.piece[10])
     gather_a = Gather(piece_a)
     gather_a.stage1()
-    piece_c, piece_d = mlp_pieces(tie(fc1_weight, piece_a), fc2_weight)
-
-    small = (ln1_gain, ln1_bias, qkv_bias, rope_freqs, out_bias, ln2_gain, ln2_bias, fc1_bias, fc2_bias)
-    sizes = [s.shape[0] for s in small]
-    mine = jnp.concatenate(small)
-    packed = lax.all_to_all(jnp.broadcast_to(mine[None], (SHARDS, mine.shape[0])), "fsdp", 0, 0, tiled=True)
-    gather_a.stage2(packed)
-    a, a_t, cos, sin, vec, b1, bias, sel = prepare(sizes, packed, tie(x, gather_a.piece[12]), patch_cols, patch_rows)
+    gather_a.stage2(*first(gather_a))
     gather_a.stage3()
+    pieces_a = gather_a.cores()
     gather_b = Gather(piece_b)
     gather_b.stage1(gather_a.piece[12])
-    gather_b.stage2(a)
+    a_t, cos, sin, vec, b1, bias, sel = prepare(sizes, order, x, patch_cols, patch_rows, pieces_a)
+    gather_b.stage2(sel)
+    q, k, v = project_group(0, order, a_t, bias, cos, sin, pieces_a)
+    gather_b.hold((12, 6, 10), q)
     gather_b.stage3()
-    gather_c = Gather(piece_c)
-    gather_c.stage1(a)
-    pieces_a = gather_a.cores()
-    q, k, v = project_group(0, order, a, bias, cos, sin, pieces_a)
-    pieces_d = [lax.all_gather(tie(piece_d, gather_b.piece[12]), "fsdp", axis=0)]
     heads = [(q, k, v) + tuple(attend(counts, q, k, v))]
-    gather_c.stage2(q)
+    gather_b.hold((14,), heads[0][3])
     pieces_b = gather_b.cores()
-    q, k, v = project_group(1, order, a, bias, cos, sin, pieces_b)
-    gather_c.stage3(q)
+    q, k, v = project_group(1, order, a_t, bias, cos, sin, pieces_b)
     heads.append((q, k, v) + tuple(attend(counts, q, k, v)))
-    pieces_c = gather_c.cores()
-    pieces_all = (pieces_a, pieces_b)
     o = [t[3] for t in heads]
-    at_out = piece_a.shape[0]
+    at_out = piece_b.shape[0] - 2 * out_weight.shape[0]
     h, c, c_t = out_project_fast(order, o, x, vec, pieces_b, at_out)
     y, dc, g_c, g_b1a = mlp_half(0, order, c, c_t, dy, b1, vec, (h,), pieces_c, False)
-    mlp_c = lax.psum_scatter(tie(g_c, *pieces_d), "fsdp", scatter_dimension=0, tiled=True)[0]
+    mlp_c = lax.psum_scatter(tie(g_c, pieces_d[0]), "fsdp", scatter_dimension=0, tiled=True)[0]
     y, dc, near_d, far_d, g_b1b = mlp_half(1, order, c, c_t, dy, b1, vec, (y, dc), pieces_d, True)
-    scatter_d = Scatter(near_d, far_d)
+    scatter_d = SplitScatter(near_d, far_d)
     dh, do, near_o, far_o, sums2 = out_back_fast(order, dc, h, dy, vec, o, pieces_b, at_out)
 
     def back(g, do):
@@ -1355,31 +1438,42 @@
         *three, dangle = heads_back(g, counts, q, k, v, og, do, lse, cos, sin)
         return three, dangle
 
-    sent = scatter_d.step()
+    sent = scatter_d.split()
     grads_b, dangle_b = back(1, tie(do, sent))
     near_b, far_b, bias_b, freq_b = qkv_grad(order, a_t, sel, dangle_b, *grads_b, near_o, far_o)
     scatter_b = Scatter(near_b, far_b)
-    grads_a, dangle_a = back(0, tie(do, near_b))
-    sent = (scatter_b.step(), scatter_d.step())
+    scatter_d.hold(near_b)
+    sent = scatter_d.step()
+    grads_a, dangle_a = back(0, tie(do, sent, near_b))
+    scatter_d.hold(dangle_a)
+    scatter_b.hold(dangle_a)
+    sent = (scatter_d.step(), scatter_b.step())
     near_a, far_a, bias_a, freq_a = qkv_grad(order, a_t, sel, tie(dangle_a, *sent), *grads_a)
     scatter_a = Scatter(near_a, far_a)
-    sent = (scatter_a.step(), scatter_d.step(), scatter_b.step())
-    dx, sums1 = input_back(order, x, tie(dh, *sent), vec, grads_a + grads_b, pieces_all)
-    for _ in range(2):
-        scatter_a.step()
-    scatter_b.step()
+    scatter_d.hold(near_a)
+    sent = scatter_d.step()
+    da = input_part(order, lax.optimization_barrier((grads_b, near_a, sent))[0], pieces_b, width)
+    scatter_a.hold(da)
+    scatter_b.hold(da)
+    scatter_d.hold(da)
+    sent = (scatter_a.step(), scatter_b.step())
     mlp_d = scatter_d.finish()
+    dx, sums1 = input_back(order, x, dh, vec, tie(da, mlp_d[0], *sent), grads_a, pieces_a)
+    scatter_a.hold(sums1)
+    scatter_b.hold(sums1)
+    sent = (scatter_a.step(), scatter_b.step(), across(mlp_c))
+    other_c = sent[2]
+    block = pack(sum(sizes), tie(sums1, *sent), sums2, g_b1a, g_b1b, bias_a, bias_b, freq_a, freq_b)
+    scatter_a.step()
     mine_b = scatter_b.finish()
     mine_a = scatter_a.finish()
-    other_c = lax.ppermute(mlp_c, "rep", [(0, 1), (1, 0)])
     s_a = mine_a[0].astype(F32) + mine_a[1].astype(F32)
     s_b = mine_b[0].astype(F32) + mine_b[1].astype(F32)
     rows1 = width // SHARDS
-    s_w1, s_w2 = mlp_join(rows1, (mlp_c, other_c) + mlp_d)
+    s_w1, s_w2 = mlp_join(rows1, order, (mlp_c, other_c) + mlp_d)
     s_wqkv = jnp.concatenate([s[i * rows1 : (i + 1) * rows1] for i in range(3) for s in (s_a, s_b)], axis=1)
     s_wout = jnp.concatenate([s_b[3 * rows1 : 4 * rows1], s_b[4 * rows1 :]], axis=1)
 
-    block = pack(sum(sizes), sums1, sums2, g_b1a, g_b1b, bias_a, bias_b, freq_a, freq_b)
     mine = jnp.sum(lax.all_to_all(block, "fsdp", 0, 0, tiled=True), axis=0)
     mine = mine + lax.ppermute(mine, "rep", [(0, 1), (1, 0)])
     outs = []

time: 374 us -> 330 us (0.88)
  waiting for transfers between devices: 92.8 us -> 61.5 us
  blocking collectives: 10.3 us -> 0 us
  Pallas kernels: 172 us -> 181 us
  local copies, waits for them, and re-layouts: 13.8 us -> 6.46 us
  other arithmetic: 20.1 us -> 15.9 us
    ppermute x57 -> x42, waiting for transfers between devices: 77.1 us -> 39.3 us  [swap(): return lax.ppermute(v, 'fsdp', [(i, i ^ mask) for i in range(SHARDS)])]
    all_to_all x1 -> x0, blocking collectives: 10.3 us -> none  [body_fast(): lax.all_to_all(jnp.broadcast_to(mine[None], (SHARDS, mine.shape[0])), 'fs...]
    pallas_call x9 -> x10, Pallas kernels: 70.3 us -> 79.5 us  [the longest x2 27.3 us: heads_back(): pl.pallas_call(heads_back_kernel, grid=(steps,), in_specs=[SMEM] + [head]...]
    unnamed x180 -> x99, local copies, waits for them, and re-layouts: 10.6 us -> 2.43 us
    ppermute x4 -> x5, waiting for transfers between devices: 10.6 us -> 15.3 us  [across(): return lax.ppermute(v, 'rep', [(0, 1), (1, 0)])]
    ppermute x57 -> x42, starting transfers between devices: 34.4 us -> 34.5 us  [swap(): return lax.ppermute(v, 'fsdp', [(i, i ^ mask) for i in range(SHARDS)])]
  transfers between devices with their start and end apart: 65 -> 52, of which waited for: 21 -> 22; matrix products, arithmetic and copies ran while one was open for 6% -> 6% of each run, Pallas kernels for 38% -> 47%
where the time goes in v3:
time: 330 us; the launch traced here: 326 us
  Pallas kernels  181 us (55%)
  waiting for transfers between devices  61.5 us (19%)
  starting transfers between devices  46 us (14%)
  other arithmetic  15.9 us (5%)
  between operations  14.7 us (4%)
  local copies, waits for them, and re-layouts  6.46 us (2%)
    pallas_call x2, Pallas kernels, mlp_half(): pl.pallas_call(partial(mlp_half_kernel, part, first, split, len(pieces)),...  51 us
    ppermute x42, waiting for transfers between devices, swap(): return lax.ppermute(v, 'fsdp', [(i, i ^ mask) for i in range(SHARDS)])  39.3 us
    ppermute x42, starting transfers between devices, swap(): return lax.ppermute(v, 'fsdp', [(i, i ^ mask) for i in range(SHARDS)])  34.5 us
    pallas_call x2, Pallas kernels, heads_back(): pl.pallas_call(heads_back_kernel, grid=(steps,), in_specs=[SMEM] + [head]...  27.3 us
    pallas_call x2, Pallas kernels, attend(): pl.pallas_call(attend_kernel, grid=(heads // each,), in_specs=[pl.BlockSp...  17.6 us
    pallas_call x2, Pallas kernels, qkv_grad(): pl.pallas_call(qkv_grad_kernel, in_specs=[SMEM] + [VMEM] * (6 + len(more)...  15.3 us
    ppermute x5, waiting for transfers between devices, across(): return lax.ppermute(v, 'rep', [(0, 1), (1, 0)])  15.3 us
    pallas_call x2, Pallas kernels, project_group(): pl.pallas_call(group_kernel, grid=(slots // blk,), in_specs=[SMEM, tall(w...  13.8 us
  transfers between devices with their start and end apart: 52, of which 22 were waited for; matrix products, arithmetic and copies ran while one was open for 6% of the time, Pallas kernels for 47%

profile of v3, /device:TPU:0, one launch (start us, length us, event | category | flops | bytes accessed | tf_op | source)
XLA Modules:
  0.0 326.0 jit_solution(2561191768268599203)
XLA Ops:
  12.6 4.0 %collective-permute-start.5 = (bf16[160,384]{1,0:T(8,128)(2,1)}, bf16[160,384]{1,0:T(8,128)(2,1)S(1)}, u32[]{:S(2)}, u32[]{:S(2)}) collective-permute-start(bf16[160,384]{1,0:T(8,128)(2,1)} %get-tuple-element.100.rest_0_.rest_3_), channel_id=1, source_target_pairs={{0,8},{1,9},{2,10},{3,11},{4,12},{5,13},{6,14},{7,15},{8,0},{9,1},... | collective-permute-start | bytes 368648 | tf_op jit(solution)/shard_map/ppermute | solution.py:564
  27.2 5.2 %collective-permute-done.11.rest_12_.rest_15_ = bf16[160,384]{1,0:T(8,128)(2,1)S(1)} collective-permute-done((bf16[160,384]{1,0:T(8,128)(2,1)S(1)}, bf16[160,384]{1,0:T(8,128)(2,1)S(1)}, u32[]{:S(2)}, u32[]{:S(2)}) %collective-permute-start.11) | collective-permute-done | bytes 122912 | tf_op jit(solution)/shard_map/ppermute | solution.py:564
  44.8 9.8 %prepare.1 = (bf16[768,1024]{1,0:T(8,128)(2,1)}, f32[384,1024]{1,0:T(8,128)}, f32[384,1024]{1,0:T(8,128)}, f32[8,768]{1,0:T(8,128)}, f32[2,1536]{1,0:T(2,128)}, ...) custom-call(s32[17]{0:T(128)} %pad_add_fusion.order_ref, bf16[1024,768]{1,0:T(8,128)(2,1)} %bitcast.54, s32[1,1024]{1,0:T(1,128)} %cols_ref.1, ...), custom_call_target="tpu_custom_call" | custom-call | flops 8800000000 | bytes 65536 | tf_op jit(solution)/shard_map/prepare/pallas_call | solution.py:811
  58.9 6.9 %qkv_group.2 = (bf16[384,1024]{1,0:T(8,128)(2,1)}, bf16[384,1024]{1,0:T(8,128)(2,1)}, bf16[384,1024]{1,0:T(8,128)(2,1)}) custom-call(s32[17]{0:T(128)} %pad_add_fusion.order_ref, bf16[768,1024]{1,0:T(8,128)(2,1)} %get-tuple-element.104.at_ref, f32[2304,1]{1,0:T(8,128)} %get-tuple-element.105.bq_ref.bk_ref.bv_ref, ...), custom_call_target="tpu_custom_call" | custom-call | flops 7699999744 | bytes 65536 | tf_op jit(solution)/shard_map/qkv_group/pallas_call | solution.py:905
  65.9 5.9 %collective-permute-done.26.rest_12_.rest_15_.rest_14_ = bf16[240,384]{1,0:T(8,128)(2,1)S(1)} collective-permute-done((bf16[240,384]{1,0:T(8,128)(2,1)S(1)}, bf16[240,384]{1,0:T(8,128)(2,1)S(1)}, u32[]{:S(2)}, u32[]{:S(2)}) %collective-permute-start.26) | collective-permute-done | bytes 184352 | tf_op jit(solution)/shard_map/ppermute | solution.py:564
  73.9 8.8 %attend.2 = (bf16[384,1024]{1,0:T(8,128)(2,1)}, f32[6,1,1024]{2,1,0:T(1,128)}) custom-call(s32[3]{0:T(128)} %bitcast.59, bf16[384,1024]{1,0:T(8,128)(2,1)} %get-tuple-element.108.q_ref, bf16[384,1024]{1,0:T(8,128)(2,1)} %get-tuple-element.109.k_ref, bf16[384,1024]{1,0:T(8,128)(2,1)} %get-tuple-element.110.v_ref), custom_call_target="tpu_custom_call" | custom-call | flops 8800000000 | bytes 65536 | tf_op jit(solution)/shard_map/attend/pallas_call | solution.py:180
  86.4 6.9 %qkv_group.3 = (bf16[384,1024]{1,0:T(8,128)(2,1)}, bf16[384,1024]{1,0:T(8,128)(2,1)}, bf16[384,1024]{1,0:T(8,128)(2,1)}) custom-call(s32[17]{0:T(128)} %pad_add_fusion.order_ref, bf16[768,1024]{1,0:T(8,128)(2,1)} %get-tuple-element.104.at_ref, f32[2304,1]{1,0:T(8,128)} %get-tuple-element.105.bq_ref.bk_ref.bv_ref, ...), custom_call_target="tpu_custom_call" | custom-call | flops 7699999744 | bytes 65536 | tf_op jit(solution)/shard_map/qkv_group/pallas_call | solution.py:905
  93.3 8.8 %attend.3 = (bf16[384,1024]{1,0:T(8,128)(2,1)}, f32[6,1,1024]{2,1,0:T(1,128)}) custom-call(s32[3]{0:T(128)} %bitcast.60, bf16[384,1024]{1,0:T(8,128)(2,1)} %get-tuple-element.121.q_ref, bf16[384,1024]{1,0:T(8,128)(2,1)} %get-tuple-element.122.k_ref, bf16[384,1024]{1,0:T(8,128)(2,1)} %get-tuple-element.123.v_ref), custom_call_target="tpu_custom_call" | custom-call | flops 8800000000 | bytes 65536 | tf_op jit(solution)/shard_map/attend/pallas_call | solution.py:180
  102.2 8.6 %out_project.1 = (f32[1024,768]{1,0:T(8,128)}, bf16[1024,768]{1,0:T(8,128)(2,1)}, bf16[768,1024]{1,0:T(8,128)(2,1)}) custom-call(s32[17]{0:T(128)} %pad_add_fusion.order_ref, f32[8,768]{1,0:T(8,128)} %get-tuple-element.103.vec_ref, bf16[384,1024]{1,0:T(8,128)(2,1)} %get-tuple-element.111.rest_0_.o_ref, bf16[384,1024]{1,0:T(8,128)(2,1)} %get-tuple-element.124.rest_1_.o_ref, ...), custom_call_target="tpu_custom_call" | custom-call | flops 8800000000 | bytes 65536 | tf_op jit(solution)/shard_map/out_project/pallas_call | solution.py:959
  110.8 25.2 %mlp_half.2 = (f32[1024,768]{1,0:T(8,128)}, f32[1024,768]{1,0:T(8,128)}, bf16[16,192,768]{2,1,0:T(8,128)(2,1)}, f32[1,1536]{1,0:T(1,128)}) custom-call(s32[17]{0:T(128)} %pad_add_fusion.order_ref, bf16[1024,768]{1,0:T(8,128)(2,1)} %get-tuple-element.125.c_ref, bf16[768,1024]{1,0:T(8,128)(2,1)} %get-tuple-element.126.ct_ref, bf16[1024,768]{1,0:T(8,128)(2,1)} %bitcast.51, ...), custom_call_target="tpu_custom_call" | custom-call | flops 25300000768 | bytes 65536 | tf_op jit(solution)/shard_map/mlp_half/pallas_call | solution.py:1074
  136.0 25.8 %mlp_half.3 = (bf16[1024,768]{1,0:T(8,128)(2,1)}, f32[1024,768]{1,0:T(8,128)}, bf16[2,8,96,768]{3,2,1,0:T(8,128)(2,1)}, bf16[2,8,96,768]{3,2,1,0:T(8,128)(2,1)}, f32[1,1536]{1,0:T(1,128)}) custom-call(s32[17]{0:T(128)} %pad_add_fusion.order_ref, bf16[1024,768]{1,0:T(8,128)(2,1)} %get-tuple-element.125.c_ref, bf16[768,1024]{1,0:T(8,128)(2,1)} %get-tuple-element.126.ct_ref, ...), custom_call_target="tpu_custom_call" | custom-call | flops 25300000768 | bytes 65536 | tf_op jit(solution)/shard_map/mlp_half/pallas_call | solution.py:1074
  162.2 12.2 %out_back.1 = (f32[1024,768]{1,0:T(8,128)}, bf16[768,1024]{1,0:T(8,128)(2,1)}, bf16[8,96,384]{2,1,0:T(8,128)(2,1)}, bf16[8,96,384]{2,1,0:T(8,128)(2,1)}, f32[8,768]{1,0:T(8,128)}) custom-call(s32[17]{0:T(128)} %pad_add_fusion.order_ref, f32[1024,768]{1,0:T(8,128)} %get-tuple-element.134.dc_ref, f32[1024,768]{1,0:T(8,128)} %get-tuple-element.128.rest_0_.h_ref, ...), custom_call_target="tpu_custom_call" | custom-call | flops 13200000000 | bytes 65536 | tf_op jit(solution)/shard_map/out_back/pallas_call | solution.py:1151
  176.4 13.9 %heads_back.2 = (bf16[384,1024]{1,0:T(8,128)(2,1)}, bf16[384,1024]{1,0:T(8,128)(2,1)}, bf16[384,1024]{1,0:T(8,128)(2,1)}, bf16[192,1024]{1,0:T(8,128)(2,1)}) custom-call(s32[3]{0:T(128)} %bitcast.61, bf16[384,1024]{1,0:T(8,128)(2,1)} %get-tuple-element.121.q_ref, bf16[384,1024]{1,0:T(8,128)(2,1)} %get-tuple-element.122.k_ref, ...), custom_call_target="tpu_custom_call" | custom-call | flops 14300000256 | bytes 65536 | tf_op jit(solution)/shard_map/heads_back/pallas_call | solution.py:1246
  190.3 7.9 %qkv_grad.2 = (bf16[8,240,384]{2,1,0:T(8,128)(2,1)}, bf16[8,240,384]{2,1,0:T(8,128)(2,1)}, f32[16,1152]{1,0:T(8,128)}, f32[16,192]{1,0:T(8,128)}) custom-call(s32[17]{0:T(128)} %pad_add_fusion.order_ref, bf16[768,1024]{1,0:T(8,128)(2,1)} %get-tuple-element.104.at_ref, bf16[16,1024]{1,0:T(8,128)(2,1)} %get-tuple-element.114.sel_ref, ...), custom_call_target="tpu_custom_call" | custom-call | flops 6600000000 | bytes 65536 | tf_op jit(solution)/shard_map/qkv_grad/pallas_call | solution.py:1289
  198.2 4.6 %collective-permute-done.31 = bf16[8,96,768]{2,1,0:T(8,128)(2,1)S(1)} collective-permute-done((bf16[8,96,768]{2,1,0:T(8,128)(2,1)S(1)}, bf16[8,96,768]{2,1,0:T(8,128)(2,1)S(1)}, u32[]{:S(2)}, u32[]{:S(2)}) %collective-permute-start.31) | collective-permute-done | bytes 1179680 | tf_op jit(solution)/shard_map/ppermute | solution.py:640
  205.6 13.5 %heads_back.3 = (bf16[384,1024]{1,0:T(8,128)(2,1)}, bf16[384,1024]{1,0:T(8,128)(2,1)}, bf16[384,1024]{1,0:T(8,128)(2,1)}, bf16[192,1024]{1,0:T(8,128)(2,1)}) custom-call(s32[3]{0:T(128)} %bitcast.62, bf16[384,1024]{1,0:T(8,128)(2,1)} %get-tuple-element.108.q_ref, bf16[384,1024]{1,0:T(8,128)(2,1)} %get-tuple-element.109.k_ref, ...), custom_call_target="tpu_custom_call" | custom-call | flops 14300000256 | bytes 65536 | tf_op jit(solution)/shard_map/heads_back/pallas_call | solution.py:1246
  222.6 7.4 %qkv_grad.3 = (bf16[8,144,384]{2,1,0:T(8,128)(2,1)}, bf16[8,144,384]{2,1,0:T(8,128)(2,1)}, f32[16,1152]{1,0:T(8,128)}, f32[16,192]{1,0:T(8,128)}) custom-call(s32[17]{0:T(128)} %pad_add_fusion.order_ref, bf16[768,1024]{1,0:T(8,128)(2,1)} %get-tuple-element.104.at_ref, bf16[16,1024]{1,0:T(8,128)(2,1)} %get-tuple-element.114.sel_ref, ...), custom_call_target="tpu_custom_call" | custom-call | flops 6600000000 | bytes 65536 | tf_op jit(solution)/shard_map/qkv_grad/pallas_call | solution.py:1289
  230.1 4.3 %collective-permute-done.34 = bf16[2,96,768]{2,1,0:T(8,128)(2,1)S(1)} collective-permute-done((bf16[2,96,768]{2,1,0:T(8,128)(2,1)}, bf16[2,96,768]{2,1,0:T(8,128)(2,1)S(1)}, u32[]{:S(2)}, u32[]{:S(2)}) %collective-permute-start.34) | collective-permute-done | bytes 294944 | tf_op jit(solution)/shard_map/ppermute | solution.py:564
  237.4 6.9 %input_part.1.da_ref = f32[768,1024]{1,0:T(8,128)} custom-call(s32[17]{0:T(128)} %pad_add_fusion.order_ref, bf16[384,1024]{1,0:T(8,128)(2,1)} %get-tuple-element.161.dq_ref.rest_0_, bf16[384,1024]{1,0:T(8,128)(2,1)} %get-tuple-element.162.dk_ref.rest_1_, bf16[384,1024]{1,0:T(8,128)(2,1)} %get-tuple-element.163.dv_ref.rest_2_, ...), custom_call_target="tpu_custom_call" | custom-call | flops 6600000000 | bytes 65536 | tf_op jit(solution)/shard_map/input_part/pallas_call | solution.py:1339
  256.1 10.8 %input_back.1 = (bf16[1024,768]{1,0:T(8,128)(2,1)}, f32[8,768]{1,0:T(8,128)}) custom-call(s32[17]{0:T(128)} %pad_add_fusion.order_ref, bf16[1024,768]{1,0:T(8,128)(2,1)} %bitcast.56, f32[1024,768]{1,0:T(8,128)} %get-tuple-element.135.dh_ref, f32[8,768]{1,0:T(8,128)} %get-tuple-element.103.vec_ref, f32[768,1024]{1,0:T(8,128)} %input_part.1.da_ref, ...), custom_call_target="tpu_custom_call" | custom-call | flops 11000000512 | bytes 65536 | tf_op jit(solution)/shard_map/input_back/pallas_call | solution.py:1372
  270.5 6.0 %collective-permute-done.42 = bf16[2,144,384]{2,1,0:T(8,128)(2,1)S(1)} collective-permute-done((bf16[2,144,384]{2,1,0:T(8,128)(2,1)S(1)}, bf16[2,144,384]{2,1,0:T(8,128)(2,1)S(1)}, u32[]{:S(2)}, u32[]{:S(2)}) %collective-permute-start.42) | collective-permute-done | bytes 221216 | tf_op jit(solution)/shard_map/ppermute | solution.py:564
  292.0 6.1 %collective-permute-done.40.c_other_ref = bf16[192,768]{1,0:T(8,128)(2,1)S(1)} collective-permute-done((bf16[192,768]{1,0:T(8,128)(2,1)}, bf16[192,768]{1,0:T(8,128)(2,1)S(1)}, u32[]{:S(2)}, u32[]{:S(2)}) %collective-permute-start.40) | collective-permute-done | bytes 294944 | tf_op jit(solution)/shard_map/ppermute | solution.py:640
  301.6 5.3 %all-to-all-start = ((f32[16,1,672]{2,1,0:T(1,128)}), f32[16,1,672]{2,1,0:T(1,128)S(1)}, u32[]{:S(2)}, u32[]{:S(2)}) async-start(f32[16,1,672]{2,1,0:T(1,128)} %copy.33), calls=%async_computation.1 | async-start | bytes 98304 | tf_op jit(solution)/shard_map/all_to_all | solution.py:1477
  307.6 6.1 %all-to-all-done = f32[16,1,672]{2,1,0:T(1,128)S(1)} async-done(((f32[16,1,672]{2,1,0:T(1,128)}), f32[16,1,672]{2,1,0:T(1,128)S(1)}, u32[]{:S(2)}, u32[]{:S(2)}) %all-to-all-start) | async-done | bytes 43040 | tf_op jit(solution)/shard_map/all_to_all | solution.py:1477
  (229 shorter events, 90.4 us)
Async XLA Ops:
  7.3 103.5 %all-gather.5.cloned.1.call-start = ((), (), s32[]{:S(2)}) async-start(), calls=%async_computation.3 | async-start | bytes 5013504 | tf_op jit(solution)/shard_map/all_gather | solution.py:1406
  9.3 126.6 %all-gather.7.cloned.1.call-start = ((), (), s32[]{:S(2)}) async-start(), calls=%async_computation.4 | async-start | bytes 5013504 | tf_op jit(solution)/shard_map/all_gather | solution.py:1407
  10.1 281.0 %reduce-scatter.2.cloned.1.call-start = ((), (), s32[]{:S(2)}) async-start(), calls=%async_computation.2 | async-start | bytes 5013504 | tf_op jit(solution)/shard_map/reduce_scatter | solution.py:1431
  37.9 45.4 %collective-permute-start.15 = (bf16[240,384]{1,0:T(8,128)(2,1)}, bf16[240,384]{1,0:T(8,128)(2,1)S(1)}, u32[]{:S(2)}, u32[]{:S(2)}) collective-permute-start(bf16[240,384]{1,0:T(8,128)(2,1)} %get-tuple-element.113.rest_0_.rest_3_.rest_2_), channel_id=1, source_target_pairs={{0,1},{1,0},{2,3},{3,2},{4,5},{5,4},{6,7},{7,6},{8,9},{9,8},{10,11... | collective-permute-start | bytes 552968 | tf_op jit(solution)/shard_map/ppermute | solution.py:564
  38.4 18.7 %collective-permute-start.22 = (bf16[240,384]{1,0:T(8,128)(2,1)}, bf16[240,384]{1,0:T(8,128)(2,1)S(1)}, u32[]{:S(2)}, u32[]{:S(2)}) collective-permute-start(bf16[240,384]{1,0:T(8,128)(2,1)} %get-tuple-element.113.rest_0_.rest_3_.rest_2_), channel_id=1, source_target_pairs={{0,8},{1,9},{2,10},{3,11},{4,12},{5,13},{6,14},{7,15},{8,0},{9,1},... | collective-permute-start | bytes 552968 | tf_op jit(solution)/shard_map/ppermute | solution.py:564
  39.8 26.0 %collective-permute-start.18 = (bf16[240,384]{1,0:T(8,128)(2,1)}, bf16[240,384]{1,0:T(8,128)(2,1)S(1)}, u32[]{:S(2)}, u32[]{:S(2)}) collective-permute-start(bf16[240,384]{1,0:T(8,128)(2,1)} %get-tuple-element.113.rest_0_.rest_3_.rest_2_), channel_id=1, source_target_pairs={{0,4},{1,5},{2,6},{3,7},{4,0},{5,1},{6,2},{7,3},{8,12},{9,13},{10,... | collective-permute-start | bytes 552968 | tf_op jit(solution)/shard_map/ppermute | solution.py:564
  42.6 29.2 %collective-permute-start.16 = (bf16[240,384]{1,0:T(8,128)(2,1)}, bf16[240,384]{1,0:T(8,128)(2,1)S(1)}, u32[]{:S(2)}, u32[]{:S(2)}) collective-permute-start(bf16[240,384]{1,0:T(8,128)(2,1)} %get-tuple-element.113.rest_0_.rest_3_.rest_2_), channel_id=1, source_target_pairs={{0,2},{1,3},{2,0},{3,1},{4,6},{5,7},{6,4},{7,5},{8,10},{9,11},{10,... | collective-permute-start | bytes 552968 | tf_op jit(solution)/shard_map/ppermute | solution.py:564
  57.2 14.6 %collective-permute-start.26 = (bf16[240,384]{1,0:T(8,128)(2,1)S(1)}, bf16[240,384]{1,0:T(8,128)(2,1)S(1)}, u32[]{:S(2)}, u32[]{:S(2)}) collective-permute-start(bf16[240,384]{1,0:T(8,128)(2,1)S(1)} %collective-permute-done.22.rest_8_.rest_11_.rest_10_), channel_id=1, source_target_pairs={{0,4},{1,5},{2,6},{3,7},{4,0},{5,1},{6,2},{7,3},{8,12},{9,13},{10,... | collective-permute-start | bytes 552968 | tf_op jit(solution)/shard_map/ppermute | solution.py:564
  57.2 16.4 %collective-permute-start.24 = (bf16[240,384]{1,0:T(8,128)(2,1)S(1)}, bf16[240,384]{1,0:T(8,128)(2,1)S(1)}, u32[]{:S(2)}, u32[]{:S(2)}) collective-permute-start(bf16[240,384]{1,0:T(8,128)(2,1)S(1)} %collective-permute-done.22.rest_8_.rest_11_.rest_10_), channel_id=1, source_target_pairs={{0,2},{1,3},{2,0},{3,1},{4,6},{5,7},{6,4},{7,5},{8,10},{9,11},{10,... | collective-permute-start | bytes 552968 | tf_op jit(solution)/shard_map/ppermute | solution.py:564
  65.8 17.6 %collective-permute-start.23 = (bf16[240,384]{1,0:T(8,128)(2,1)S(1)}, bf16[240,384]{1,0:T(8,128)(2,1)S(1)}, u32[]{:S(2)}, u32[]{:S(2)}) collective-permute-start(bf16[240,384]{1,0:T(8,128)(2,1)S(1)} %collective-permute-done.22.rest_8_.rest_11_.rest_10_), channel_id=1, source_target_pairs={{0,1},{1,0},{2,3},{3,2},{4,5},{5,4},{6,7},{7,6},{8,9},{9,8},{10,11... | collective-permute-start | bytes 552968 | tf_op jit(solution)/shard_map/ppermute | solution.py:564
  71.8 12.2 %collective-permute-start.19 = (bf16[240,384]{1,0:T(8,128)(2,1)S(1)}, bf16[240,384]{1,0:T(8,128)(2,1)S(1)}, u32[]{:S(2)}, u32[]{:S(2)}) collective-permute-start(bf16[240,384]{1,0:T(8,128)(2,1)S(1)} %collective-permute-done.18.rest_4_.rest_7_.rest_6_), channel_id=1, source_target_pairs={{0,1},{1,0},{2,3},{3,2},{4,5},{5,4},{6,7},{7,6},{8,9},{9,8},{10,11... | collective-permute-start | bytes 552968 | tf_op jit(solution)/shard_map/ppermute | solution.py:564
  161.8 12.7 %collective-permute-start.30 = (bf16[2,8,96,768]{3,2,1,0:T(8,128)(2,1)}, bf16[2,8,96,768]{3,2,1,0:T(8,128)(2,1)S(1)}, u32[]{:S(2)}, u32[]{:S(2)}) collective-permute-start(bf16[2,8,96,768]{3,2,1,0:T(8,128)(2,1)} %get-tuple-element.138), channel_id=1, source_target_pairs={{0,1},{1,0},{2,3},{3,2},{4,5},{5,4},{6,7},{7,6},{8,9},{9,8},{10,11... | collective-permute-start | bytes 7077896 | tf_op jit(solution)/shard_map/ppermute | solution.py:564
  174.8 28.1 %collective-permute-start.31 = (bf16[8,96,768]{2,1,0:T(8,128)(2,1)S(1)}, bf16[8,96,768]{2,1,0:T(8,128)(2,1)S(1)}, u32[]{:S(2)}, u32[]{:S(2)}) collective-permute-start(bf16[8,96,768]{2,1,0:T(8,128)(2,1)S(1)} %fusion), channel_id=1, source_target_pairs={{0,16},{16,0},{1,17},{17,1},{2,18},{18,2},{3,19},{19,3},{4,20},{20... | collective-permute-start | bytes 3538952 | tf_op jit(solution)/shard_map/ppermute | solution.py:640
  198.2 20.9 %collective-permute-start.33 = (bf16[8,240,384]{2,1,0:T(8,128)(2,1)}, bf16[8,240,384]{2,1,0:T(8,128)(2,1)}, u32[]{:S(2)}, u32[]{:S(2)}) collective-permute-start(bf16[8,240,384]{2,1,0:T(8,128)(2,1)} %get-tuple-element.153), channel_id=1, source_target_pairs={{0,1},{1,0},{2,3},{3,2},{4,5},{5,4},{6,7},{7,6},{8,9},{9,8},{10,11... | collective-permute-start | bytes 4423688 | tf_op jit(solution)/shard_map/ppermute | solution.py:564
  203.9 17.7 %collective-permute-start.32 = (bf16[4,96,768]{2,1,0:T(8,128)(2,1)}, bf16[4,96,768]{2,1,0:T(8,128)(2,1)S(1)}, u32[]{:S(2)}, u32[]{:S(2)}) collective-permute-start(bf16[4,96,768]{2,1,0:T(8,128)(2,1)} %fusion.1), channel_id=1, source_target_pairs={{0,2},{1,3},{2,0},{3,1},{4,6},{5,7},{6,4},{7,5},{8,10},{9,11},{10,... | collective-permute-start | bytes 1769480 | tf_op jit(solution)/shard_map/ppermute | solution.py:564
  221.3 29.8 %collective-permute-start.37 = (bf16[4,240,384]{2,1,0:T(8,128)(2,1)}, bf16[4,240,384]{2,1,0:T(8,128)(2,1)}, u32[]{:S(2)}, u32[]{:S(2)}) collective-permute-start(bf16[4,240,384]{2,1,0:T(8,128)(2,1)} %add_convert_fusion.1), channel_id=1, source_target_pairs={{0,2},{1,3},{2,0},{3,1},{4,6},{5,7},{6,4},{7,5},{8,10},{9,11},{10,... | collective-permute-start | bytes 2211848 | tf_op jit(solution)/shard_map/ppermute | solution.py:564
  222.5 11.9 %collective-permute-start.34 = (bf16[2,96,768]{2,1,0:T(8,128)(2,1)}, bf16[2,96,768]{2,1,0:T(8,128)(2,1)S(1)}, u32[]{:S(2)}, u32[]{:S(2)}) collective-permute-start(bf16[2,96,768]{2,1,0:T(8,128)(2,1)} %fusion.3), channel_id=1, source_target_pairs={{0,4},{1,5},{2,6},{3,7},{4,0},{5,1},{6,2},{7,3},{8,12},{9,13},{10,... | collective-permute-start | bytes 884744 | tf_op jit(solution)/shard_map/ppermute | solution.py:564
  230.0 22.3 %collective-permute-start.36 = (bf16[8,144,384]{2,1,0:T(8,128)(2,1)}, bf16[8,144,384]{2,1,0:T(8,128)(2,1)}, u32[]{:S(2)}, u32[]{:S(2)}) collective-permute-start(bf16[8,144,384]{2,1,0:T(8,128)(2,1)} %get-tuple-element.165), channel_id=1, source_target_pairs={{0,1},{1,0},{2,3},{3,2},{4,5},{5,4},{6,7},{7,6},{8,9},{9,8},{10,11... | collective-permute-start | bytes 2654216 | tf_op jit(solution)/shard_map/ppermute | solution.py:564
  235.2 12.5 %collective-permute-start.35 = (bf16[1,96,768]{2,1,0:T(8,128)(2,1)}, bf16[1,96,768]{2,1,0:T(8,128)(2,1)}, u32[]{:S(2)}, u32[]{:S(2)}) collective-permute-start(bf16[1,96,768]{2,1,0:T(8,128)(2,1)} %fusion.10), channel_id=1, source_target_pairs={{0,8},{1,9},{2,10},{3,11},{4,12},{5,13},{6,14},{7,15},{8,0},{9,1},... | collective-permute-start | bytes 442376 | tf_op jit(solution)/shard_map/ppermute | solution.py:564
  249.5 64.8 %collective-permute-start.47 = (bf16[96,768]{1,0:T(8,128)(2,1)}, bf16[96,768]{1,0:T(8,128)(2,1)S(1)}, u32[]{:S(2)}, u32[]{:S(2)}) collective-permute-start(bf16[96,768]{1,0:T(8,128)(2,1)} %fusion.12.d_ref), channel_id=1, source_target_pairs={{0,16},{16,0},{1,17},{17,1},{2,18},{18,2},{3,19},{19,3},{4,20},{20... | collective-permute-start | bytes 442376 | tf_op jit(solution)/shard_map/ppermute | solution.py:640
  252.3 14.6 %collective-permute-start.39 = (bf16[2,240,384]{2,1,0:T(8,128)(2,1)S(1)}, bf16[2,240,384]{2,1,0:T(8,128)(2,1)S(1)}, u32[]{:S(2)}, u32[]{:S(2)}) collective-permute-start(bf16[2,240,384]{2,1,0:T(8,128)(2,1)S(1)} %add_convert_fusion.3), channel_id=1, source_target_pairs={{0,4},{1,5},{2,6},{3,7},{4,0},{5,1},{6,2},{7,3},{8,12},{9,13},{10,... | collective-permute-start | bytes 1105928 | tf_op jit(solution)/shard_map/ppermute | solution.py:564
  253.5 13.4 %collective-permute-start.38 = (bf16[4,144,384]{2,1,0:T(8,128)(2,1)S(1)}, bf16[4,144,384]{2,1,0:T(8,128)(2,1)S(1)}, u32[]{:S(2)}, u32[]{:S(2)}) collective-permute-start(bf16[4,144,384]{2,1,0:T(8,128)(2,1)S(1)} %add_convert_fusion.2), channel_id=1, source_target_pairs={{0,2},{1,3},{2,0},{3,1},{4,6},{5,7},{6,4},{7,5},{8,10},{9,11},{10,... | collective-permute-start | bytes 1327112 | tf_op jit(solution)/shard_map/ppermute | solution.py:564
  270.1 12.1 %collective-permute-start.45 = (bf16[1,240,384]{2,1,0:T(8,128)(2,1)S(1)}, bf16[1,240,384]{2,1,0:T(8,128)(2,1)S(1)}, u32[]{:S(2)}, u32[]{:S(2)}) collective-permute-start(bf16[1,240,384]{2,1,0:T(8,128)(2,1)S(1)} %add_convert_fusion.6), channel_id=1, source_target_pairs={{0,8},{1,9},{2,10},{3,11},{4,12},{5,13},{6,14},{7,15},{8,0},{9,1},... | collective-permute-start | bytes 552968 | tf_op jit(solution)/shard_map/ppermute | solution.py:564
  301.6 12.1 %all-to-all-start = ((f32[16,1,672]{2,1,0:T(1,128)}), f32[16,1,672]{2,1,0:T(1,128)S(1)}, u32[]{:S(2)}, u32[]{:S(2)}) async-start(f32[16,1,672]{2,1,0:T(1,128)} %copy.33), calls=%async_computation.1 | async-start | bytes 98304 | tf_op jit(solution)/shard_map/all_to_all | solution.py:1477
  (75 other events, 488.9 us)
Sparse Core Ops, SparseCore 0:
  11.0 64.0 all-gather.4
  77.9 53.5 all-gather.6
  162.3 85.5 reduce-scatter.1

commit v4 on v3

--- a/solution.py
+++ b/solution.py
@@ -609,8 +609,8 @@
             out = out + g[lo:hi].astype(F32)
         return out.astype(BF)
 
-    def hold(self, after):
-        self.got[-1] = tie(self.got[-1], after)
+    def hold(self, *after):
+        self.got[-1] = tie(self.got[-1], *after)
 
     def step(self):
         lo = self.size
@@ -659,6 +659,7 @@
 
 
 ANY = pl.BlockSpec(memory_space=pl.ANY)
+HBM = pl.BlockSpec(memory_space=pltpu.HBM)
 SMEM = pl.BlockSpec(memory_space=pltpu.SMEM)
 VMEM = pl.BlockSpec(memory_space=pltpu.VMEM)
 
@@ -742,7 +743,7 @@
             jax.ShapeDtypeStruct((rows1, 2 * own * SHARDS), F32),
             jax.ShapeDtypeStruct((2 * own, parts[0].shape[1]), F32),
         ],
-        compiler_params=params(),
+        compiler_params=params(8),
         cost_estimate=cost(3),
         name="mlp_join",
     )(order, *parts)
@@ -811,7 +812,7 @@
     return pl.pallas_call(
         partial(prepare_kernel, sizes),
         grid=(slots // blk,),
-        in_specs=[SMEM, pl.BlockSpec((blk, width), lambda i: (i, 0)), tall(1), tall(1)] + [ANY] * SHARDS,
+        in_specs=[SMEM, pl.BlockSpec((blk, width), lambda i: (i, 0)), tall(1), tall(1)] + [HBM] * SHARDS,
         out_specs=[
             tall(width), tall(width // 2), tall(width // 2),
             whole(8, width), whole(2, own * SHARDS), whole(3 * width, 1), tall(16),
@@ -863,7 +864,7 @@
         in_specs=[VMEM] * len(sums),
         out_specs=VMEM,
         out_shape=jax.ShapeDtypeStruct((SHARDS, size), F32),
-        compiler_params=params(),
+        compiler_params=params(4),
         cost_estimate=cost(3),
         name="pack",
     )(*sums)
@@ -908,7 +909,7 @@
         in_specs=[SMEM, tall(width, 0)]
         + [pl.BlockSpec((cols, 1), lambda i, n=n: (n * GROUPS + group, 0)) for n in range(3)]
         + [tall(cols // 2, group)] * 2
-        + [ANY] * SHARDS,
+        + [HBM] * SHARDS,
         out_specs=[tall(cols, 0)] * 3,
         out_shape=[jax.ShapeDtypeStruct((cols, slots), BF)] * 3,
         scratch_shapes=[
@@ -959,7 +960,7 @@
     return pl.pallas_call(
         partial(out_group_kernel, start),
         grid=(slots // blk,),
-        in_specs=[SMEM, VMEM] + [pl.BlockSpec((width // GROUPS, blk), lambda i: (0, i))] * GROUPS + [rows] + [ANY] * SHARDS,
+        in_specs=[SMEM, VMEM] + [pl.BlockSpec((width // GROUPS, blk), lambda i: (0, i))] * GROUPS + [rows] + [HBM] * SHARDS,
         out_specs=[rows, rows, cols],
         out_shape=[
             jax.ShapeDtypeStruct((slots, width), F32),
@@ -1073,7 +1074,7 @@
         block = jax.ShapeDtypeStruct((2, SHARDS // 2, rows2, width), BF)
     return pl.pallas_call(
         partial(mlp_half_kernel, part, first, split, len(pieces)),
-        in_specs=[SMEM] + [VMEM] * 5 + [ANY] * (len(sums) + len(pieces)),
+        in_specs=[SMEM] + [VMEM] * 5 + [ANY] * len(sums) + [HBM] * len(pieces),
         out_specs=[ANY, ANY] + [ANY] * (2 if split else 1) + [VMEM],
         out_shape=[jax.ShapeDtypeStruct((slots, width), F32 if first else BF), jax.ShapeDtypeStruct((slots, width), F32)]
         + [block] * (2 if split else 1)
@@ -1153,7 +1154,7 @@
         grid=(slots // blk,),
         in_specs=[SMEM, rows, rows, rows, VMEM]
         + [pl.BlockSpec((width // GROUPS, blk), lambda i: (0, i))] * GROUPS
-        + [ANY] * SHARDS,
+        + [HBM] * SHARDS,
         out_specs=[rows, cols, ANY, ANY, whole(8, width)],
         out_shape=[
             jax.ShapeDtypeStruct((slots, width), F32),
@@ -1250,7 +1251,7 @@
         out_specs=[head] * 3 + [half],
         out_shape=[jax.ShapeDtypeStruct((width, slots), BF)] * 3 + [jax.ShapeDtypeStruct((width // 2, slots), BF)],
         scratch_shapes=[pltpu.VMEM((slots - FIRST, slots - CUT), F32)],
-        compiler_params=params(),
+        compiler_params=params(20),
         cost_estimate=cost(13),
         name="heads_back",
     )(counts, q, k, v, o, do, lse, cos, sin)
@@ -1297,7 +1298,7 @@
             pltpu.SemaphoreType.DMA((SHARDS,)),
             pltpu.SemaphoreType.DMA((2, SHARDS // 2)),
         ],
-        compiler_params=params(),
+        compiler_params=params(16),
         cost_estimate=cost(6),
         name="qkv_grad",
     )(order, at, sel, dangle, dq, dk, dv, *more)
@@ -1339,11 +1340,11 @@
     return pl.pallas_call(
         part_kernel,
         grid=(slots // blk,),
-        in_specs=[SMEM] + [pl.BlockSpec((cols, blk), lambda i: (0, i))] * 3 + [ANY] * SHARDS,
+        in_specs=[SMEM] + [pl.BlockSpec((cols, blk), lambda i: (0, i))] * 3 + [HBM] * SHARDS,
         out_specs=pl.BlockSpec((width, blk), lambda i: (0, i)),
         out_shape=jax.ShapeDtypeStruct((width, slots), F32),
         scratch_shapes=[pltpu.VMEM((SHARDS, 3 * width // SHARDS, cols), BF), pltpu.SemaphoreType.DMA((SHARDS,))],
-        compiler_params=params(),
+        compiler_params=params(16),
         cost_estimate=cost(6),
         name="input_part",
     )(order, *grads, *pieces)
@@ -1374,11 +1375,11 @@
         grid=(slots // blk,),
         in_specs=[SMEM, rows, rows, VMEM, pl.BlockSpec((width, blk), lambda i: (0, i))]
         + [pl.BlockSpec((cols, blk), lambda i: (0, i))] * 3
-        + [ANY] * SHARDS,
+        + [HBM] * SHARDS,
         out_specs=[rows, pl.BlockSpec((8, width), lambda i: (0, 0))],
         out_shape=[jax.ShapeDtypeStruct((slots, width), BF), jax.ShapeDtypeStruct((8, width), F32)],
         scratch_shapes=[pltpu.VMEM((SHARDS, 3 * width // SHARDS, cols), BF), pltpu.SemaphoreType.DMA((SHARDS,))],
-        compiler_params=params(),
+        compiler_params=params(20),
         cost_estimate=cost(10),
         name="input_back",
     )(order, x, dh, vec, da, *grads, *pieces)
@@ -1450,32 +1451,34 @@
     sent = (scatter_d.step(), scatter_b.step())
     near_a, far_a, bias_a, freq_a = qkv_grad(order, a_t, sel, tie(dangle_a, *sent), *grads_a)
     scatter_a = Scatter(near_a, far_a)
-    scatter_d.hold(near_a)
-    sent = scatter_d.step()
-    da = input_part(order, lax.optimization_barrier((grads_b, near_a, sent))[0], pieces_b, width)
-    scatter_a.hold(da)
-    scatter_b.hold(da)
-    scatter_d.hold(da)
-    sent = (scatter_a.step(), scatter_b.step())
+    da = input_part(order, lax.optimization_barrier((grads_b, near_a))[0], pieces_b, width)
+    for scatter in (scatter_d, scatter_b, scatter_a):
+        scatter.hold(da)
+    sent = (scatter_a.step(), scatter_b.step(), scatter_d.step())
+    dx, sums1 = input_back(order, x, dh, vec, tie(da, *sent), grads_a, pieces_a)
+    scatter_a.hold(sums1, scatter_b.got[-1], scatter_d.got[-1])
+    sent = scatter_a.step()
+    scatter_b.hold(sent)
+    scatter_d.hold(sent)
+    other_c = across(tie(mlp_c, sent))
+    sent = (sent, scatter_b.step())
+    block = pack(sum(sizes), tie(sums1, *sent), sums2, g_b1a, g_b1b, bias_a, bias_b, freq_a, freq_b)
     mlp_d = scatter_d.finish()
-    dx, sums1 = input_back(order, x, dh, vec, tie(da, mlp_d[0], *sent), grads_a, pieces_a)
-    scatter_a.hold(sums1)
-    scatter_b.hold(sums1)
-    sent = (scatter_a.step(), scatter_b.step(), across(mlp_c))
-    other_c = sent[2]
-    block = pack(sum(sizes), tie(sums1, *sent), sums2, g_b1a, g_b1b, bias_a, bias_b, freq_a, freq_b)
-    scatter_a.step()
+    scatter_a.hold(block)
+    sent = scatter_a.step()
     mine_b = scatter_b.finish()
+    mine = jnp.sum(lax.all_to_all(block, "fsdp", 0, 0, tiled=True), axis=0)
+    rows1 = width // SHARDS
+    s_w1, s_w2 = mlp_join(rows1, order, (mlp_c, other_c) + mlp_d)
+    scatter_a.hold(mine, other_c)
     mine_a = scatter_a.finish()
+    mine_a = (mine_a[0], tie(mine_a[1], s_w1))
+    mine = mine + across(mine)
     s_a = mine_a[0].astype(F32) + mine_a[1].astype(F32)
     s_b = mine_b[0].astype(F32) + mine_b[1].astype(F32)
-    rows1 = width // SHARDS
-    s_w1, s_w2 = mlp_join(rows1, order, (mlp_c, other_c) + mlp_d)
     s_wqkv = jnp.concatenate([s[i * rows1 : (i + 1) * rows1] for i in range(3) for s in (s_a, s_b)], axis=1)
     s_wout = jnp.concatenate([s_b[3 * rows1 : 4 * rows1], s_b[4 * rows1 :]], axis=1)
 
-    mine = jnp.sum(lax.all_to_all(block, "fsdp", 0, 0, tiled=True), axis=0)
-    mine = mine + lax.ppermute(mine, "rep", [(0, 1), (1, 0)])
     outs = []
     at = 0
     for size in sizes:

time: 330 us -> 308 us (0.933)
  waiting for transfers between devices: 61.5 us -> 42.1 us
  Pallas kernels: 181 us -> 174 us
  starting transfers between devices: 46 us -> 50.5 us
    ppermute x42, waiting for transfers between devices: 39.3 us -> 25.7 us  [swap(): return lax.ppermute(v, 'fsdp', [(i, i ^ mask) for i in range(SHARDS)])]
    ppermute x42, starting transfers between devices: 34.5 us -> 39.4 us  [swap(): return lax.ppermute(v, 'fsdp', [(i, i ^ mask) for i in range(SHARDS)])]
    pallas_call x2, Pallas kernels: 27.3 us -> 23.3 us  [heads_back(): pl.pallas_call(heads_back_kernel, grid=(steps,), in_specs=[SMEM] + [head]...]
    ppermute x5 -> x6, waiting for transfers between devices: 15.3 us -> 12.8 us  [across(): return lax.ppermute(v, 'rep', [(0, 1), (1, 0)])]
    ppermute x5 -> x6, starting transfers between devices: 5.47 us -> 7.5 us  [across(): return lax.ppermute(v, 'rep', [(0, 1), (1, 0)])]
  transfers between devices with their start and end apart: 52 -> 52, of which waited for: 22 -> 21; matrix products, arithmetic and copies ran while one was open for 6% -> 6% of each run, Pallas kernels for 47% -> 48%
where the time goes in v4:
time: 308 us; the launch traced here: 305 us
  Pallas kernels  174 us (56%)
  starting transfers between devices  50.5 us (16%)
  waiting for transfers between devices  42.1 us (14%)
  between operations  15.5 us (5%)
  other arithmetic  14.7 us (5%)
  local copies, waits for them, and re-layouts  7.94 us (3%)
    pallas_call x2, Pallas kernels, mlp_half(): pl.pallas_call(partial(mlp_half_kernel, part, first, split, len(pieces)),...  51.1 us
    ppermute x42, starting transfers between devices, swap(): return lax.ppermute(v, 'fsdp', [(i, i ^ mask) for i in range(SHARDS)])  39.4 us
    ppermute x42, waiting for transfers between devices, swap(): return lax.ppermute(v, 'fsdp', [(i, i ^ mask) for i in range(SHARDS)])  25.7 us
    pallas_call x2, Pallas kernels, heads_back(): pl.pallas_call(heads_back_kernel, grid=(steps,), in_specs=[SMEM] + [head]...  23.3 us
    pallas_call x2, Pallas kernels, attend(): pl.pallas_call(attend_kernel, grid=(heads // each,), in_specs=[pl.BlockSp...  17.6 us
    pallas_call x2, Pallas kernels, qkv_grad(): pl.pallas_call(qkv_grad_kernel, in_specs=[SMEM] + [VMEM] * (6 + len(more)...  14.8 us
    pallas_call x2, Pallas kernels, project_group(): pl.pallas_call(group_kernel, grid=(slots // blk,), in_specs=[SMEM, tall(w...  13.9 us
    pallas_call x1, Pallas kernels, out_back_fast(): pl.pallas_call(partial(out_back_fast_kernel, start), grid=(slots // blk,)...  13.1 us
  transfers between devices with their start and end apart: 52, of which 21 were waited for; matrix products, arithmetic and copies ran while one was open for 6% of the time, Pallas kernels for 48%

profile of v4, /device:TPU:0, one launch (start us, length us, event | category | flops | bytes accessed | tf_op | source)
XLA Modules:
  0.0 304.6 jit_solution(6414837296956389018)
XLA Ops:
  12.6 4.0 %collective-permute-start.5 = (bf16[160,384]{1,0:T(8,128)(2,1)}, bf16[160,384]{1,0:T(8,128)(2,1)S(1)}, u32[]{:S(2)}, u32[]{:S(2)}) collective-permute-start(bf16[160,384]{1,0:T(8,128)(2,1)} %get-tuple-element.104.rest_0_.rest_3_), channel_id=1, source_target_pairs={{0,8},{1,9},{2,10},{3,11},{4,12},{5,13},{6,14},{7,15},{8,0},{9,1},... | collective-permute-start | bytes 368648 | tf_op jit(solution)/shard_map/ppermute | solution.py:564
  19.8 3.2 %collective-permute-done.5.rest_8_.rest_11_ = bf16[160,384]{1,0:T(8,128)(2,1)S(1)} collective-permute-done((bf16[160,384]{1,0:T(8,128)(2,1)}, bf16[160,384]{1,0:T(8,128)(2,1)S(1)}, u32[]{:S(2)}, u32[]{:S(2)}) %collective-permute-start.5) | collective-permute-done | bytes 122912 | tf_op jit(solution)/shard_map/ppermute | solution.py:564
  27.2 5.2 %collective-permute-done.11.rest_12_.rest_15_ = bf16[160,384]{1,0:T(8,128)(2,1)S(1)} collective-permute-done((bf16[160,384]{1,0:T(8,128)(2,1)S(1)}, bf16[160,384]{1,0:T(8,128)(2,1)S(1)}, u32[]{:S(2)}, u32[]{:S(2)}) %collective-permute-start.11) | collective-permute-done | bytes 122912 | tf_op jit(solution)/shard_map/ppermute | solution.py:564
  39.7 2.8 collective-permute-start.18
  44.7 9.8 %prepare.1 = (bf16[768,1024]{1,0:T(8,128)(2,1)}, f32[384,1024]{1,0:T(8,128)}, f32[384,1024]{1,0:T(8,128)}, f32[8,768]{1,0:T(8,128)}, f32[2,1536]{1,0:T(2,128)}, ...) custom-call(s32[17]{0:T(128)} %pad_add_fusion.order_ref, bf16[1024,768]{1,0:T(8,128)(2,1)} %bitcast.49, s32[1,1024]{1,0:T(1,128)} %cols_ref.1, ...), custom_call_target="tpu_custom_call" | custom-call | flops 8800000000 | bytes 65536 | tf_op jit(solution)/shard_map/prepare/pallas_call | solution.py:812
  58.8 6.9 %qkv_group.2 = (bf16[384,1024]{1,0:T(8,128)(2,1)}, bf16[384,1024]{1,0:T(8,128)(2,1)}, bf16[384,1024]{1,0:T(8,128)(2,1)}) custom-call(s32[17]{0:T(128)} %pad_add_fusion.order_ref, bf16[768,1024]{1,0:T(8,128)(2,1)} %get-tuple-element.108.at_ref, f32[2304,1]{1,0:T(8,128)} %get-tuple-element.109.bq_ref.bk_ref.bv_ref, ...), custom_call_target="tpu_custom_call" | custom-call | flops 7699999744 | bytes 65536 | tf_op jit(solution)/shard_map/qkv_group/pallas_call | solution.py:906
  65.9 5.9 %collective-permute-done.26.rest_12_.rest_15_.rest_14_ = bf16[240,384]{1,0:T(8,128)(2,1)S(1)} collective-permute-done((bf16[240,384]{1,0:T(8,128)(2,1)S(1)}, bf16[240,384]{1,0:T(8,128)(2,1)S(1)}, u32[]{:S(2)}, u32[]{:S(2)}) %collective-permute-start.26) | collective-permute-done | bytes 184352 | tf_op jit(solution)/shard_map/ppermute | solution.py:564
  73.9 8.8 %attend.2 = (bf16[384,1024]{1,0:T(8,128)(2,1)}, f32[6,1,1024]{2,1,0:T(1,128)}) custom-call(s32[3]{0:T(128)} %bitcast.54, bf16[384,1024]{1,0:T(8,128)(2,1)} %get-tuple-element.112.q_ref, bf16[384,1024]{1,0:T(8,128)(2,1)} %get-tuple-element.113.k_ref, bf16[384,1024]{1,0:T(8,128)(2,1)} %get-tuple-element.114.v_ref), custom_call_target="tpu_custom_call" | custom-call | flops 8800000000 | bytes 65536 | tf_op jit(solution)/shard_map/attend/pallas_call | solution.py:180
  86.4 6.9 %qkv_group.3 = (bf16[384,1024]{1,0:T(8,128)(2,1)}, bf16[384,1024]{1,0:T(8,128)(2,1)}, bf16[384,1024]{1,0:T(8,128)(2,1)}) custom-call(s32[17]{0:T(128)} %pad_add_fusion.order_ref, bf16[768,1024]{1,0:T(8,128)(2,1)} %get-tuple-element.108.at_ref, f32[2304,1]{1,0:T(8,128)} %get-tuple-element.109.bq_ref.bk_ref.bv_ref, ...), custom_call_target="tpu_custom_call" | custom-call | flops 7699999744 | bytes 65536 | tf_op jit(solution)/shard_map/qkv_group/pallas_call | solution.py:906
  93.4 8.8 %attend.3 = (bf16[384,1024]{1,0:T(8,128)(2,1)}, f32[6,1,1024]{2,1,0:T(1,128)}) custom-call(s32[3]{0:T(128)} %bitcast.55, bf16[384,1024]{1,0:T(8,128)(2,1)} %get-tuple-element.125.q_ref, bf16[384,1024]{1,0:T(8,128)(2,1)} %get-tuple-element.126.k_ref, bf16[384,1024]{1,0:T(8,128)(2,1)} %get-tuple-element.127.v_ref), custom_call_target="tpu_custom_call" | custom-call | flops 8800000000 | bytes 65536 | tf_op jit(solution)/shard_map/attend/pallas_call | solution.py:180
  102.2 8.6 %out_project.1 = (f32[1024,768]{1,0:T(8,128)}, bf16[1024,768]{1,0:T(8,128)(2,1)}, bf16[768,1024]{1,0:T(8,128)(2,1)}) custom-call(s32[17]{0:T(128)} %pad_add_fusion.order_ref, f32[8,768]{1,0:T(8,128)} %get-tuple-element.107.vec_ref, bf16[384,1024]{1,0:T(8,128)(2,1)} %get-tuple-element.115.rest_0_.o_ref, bf16[384,1024]{1,0:T(8,128)(2,1)} %get-tuple-element.128.rest_1_.o_ref, ...), custom_call_target="tpu_custom_call" | custom-call | flops 8800000000 | bytes 65536 | tf_op jit(solution)/shard_map/out_project/pallas_call | solution.py:960
  110.8 25.3 %mlp_half.2 = (f32[1024,768]{1,0:T(8,128)}, f32[1024,768]{1,0:T(8,128)}, bf16[16,192,768]{2,1,0:T(8,128)(2,1)}, f32[1,1536]{1,0:T(1,128)}) custom-call(s32[17]{0:T(128)} %pad_add_fusion.order_ref, bf16[1024,768]{1,0:T(8,128)(2,1)} %get-tuple-element.129.c_ref, bf16[768,1024]{1,0:T(8,128)(2,1)} %get-tuple-element.130.ct_ref, bf16[1024,768]{1,0:T(8,128)(2,1)} %bitcast.60, ...), custom_call_target="tpu_custom_call" | custom-call | flops 25300000768 | bytes 65536 | tf_op jit(solution)/shard_map/mlp_half/pallas_call | solution.py:1075
  136.1 25.8 %mlp_half.3 = (bf16[1024,768]{1,0:T(8,128)(2,1)}, f32[1024,768]{1,0:T(8,128)}, bf16[2,8,96,768]{3,2,1,0:T(8,128)(2,1)}, bf16[2,8,96,768]{3,2,1,0:T(8,128)(2,1)}, f32[1,1536]{1,0:T(1,128)}) custom-call(s32[17]{0:T(128)} %pad_add_fusion.order_ref, bf16[1024,768]{1,0:T(8,128)(2,1)} %get-tuple-element.129.c_ref, bf16[768,1024]{1,0:T(8,128)(2,1)} %get-tuple-element.130.ct_ref, ...), custom_call_target="tpu_custom_call" | custom-call | flops 25300000768 | bytes 65536 | tf_op jit(solution)/shard_map/mlp_half/pallas_call | solution.py:1075
  162.4 13.1 %out_back.1 = (f32[1024,768]{1,0:T(8,128)}, bf16[768,1024]{1,0:T(8,128)(2,1)}, bf16[8,96,384]{2,1,0:T(8,128)(2,1)}, bf16[8,96,384]{2,1,0:T(8,128)(2,1)}, f32[8,768]{1,0:T(8,128)}) custom-call(s32[17]{0:T(128)} %pad_add_fusion.order_ref, f32[1024,768]{1,0:T(8,128)} %get-tuple-element.138.dc_ref, f32[1024,768]{1,0:T(8,128)} %get-tuple-element.132.rest_0_.h_ref, ...), custom_call_target="tpu_custom_call" | custom-call | flops 13200000000 | bytes 65536 | tf_op jit(solution)/shard_map/out_back/pallas_call | solution.py:1152
  180.1 11.7 %heads_back.2 = (bf16[384,1024]{1,0:T(8,128)(2,1)S(1)}, bf16[384,1024]{1,0:T(8,128)(2,1)S(1)}, bf16[384,1024]{1,0:T(8,128)(2,1)S(1)}, bf16[192,1024]{1,0:T(8,128)(2,1)S(1)}) custom-call(s32[3]{0:T(128)S(1)} %bitcast.56, bf16[384,1024]{1,0:T(8,128)(2,1)S(1)} %copy-done.70, bf16[384,1024]{1,0:T(8,128)(2,1)S(1)} %copy-done.71, ...), custom_call_target="tpu_custom_call" | custom-call | flops 14300000256 | bytes 65536 | tf_op jit(solution)/shard_map/heads_back/pallas_call | solution.py:1247
  191.8 8.4 %qkv_grad.2 = (bf16[8,240,384]{2,1,0:T(8,128)(2,1)S(1)}, bf16[8,240,384]{2,1,0:T(8,128)(2,1)S(1)}, f32[16,1152]{1,0:T(8,128)S(1)}, f32[16,192]{1,0:T(8,128)S(1)}) custom-call(s32[17]{0:T(128)S(1)} %copy-done.65, bf16[768,1024]{1,0:T(8,128)(2,1)S(1)} %copy-done.66, bf16[16,1024]{1,0:T(8,128)(2,1)S(1)} %copy-done.82, ...), custom_call_target="tpu_custom_call" | custom-call | flops 6600000000 | bytes 65536 | tf_op jit(solution)/shard_map/qkv_grad/pallas_call | solution.py:1290
  200.4 4.6 %collective-permute-done.31 = bf16[8,96,768]{2,1,0:T(8,128)(2,1)S(1)} collective-permute-done((bf16[8,96,768]{2,1,0:T(8,128)(2,1)S(1)}, bf16[8,96,768]{2,1,0:T(8,128)(2,1)S(1)}, u32[]{:S(2)}, u32[]{:S(2)}) %collective-permute-start.31) | collective-permute-done | bytes 1179680 | tf_op jit(solution)/shard_map/ppermute | solution.py:640
  208.7 11.7 %heads_back.3 = (bf16[384,1024]{1,0:T(8,128)(2,1)S(1)}, bf16[384,1024]{1,0:T(8,128)(2,1)S(1)}, bf16[384,1024]{1,0:T(8,128)(2,1)S(1)}, bf16[192,1024]{1,0:T(8,128)(2,1)S(1)}) custom-call(s32[3]{0:T(128)S(1)} %bitcast.57, bf16[384,1024]{1,0:T(8,128)(2,1)S(1)} %copy-done.73, bf16[384,1024]{1,0:T(8,128)(2,1)S(1)} %copy-done.74, ...), custom_call_target="tpu_custom_call" | custom-call | flops 14300000256 | bytes 65536 | tf_op jit(solution)/shard_map/heads_back/pallas_call | solution.py:1247
  223.6 6.4 %qkv_grad.3 = (bf16[8,144,384]{2,1,0:T(8,128)(2,1)S(1)}, bf16[8,144,384]{2,1,0:T(8,128)(2,1)S(1)}, f32[16,1152]{1,0:T(8,128)S(1)}, f32[16,192]{1,0:T(8,128)S(1)}) custom-call(s32[17]{0:T(128)S(1)} %copy-done.65, bf16[768,1024]{1,0:T(8,128)(2,1)S(1)} %copy-done.66, bf16[16,1024]{1,0:T(8,128)(2,1)S(1)} %copy-done.82, ...), custom_call_target="tpu_custom_call" | custom-call | flops 6600000000 | bytes 65536 | tf_op jit(solution)/shard_map/qkv_grad/pallas_call | solution.py:1290
  230.3 6.4 %input_part.1.da_ref = f32[768,1024]{1,0:T(8,128)S(1)} custom-call(s32[17]{0:T(128)S(1)} %copy-done.65, bf16[384,1024]{1,0:T(8,128)(2,1)S(1)} %get-tuple-element.164.dq_ref.rest_0_, bf16[384,1024]{1,0:T(8,128)(2,1)S(1)} %get-tuple-element.165.dk_ref.rest_1_, bf16[384,1024]{1,0:T(8,128)(2,1)S(1)} %get-tuple-element.166.dv_ref.rest_2_, ...), custom_call_target="tpu_custom_call" | custom-call | flops 6600000000 | bytes 65536 | tf_op jit(solution)/shard_map/input_part/pallas_call | solution.py:1340
  247.5 9.5 %input_back.1 = (bf16[1024,768]{1,0:T(8,128)(2,1)}, f32[8,768]{1,0:T(8,128)S(1)}) custom-call(s32[17]{0:T(128)S(1)} %copy-done.65, bf16[1024,768]{1,0:T(8,128)(2,1)S(1)} %bitcast.51, f32[1024,768]{1,0:T(8,128)S(1)} %copy-done.69, f32[8,768]{1,0:T(8,128)S(1)} %copy-done.85, f32[768,1024]{1,0:T(8,128)S(1)} %input_part.1.da_ref, ...), custom_call_target="tpu_custom_call" | custom-call | flops 11000000512 | bytes 65536 | tf_op jit(solution)/shard_map/input_back/pallas_call | solution.py:1373
  259.8 3.5 %all-to-all-start = ((f32[16,1,672]{2,1,0:T(1,128)}), f32[16,1,672]{2,1,0:T(1,128)S(1)}, u32[]{:S(2)}, u32[]{:S(2)}) async-start(f32[16,1,672]{2,1,0:T(1,128)} %copy.33), calls=%async_computation | async-start | bytes 98304 | tf_op jit(solution)/shard_map/all_to_all | solution.py:1470
  267.5 2.8 all-to-all-done
  281.5 4.6 %collective-permute-done.47 = bf16[240,384]{1,0:T(8,128)(2,1)S(1)} collective-permute-done((bf16[240,384]{1,0:T(8,128)(2,1)}, bf16[240,384]{1,0:T(8,128)(2,1)S(1)}, u32[]{:S(2)}, u32[]{:S(2)}) %collective-permute-start.47) | collective-permute-done | bytes 184352 | tf_op jit(solution)/shard_map/ppermute | solution.py:640
  (351 shorter events, 84.3 us)
Async XLA Ops:
  7.3 103.5 %all-gather.5.cloned.1.call-start = ((), (), s32[]{:S(2)}) async-start(), calls=%async_computation.3 | async-start | bytes 5013504 | tf_op jit(solution)/shard_map/all_gather | solution.py:1407
  9.4 126.8 %all-gather.7.cloned.1.call-start = ((), (), s32[]{:S(2)}) async-start(), calls=%async_computation.4 | async-start | bytes 5013504 | tf_op jit(solution)/shard_map/all_gather | solution.py:1408
  10.1 270.0 %reduce-scatter.2.cloned.1.call-start = ((), (), s32[]{:S(2)}) async-start(), calls=%async_computation.2 | async-start | bytes 5013504 | tf_op jit(solution)/shard_map/reduce_scatter | solution.py:1432
  37.9 45.4 %collective-permute-start.15 = (bf16[240,384]{1,0:T(8,128)(2,1)}, bf16[240,384]{1,0:T(8,128)(2,1)S(1)}, u32[]{:S(2)}, u32[]{:S(2)}) collective-permute-start(bf16[240,384]{1,0:T(8,128)(2,1)} %get-tuple-element.117.rest_0_.rest_3_.rest_2_), channel_id=1, source_target_pairs={{0,1},{1,0},{2,3},{3,2},{4,5},{5,4},{6,7},{7,6},{8,9},{9,8},{10,11... | collective-permute-start | bytes 552968 | tf_op jit(solution)/shard_map/ppermute | solution.py:564
  38.4 18.7 %collective-permute-start.22 = (bf16[240,384]{1,0:T(8,128)(2,1)}, bf16[240,384]{1,0:T(8,128)(2,1)S(1)}, u32[]{:S(2)}, u32[]{:S(2)}) collective-permute-start(bf16[240,384]{1,0:T(8,128)(2,1)} %get-tuple-element.117.rest_0_.rest_3_.rest_2_), channel_id=1, source_target_pairs={{0,8},{1,9},{2,10},{3,11},{4,12},{5,13},{6,14},{7,15},{8,0},{9,1},... | collective-permute-start | bytes 552968 | tf_op jit(solution)/shard_map/ppermute | solution.py:564
  39.7 26.0 %collective-permute-start.18 = (bf16[240,384]{1,0:T(8,128)(2,1)}, bf16[240,384]{1,0:T(8,128)(2,1)S(1)}, u32[]{:S(2)}, u32[]{:S(2)}) collective-permute-start(bf16[240,384]{1,0:T(8,128)(2,1)} %get-tuple-element.117.rest_0_.rest_3_.rest_2_), channel_id=1, source_target_pairs={{0,4},{1,5},{2,6},{3,7},{4,0},{5,1},{6,2},{7,3},{8,12},{9,13},{10,... | collective-permute-start | bytes 552968 | tf_op jit(solution)/shard_map/ppermute | solution.py:564
  42.6 29.2 %collective-permute-start.16 = (bf16[240,384]{1,0:T(8,128)(2,1)}, bf16[240,384]{1,0:T(8,128)(2,1)S(1)}, u32[]{:S(2)}, u32[]{:S(2)}) collective-permute-start(bf16[240,384]{1,0:T(8,128)(2,1)} %get-tuple-element.117.rest_0_.rest_3_.rest_2_), channel_id=1, source_target_pairs={{0,2},{1,3},{2,0},{3,1},{4,6},{5,7},{6,4},{7,5},{8,10},{9,11},{10,... | collective-permute-start | bytes 552968 | tf_op jit(solution)/shard_map/ppermute | solution.py:564
  57.1 14.6 %collective-permute-start.26 = (bf16[240,384]{1,0:T(8,128)(2,1)S(1)}, bf16[240,384]{1,0:T(8,128)(2,1)S(1)}, u32[]{:S(2)}, u32[]{:S(2)}) collective-permute-start(bf16[240,384]{1,0:T(8,128)(2,1)S(1)} %collective-permute-done.22.rest_8_.rest_11_.rest_10_), channel_id=1, source_target_pairs={{0,4},{1,5},{2,6},{3,7},{4,0},{5,1},{6,2},{7,3},{8,12},{9,13},{10,... | collective-permute-start | bytes 552968 | tf_op jit(solution)/shard_map/ppermute | solution.py:564
  57.1 16.4 %collective-permute-start.24 = (bf16[240,384]{1,0:T(8,128)(2,1)S(1)}, bf16[240,384]{1,0:T(8,128)(2,1)S(1)}, u32[]{:S(2)}, u32[]{:S(2)}) collective-permute-start(bf16[240,384]{1,0:T(8,128)(2,1)S(1)} %collective-permute-done.22.rest_8_.rest_11_.rest_10_), channel_id=1, source_target_pairs={{0,2},{1,3},{2,0},{3,1},{4,6},{5,7},{6,4},{7,5},{8,10},{9,11},{10,... | collective-permute-start | bytes 552968 | tf_op jit(solution)/shard_map/ppermute | solution.py:564
  65.8 17.6 %collective-permute-start.23 = (bf16[240,384]{1,0:T(8,128)(2,1)S(1)}, bf16[240,384]{1,0:T(8,128)(2,1)S(1)}, u32[]{:S(2)}, u32[]{:S(2)}) collective-permute-start(bf16[240,384]{1,0:T(8,128)(2,1)S(1)} %collective-permute-done.22.rest_8_.rest_11_.rest_10_), channel_id=1, source_target_pairs={{0,1},{1,0},{2,3},{3,2},{4,5},{5,4},{6,7},{7,6},{8,9},{9,8},{10,11... | collective-permute-start | bytes 552968 | tf_op jit(solution)/shard_map/ppermute | solution.py:564
  71.7 12.2 %collective-permute-start.19 = (bf16[240,384]{1,0:T(8,128)(2,1)S(1)}, bf16[240,384]{1,0:T(8,128)(2,1)S(1)}, u32[]{:S(2)}, u32[]{:S(2)}) collective-permute-start(bf16[240,384]{1,0:T(8,128)(2,1)S(1)} %collective-permute-done.18.rest_4_.rest_7_.rest_6_), channel_id=1, source_target_pairs={{0,1},{1,0},{2,3},{3,2},{4,5},{5,4},{6,7},{7,6},{8,9},{9,8},{10,11... | collective-permute-start | bytes 552968 | tf_op jit(solution)/shard_map/ppermute | solution.py:564
  161.9 13.6 %collective-permute-start.30 = (bf16[2,8,96,768]{3,2,1,0:T(8,128)(2,1)}, bf16[2,8,96,768]{3,2,1,0:T(8,128)(2,1)S(1)}, u32[]{:S(2)}, u32[]{:S(2)}) collective-permute-start(bf16[2,8,96,768]{3,2,1,0:T(8,128)(2,1)} %get-tuple-element.142), channel_id=1, source_target_pairs={{0,1},{1,0},{2,3},{3,2},{4,5},{5,4},{6,7},{7,6},{8,9},{9,8},{10,11... | collective-permute-start | bytes 7077896 | tf_op jit(solution)/shard_map/ppermute | solution.py:564
  177.0 28.0 %collective-permute-start.31 = (bf16[8,96,768]{2,1,0:T(8,128)(2,1)S(1)}, bf16[8,96,768]{2,1,0:T(8,128)(2,1)S(1)}, u32[]{:S(2)}, u32[]{:S(2)}) collective-permute-start(bf16[8,96,768]{2,1,0:T(8,128)(2,1)S(1)} %fusion), channel_id=1, source_target_pairs={{0,16},{16,0},{1,17},{17,1},{2,18},{18,2},{3,19},{19,3},{4,20},{20... | collective-permute-start | bytes 3538952 | tf_op jit(solution)/shard_map/ppermute | solution.py:640
  200.2 20.1 %collective-permute-start.33 = (bf16[8,240,384]{2,1,0:T(8,128)(2,1)S(1)}, bf16[8,240,384]{2,1,0:T(8,128)(2,1)S(1)}, u32[]{:S(2)}, u32[]{:S(2)}) collective-permute-start(bf16[8,240,384]{2,1,0:T(8,128)(2,1)S(1)} %get-tuple-element.157), channel_id=1, source_target_pairs={{0,1},{1,0},{2,3},{3,2},{4,5},{5,4},{6,7},{7,6},{8,9},{9,8},{10,11... | collective-permute-start | bytes 4423688 | tf_op jit(solution)/shard_map/ppermute | solution.py:564
  206.9 14.8 %collective-permute-start.32 = (bf16[4,96,768]{2,1,0:T(8,128)(2,1)S(1)}, bf16[4,96,768]{2,1,0:T(8,128)(2,1)S(1)}, u32[]{:S(2)}, u32[]{:S(2)}) collective-permute-start(bf16[4,96,768]{2,1,0:T(8,128)(2,1)S(1)} %fusion.1), channel_id=1, source_target_pairs={{0,2},{1,3},{2,0},{3,1},{4,6},{5,7},{6,4},{7,5},{8,10},{9,11},{10,... | collective-permute-start | bytes 1769480 | tf_op jit(solution)/shard_map/ppermute | solution.py:564
  220.6 21.7 %collective-permute-start.35 = (bf16[4,240,384]{2,1,0:T(8,128)(2,1)S(1)}, bf16[4,240,384]{2,1,0:T(8,128)(2,1)S(1)}, u32[]{:S(2)}, u32[]{:S(2)}) collective-permute-start(bf16[4,240,384]{2,1,0:T(8,128)(2,1)S(1)} %add_convert_fusion.1), channel_id=1, source_target_pairs={{0,2},{1,3},{2,0},{3,1},{4,6},{5,7},{6,4},{7,5},{8,10},{9,11},{10,... | collective-permute-start | bytes 2211848 | tf_op jit(solution)/shard_map/ppermute | solution.py:564
  223.1 15.5 %collective-permute-start.36 = (bf16[2,96,768]{2,1,0:T(8,128)(2,1)S(1)}, bf16[2,96,768]{2,1,0:T(8,128)(2,1)S(1)}, u32[]{:S(2)}, u32[]{:S(2)}) collective-permute-start(bf16[2,96,768]{2,1,0:T(8,128)(2,1)S(1)} %fusion.3), channel_id=1, source_target_pairs={{0,4},{1,5},{2,6},{3,7},{4,0},{5,1},{6,2},{7,3},{8,12},{9,13},{10,... | collective-permute-start | bytes 884744 | tf_op jit(solution)/shard_map/ppermute | solution.py:564
  230.1 15.2 %collective-permute-start.34 = (bf16[8,144,384]{2,1,0:T(8,128)(2,1)S(1)}, bf16[8,144,384]{2,1,0:T(8,128)(2,1)S(1)}, u32[]{:S(2)}, u32[]{:S(2)}) collective-permute-start(bf16[8,144,384]{2,1,0:T(8,128)(2,1)S(1)} %get-tuple-element.167), channel_id=1, source_target_pairs={{0,1},{1,0},{2,3},{3,2},{4,5},{5,4},{6,7},{7,6},{8,9},{9,8},{10,11... | collective-permute-start | bytes 2654216 | tf_op jit(solution)/shard_map/ppermute | solution.py:564
  240.1 17.0 %collective-permute-start.39 = (bf16[1,96,768]{2,1,0:T(8,128)(2,1)S(1)}, bf16[1,96,768]{2,1,0:T(8,128)(2,1)S(1)}, u32[]{:S(2)}, u32[]{:S(2)}) collective-permute-start(bf16[1,96,768]{2,1,0:T(8,128)(2,1)S(1)} %fusion.10), channel_id=1, source_target_pairs={{0,8},{1,9},{2,10},{3,11},{4,12},{5,13},{6,14},{7,15},{8,0},{9,1},... | collective-permute-start | bytes 442376 | tf_op jit(solution)/shard_map/ppermute | solution.py:564
  242.5 14.6 %collective-permute-start.38 = (bf16[2,240,384]{2,1,0:T(8,128)(2,1)S(1)}, bf16[2,240,384]{2,1,0:T(8,128)(2,1)S(1)}, u32[]{:S(2)}, u32[]{:S(2)}) collective-permute-start(bf16[2,240,384]{2,1,0:T(8,128)(2,1)S(1)} %add_convert_fusion.3), channel_id=1, source_target_pairs={{0,4},{1,5},{2,6},{3,7},{4,0},{5,1},{6,2},{7,3},{8,12},{9,13},{10,... | collective-permute-start | bytes 1105928 | tf_op jit(solution)/shard_map/ppermute | solution.py:564
  245.4 11.7 %collective-permute-start.37 = (bf16[4,144,384]{2,1,0:T(8,128)(2,1)S(1)}, bf16[4,144,384]{2,1,0:T(8,128)(2,1)S(1)}, u32[]{:S(2)}, u32[]{:S(2)}) collective-permute-start(bf16[4,144,384]{2,1,0:T(8,128)(2,1)S(1)} %add_convert_fusion.2), channel_id=1, source_target_pairs={{0,2},{1,3},{2,0},{3,1},{4,6},{5,7},{6,4},{7,5},{8,10},{9,11},{10,... | collective-permute-start | bytes 1327112 | tf_op jit(solution)/shard_map/ppermute | solution.py:564
  263.3 13.1 %collective-permute-start.46 = (bf16[1,240,384]{2,1,0:T(8,128)(2,1)}, bf16[1,240,384]{2,1,0:T(8,128)(2,1)}, u32[]{:S(2)}, u32[]{:S(2)}) collective-permute-start(bf16[1,240,384]{2,1,0:T(8,128)(2,1)} %add_convert_fusion.6), channel_id=1, source_target_pairs={{0,8},{1,9},{2,10},{3,11},{4,12},{5,13},{6,14},{7,15},{8,0},{9,1},... | collective-permute-start | bytes 552968 | tf_op jit(solution)/shard_map/ppermute | solution.py:564
  266.0 14.1 %collective-permute-start.41 = (bf16[2,144,384]{2,1,0:T(8,128)(2,1)}, bf16[2,144,384]{2,1,0:T(8,128)(2,1)}, u32[]{:S(2)}, u32[]{:S(2)}) collective-permute-start(bf16[2,144,384]{2,1,0:T(8,128)(2,1)} %add_convert_fusion.4), channel_id=1, source_target_pairs={{0,4},{1,5},{2,6},{3,7},{4,0},{5,1},{6,2},{7,3},{8,12},{9,13},{10,... | collective-permute-start | bytes 663560 | tf_op jit(solution)/shard_map/ppermute | solution.py:564
  273.5 20.3 %collective-permute-start.45 = (bf16[96,768]{1,0:T(8,128)(2,1)S(1)}, bf16[96,768]{1,0:T(8,128)(2,1)S(1)}, u32[]{:S(2)}, u32[]{:S(2)}) collective-permute-start(bf16[96,768]{1,0:T(8,128)(2,1)S(1)} %fusion.12.d_ref), channel_id=1, source_target_pairs={{0,16},{16,0},{1,17},{17,1},{2,18},{18,2},{3,19},{19,3},{4,20},{20... | collective-permute-start | bytes 442376 | tf_op jit(solution)/shard_map/ppermute | solution.py:640
  (136 other events, 1049.5 us)
Sparse Core Ops, SparseCore 0:
  11.0 64.0 all-gather.4
  77.9 53.5 all-gather.6
  162.5 79.3 reduce-scatter.1

commit v5 on v4

--- a/solution.py
+++ b/solution.py
@@ -150,13 +150,13 @@
 
     def part(scores, first, values):
         peak = jnp.max(scores, axis=0, keepdims=True)
-        weights = jnp.exp(scores - peak)
-        total = jnp.sum(weights, axis=0, keepdims=True)
-        wb = weights.astype(BF)
+        wb = jnp.exp(scores - peak).astype(BF)
         gap = jnp.zeros((values.shape[1] - wb.shape[0], wb.shape[1]), BF)
         wb = jnp.concatenate([wb, gap] if first else [gap, wb], axis=0)
-        mixed = nn(values, wb) * (1.0 / total)
-        return mixed, peak + jnp.log(total)
+        lines = jnp.concatenate([values, jnp.ones((16, values.shape[1]), BF)], axis=0)
+        mixed = nn(lines, wb)
+        total = mixed[HEAD_DIM : HEAD_DIM + 1]
+        return mixed[:HEAD_DIM] * (1.0 / total), peak + jnp.log(total)
 
     edge = lax.broadcasted_iota(jnp.int32, (1, WIDE - CUT), 1) < FIRST - CUT
     for h in range(q_ref.shape[0] // HEAD_DIM):
@@ -974,14 +974,14 @@
     )(order, vec, *o, x, *pieces)
 
 
-def mlp_half_kernel(part, first, split, n_in, order_ref, c_ref, ct_ref, dy_ref, b1_ref, vec_ref, *rest):
+def mlp_half_kernel(part, first, split, n_in, order_ref, c_in, ct_in, dy_in, b1_ref, vec_ref, *rest):
     acc_in, rest = (rest[:1], rest[1:]) if first else (rest[:2], rest[2:])
     pieces, rest = rest[:n_in], rest[n_in:]
     n_g = 2 if split else 1
     y_ref, dc_ref = rest[:2]
     g_refs = rest[2 : 2 + n_g]
-    gb1_ref, w1_scr, w2_scr, g1_scr, g2_scr, hb_scr, dp_scr, y_acc, dc_acc, sem, load_sem = rest[2 + n_g : 13 + n_g]
-    y_out = y_acc if first else rest[13 + n_g]
+    gb1_ref, w1_scr, w2_scr, g1_scr, g2_scr, hb_scr, dp_scr, y_acc, dc_acc = rest[2 + n_g : 11 + n_g]
+    c_ref, ct_ref, dy_ref, y_out, dc_out, sem, load_sem = rest[11 + n_g :]
     slots, width = c_ref.shape
     rows1 = w1_scr.shape[2]
     rows2 = w2_scr.shape[1]
@@ -996,17 +996,18 @@
         for j in range(steps)
     ]
     loads.insert(1, fetch(refs, places, [(slice(steps * rows1, steps * rows1 + rows2), lambda d: w2_scr.at[d])], sem.at[steps]))
-    sums = [pltpu.make_async_copy(src, dst, load_sem.at[i]) for i, (src, dst) in enumerate(zip(acc_in, (y_acc, dc_acc)))]
-    for copies in loads[:2] + [sums] + loads[2:]:
+    sums = list(zip(acc_in, (y_acc,) if first else (y_out, dc_out)))
+    rows_in = [(c_in, c_ref), (dy_in, dy_ref), (ct_in, ct_ref)]
+    whole = [pltpu.make_async_copy(src, dst, load_sem.at[i]) for i, (src, dst) in enumerate(rows_in + sums)]
+    (c_load, dy_load, ct_load), sums = whole[:3], whole[3:]
+    for copies in [[c_load], loads[0], [dy_load], loads[1], sums, [ct_load]] + loads[2:]:
         start_all(copies)
     sends = []
     for j in range(steps):
         cols = slice(j * blk, (j + 1) * blk)
-        wait_all(loads[0] if j == 0 else loads[1 + j])
+        wait_all([c_load] + loads[0] if j == 0 else loads[1 + j])
         w1 = w1_scr[j].reshape(width, blk)
-        if j == 0:
-            wait_all(loads[1] + sums)
-        w2 = w2_scr[j * per : (j + 1) * per].reshape(blk, width)
+        w2 = None
         total = None
         for i in range(slots // tile):
             rows = slice(i * tile, (i + 1) * tile)
@@ -1017,7 +1018,12 @@
             hb = (pre * cdf).astype(BF)
             slope = cdf + 0.5 * pre * (1.0 - th * th) * (GELU_C * (1.0 + (3.0 * GELU_A) * square))
             hb_scr[rows, :] = hb
-            y = y_acc[rows, :] + nn(hb, w2)
+            if w2 is None:
+                if j == 0:
+                    wait_all(loads[1] + [dy_load] + sums)
+                w2 = w2_scr[j * per : (j + 1) * per].reshape(blk, width)
+            before = y_acc if first or j else y_out
+            y = before[rows, :].astype(F32) + nn(hb, w2)
             if first and j == 0:
                 y = y + vec_ref[4:5, :]
             dpre = (nt(dy_ref[rows, :], w2) * slope).astype(BF)
@@ -1025,19 +1031,22 @@
             term = jnp.sum(dpre.astype(F32), axis=0, keepdims=True)
             total = term if total is None else total + term
             dc = nt(dpre, w1)
-            if not (first and j == 0):
-                dc = dc + dc_acc[rows, :]
-            dc_acc[rows, :] = dc
+            if j or not first:
+                dc = dc + (dc_acc if j else dc_out)[rows, :].astype(F32)
             if j == steps - 1:
-                y_out[rows, :] = y.astype(y_out.dtype)
+                y_out[rows, :] = y.astype(BF)
+                dc_out[rows, :] = dc.astype(BF)
                 sends += [
-                    pltpu.make_async_copy(y_out.at[rows], y_ref.at[rows], load_sem.at[2 + 2 * i]),
-                    pltpu.make_async_copy(dc_acc.at[rows], dc_ref.at[rows], load_sem.at[3 + 2 * i]),
+                    pltpu.make_async_copy(y_out.at[rows], y_ref.at[rows], load_sem.at[5 + 2 * i]),
+                    pltpu.make_async_copy(dc_out.at[rows], dc_ref.at[rows], load_sem.at[6 + 2 * i]),
                 ]
                 start_all(sends[-2:])
             else:
                 y_acc[rows, :] = y
+                dc_acc[rows, :] = dc
         gb1_ref[:, cols] = total
+        if j == 0:
+            wait_all([ct_load])
         g1_scr[j] = nn(ct_ref[...], dp_scr[...]).astype(BF).reshape(SHARDS, rows1, blk)
         if split:
             mine = order_ref[SHARDS]
@@ -1074,9 +1083,9 @@
         block = jax.ShapeDtypeStruct((2, SHARDS // 2, rows2, width), BF)
     return pl.pallas_call(
         partial(mlp_half_kernel, part, first, split, len(pieces)),
-        in_specs=[SMEM] + [VMEM] * 5 + [ANY] * len(sums) + [HBM] * len(pieces),
+        in_specs=[SMEM] + [ANY] * 3 + [VMEM] * 2 + [ANY] * len(sums) + [HBM] * len(pieces),
         out_specs=[ANY, ANY] + [ANY] * (2 if split else 1) + [VMEM],
-        out_shape=[jax.ShapeDtypeStruct((slots, width), F32 if first else BF), jax.ShapeDtypeStruct((slots, width), F32)]
+        out_shape=[jax.ShapeDtypeStruct((slots, width), BF)] * 2
         + [block] * (2 if split else 1)
         + [jax.ShapeDtypeStruct((1, hidden), F32)],
         scratch_shapes=[
@@ -1088,10 +1097,14 @@
             pltpu.VMEM((slots, blk), BF),
             pltpu.VMEM((slots, width), F32),
             pltpu.VMEM((slots, width), F32),
+            pltpu.VMEM((slots, width), BF),
+            pltpu.VMEM((width, slots), BF),
+            pltpu.VMEM((slots, width), BF),
+            pltpu.VMEM((slots, width), BF),
+            pltpu.VMEM((slots, width), BF),
             pltpu.SemaphoreType.DMA((steps + 1, SHARDS)),
-            pltpu.SemaphoreType.DMA((8,)),
-        ]
-        + ([] if first else [pltpu.VMEM((slots, width), BF)]),
+            pltpu.SemaphoreType.DMA((9,)),
+        ],
         compiler_params=params(),
         cost_estimate=cost(23),
         name="mlp_half",
@@ -1115,10 +1128,10 @@
         wait_all(copies)
 
     dy = dy_ref[...].astype(F32)
-    part, dgain, dshift = norm_back(dc_ref[...], h_ref[...], vec_ref[2:3, :])
+    part, dgain, dshift = norm_back(dc_ref[...].astype(F32), h_ref[...], vec_ref[2:3, :])
     dh = dy + part
-    dh_ref[...] = dh
     dhb = dh.astype(BF)
+    dh_ref[...] = dhb
     do_ref[...] = nt(w_scr[...].reshape(width, width), dhb).astype(BF)
     rows = width // GROUPS
     for g in range(GROUPS):
@@ -1157,7 +1170,7 @@
         + [HBM] * SHARDS,
         out_specs=[rows, cols, ANY, ANY, whole(8, width)],
         out_shape=[
-            jax.ShapeDtypeStruct((slots, width), F32),
+            jax.ShapeDtypeStruct((slots, width), BF),
             jax.ShapeDtypeStruct((width, slots), BF),
             block,
             block,
@@ -1360,7 +1373,7 @@
 
     da = da_ref[...] + group_product(grads, w_scr)
     out, dgain, dshift = norm_back(da.T, x_ref[...].astype(F32), vec_ref[1:2, :])
-    dx_ref[...] = (dh_ref[...] + out).astype(BF)
+    dx_ref[...] = (dh_ref[...].astype(F32) + out).astype(BF)
     sums_ref[0:1, :] += dgain
     sums_ref[1:2, :] += dshift
 
@@ -1458,19 +1471,21 @@
     dx, sums1 = input_back(order, x, dh, vec, tie(da, *sent), grads_a, pieces_a)
     scatter_a.hold(sums1, scatter_b.got[-1], scatter_d.got[-1])
     sent = scatter_a.step()
+    other_c = across(tie(mlp_c, sent))
     scatter_b.hold(sent)
     scatter_d.hold(sent)
-    other_c = across(tie(mlp_c, sent))
-    sent = (sent, scatter_b.step())
-    block = pack(sum(sizes), tie(sums1, *sent), sums2, g_b1a, g_b1b, bias_a, bias_b, freq_a, freq_b)
-    mlp_d = scatter_d.finish()
+    block = pack(sum(sizes), tie(sums1, sent), sums2, g_b1a, g_b1b, bias_a, bias_b, freq_a, freq_b)
     scatter_a.hold(block)
     sent = scatter_a.step()
+    scatter_b.step()
+    mlp_d = scatter_d.finish()
+    scatter_b.hold(other_c, sent)
     mine_b = scatter_b.finish()
-    mine = jnp.sum(lax.all_to_all(block, "fsdp", 0, 0, tiled=True), axis=0)
+    mine = jnp.sum(tie(lax.all_to_all(block, "fsdp", 0, 0, tiled=True), sent), axis=0)
+    mine = tie(mine, scatter_a.got[-1])
     rows1 = width // SHARDS
     s_w1, s_w2 = mlp_join(rows1, order, (mlp_c, other_c) + mlp_d)
-    scatter_a.hold(mine, other_c)
+    scatter_a.hold(mine)
     mine_a = scatter_a.finish()
     mine_a = (mine_a[0], tie(mine_a[1], s_w1))
     mine = mine + across(mine)

time: 308 us -> 303 us (0.984)
  Pallas kernels: 174 us -> 169 us
  waiting for transfers between devices: 42.1 us -> 37.7 us
    ppermute x6, waiting for transfers between devices: 12.8 us -> 8.88 us  [across(): return lax.ppermute(v, 'rep', [(0, 1), (1, 0)])]
    pallas_call x2, Pallas kernels: 51.1 us -> 47.2 us  [mlp_half(): pl.pallas_call(partial(mlp_half_kernel, part, first, split, len(pieces)),...]
    unnamed x221 -> x226, local copies, waits for them, and re-layouts: 4.71 us -> 6.21 us
  transfers between devices with their start and end apart: 52 -> 52, of which waited for: 21 -> 16; matrix products, arithmetic and copies ran while one was open for 6% -> 7% of each run, Pallas kernels for 48% -> 48%
where the time goes in v5:
time: 303 us; the launch traced here: 299 us
  Pallas kernels  169 us (56%)
  starting transfers between devices  52 us (17%)
  waiting for transfers between devices  37.7 us (12%)
  other arithmetic  15.7 us (5%)
  between operations  15.6 us (5%)
  local copies, waits for them, and re-layouts  9.45 us (3%)
    pallas_call x2, Pallas kernels, mlp_half(): pl.pallas_call(partial(mlp_half_kernel, part, first, split, len(pieces)),...  47.2 us
    ppermute x42, starting transfers between devices, swap(): return lax.ppermute(v, 'fsdp', [(i, i ^ mask) for i in range(SHARDS)])  39.6 us
    ppermute x42, waiting for transfers between devices, swap(): return lax.ppermute(v, 'fsdp', [(i, i ^ mask) for i in range(SHARDS)])  28.1 us
    pallas_call x2, Pallas kernels, heads_back(): pl.pallas_call(heads_back_kernel, grid=(steps,), in_specs=[SMEM] + [head]...  23.3 us
    pallas_call x2, Pallas kernels, attend(): pl.pallas_call(attend_kernel, grid=(heads // each,), in_specs=[pl.BlockSp...  16.9 us
    pallas_call x2, Pallas kernels, qkv_grad(): pl.pallas_call(qkv_grad_kernel, in_specs=[SMEM] + [VMEM] * (6 + len(more)...  14.8 us
    pallas_call x2, Pallas kernels, project_group(): pl.pallas_call(group_kernel, grid=(slots // blk,), in_specs=[SMEM, tall(w...  13.9 us
    pallas_call x1, Pallas kernels, out_back_fast(): pl.pallas_call(partial(out_back_fast_kernel, start), grid=(slots // blk,)...  12.4 us
  transfers between devices with their start and end apart: 52, of which 16 were waited for; matrix products, arithmetic and copies ran while one was open for 7% of the time, Pallas kernels for 48%

profile of v5, /device:TPU:0, one launch (start us, length us, event | category | flops | bytes accessed | tf_op | source)
XLA Modules:
  0.0 299.0 jit_solution(13473755532418714625)
XLA Ops:
  12.6 4.0 %collective-permute-start.5 = (bf16[160,384]{1,0:T(8,128)(2,1)}, bf16[160,384]{1,0:T(8,128)(2,1)S(1)}, u32[]{:S(2)}, u32[]{:S(2)}) collective-permute-start(bf16[160,384]{1,0:T(8,128)(2,1)} %get-tuple-element.107.rest_0_.rest_3_), channel_id=1, source_target_pairs={{0,8},{1,9},{2,10},{3,11},{4,12},{5,13},{6,14},{7,15},{8,0},{9,1},... | collective-permute-start | bytes 368648 | tf_op jit(solution)/shard_map/ppermute | solution.py:564
  19.8 3.2 %collective-permute-done.5.rest_8_.rest_11_ = bf16[160,384]{1,0:T(8,128)(2,1)S(1)} collective-permute-done((bf16[160,384]{1,0:T(8,128)(2,1)}, bf16[160,384]{1,0:T(8,128)(2,1)S(1)}, u32[]{:S(2)}, u32[]{:S(2)}) %collective-permute-start.5) | collective-permute-done | bytes 122912 | tf_op jit(solution)/shard_map/ppermute | solution.py:564
  27.2 5.2 %collective-permute-done.11.rest_12_.rest_15_ = bf16[160,384]{1,0:T(8,128)(2,1)S(1)} collective-permute-done((bf16[160,384]{1,0:T(8,128)(2,1)S(1)}, bf16[160,384]{1,0:T(8,128)(2,1)S(1)}, u32[]{:S(2)}, u32[]{:S(2)}) %collective-permute-start.11) | collective-permute-done | bytes 122912 | tf_op jit(solution)/shard_map/ppermute | solution.py:564
  39.7 2.8 collective-permute-start.18
  44.7 9.8 %prepare.1 = (bf16[768,1024]{1,0:T(8,128)(2,1)}, f32[384,1024]{1,0:T(8,128)}, f32[384,1024]{1,0:T(8,128)}, f32[8,768]{1,0:T(8,128)}, f32[2,1536]{1,0:T(2,128)}, ...) custom-call(s32[17]{0:T(128)} %pad_add_fusion.order_ref, bf16[1024,768]{1,0:T(8,128)(2,1)} %bitcast.52, s32[1,1024]{1,0:T(1,128)} %cols_ref.1, ...), custom_call_target="tpu_custom_call" | custom-call | flops 8800000000 | bytes 65536 | tf_op jit(solution)/shard_map/prepare/pallas_call | solution.py:812
  58.8 6.9 %qkv_group.2 = (bf16[384,1024]{1,0:T(8,128)(2,1)}, bf16[384,1024]{1,0:T(8,128)(2,1)}, bf16[384,1024]{1,0:T(8,128)(2,1)}) custom-call(s32[17]{0:T(128)} %pad_add_fusion.order_ref, bf16[768,1024]{1,0:T(8,128)(2,1)} %get-tuple-element.111.at_ref, f32[2304,1]{1,0:T(8,128)} %get-tuple-element.112.bq_ref.bk_ref.bv_ref, ...), custom_call_target="tpu_custom_call" | custom-call | flops 7699999744 | bytes 65536 | tf_op jit(solution)/shard_map/qkv_group/pallas_call | solution.py:906
  65.9 5.9 %collective-permute-done.26.rest_12_.rest_15_.rest_14_ = bf16[240,384]{1,0:T(8,128)(2,1)S(1)} collective-permute-done((bf16[240,384]{1,0:T(8,128)(2,1)S(1)}, bf16[240,384]{1,0:T(8,128)(2,1)S(1)}, u32[]{:S(2)}, u32[]{:S(2)}) %collective-permute-start.26) | collective-permute-done | bytes 184352 | tf_op jit(solution)/shard_map/ppermute | solution.py:564
  73.9 8.4 %attend.2 = (bf16[384,1024]{1,0:T(8,128)(2,1)}, f32[6,1,1024]{2,1,0:T(1,128)}) custom-call(s32[3]{0:T(128)} %bitcast.57, bf16[384,1024]{1,0:T(8,128)(2,1)} %get-tuple-element.115.q_ref, bf16[384,1024]{1,0:T(8,128)(2,1)} %get-tuple-element.116.k_ref, bf16[384,1024]{1,0:T(8,128)(2,1)} %get-tuple-element.117.v_ref), custom_call_target="tpu_custom_call" | custom-call | flops 8800000000 | bytes 65536 | tf_op jit(solution)/shard_map/attend/pallas_call | solution.py:180
  86.2 7.0 %qkv_group.3 = (bf16[384,1024]{1,0:T(8,128)(2,1)}, bf16[384,1024]{1,0:T(8,128)(2,1)}, bf16[384,1024]{1,0:T(8,128)(2,1)}) custom-call(s32[17]{0:T(128)} %pad_add_fusion.order_ref, bf16[768,1024]{1,0:T(8,128)(2,1)} %get-tuple-element.111.at_ref, f32[2304,1]{1,0:T(8,128)} %get-tuple-element.112.bq_ref.bk_ref.bv_ref, ...), custom_call_target="tpu_custom_call" | custom-call | flops 7699999744 | bytes 65536 | tf_op jit(solution)/shard_map/qkv_group/pallas_call | solution.py:906
  93.2 8.5 %attend.3 = (bf16[384,1024]{1,0:T(8,128)(2,1)}, f32[6,1,1024]{2,1,0:T(1,128)}) custom-call(s32[3]{0:T(128)} %bitcast.58, bf16[384,1024]{1,0:T(8,128)(2,1)} %get-tuple-element.128.q_ref, bf16[384,1024]{1,0:T(8,128)(2,1)} %get-tuple-element.129.k_ref, bf16[384,1024]{1,0:T(8,128)(2,1)} %get-tuple-element.130.v_ref), custom_call_target="tpu_custom_call" | custom-call | flops 8800000000 | bytes 65536 | tf_op jit(solution)/shard_map/attend/pallas_call | solution.py:180
  101.6 8.6 %out_project.1 = (f32[1024,768]{1,0:T(8,128)}, bf16[1024,768]{1,0:T(8,128)(2,1)}, bf16[768,1024]{1,0:T(8,128)(2,1)}) custom-call(s32[17]{0:T(128)} %pad_add_fusion.order_ref, f32[8,768]{1,0:T(8,128)} %get-tuple-element.110.vec_ref, bf16[384,1024]{1,0:T(8,128)(2,1)} %get-tuple-element.118.rest_0_.o_ref, bf16[384,1024]{1,0:T(8,128)(2,1)} %get-tuple-element.131.rest_1_.o_ref, ...), custom_call_target="tpu_custom_call" | custom-call | flops 8800000000 | bytes 65536 | tf_op jit(solution)/shard_map/out_project/pallas_call | solution.py:960
  110.2 23.5 %mlp_half.2 = (bf16[1024,768]{1,0:T(8,128)(2,1)}, bf16[1024,768]{1,0:T(8,128)(2,1)}, bf16[16,192,768]{2,1,0:T(8,128)(2,1)}, f32[1,1536]{1,0:T(1,128)}) custom-call(s32[17]{0:T(128)} %pad_add_fusion.order_ref, bf16[1024,768]{1,0:T(8,128)(2,1)} %get-tuple-element.132.c_in, bf16[768,1024]{1,0:T(8,128)(2,1)} %get-tuple-element.133.ct_in, ...), custom_call_target="tpu_custom_call" | custom-call | flops 25300000768 | bytes 65536 | tf_op jit(solution)/shard_map/mlp_half/pallas_call | solution.py:1084
  133.8 23.7 %mlp_half.3 = (bf16[1024,768]{1,0:T(8,128)(2,1)}, bf16[1024,768]{1,0:T(8,128)(2,1)}, bf16[2,8,96,768]{3,2,1,0:T(8,128)(2,1)}, bf16[2,8,96,768]{3,2,1,0:T(8,128)(2,1)}, f32[1,1536]{1,0:T(1,128)}) custom-call(s32[17]{0:T(128)} %pad_add_fusion.order_ref, bf16[1024,768]{1,0:T(8,128)(2,1)} %get-tuple-element.132.c_in, ...), custom_call_target="tpu_custom_call" | custom-call | flops 25300000768 | bytes 65536 | tf_op jit(solution)/shard_map/mlp_half/pallas_call | solution.py:1084
  157.8 12.4 %out_back.1 = (bf16[1024,768]{1,0:T(8,128)(2,1)}, bf16[768,1024]{1,0:T(8,128)(2,1)}, bf16[8,96,384]{2,1,0:T(8,128)(2,1)}, bf16[8,96,384]{2,1,0:T(8,128)(2,1)}, f32[8,768]{1,0:T(8,128)}) custom-call(s32[17]{0:T(128)} %pad_add_fusion.order_ref, bf16[1024,768]{1,0:T(8,128)(2,1)} %get-tuple-element.141.dc_ref, f32[1024,768]{1,0:T(8,128)} %get-tuple-element.135.rest_0_.h_ref, ...), custom_call_target="tpu_custom_call" | custom-call | flops 13200000000 | bytes 65536 | tf_op jit(solution)/shard_map/out_back/pallas_call | solution.py:1165
  174.7 11.7 %heads_back.2 = (bf16[384,1024]{1,0:T(8,128)(2,1)S(1)}, bf16[384,1024]{1,0:T(8,128)(2,1)S(1)}, bf16[384,1024]{1,0:T(8,128)(2,1)S(1)}, bf16[192,1024]{1,0:T(8,128)(2,1)S(1)}) custom-call(s32[3]{0:T(128)S(1)} %bitcast.59, bf16[384,1024]{1,0:T(8,128)(2,1)S(1)} %copy-done.69, bf16[384,1024]{1,0:T(8,128)(2,1)S(1)} %copy-done.70, ...), custom_call_target="tpu_custom_call" | custom-call | flops 14300000256 | bytes 65536 | tf_op jit(solution)/shard_map/heads_back/pallas_call | solution.py:1260
  186.5 8.4 %qkv_grad.2 = (bf16[8,240,384]{2,1,0:T(8,128)(2,1)S(1)}, bf16[8,240,384]{2,1,0:T(8,128)(2,1)S(1)}, f32[16,1152]{1,0:T(8,128)S(1)}, f32[16,192]{1,0:T(8,128)S(1)}) custom-call(s32[17]{0:T(128)S(1)} %copy-done.65, bf16[768,1024]{1,0:T(8,128)(2,1)S(1)} %copy-done.66, bf16[16,1024]{1,0:T(8,128)(2,1)S(1)} %copy-done.83, ...), custom_call_target="tpu_custom_call" | custom-call | flops 6600000000 | bytes 65536 | tf_op jit(solution)/shard_map/qkv_grad/pallas_call | solution.py:1303
  195.3 4.6 %collective-permute-done.31 = bf16[8,96,768]{2,1,0:T(8,128)(2,1)S(1)} collective-permute-done((bf16[8,96,768]{2,1,0:T(8,128)(2,1)S(1)}, bf16[8,96,768]{2,1,0:T(8,128)(2,1)S(1)}, u32[]{:S(2)}, u32[]{:S(2)}) %collective-permute-start.31) | collective-permute-done | bytes 1179680 | tf_op jit(solution)/shard_map/ppermute | solution.py:640
  203.4 11.7 %heads_back.3 = (bf16[384,1024]{1,0:T(8,128)(2,1)S(1)}, bf16[384,1024]{1,0:T(8,128)(2,1)S(1)}, bf16[384,1024]{1,0:T(8,128)(2,1)S(1)}, bf16[192,1024]{1,0:T(8,128)(2,1)S(1)}) custom-call(s32[3]{0:T(128)S(1)} %bitcast.60, bf16[384,1024]{1,0:T(8,128)(2,1)S(1)} %copy-done.72, bf16[384,1024]{1,0:T(8,128)(2,1)S(1)} %copy-done.73, ...), custom_call_target="tpu_custom_call" | custom-call | flops 14300000256 | bytes 65536 | tf_op jit(solution)/shard_map/heads_back/pallas_call | solution.py:1260
  219.3 6.4 %qkv_grad.3 = (bf16[8,144,384]{2,1,0:T(8,128)(2,1)S(1)}, bf16[8,144,384]{2,1,0:T(8,128)(2,1)S(1)}, f32[16,1152]{1,0:T(8,128)S(1)}, f32[16,192]{1,0:T(8,128)S(1)}) custom-call(s32[17]{0:T(128)S(1)} %copy-done.65, bf16[768,1024]{1,0:T(8,128)(2,1)S(1)} %copy-done.66, bf16[16,1024]{1,0:T(8,128)(2,1)S(1)} %copy-done.83, ...), custom_call_target="tpu_custom_call" | custom-call | flops 6600000000 | bytes 65536 | tf_op jit(solution)/shard_map/qkv_grad/pallas_call | solution.py:1303
  225.9 6.4 %input_part.1.da_ref = f32[768,1024]{1,0:T(8,128)S(1)} custom-call(s32[17]{0:T(128)S(1)} %copy-done.65, bf16[384,1024]{1,0:T(8,128)(2,1)S(1)} %get-tuple-element.167.dq_ref.rest_0_, bf16[384,1024]{1,0:T(8,128)(2,1)S(1)} %get-tuple-element.168.dk_ref.rest_1_, bf16[384,1024]{1,0:T(8,128)(2,1)S(1)} %get-tuple-element.169.dv_ref.rest_2_, ...), custom_call_target="tpu_custom_call" | custom-call | flops 6600000000 | bytes 65536 | tf_op jit(solution)/shard_map/input_part/pallas_call | solution.py:1353
  238.2 4.1 %collective-permute-start.37 = (bf16[4,144,384]{2,1,0:T(8,128)(2,1)S(1)}, bf16[4,144,384]{2,1,0:T(8,128)(2,1)S(1)}, u32[]{:S(2)}, u32[]{:S(2)}) collective-permute-start(bf16[4,144,384]{2,1,0:T(8,128)(2,1)S(1)} %add_convert_fusion.2), channel_id=1, source_target_pairs={{0,2},{1,3},{2,0},{3,1},{4,6},{5,7},{6,4},{7,5},{8,10},{9,11},{10,... | collective-permute-start | bytes 1327112 | tf_op jit(solution)/shard_map/ppermute | solution.py:564
  242.5 9.5 %input_back.1 = (bf16[1024,768]{1,0:T(8,128)(2,1)}, f32[8,768]{1,0:T(8,128)S(1)}) custom-call(s32[17]{0:T(128)S(1)} %copy-done.65, bf16[1024,768]{1,0:T(8,128)(2,1)S(1)} %bitcast.54, bf16[1024,768]{1,0:T(8,128)(2,1)S(1)} %copy-done.75, f32[8,768]{1,0:T(8,128)S(1)} %copy-done.86, f32[768,1024]{1,0:T(8,128)S(1)} %input_part.1.da_ref, ...), custom_call_target="tpu_custom_call" | custom-call | flops 11000000512 | bytes 65536 | tf_op jit(solution)/shard_map/input_back/pallas_call | solution.py:1386
  254.1 4.1 %all-to-all-start = ((f32[16,1,672]{2,1,0:T(1,128)}), f32[16,1,672]{2,1,0:T(1,128)}, u32[]{:S(2)}, u32[]{:S(2)}) async-start(f32[16,1,672]{2,1,0:T(1,128)} %copy.33), calls=%async_computation | async-start | bytes 98304 | tf_op jit(solution)/shard_map/all_to_all | solution.py:1484
  269.9 6.1 %collective-permute-done.41 = bf16[1,144,384]{2,1,0:T(8,128)(2,1)} collective-permute-done((bf16[1,144,384]{2,1,0:T(8,128)(2,1)}, bf16[1,144,384]{2,1,0:T(8,128)(2,1)}, u32[]{:S(2)}, u32[]{:S(2)}) %collective-permute-start.41) | collective-permute-done | bytes 110624 | tf_op jit(solution)/shard_map/ppermute | solution.py:564
  (356 shorter events, 80.5 us)
Async XLA Ops:
  7.3 103.0 %all-gather.5.cloned.1.call-start = ((), (), s32[]{:S(2)}) async-start(), calls=%async_computation.3 | async-start | bytes 5013504 | tf_op jit(solution)/shard_map/all_gather | solution.py:1420
  9.4 124.4 %all-gather.7.cloned.1.call-start = ((), (), s32[]{:S(2)}) async-start(), calls=%async_computation.4 | async-start | bytes 5013504 | tf_op jit(solution)/shard_map/all_gather | solution.py:1421
  10.1 266.3 %reduce-scatter.2.cloned.1.call-start = ((), (), s32[]{:S(2)}) async-start(), calls=%async_computation.2 | async-start | bytes 5013504 | tf_op jit(solution)/shard_map/reduce_scatter | solution.py:1445
  37.9 45.1 %collective-permute-start.15 = (bf16[240,384]{1,0:T(8,128)(2,1)}, bf16[240,384]{1,0:T(8,128)(2,1)S(1)}, u32[]{:S(2)}, u32[]{:S(2)}) collective-permute-start(bf16[240,384]{1,0:T(8,128)(2,1)} %get-tuple-element.120.rest_0_.rest_3_.rest_2_), channel_id=1, source_target_pairs={{0,1},{1,0},{2,3},{3,2},{4,5},{5,4},{6,7},{7,6},{8,9},{9,8},{10,11... | collective-permute-start | bytes 552968 | tf_op jit(solution)/shard_map/ppermute | solution.py:564
  38.4 18.7 %collective-permute-start.22 = (bf16[240,384]{1,0:T(8,128)(2,1)}, bf16[240,384]{1,0:T(8,128)(2,1)S(1)}, u32[]{:S(2)}, u32[]{:S(2)}) collective-permute-start(bf16[240,384]{1,0:T(8,128)(2,1)} %get-tuple-element.120.rest_0_.rest_3_.rest_2_), channel_id=1, source_target_pairs={{0,8},{1,9},{2,10},{3,11},{4,12},{5,13},{6,14},{7,15},{8,0},{9,1},... | collective-permute-start | bytes 552968 | tf_op jit(solution)/shard_map/ppermute | solution.py:564
  39.7 26.0 %collective-permute-start.18 = (bf16[240,384]{1,0:T(8,128)(2,1)}, bf16[240,384]{1,0:T(8,128)(2,1)S(1)}, u32[]{:S(2)}, u32[]{:S(2)}) collective-permute-start(bf16[240,384]{1,0:T(8,128)(2,1)} %get-tuple-element.120.rest_0_.rest_3_.rest_2_), channel_id=1, source_target_pairs={{0,4},{1,5},{2,6},{3,7},{4,0},{5,1},{6,2},{7,3},{8,12},{9,13},{10,... | collective-permute-start | bytes 552968 | tf_op jit(solution)/shard_map/ppermute | solution.py:564
  42.6 29.2 %collective-permute-start.16 = (bf16[240,384]{1,0:T(8,128)(2,1)}, bf16[240,384]{1,0:T(8,128)(2,1)S(1)}, u32[]{:S(2)}, u32[]{:S(2)}) collective-permute-start(bf16[240,384]{1,0:T(8,128)(2,1)} %get-tuple-element.120.rest_0_.rest_3_.rest_2_), channel_id=1, source_target_pairs={{0,2},{1,3},{2,0},{3,1},{4,6},{5,7},{6,4},{7,5},{8,10},{9,11},{10,... | collective-permute-start | bytes 552968 | tf_op jit(solution)/shard_map/ppermute | solution.py:564
  57.1 14.6 %collective-permute-start.26 = (bf16[240,384]{1,0:T(8,128)(2,1)S(1)}, bf16[240,384]{1,0:T(8,128)(2,1)S(1)}, u32[]{:S(2)}, u32[]{:S(2)}) collective-permute-start(bf16[240,384]{1,0:T(8,128)(2,1)S(1)} %collective-permute-done.22.rest_8_.rest_11_.rest_10_), channel_id=1, source_target_pairs={{0,4},{1,5},{2,6},{3,7},{4,0},{5,1},{6,2},{7,3},{8,12},{9,13},{10,... | collective-permute-start | bytes 552968 | tf_op jit(solution)/shard_map/ppermute | solution.py:564
  57.1 16.4 %collective-permute-start.24 = (bf16[240,384]{1,0:T(8,128)(2,1)S(1)}, bf16[240,384]{1,0:T(8,128)(2,1)S(1)}, u32[]{:S(2)}, u32[]{:S(2)}) collective-permute-start(bf16[240,384]{1,0:T(8,128)(2,1)S(1)} %collective-permute-done.22.rest_8_.rest_11_.rest_10_), channel_id=1, source_target_pairs={{0,2},{1,3},{2,0},{3,1},{4,6},{5,7},{6,4},{7,5},{8,10},{9,11},{10,... | collective-permute-start | bytes 552968 | tf_op jit(solution)/shard_map/ppermute | solution.py:564
  65.8 17.5 %collective-permute-start.23 = (bf16[240,384]{1,0:T(8,128)(2,1)S(1)}, bf16[240,384]{1,0:T(8,128)(2,1)S(1)}, u32[]{:S(2)}, u32[]{:S(2)}) collective-permute-start(bf16[240,384]{1,0:T(8,128)(2,1)S(1)} %collective-permute-done.22.rest_8_.rest_11_.rest_10_), channel_id=1, source_target_pairs={{0,1},{1,0},{2,3},{3,2},{4,5},{5,4},{6,7},{7,6},{8,9},{9,8},{10,11... | collective-permute-start | bytes 552968 | tf_op jit(solution)/shard_map/ppermute | solution.py:564
  157.5 12.6 %collective-permute-start.30 = (bf16[2,8,96,768]{3,2,1,0:T(8,128)(2,1)}, bf16[2,8,96,768]{3,2,1,0:T(8,128)(2,1)S(1)}, u32[]{:S(2)}, u32[]{:S(2)}) collective-permute-start(bf16[2,8,96,768]{3,2,1,0:T(8,128)(2,1)} %get-tuple-element.145), channel_id=1, source_target_pairs={{0,1},{1,0},{2,3},{3,2},{4,5},{5,4},{6,7},{7,6},{8,9},{9,8},{10,11... | collective-permute-start | bytes 7077896 | tf_op jit(solution)/shard_map/ppermute | solution.py:564
  171.6 28.3 %collective-permute-start.31 = (bf16[8,96,768]{2,1,0:T(8,128)(2,1)S(1)}, bf16[8,96,768]{2,1,0:T(8,128)(2,1)S(1)}, u32[]{:S(2)}, u32[]{:S(2)}) collective-permute-start(bf16[8,96,768]{2,1,0:T(8,128)(2,1)S(1)} %fusion), channel_id=1, source_target_pairs={{0,16},{16,0},{1,17},{17,1},{2,18},{18,2},{3,19},{19,3},{4,20},{20... | collective-permute-start | bytes 3538952 | tf_op jit(solution)/shard_map/ppermute | solution.py:640
  194.9 20.2 %collective-permute-start.33 = (bf16[8,240,384]{2,1,0:T(8,128)(2,1)S(1)}, bf16[8,240,384]{2,1,0:T(8,128)(2,1)S(1)}, u32[]{:S(2)}, u32[]{:S(2)}) collective-permute-start(bf16[8,240,384]{2,1,0:T(8,128)(2,1)S(1)} %get-tuple-element.160), channel_id=1, source_target_pairs={{0,1},{1,0},{2,3},{3,2},{4,5},{5,4},{6,7},{7,6},{8,9},{9,8},{10,11... | collective-permute-start | bytes 4423688 | tf_op jit(solution)/shard_map/ppermute | solution.py:564
  201.8 15.0 %collective-permute-start.32 = (bf16[4,96,768]{2,1,0:T(8,128)(2,1)S(1)}, bf16[4,96,768]{2,1,0:T(8,128)(2,1)S(1)}, u32[]{:S(2)}, u32[]{:S(2)}) collective-permute-start(bf16[4,96,768]{2,1,0:T(8,128)(2,1)S(1)} %fusion.1), channel_id=1, source_target_pairs={{0,2},{1,3},{2,0},{3,1},{4,6},{5,7},{6,4},{7,5},{8,10},{9,11},{10,... | collective-permute-start | bytes 1769480 | tf_op jit(solution)/shard_map/ppermute | solution.py:564
  215.3 20.9 %collective-permute-start.35 = (bf16[4,240,384]{2,1,0:T(8,128)(2,1)S(1)}, bf16[4,240,384]{2,1,0:T(8,128)(2,1)S(1)}, u32[]{:S(2)}, u32[]{:S(2)}) collective-permute-start(bf16[4,240,384]{2,1,0:T(8,128)(2,1)S(1)} %add_convert_fusion.1), channel_id=1, source_target_pairs={{0,2},{1,3},{2,0},{3,1},{4,6},{5,7},{6,4},{7,5},{8,10},{9,11},{10,... | collective-permute-start | bytes 2211848 | tf_op jit(solution)/shard_map/ppermute | solution.py:564
  218.2 14.2 %collective-permute-start.36 = (bf16[2,96,768]{2,1,0:T(8,128)(2,1)S(1)}, bf16[2,96,768]{2,1,0:T(8,128)(2,1)S(1)}, u32[]{:S(2)}, u32[]{:S(2)}) collective-permute-start(bf16[2,96,768]{2,1,0:T(8,128)(2,1)S(1)} %fusion.3), channel_id=1, source_target_pairs={{0,4},{1,5},{2,6},{3,7},{4,0},{5,1},{6,2},{7,3},{8,12},{9,13},{10,... | collective-permute-start | bytes 884744 | tf_op jit(solution)/shard_map/ppermute | solution.py:564
  225.7 12.4 %collective-permute-start.34 = (bf16[8,144,384]{2,1,0:T(8,128)(2,1)S(1)}, bf16[8,144,384]{2,1,0:T(8,128)(2,1)S(1)}, u32[]{:S(2)}, u32[]{:S(2)}) collective-permute-start(bf16[8,144,384]{2,1,0:T(8,128)(2,1)S(1)} %get-tuple-element.170), channel_id=1, source_target_pairs={{0,1},{1,0},{2,3},{3,2},{4,5},{5,4},{6,7},{7,6},{8,9},{9,8},{10,11... | collective-permute-start | bytes 2654216 | tf_op jit(solution)/shard_map/ppermute | solution.py:564
  233.9 18.2 %collective-permute-start.39 = (bf16[1,96,768]{2,1,0:T(8,128)(2,1)S(1)}, bf16[1,96,768]{2,1,0:T(8,128)(2,1)S(1)}, u32[]{:S(2)}, u32[]{:S(2)}) collective-permute-start(bf16[1,96,768]{2,1,0:T(8,128)(2,1)S(1)} %fusion.10), channel_id=1, source_target_pairs={{0,8},{1,9},{2,10},{3,11},{4,12},{5,13},{6,14},{7,15},{8,0},{9,1},... | collective-permute-start | bytes 442376 | tf_op jit(solution)/shard_map/ppermute | solution.py:564
  236.4 15.7 %collective-permute-start.38 = (bf16[2,240,384]{2,1,0:T(8,128)(2,1)S(1)}, bf16[2,240,384]{2,1,0:T(8,128)(2,1)S(1)}, u32[]{:S(2)}, u32[]{:S(2)}) collective-permute-start(bf16[2,240,384]{2,1,0:T(8,128)(2,1)S(1)} %add_convert_fusion.3), channel_id=1, source_target_pairs={{0,4},{1,5},{2,6},{3,7},{4,0},{5,1},{6,2},{7,3},{8,12},{9,13},{10,... | collective-permute-start | bytes 1105928 | tf_op jit(solution)/shard_map/ppermute | solution.py:564
  238.2 13.9 %collective-permute-start.37 = (bf16[4,144,384]{2,1,0:T(8,128)(2,1)S(1)}, bf16[4,144,384]{2,1,0:T(8,128)(2,1)S(1)}, u32[]{:S(2)}, u32[]{:S(2)}) collective-permute-start(bf16[4,144,384]{2,1,0:T(8,128)(2,1)S(1)} %add_convert_fusion.2), channel_id=1, source_target_pairs={{0,2},{1,3},{2,0},{3,1},{4,6},{5,7},{6,4},{7,5},{8,10},{9,11},{10,... | collective-permute-start | bytes 1327112 | tf_op jit(solution)/shard_map/ppermute | solution.py:564
  254.1 13.6 %all-to-all-start = ((f32[16,1,672]{2,1,0:T(1,128)}), f32[16,1,672]{2,1,0:T(1,128)}, u32[]{:S(2)}, u32[]{:S(2)}) async-start(f32[16,1,672]{2,1,0:T(1,128)} %copy.33), calls=%async_computation | async-start | bytes 98304 | tf_op jit(solution)/shard_map/all_to_all | solution.py:1484
  259.6 28.2 %collective-permute-start.45 = (bf16[96,768]{1,0:T(8,128)(2,1)S(1)}, bf16[96,768]{1,0:T(8,128)(2,1)S(1)}, u32[]{:S(2)}, u32[]{:S(2)}) collective-permute-start(bf16[96,768]{1,0:T(8,128)(2,1)S(1)} %fusion.12.d_ref), channel_id=1, source_target_pairs={{0,16},{16,0},{1,17},{17,1},{2,18},{18,2},{3,19},{19,3},{4,20},{20... | collective-permute-start | bytes 442376 | tf_op jit(solution)/shard_map/ppermute | solution.py:640
  262.9 13.0 %collective-permute-start.41 = (bf16[1,144,384]{2,1,0:T(8,128)(2,1)}, bf16[1,144,384]{2,1,0:T(8,128)(2,1)}, u32[]{:S(2)}, u32[]{:S(2)}) collective-permute-start(bf16[1,144,384]{2,1,0:T(8,128)(2,1)} %add_convert_fusion.8), channel_id=1, source_target_pairs={{0,8},{1,9},{2,10},{3,11},{4,12},{5,13},{6,14},{7,15},{8,0},{9,1},... | collective-permute-start | bytes 331784 | tf_op jit(solution)/shard_map/ppermute | solution.py:564
  267.4 14.0 %collective-permute-start.46 = (bf16[1,240,384]{2,1,0:T(8,128)(2,1)}, bf16[1,240,384]{2,1,0:T(8,128)(2,1)}, u32[]{:S(2)}, u32[]{:S(2)}) collective-permute-start(bf16[1,240,384]{2,1,0:T(8,128)(2,1)} %add_convert_fusion.6), channel_id=1, source_target_pairs={{0,8},{1,9},{2,10},{3,11},{4,12},{5,13},{6,14},{7,15},{8,0},{9,1},... | collective-permute-start | bytes 552968 | tf_op jit(solution)/shard_map/ppermute | solution.py:564
  (138 other events, 1094.1 us)
Sparse Core Ops, SparseCore 0:
  11.0 64.0 all-gather.4
  77.9 53.5 all-gather.6
  157.9 79.8 reduce-scatter.1

commit v6 on v5

--- a/solution.py
+++ b/solution.py
@@ -848,14 +848,12 @@
         sums1_ref[0:1, :], sums1_ref[1:2, :], b_qkv, g_freq, sums2_ref[2:3, :], sums2_ref[0:1, :], sums2_ref[1:2, :],
         b1a_ref[...], b1b_ref[...], sums2_ref[3:4, :],
     )
-    lines = []
     for j in range(SHARDS):
         runs = []
         for v in vectors:
             n = v.shape[1] // SHARDS
             runs.append(v[:, j * n : (j + 1) * n])
-        lines.append(jnp.concatenate(runs, axis=1))
-    out_ref[...] = jnp.concatenate(lines, axis=0)
+        out_ref[j] = jnp.concatenate(runs, axis=1)
 
 
 def pack(size, *sums):
@@ -863,7 +861,7 @@
         pack_kernel,
         in_specs=[VMEM] * len(sums),
         out_specs=VMEM,
-        out_shape=jax.ShapeDtypeStruct((SHARDS, size), F32),
+        out_shape=jax.ShapeDtypeStruct((SHARDS, 1, size), F32),
         compiler_params=params(4),
         cost_estimate=cost(3),
         name="pack",
@@ -945,7 +943,7 @@
     width = x_ref.shape[1]
     o = jnp.concatenate([r[...].T for r in o_refs], axis=1)
     h = x_ref[...].astype(F32) + (nn(o, w_scr[...].reshape(width, width)) + vec_ref[0:1, :])
-    h_ref[...] = h
+    h_ref[...] = h.astype(BF)
     xhat, _ = norm_parts(h)
     c = (xhat * vec_ref[2:3, :] + vec_ref[3:4, :]).astype(BF)
     c_ref[...] = c
@@ -963,7 +961,7 @@
         in_specs=[SMEM, VMEM] + [pl.BlockSpec((width // GROUPS, blk), lambda i: (0, i))] * GROUPS + [rows] + [HBM] * SHARDS,
         out_specs=[rows, rows, cols],
         out_shape=[
-            jax.ShapeDtypeStruct((slots, width), F32),
+            jax.ShapeDtypeStruct((slots, width), BF),
             jax.ShapeDtypeStruct((slots, width), BF),
             jax.ShapeDtypeStruct((width, slots), BF),
         ],
@@ -996,7 +994,7 @@
         for j in range(steps)
     ]
     loads.insert(1, fetch(refs, places, [(slice(steps * rows1, steps * rows1 + rows2), lambda d: w2_scr.at[d])], sem.at[steps]))
-    sums = list(zip(acc_in, (y_acc,) if first else (y_out, dc_out)))
+    sums = list(zip(acc_in, (y_out, dc_out)))
     rows_in = [(c_in, c_ref), (dy_in, dy_ref), (ct_in, ct_ref)]
     whole = [pltpu.make_async_copy(src, dst, load_sem.at[i]) for i, (src, dst) in enumerate(rows_in + sums)]
     (c_load, dy_load, ct_load), sums = whole[:3], whole[3:]
@@ -1022,7 +1020,7 @@
                 if j == 0:
                     wait_all(loads[1] + [dy_load] + sums)
                 w2 = w2_scr[j * per : (j + 1) * per].reshape(blk, width)
-            before = y_acc if first or j else y_out
+            before = y_acc if j else y_out
             y = before[rows, :].astype(F32) + nn(hb, w2)
             if first and j == 0:
                 y = y + vec_ref[4:5, :]
@@ -1128,7 +1126,7 @@
         wait_all(copies)
 
     dy = dy_ref[...].astype(F32)
-    part, dgain, dshift = norm_back(dc_ref[...].astype(F32), h_ref[...], vec_ref[2:3, :])
+    part, dgain, dshift = norm_back(dc_ref[...].astype(F32), h_ref[...].astype(F32), vec_ref[2:3, :])
     dh = dy + part
     dhb = dh.astype(BF)
     dh_ref[...] = dhb
@@ -1149,7 +1147,7 @@
             for n, p in enumerate(LEAVING):
                 for k in range(2):
                     src = g_scr.at[order_ref[p + b], :, pl.ds(k * half, half)]
-                    dst = out.at[n, pl.ds(k * each, each)]
+                    dst = out.at[n, pl.ds((3 + k) * each, each)]
                     copies.append(pltpu.make_async_copy(src, dst, sem.at[len(copies)]))
         start_all(copies)
         wait_all(copies)
@@ -1161,7 +1159,7 @@
     rows = pl.BlockSpec((blk, width), lambda i: (i, 0))
     cols = pl.BlockSpec((width, blk), lambda i: (0, i))
     whole = lambda r, k: pl.BlockSpec((r, k), lambda i: (0, 0))
-    block = jax.ShapeDtypeStruct((SHARDS // 2, 2 * width // SHARDS, width // 2), BF)
+    block = jax.ShapeDtypeStruct((SHARDS // 2, 5 * width // SHARDS, width // 2), BF)
     return pl.pallas_call(
         partial(out_back_fast_kernel, start),
         grid=(slots // blk,),
@@ -1271,15 +1269,9 @@
 
 
 def qkv_grad_kernel(order_ref, at_ref, sel_ref, dangle_ref, dq_ref, dk_ref, dv_ref, *rest):
-    more, (near_ref, far_ref, bias_ref, freq_ref, g_scr, sem, more_sem) = rest[:-7], rest[-7:]
+    near_ref, far_ref, bias_ref, freq_ref, g_scr, sem = rest[-6:]
     part = g_scr.shape[1] // 3
     outs = (near_ref, far_ref)
-    extra = [
-        pltpu.make_async_copy(ref.at[n], out.at[n, pl.ds(3 * part, ref.shape[1])], more_sem.at[b, n])
-        for b, (ref, out) in enumerate(zip(more, outs))
-        for n in range(SHARDS // 2)
-    ]
-    start_all(extra)
     at = at_ref[...]
     for i, ref in enumerate((dq_ref, dk_ref, dv_ref)):
         g = nt(at, ref[...]).astype(BF)
@@ -1292,25 +1284,25 @@
             dst = out.at[n, pl.ds(0, 3 * part)]
             copies.append(pltpu.make_async_copy(g_scr.at[order_ref[p + b]], dst, sem.at[len(copies)]))
     start_all(copies)
-    wait_all(copies + extra)
+    wait_all(copies)
 
 
 def qkv_grad(order, at, sel, dangle, dq, dk, dv, *more):
     width, slots = at.shape
     cols = dq.shape[0]
     rows = 3 * width // SHARDS
-    total = rows + (more[0].shape[1] if more else 0)
+    total = more[0].shape[1] if more else rows
     return pl.pallas_call(
         qkv_grad_kernel,
-        in_specs=[SMEM] + [VMEM] * (6 + len(more)),
+        in_specs=[SMEM] + [VMEM] * 6 + [ANY] * len(more),
         out_specs=[ANY, ANY, VMEM, VMEM],
         out_shape=[jax.ShapeDtypeStruct((SHARDS // 2, total, cols), BF)] * 2
         + [jax.ShapeDtypeStruct((sel.shape[0], 3 * cols), F32), jax.ShapeDtypeStruct((sel.shape[0], cols // 2), F32)],
         scratch_shapes=[
             pltpu.VMEM((SHARDS, rows, cols), BF),
             pltpu.SemaphoreType.DMA((SHARDS,)),
-            pltpu.SemaphoreType.DMA((2, SHARDS // 2)),
-        ],
+        ],
+        input_output_aliases={7: 0, 8: 1} if more else {},
         compiler_params=params(16),
         cost_estimate=cost(6),
         name="qkv_grad",
@@ -1474,15 +1466,15 @@
     other_c = across(tie(mlp_c, sent))
     scatter_b.hold(sent)
     scatter_d.hold(sent)
-    block = pack(sum(sizes), tie(sums1, sent), sums2, g_b1a, g_b1b, bias_a, bias_b, freq_a, freq_b)
+    sent = (sent, scatter_b.step())
+    block = pack(sum(sizes), tie(sums1, *sent), sums2, g_b1a, g_b1b, bias_a, bias_b, freq_a, freq_b)
     scatter_a.hold(block)
     sent = scatter_a.step()
-    scatter_b.step()
     mlp_d = scatter_d.finish()
     scatter_b.hold(other_c, sent)
     mine_b = scatter_b.finish()
     mine = jnp.sum(tie(lax.all_to_all(block, "fsdp", 0, 0, tiled=True), sent), axis=0)
-    mine = tie(mine, scatter_a.got[-1])
+    mine = tie(mine[0], scatter_a.got[-1])
     rows1 = width // SHARDS
     s_w1, s_w2 = mlp_join(rows1, order, (mlp_c, other_c) + mlp_d)
     scatter_a.hold(mine)

time: 303 us -> 299 us (0.987)
    unnamed x226 -> x221, local copies, waits for them, and re-layouts: 6.21 us -> 4.83 us
  transfers between devices with their start and end apart: 52 -> 52, of which waited for: 16 -> 18; matrix products, arithmetic and copies ran while one was open for 7% -> 5% of each run, Pallas kernels for 48% -> 48%
where the time goes in v6:
time: 299 us; the launch traced here: 294 us
  Pallas kernels  167 us (56%)
  starting transfers between devices  53.3 us (18%)
  waiting for transfers between devices  36.8 us (12%)
  between operations  15.5 us (5%)
  other arithmetic  13.9 us (5%)
  local copies, waits for them, and re-layouts  7.4 us (2%)
    pallas_call x2, Pallas kernels, mlp_half(): pl.pallas_call(partial(mlp_half_kernel, part, first, split, len(pieces)),...  47.3 us
    ppermute x42, starting transfers between devices, swap(): return lax.ppermute(v, 'fsdp', [(i, i ^ mask) for i in range(SHARDS)])  38.8 us
    ppermute x42, waiting for transfers between devices, swap(): return lax.ppermute(v, 'fsdp', [(i, i ^ mask) for i in range(SHARDS)])  25.3 us
    pallas_call x2, Pallas kernels, heads_back(): pl.pallas_call(heads_back_kernel, grid=(steps,), in_specs=[SMEM] + [head]...  23.7 us
    pallas_call x2, Pallas kernels, attend(): pl.pallas_call(attend_kernel, grid=(heads // each,), in_specs=[pl.BlockSp...  16.9 us
    pallas_call x2, Pallas kernels, project_group(): pl.pallas_call(group_kernel, grid=(slots // blk,), in_specs=[SMEM, tall(w...  13.9 us
    pallas_call x2, Pallas kernels, qkv_grad(): pl.pallas_call(qkv_grad_kernel, in_specs=[SMEM] + [VMEM] * 6 + [ANY] * le...  12.5 us
    pallas_call x1, Pallas kernels, out_back_fast(): pl.pallas_call(partial(out_back_fast_kernel, start), grid=(slots // blk,)...  12.3 us
  transfers between devices with their start and end apart: 52, of which 18 were waited for; matrix products, arithmetic and copies ran while one was open for 5% of the time, Pallas kernels for 48%

profile of v6, /device:TPU:0, one launch (start us, length us, event | category | flops | bytes accessed | tf_op | source)
XLA Modules:
  0.0 294.3 jit_solution(4413307857149425540)
XLA Ops:
  12.6 4.0 %collective-permute-start.5 = (bf16[160,384]{1,0:T(8,128)(2,1)}, bf16[160,384]{1,0:T(8,128)(2,1)S(1)}, u32[]{:S(2)}, u32[]{:S(2)}) collective-permute-start(bf16[160,384]{1,0:T(8,128)(2,1)} %get-tuple-element.107.rest_0_.rest_3_), channel_id=1, source_target_pairs={{0,8},{1,9},{2,10},{3,11},{4,12},{5,13},{6,14},{7,15},{8,0},{9,1},... | collective-permute-start | bytes 368648 | tf_op jit(solution)/shard_map/ppermute | solution.py:564
  19.8 3.2 %collective-permute-done.5.rest_8_.rest_11_ = bf16[160,384]{1,0:T(8,128)(2,1)S(1)} collective-permute-done((bf16[160,384]{1,0:T(8,128)(2,1)}, bf16[160,384]{1,0:T(8,128)(2,1)S(1)}, u32[]{:S(2)}, u32[]{:S(2)}) %collective-permute-start.5) | collective-permute-done | bytes 122912 | tf_op jit(solution)/shard_map/ppermute | solution.py:564
  27.2 5.2 %collective-permute-done.11.rest_12_.rest_15_ = bf16[160,384]{1,0:T(8,128)(2,1)S(1)} collective-permute-done((bf16[160,384]{1,0:T(8,128)(2,1)S(1)}, bf16[160,384]{1,0:T(8,128)(2,1)S(1)}, u32[]{:S(2)}, u32[]{:S(2)}) %collective-permute-start.11) | collective-permute-done | bytes 122912 | tf_op jit(solution)/shard_map/ppermute | solution.py:564
  39.7 2.8 collective-permute-start.18
  44.7 9.8 %prepare.1 = (bf16[768,1024]{1,0:T(8,128)(2,1)}, f32[384,1024]{1,0:T(8,128)}, f32[384,1024]{1,0:T(8,128)}, f32[8,768]{1,0:T(8,128)}, f32[2,1536]{1,0:T(2,128)}, ...) custom-call(s32[17]{0:T(128)} %pad_add_fusion.order_ref, bf16[1024,768]{1,0:T(8,128)(2,1)} %bitcast.47, s32[1,1024]{1,0:T(1,128)} %cols_ref.1, ...), custom_call_target="tpu_custom_call" | custom-call | flops 8800000000 | bytes 65536 | tf_op jit(solution)/shard_map/prepare/pallas_call | solution.py:812
  54.5 2.6 collective-permute-done.22.rest_8_.rest_11_.rest_10_
  58.8 7.0 %qkv_group.2 = (bf16[384,1024]{1,0:T(8,128)(2,1)}, bf16[384,1024]{1,0:T(8,128)(2,1)}, bf16[384,1024]{1,0:T(8,128)(2,1)}) custom-call(s32[17]{0:T(128)} %pad_add_fusion.order_ref, bf16[768,1024]{1,0:T(8,128)(2,1)} %get-tuple-element.111.at_ref, f32[2304,1]{1,0:T(8,128)} %get-tuple-element.112.bq_ref.bk_ref.bv_ref, ...), custom_call_target="tpu_custom_call" | custom-call | flops 7699999744 | bytes 65536 | tf_op jit(solution)/shard_map/qkv_group/pallas_call | solution.py:904
  65.9 5.8 %collective-permute-done.26.rest_12_.rest_15_.rest_14_ = bf16[240,384]{1,0:T(8,128)(2,1)S(1)} collective-permute-done((bf16[240,384]{1,0:T(8,128)(2,1)S(1)}, bf16[240,384]{1,0:T(8,128)(2,1)S(1)}, u32[]{:S(2)}, u32[]{:S(2)}) %collective-permute-start.26) | collective-permute-done | bytes 184352 | tf_op jit(solution)/shard_map/ppermute | solution.py:564
  73.9 8.4 %attend.2 = (bf16[384,1024]{1,0:T(8,128)(2,1)}, f32[6,1,1024]{2,1,0:T(1,128)}) custom-call(s32[3]{0:T(128)} %bitcast.52, bf16[384,1024]{1,0:T(8,128)(2,1)} %get-tuple-element.115.q_ref, bf16[384,1024]{1,0:T(8,128)(2,1)} %get-tuple-element.116.k_ref, bf16[384,1024]{1,0:T(8,128)(2,1)} %get-tuple-element.117.v_ref), custom_call_target="tpu_custom_call" | custom-call | flops 8800000000 | bytes 65536 | tf_op jit(solution)/shard_map/attend/pallas_call | solution.py:180
  86.3 6.9 %qkv_group.3 = (bf16[384,1024]{1,0:T(8,128)(2,1)}, bf16[384,1024]{1,0:T(8,128)(2,1)}, bf16[384,1024]{1,0:T(8,128)(2,1)}) custom-call(s32[17]{0:T(128)} %pad_add_fusion.order_ref, bf16[768,1024]{1,0:T(8,128)(2,1)} %get-tuple-element.111.at_ref, f32[2304,1]{1,0:T(8,128)} %get-tuple-element.112.bq_ref.bk_ref.bv_ref, ...), custom_call_target="tpu_custom_call" | custom-call | flops 7699999744 | bytes 65536 | tf_op jit(solution)/shard_map/qkv_group/pallas_call | solution.py:904
  93.2 8.5 %attend.3 = (bf16[384,1024]{1,0:T(8,128)(2,1)}, f32[6,1,1024]{2,1,0:T(1,128)}) custom-call(s32[3]{0:T(128)} %bitcast.53, bf16[384,1024]{1,0:T(8,128)(2,1)} %get-tuple-element.128.q_ref, bf16[384,1024]{1,0:T(8,128)(2,1)} %get-tuple-element.129.k_ref, bf16[384,1024]{1,0:T(8,128)(2,1)} %get-tuple-element.130.v_ref), custom_call_target="tpu_custom_call" | custom-call | flops 8800000000 | bytes 65536 | tf_op jit(solution)/shard_map/attend/pallas_call | solution.py:180
  101.7 8.4 %out_project.1 = (bf16[1024,768]{1,0:T(8,128)(2,1)}, bf16[1024,768]{1,0:T(8,128)(2,1)}, bf16[768,1024]{1,0:T(8,128)(2,1)}) custom-call(s32[17]{0:T(128)} %pad_add_fusion.order_ref, f32[8,768]{1,0:T(8,128)} %get-tuple-element.110.vec_ref, bf16[384,1024]{1,0:T(8,128)(2,1)} %get-tuple-element.118.rest_0_.o_ref, ...), custom_call_target="tpu_custom_call" | custom-call | flops 8800000000 | bytes 65536 | tf_op jit(solution)/shard_map/out_project/pallas_call | solution.py:958
  110.2 23.6 %mlp_half.2 = (bf16[1024,768]{1,0:T(8,128)(2,1)}, bf16[1024,768]{1,0:T(8,128)(2,1)}, bf16[16,192,768]{2,1,0:T(8,128)(2,1)}, f32[1,1536]{1,0:T(1,128)}) custom-call(s32[17]{0:T(128)} %pad_add_fusion.order_ref, bf16[1024,768]{1,0:T(8,128)(2,1)} %get-tuple-element.132.c_in, bf16[768,1024]{1,0:T(8,128)(2,1)} %get-tuple-element.133.ct_in, ...), custom_call_target="tpu_custom_call" | custom-call | flops 25300000768 | bytes 65536 | tf_op jit(solution)/shard_map/mlp_half/pallas_call | solution.py:1082
  133.8 23.7 %mlp_half.3 = (bf16[1024,768]{1,0:T(8,128)(2,1)}, bf16[1024,768]{1,0:T(8,128)(2,1)}, bf16[2,8,96,768]{3,2,1,0:T(8,128)(2,1)}, bf16[2,8,96,768]{3,2,1,0:T(8,128)(2,1)}, f32[1,1536]{1,0:T(1,128)}) custom-call(s32[17]{0:T(128)} %pad_add_fusion.order_ref, bf16[1024,768]{1,0:T(8,128)(2,1)} %get-tuple-element.132.c_in, ...), custom_call_target="tpu_custom_call" | custom-call | flops 25300000768 | bytes 65536 | tf_op jit(solution)/shard_map/mlp_half/pallas_call | solution.py:1082
  157.9 12.3 %out_back.1 = (bf16[1024,768]{1,0:T(8,128)(2,1)}, bf16[768,1024]{1,0:T(8,128)(2,1)}, bf16[8,240,384]{2,1,0:T(8,128)(2,1)}, bf16[8,240,384]{2,1,0:T(8,128)(2,1)}, f32[8,768]{1,0:T(8,128)}) custom-call(s32[17]{0:T(128)} %pad_add_fusion.order_ref, bf16[1024,768]{1,0:T(8,128)(2,1)} %get-tuple-element.141.dc_ref, ...), custom_call_target="tpu_custom_call" | custom-call | flops 13200000000 | bytes 65536 | tf_op jit(solution)/shard_map/out_back/pallas_call | solution.py:1163
  174.8 12.1 %heads_back.2 = (bf16[384,1024]{1,0:T(8,128)(2,1)S(1)}, bf16[384,1024]{1,0:T(8,128)(2,1)S(1)}, bf16[384,1024]{1,0:T(8,128)(2,1)S(1)}, bf16[192,1024]{1,0:T(8,128)(2,1)S(1)}) custom-call(s32[3]{0:T(128)S(1)} %bitcast.54, bf16[384,1024]{1,0:T(8,128)(2,1)S(1)} %copy-done.71, bf16[384,1024]{1,0:T(8,128)(2,1)S(1)} %copy-done.72, ...), custom_call_target="tpu_custom_call" | custom-call | flops 14300000256 | bytes 65536 | tf_op jit(solution)/shard_map/heads_back/pallas_call | solution.py:1258
  187.0 6.3 %qkv_grad.2 = (bf16[8,240,384]{2,1,0:T(8,128)(2,1)S(1)}, bf16[8,240,384]{2,1,0:T(8,128)(2,1)S(1)}, f32[16,1152]{1,0:T(8,128)S(1)}, f32[16,192]{1,0:T(8,128)S(1)}) custom-call(s32[17]{0:T(128)S(1)} %copy-done.67, bf16[768,1024]{1,0:T(8,128)(2,1)S(1)} %copy-done.68, bf16[16,1024]{1,0:T(8,128)(2,1)S(1)} %copy-done.82, ...), custom_call_target="tpu_custom_call", output_to_operand_aliasing={{0}: (7, {}), {1}: (8, {})} | custom-call | flops 6600000000 | bytes 65536 | tf_op jit(solution)/shard_map/qkv_grad/pallas_call | solution.py:1295
  193.5 6.4 %collective-permute-done.31 = bf16[8,96,768]{2,1,0:T(8,128)(2,1)S(1)} collective-permute-done((bf16[8,96,768]{2,1,0:T(8,128)(2,1)S(1)}, bf16[8,96,768]{2,1,0:T(8,128)(2,1)S(1)}, u32[]{:S(2)}, u32[]{:S(2)}) %collective-permute-start.31) | collective-permute-done | bytes 1179680 | tf_op jit(solution)/shard_map/ppermute | solution.py:640
  203.6 11.7 %heads_back.3 = (bf16[384,1024]{1,0:T(8,128)(2,1)S(1)}, bf16[384,1024]{1,0:T(8,128)(2,1)S(1)}, bf16[384,1024]{1,0:T(8,128)(2,1)S(1)}, bf16[192,1024]{1,0:T(8,128)(2,1)S(1)}) custom-call(s32[3]{0:T(128)S(1)} %bitcast.55, bf16[384,1024]{1,0:T(8,128)(2,1)S(1)} %copy-done.74, bf16[384,1024]{1,0:T(8,128)(2,1)S(1)} %copy-done.75, ...), custom_call_target="tpu_custom_call" | custom-call | flops 14300000256 | bytes 65536 | tf_op jit(solution)/shard_map/heads_back/pallas_call | solution.py:1258
  219.5 6.3 %qkv_grad.3 = (bf16[8,144,384]{2,1,0:T(8,128)(2,1)S(1)}, bf16[8,144,384]{2,1,0:T(8,128)(2,1)S(1)}, f32[16,1152]{1,0:T(8,128)S(1)}, f32[16,192]{1,0:T(8,128)S(1)}) custom-call(s32[17]{0:T(128)S(1)} %copy-done.67, bf16[768,1024]{1,0:T(8,128)(2,1)S(1)} %copy-done.68, bf16[16,1024]{1,0:T(8,128)(2,1)S(1)} %copy-done.82, ...), custom_call_target="tpu_custom_call" | custom-call | flops 6600000000 | bytes 65536 | tf_op jit(solution)/shard_map/qkv_grad/pallas_call | solution.py:1295
  226.0 6.4 %input_part.1.da_ref = f32[768,1024]{1,0:T(8,128)S(1)} custom-call(s32[17]{0:T(128)S(1)} %copy-done.67, bf16[384,1024]{1,0:T(8,128)(2,1)S(1)} %get-tuple-element.167.dq_ref.rest_0_, bf16[384,1024]{1,0:T(8,128)(2,1)S(1)} %get-tuple-element.168.dk_ref.rest_1_, bf16[384,1024]{1,0:T(8,128)(2,1)S(1)} %get-tuple-element.169.dv_ref.rest_2_, ...), custom_call_target="tpu_custom_call" | custom-call | flops 6600000000 | bytes 65536 | tf_op jit(solution)/shard_map/input_part/pallas_call | solution.py:1345
  238.9 3.6 %collective-permute-start.37 = (bf16[4,144,384]{2,1,0:T(8,128)(2,1)S(1)}, bf16[4,144,384]{2,1,0:T(8,128)(2,1)S(1)}, u32[]{:S(2)}, u32[]{:S(2)}) collective-permute-start(bf16[4,144,384]{2,1,0:T(8,128)(2,1)S(1)} %add_convert_fusion.2), channel_id=1, source_target_pairs={{0,2},{1,3},{2,0},{3,1},{4,6},{5,7},{6,4},{7,5},{8,10},{9,11},{10,... | collective-permute-start | bytes 1327112 | tf_op jit(solution)/shard_map/ppermute | solution.py:564
  242.7 9.5 %input_back.1 = (bf16[1024,768]{1,0:T(8,128)(2,1)}, f32[8,768]{1,0:T(8,128)S(1)}) custom-call(s32[17]{0:T(128)S(1)} %copy-done.67, bf16[1024,768]{1,0:T(8,128)(2,1)S(1)} %bitcast.49, bf16[1024,768]{1,0:T(8,128)(2,1)S(1)} %copy-done.77, f32[8,768]{1,0:T(8,128)S(1)} %copy-done.85, f32[768,1024]{1,0:T(8,128)S(1)} %input_part.1.da_ref, ...), custom_call_target="tpu_custom_call" | custom-call | flops 11000000512 | bytes 65536 | tf_op jit(solution)/shard_map/input_back/pallas_call | solution.py:1378
  254.3 5.7 %all-to-all-start = ((f32[16,1,672]{2,1,0:T(1,128)}), f32[16,1,672]{2,1,0:T(1,128)}, u32[]{:S(2)}, u32[]{:S(2)}) async-start(f32[16,1,672]{2,1,0:T(1,128)} %pack.1), calls=%async_computation | async-start | bytes 98304 | tf_op jit(solution)/shard_map/all_to_all | solution.py:1476
  (350 shorter events, 78.5 us)
Async XLA Ops:
  7.3 102.9 %all-gather.5.cloned.1.call-start = ((), (), s32[]{:S(2)}) async-start(), calls=%async_computation.3 | async-start | bytes 5013504 | tf_op jit(solution)/shard_map/all_gather | solution.py:1412
  9.4 124.5 %all-gather.7.cloned.1.call-start = ((), (), s32[]{:S(2)}) async-start(), calls=%async_computation.4 | async-start | bytes 5013504 | tf_op jit(solution)/shard_map/all_gather | solution.py:1413
  10.1 262.3 %reduce-scatter.2.cloned.1.call-start = ((), (), s32[]{:S(2)}) async-start(), calls=%async_computation.2 | async-start | bytes 5013504 | tf_op jit(solution)/shard_map/reduce_scatter | solution.py:1437
  37.9 45.1 %collective-permute-start.15 = (bf16[240,384]{1,0:T(8,128)(2,1)}, bf16[240,384]{1,0:T(8,128)(2,1)S(1)}, u32[]{:S(2)}, u32[]{:S(2)}) collective-permute-start(bf16[240,384]{1,0:T(8,128)(2,1)} %get-tuple-element.120.rest_0_.rest_3_.rest_2_), channel_id=1, source_target_pairs={{0,1},{1,0},{2,3},{3,2},{4,5},{5,4},{6,7},{7,6},{8,9},{9,8},{10,11... | collective-permute-start | bytes 552968 | tf_op jit(solution)/shard_map/ppermute | solution.py:564
  38.4 18.7 %collective-permute-start.22 = (bf16[240,384]{1,0:T(8,128)(2,1)}, bf16[240,384]{1,0:T(8,128)(2,1)S(1)}, u32[]{:S(2)}, u32[]{:S(2)}) collective-permute-start(bf16[240,384]{1,0:T(8,128)(2,1)} %get-tuple-element.120.rest_0_.rest_3_.rest_2_), channel_id=1, source_target_pairs={{0,8},{1,9},{2,10},{3,11},{4,12},{5,13},{6,14},{7,15},{8,0},{9,1},... | collective-permute-start | bytes 552968 | tf_op jit(solution)/shard_map/ppermute | solution.py:564
  39.7 26.1 %collective-permute-start.18 = (bf16[240,384]{1,0:T(8,128)(2,1)}, bf16[240,384]{1,0:T(8,128)(2,1)S(1)}, u32[]{:S(2)}, u32[]{:S(2)}) collective-permute-start(bf16[240,384]{1,0:T(8,128)(2,1)} %get-tuple-element.120.rest_0_.rest_3_.rest_2_), channel_id=1, source_target_pairs={{0,4},{1,5},{2,6},{3,7},{4,0},{5,1},{6,2},{7,3},{8,12},{9,13},{10,... | collective-permute-start | bytes 552968 | tf_op jit(solution)/shard_map/ppermute | solution.py:564
  42.6 29.2 %collective-permute-start.16 = (bf16[240,384]{1,0:T(8,128)(2,1)}, bf16[240,384]{1,0:T(8,128)(2,1)S(1)}, u32[]{:S(2)}, u32[]{:S(2)}) collective-permute-start(bf16[240,384]{1,0:T(8,128)(2,1)} %get-tuple-element.120.rest_0_.rest_3_.rest_2_), channel_id=1, source_target_pairs={{0,2},{1,3},{2,0},{3,1},{4,6},{5,7},{6,4},{7,5},{8,10},{9,11},{10,... | collective-permute-start | bytes 552968 | tf_op jit(solution)/shard_map/ppermute | solution.py:564
  57.1 14.6 %collective-permute-start.26 = (bf16[240,384]{1,0:T(8,128)(2,1)S(1)}, bf16[240,384]{1,0:T(8,128)(2,1)S(1)}, u32[]{:S(2)}, u32[]{:S(2)}) collective-permute-start(bf16[240,384]{1,0:T(8,128)(2,1)S(1)} %collective-permute-done.22.rest_8_.rest_11_.rest_10_), channel_id=1, source_target_pairs={{0,4},{1,5},{2,6},{3,7},{4,0},{5,1},{6,2},{7,3},{8,12},{9,13},{10,... | collective-permute-start | bytes 552968 | tf_op jit(solution)/shard_map/ppermute | solution.py:564
  57.1 16.4 %collective-permute-start.24 = (bf16[240,384]{1,0:T(8,128)(2,1)S(1)}, bf16[240,384]{1,0:T(8,128)(2,1)S(1)}, u32[]{:S(2)}, u32[]{:S(2)}) collective-permute-start(bf16[240,384]{1,0:T(8,128)(2,1)S(1)} %collective-permute-done.22.rest_8_.rest_11_.rest_10_), channel_id=1, source_target_pairs={{0,2},{1,3},{2,0},{3,1},{4,6},{5,7},{6,4},{7,5},{8,10},{9,11},{10,... | collective-permute-start | bytes 552968 | tf_op jit(solution)/shard_map/ppermute | solution.py:564
  65.9 17.4 %collective-permute-start.23 = (bf16[240,384]{1,0:T(8,128)(2,1)S(1)}, bf16[240,384]{1,0:T(8,128)(2,1)S(1)}, u32[]{:S(2)}, u32[]{:S(2)}) collective-permute-start(bf16[240,384]{1,0:T(8,128)(2,1)S(1)} %collective-permute-done.22.rest_8_.rest_11_.rest_10_), channel_id=1, source_target_pairs={{0,1},{1,0},{2,3},{3,2},{4,5},{5,4},{6,7},{7,6},{8,9},{9,8},{10,11... | collective-permute-start | bytes 552968 | tf_op jit(solution)/shard_map/ppermute | solution.py:564
  71.7 11.8 %collective-permute-start.19 = (bf16[240,384]{1,0:T(8,128)(2,1)S(1)}, bf16[240,384]{1,0:T(8,128)(2,1)S(1)}, u32[]{:S(2)}, u32[]{:S(2)}) collective-permute-start(bf16[240,384]{1,0:T(8,128)(2,1)S(1)} %collective-permute-done.18.rest_4_.rest_7_.rest_6_), channel_id=1, source_target_pairs={{0,1},{1,0},{2,3},{3,2},{4,5},{5,4},{6,7},{7,6},{8,9},{9,8},{10,11... | collective-permute-start | bytes 552968 | tf_op jit(solution)/shard_map/ppermute | solution.py:564
  157.5 12.7 %collective-permute-start.30 = (bf16[2,8,96,768]{3,2,1,0:T(8,128)(2,1)}, bf16[2,8,96,768]{3,2,1,0:T(8,128)(2,1)S(1)}, u32[]{:S(2)}, u32[]{:S(2)}) collective-permute-start(bf16[2,8,96,768]{3,2,1,0:T(8,128)(2,1)} %get-tuple-element.145), channel_id=1, source_target_pairs={{0,1},{1,0},{2,3},{3,2},{4,5},{5,4},{6,7},{7,6},{8,9},{9,8},{10,11... | collective-permute-start | bytes 7077896 | tf_op jit(solution)/shard_map/ppermute | solution.py:564
  171.7 28.2 %collective-permute-start.31 = (bf16[8,96,768]{2,1,0:T(8,128)(2,1)S(1)}, bf16[8,96,768]{2,1,0:T(8,128)(2,1)S(1)}, u32[]{:S(2)}, u32[]{:S(2)}) collective-permute-start(bf16[8,96,768]{2,1,0:T(8,128)(2,1)S(1)} %fusion), channel_id=1, source_target_pairs={{0,16},{16,0},{1,17},{17,1},{2,18},{18,2},{3,19},{19,3},{4,20},{20... | collective-permute-start | bytes 3538952 | tf_op jit(solution)/shard_map/ppermute | solution.py:640
  193.3 21.9 %collective-permute-start.33 = (bf16[8,240,384]{2,1,0:T(8,128)(2,1)S(1)}, bf16[8,240,384]{2,1,0:T(8,128)(2,1)S(1)}, u32[]{:S(2)}, u32[]{:S(2)}) collective-permute-start(bf16[8,240,384]{2,1,0:T(8,128)(2,1)S(1)} %get-tuple-element.160), channel_id=1, source_target_pairs={{0,1},{1,0},{2,3},{3,2},{4,5},{5,4},{6,7},{7,6},{8,9},{9,8},{10,11... | collective-permute-start | bytes 4423688 | tf_op jit(solution)/shard_map/ppermute | solution.py:564
  201.8 14.9 %collective-permute-start.32 = (bf16[4,96,768]{2,1,0:T(8,128)(2,1)S(1)}, bf16[4,96,768]{2,1,0:T(8,128)(2,1)S(1)}, u32[]{:S(2)}, u32[]{:S(2)}) collective-permute-start(bf16[4,96,768]{2,1,0:T(8,128)(2,1)S(1)} %fusion.1), channel_id=1, source_target_pairs={{0,2},{1,3},{2,0},{3,1},{4,6},{5,7},{6,4},{7,5},{8,10},{9,11},{10,... | collective-permute-start | bytes 1769480 | tf_op jit(solution)/shard_map/ppermute | solution.py:564
  215.5 21.0 %collective-permute-start.35 = (bf16[4,240,384]{2,1,0:T(8,128)(2,1)S(1)}, bf16[4,240,384]{2,1,0:T(8,128)(2,1)S(1)}, u32[]{:S(2)}, u32[]{:S(2)}) collective-permute-start(bf16[4,240,384]{2,1,0:T(8,128)(2,1)S(1)} %add_convert_fusion.1), channel_id=1, source_target_pairs={{0,2},{1,3},{2,0},{3,1},{4,6},{5,7},{6,4},{7,5},{8,10},{9,11},{10,... | collective-permute-start | bytes 2211848 | tf_op jit(solution)/shard_map/ppermute | solution.py:564
  218.1 14.3 %collective-permute-start.36 = (bf16[2,96,768]{2,1,0:T(8,128)(2,1)S(1)}, bf16[2,96,768]{2,1,0:T(8,128)(2,1)S(1)}, u32[]{:S(2)}, u32[]{:S(2)}) collective-permute-start(bf16[2,96,768]{2,1,0:T(8,128)(2,1)S(1)} %fusion.3), channel_id=1, source_target_pairs={{0,4},{1,5},{2,6},{3,7},{4,0},{5,1},{6,2},{7,3},{8,12},{9,13},{10,... | collective-permute-start | bytes 884744 | tf_op jit(solution)/shard_map/ppermute | solution.py:564
  225.7 13.1 %collective-permute-start.34 = (bf16[8,144,384]{2,1,0:T(8,128)(2,1)S(1)}, bf16[8,144,384]{2,1,0:T(8,128)(2,1)S(1)}, u32[]{:S(2)}, u32[]{:S(2)}) collective-permute-start(bf16[8,144,384]{2,1,0:T(8,128)(2,1)S(1)} %get-tuple-element.170), channel_id=1, source_target_pairs={{0,1},{1,0},{2,3},{3,2},{4,5},{5,4},{6,7},{7,6},{8,9},{9,8},{10,11... | collective-permute-start | bytes 2654216 | tf_op jit(solution)/shard_map/ppermute | solution.py:564
  233.9 18.3 %collective-permute-start.39 = (bf16[1,96,768]{2,1,0:T(8,128)(2,1)S(1)}, bf16[1,96,768]{2,1,0:T(8,128)(2,1)S(1)}, u32[]{:S(2)}, u32[]{:S(2)}) collective-permute-start(bf16[1,96,768]{2,1,0:T(8,128)(2,1)S(1)} %fusion.10), channel_id=1, source_target_pairs={{0,8},{1,9},{2,10},{3,11},{4,12},{5,13},{6,14},{7,15},{8,0},{9,1},... | collective-permute-start | bytes 442376 | tf_op jit(solution)/shard_map/ppermute | solution.py:564
  236.6 15.7 %collective-permute-start.38 = (bf16[2,240,384]{2,1,0:T(8,128)(2,1)S(1)}, bf16[2,240,384]{2,1,0:T(8,128)(2,1)S(1)}, u32[]{:S(2)}, u32[]{:S(2)}) collective-permute-start(bf16[2,240,384]{2,1,0:T(8,128)(2,1)S(1)} %add_convert_fusion.3), channel_id=1, source_target_pairs={{0,4},{1,5},{2,6},{3,7},{4,0},{5,1},{6,2},{7,3},{8,12},{9,13},{10,... | collective-permute-start | bytes 1105928 | tf_op jit(solution)/shard_map/ppermute | solution.py:564
  238.9 13.3 %collective-permute-start.37 = (bf16[4,144,384]{2,1,0:T(8,128)(2,1)S(1)}, bf16[4,144,384]{2,1,0:T(8,128)(2,1)S(1)}, u32[]{:S(2)}, u32[]{:S(2)}) collective-permute-start(bf16[4,144,384]{2,1,0:T(8,128)(2,1)S(1)} %add_convert_fusion.2), channel_id=1, source_target_pairs={{0,2},{1,3},{2,0},{3,1},{4,6},{5,7},{6,4},{7,5},{8,10},{9,11},{10,... | collective-permute-start | bytes 1327112 | tf_op jit(solution)/shard_map/ppermute | solution.py:564
  253.3 24.2 %collective-permute-start.46 = (bf16[1,240,384]{2,1,0:T(8,128)(2,1)}, bf16[1,240,384]{2,1,0:T(8,128)(2,1)}, u32[]{:S(2)}, u32[]{:S(2)}) collective-permute-start(bf16[1,240,384]{2,1,0:T(8,128)(2,1)} %add_convert_fusion.6), channel_id=1, source_target_pairs={{0,8},{1,9},{2,10},{3,11},{4,12},{5,13},{6,14},{7,15},{8,0},{9,1},... | collective-permute-start | bytes 552968 | tf_op jit(solution)/shard_map/ppermute | solution.py:564
  254.3 14.4 %all-to-all-start = ((f32[16,1,672]{2,1,0:T(1,128)}), f32[16,1,672]{2,1,0:T(1,128)}, u32[]{:S(2)}, u32[]{:S(2)}) async-start(f32[16,1,672]{2,1,0:T(1,128)} %pack.1), calls=%async_computation | async-start | bytes 98304 | tf_op jit(solution)/shard_map/all_to_all | solution.py:1476
  267.0 15.8 %collective-permute-start.45 = (bf16[96,768]{1,0:T(8,128)(2,1)S(1)}, bf16[96,768]{1,0:T(8,128)(2,1)S(1)}, u32[]{:S(2)}, u32[]{:S(2)}) collective-permute-start(bf16[96,768]{1,0:T(8,128)(2,1)S(1)} %fusion.12.d_ref), channel_id=1, source_target_pairs={{0,16},{16,0},{1,17},{17,1},{2,18},{18,2},{3,19},{19,3},{4,20},{20... | collective-permute-start | bytes 442376 | tf_op jit(solution)/shard_map/ppermute | solution.py:640
  (136 other events, 1060.0 us)
Sparse Core Ops, SparseCore 0:
  11.0 64.0 all-gather.4
  77.9 53.5 all-gather.6
  158.0 80.0 reduce-scatter.1

commit v7 on v6

--- a/solution.py
+++ b/solution.py
@@ -777,7 +777,7 @@
         own = sizes[7] // 2
         for i in range(2):
             b1_ref[i : i + 1, :] = spread(packed, starts[7] + i * own, own)
-        bias_ref[...] = column(b_qkv)
+        bias_ref[...] = b_qkv
         freq = column(freqs)
         spots = lax.broadcasted_iota(jnp.int32, (1, 128), 1).astype(F32)
         for i in range(2):
@@ -815,7 +815,7 @@
         in_specs=[SMEM, pl.BlockSpec((blk, width), lambda i: (i, 0)), tall(1), tall(1)] + [HBM] * SHARDS,
         out_specs=[
             tall(width), tall(width // 2), tall(width // 2),
-            whole(8, width), whole(2, own * SHARDS), whole(3 * width, 1), tall(16),
+            whole(8, width), whole(2, own * SHARDS), whole(1, 3 * width), tall(16),
         ],
         out_shape=[
             shape((width, slots), BF),
@@ -823,7 +823,7 @@
             shape((width // 2, slots), F32),
             shape((8, width), F32),
             shape((2, own * SHARDS), F32),
-            shape((3 * width, 1), F32),
+            shape((1, 3 * width), F32),
             shape((16, slots), BF),
         ],
         scratch_shapes=[
@@ -869,7 +869,7 @@
 
 
 def group_kernel(order_ref, at_ref, bq_ref, bk_ref, bv_ref, cos_ref, sin_ref, *rest):
-    pieces, (q_ref, k_ref, v_ref, w_scr, wt_scr, sem) = rest[:SHARDS], rest[SHARDS:]
+    pieces, (q_ref, k_ref, v_ref, w_scr, wt_scr, bias_scr, sem) = rest[:SHARDS], rest[SHARDS:]
     cols = q_ref.shape[0]
     part = w_scr.shape[1] // 3
 
@@ -880,12 +880,13 @@
         wait_all(copies)
         for i in range(3):
             wt_scr[i] = w_scr[:, i * part : (i + 1) * part, :].reshape(SHARDS * part, cols).T
+            bias_scr[i] = column((bq_ref, bk_ref, bv_ref)[i][...])
 
     a_t = at_ref[...]
     cos = cos_ref[...]
     sin = sin_ref[...]
-    for i, b_ref, out_ref, scale in ((0, bq_ref, q_ref, HEAD_DIM**-0.5), (1, bk_ref, k_ref, 1.0)):
-        u = nn(wt_scr[i], a_t) + b_ref[...]
+    for i, out_ref, scale in ((0, q_ref, HEAD_DIM**-0.5), (1, k_ref, 1.0)):
+        u = nn(wt_scr[i], a_t) + bias_scr[i]
         for h in range(cols // HEAD_DIM):
             u1 = u[h * HEAD_DIM : h * HEAD_DIM + HALF]
             u2 = u[h * HEAD_DIM + HALF : (h + 1) * HEAD_DIM]
@@ -893,7 +894,7 @@
             s = sin[h * HALF : (h + 1) * HALF]
             out_ref[h * HEAD_DIM : h * HEAD_DIM + HALF, :] = ((u1 * c - u2 * s) * scale).astype(BF)
             out_ref[h * HEAD_DIM + HALF : (h + 1) * HEAD_DIM, :] = ((u1 * s + u2 * c) * scale).astype(BF)
-    v_ref[...] = (nn(wt_scr[2], a_t) + bv_ref[...]).astype(BF)
+    v_ref[...] = (nn(wt_scr[2], a_t) + bias_scr[2]).astype(BF)
 
 
 def project_group(group, order, a_t, bias, cos, sin, pieces):
@@ -905,7 +906,7 @@
         group_kernel,
         grid=(slots // blk,),
         in_specs=[SMEM, tall(width, 0)]
-        + [pl.BlockSpec((cols, 1), lambda i, n=n: (n * GROUPS + group, 0)) for n in range(3)]
+        + [pl.BlockSpec((1, cols), lambda i, n=n: (0, n * GROUPS + group)) for n in range(3)]
         + [tall(cols // 2, group)] * 2
         + [HBM] * SHARDS,
         out_specs=[tall(cols, 0)] * 3,
@@ -913,6 +914,7 @@
         scratch_shapes=[
             pltpu.VMEM((SHARDS, 3 * width // SHARDS, cols), BF),
             pltpu.VMEM((3, cols, width), BF),
+            pltpu.VMEM((3, cols, 1), F32),
             pltpu.SemaphoreType.DMA((SHARDS,)),
         ],
         compiler_params=params(),
@@ -1471,7 +1473,7 @@
     scatter_a.hold(block)
     sent = scatter_a.step()
     mlp_d = scatter_d.finish()
-    scatter_b.hold(other_c, sent)
+    scatter_b.hold(sent)
     mine_b = scatter_b.finish()
     mine = jnp.sum(tie(lax.all_to_all(block, "fsdp", 0, 0, tiled=True), sent), axis=0)
     mine = tie(mine[0], scatter_a.got[-1])

time: 299 us -> 298 us (level)
  waiting for transfers between devices: 36.8 us -> 44.4 us
  starting transfers between devices: 53.3 us -> 48.8 us
  other arithmetic: 13.9 us -> 10.9 us
    ppermute x42, waiting for transfers between devices: 25.3 us -> 32.6 us  [swap(): return lax.ppermute(v, 'fsdp', [(i, i ^ mask) for i in range(SHARDS)])]
    convert_element_type x9, other arithmetic: 7.63 us -> 4.24 us  [total(): return out.astype(BF)]
  transfers between devices with their start and end apart: 52 -> 52, of which waited for: 18 -> 19; matrix products, arithmetic and copies ran while one was open for 5% -> 4% of each run, Pallas kernels for 48% -> 48%
where the time goes in v7:
time: 298 us; the launch traced here: 295 us
  Pallas kernels  167 us (56%)
  starting transfers between devices  48.8 us (16%)
  waiting for transfers between devices  44.4 us (15%)
  between operations  15.5 us (5%)
  other arithmetic  10.9 us (4%)
  local copies, waits for them, and re-layouts  8.32 us (3%)
    pallas_call x2, Pallas kernels, mlp_half(): pl.pallas_call(partial(mlp_half_kernel, part, first, split, len(pieces)),...  47.3 us
    ppermute x42, starting transfers between devices, swap(): return lax.ppermute(v, 'fsdp', [(i, i ^ mask) for i in range(SHARDS)])  36.6 us
    ppermute x42, waiting for transfers between devices, swap(): return lax.ppermute(v, 'fsdp', [(i, i ^ mask) for i in range(SHARDS)])  32.6 us
    pallas_call x2, Pallas kernels, heads_back(): pl.pallas_call(heads_back_kernel, grid=(steps,), in_specs=[SMEM] + [head]...  23.7 us
    pallas_call x2, Pallas kernels, attend(): pl.pallas_call(attend_kernel, grid=(heads // each,), in_specs=[pl.BlockSp...  16.9 us
    pallas_call x2, Pallas kernels, project_group(): pl.pallas_call(group_kernel, grid=(slots // blk,), in_specs=[SMEM, tall(w...  13.9 us
    pallas_call x2, Pallas kernels, qkv_grad(): pl.pallas_call(qkv_grad_kernel, in_specs=[SMEM] + [VMEM] * 6 + [ANY] * le...  12.5 us
    pallas_call x1, Pallas kernels, out_back_fast(): pl.pallas_call(partial(out_back_fast_kernel, start), grid=(slots // blk,)...  12.2 us
  transfers between devices with their start and end apart: 52, of which 19 were waited for; matrix products, arithmetic and copies ran while one was open for 4% of the time, Pallas kernels for 48%

profile of v7, /device:TPU:0, one launch (start us, length us, event | category | flops | bytes accessed | tf_op | source)
XLA Modules:
  0.0 294.5 jit_solution(17654105751694417224)
XLA Ops:
  12.6 4.0 %collective-permute-start.5 = (bf16[160,384]{1,0:T(8,128)(2,1)}, bf16[160,384]{1,0:T(8,128)(2,1)S(1)}, u32[]{:S(2)}, u32[]{:S(2)}) collective-permute-start(bf16[160,384]{1,0:T(8,128)(2,1)} %get-tuple-element.107.rest_0_.rest_3_), channel_id=1, source_target_pairs={{0,8},{1,9},{2,10},{3,11},{4,12},{5,13},{6,14},{7,15},{8,0},{9,1},... | collective-permute-start | bytes 368648 | tf_op jit(solution)/shard_map/ppermute | solution.py:564
  19.8 3.2 %collective-permute-done.5.rest_8_.rest_11_ = bf16[160,384]{1,0:T(8,128)(2,1)S(1)} collective-permute-done((bf16[160,384]{1,0:T(8,128)(2,1)}, bf16[160,384]{1,0:T(8,128)(2,1)S(1)}, u32[]{:S(2)}, u32[]{:S(2)}) %collective-permute-start.5) | collective-permute-done | bytes 122912 | tf_op jit(solution)/shard_map/ppermute | solution.py:564
  27.2 5.2 %collective-permute-done.11.rest_12_.rest_15_ = bf16[160,384]{1,0:T(8,128)(2,1)S(1)} collective-permute-done((bf16[160,384]{1,0:T(8,128)(2,1)S(1)}, bf16[160,384]{1,0:T(8,128)(2,1)S(1)}, u32[]{:S(2)}, u32[]{:S(2)}) %collective-permute-start.11) | collective-permute-done | bytes 122912 | tf_op jit(solution)/shard_map/ppermute | solution.py:564
  44.7 9.1 %prepare.1 = (bf16[768,1024]{1,0:T(8,128)(2,1)}, f32[384,1024]{1,0:T(8,128)}, f32[384,1024]{1,0:T(8,128)}, f32[8,768]{1,0:T(8,128)}, f32[2,1536]{1,0:T(2,128)}, ...) custom-call(s32[17]{0:T(128)} %pad_add_fusion.order_ref, bf16[1024,768]{1,0:T(8,128)(2,1)} %bitcast.47, s32[1,1024]{1,0:T(1,128)} %cols_ref.1, ...), custom_call_target="tpu_custom_call" | custom-call | flops 8800000000 | bytes 65536 | tf_op jit(solution)/shard_map/prepare/pallas_call | solution.py:812
  53.9 3.3 %collective-permute-done.22.rest_8_.rest_11_.rest_10_ = bf16[240,384]{1,0:T(8,128)(2,1)S(1)} collective-permute-done((bf16[240,384]{1,0:T(8,128)(2,1)}, bf16[240,384]{1,0:T(8,128)(2,1)S(1)}, u32[]{:S(2)}, u32[]{:S(2)}) %collective-permute-start.22) | collective-permute-done | bytes 184352 | tf_op jit(solution)/shard_map/ppermute | solution.py:564
  58.8 7.0 %qkv_group.2 = (bf16[384,1024]{1,0:T(8,128)(2,1)}, bf16[384,1024]{1,0:T(8,128)(2,1)}, bf16[384,1024]{1,0:T(8,128)(2,1)}) custom-call(s32[17]{0:T(128)} %pad_add_fusion.order_ref, bf16[768,1024]{1,0:T(8,128)(2,1)} %get-tuple-element.111.at_ref, f32[1,2304]{1,0:T(1,128)} %get-tuple-element.112.bq_ref.bk_ref.bv_ref, ...), custom_call_target="tpu_custom_call" | custom-call | flops 7699999744 | bytes 65536 | tf_op jit(solution)/shard_map/qkv_group/pallas_call | solution.py:905
  66.0 5.8 %collective-permute-done.26.rest_12_.rest_15_.rest_14_ = bf16[240,384]{1,0:T(8,128)(2,1)S(1)} collective-permute-done((bf16[240,384]{1,0:T(8,128)(2,1)S(1)}, bf16[240,384]{1,0:T(8,128)(2,1)S(1)}, u32[]{:S(2)}, u32[]{:S(2)}) %collective-permute-start.26) | collective-permute-done | bytes 184352 | tf_op jit(solution)/shard_map/ppermute | solution.py:564
  73.9 8.4 %attend.2 = (bf16[384,1024]{1,0:T(8,128)(2,1)}, f32[6,1,1024]{2,1,0:T(1,128)}) custom-call(s32[3]{0:T(128)} %bitcast.52, bf16[384,1024]{1,0:T(8,128)(2,1)} %get-tuple-element.115.q_ref, bf16[384,1024]{1,0:T(8,128)(2,1)} %get-tuple-element.116.k_ref, bf16[384,1024]{1,0:T(8,128)(2,1)} %get-tuple-element.117.v_ref), custom_call_target="tpu_custom_call" | custom-call | flops 8800000000 | bytes 65536 | tf_op jit(solution)/shard_map/attend/pallas_call | solution.py:180
  86.2 6.9 %qkv_group.3 = (bf16[384,1024]{1,0:T(8,128)(2,1)}, bf16[384,1024]{1,0:T(8,128)(2,1)}, bf16[384,1024]{1,0:T(8,128)(2,1)}) custom-call(s32[17]{0:T(128)} %pad_add_fusion.order_ref, bf16[768,1024]{1,0:T(8,128)(2,1)} %get-tuple-element.111.at_ref, f32[1,2304]{1,0:T(1,128)} %get-tuple-element.112.bq_ref.bk_ref.bv_ref, ...), custom_call_target="tpu_custom_call" | custom-call | flops 7699999744 | bytes 65536 | tf_op jit(solution)/shard_map/qkv_group/pallas_call | solution.py:905
  93.1 8.5 %attend.3 = (bf16[384,1024]{1,0:T(8,128)(2,1)}, f32[6,1,1024]{2,1,0:T(1,128)}) custom-call(s32[3]{0:T(128)} %bitcast.53, bf16[384,1024]{1,0:T(8,128)(2,1)} %get-tuple-element.128.q_ref, bf16[384,1024]{1,0:T(8,128)(2,1)} %get-tuple-element.129.k_ref, bf16[384,1024]{1,0:T(8,128)(2,1)} %get-tuple-element.130.v_ref), custom_call_target="tpu_custom_call" | custom-call | flops 8800000000 | bytes 65536 | tf_op jit(solution)/shard_map/attend/pallas_call | solution.py:180
  101.6 8.5 %out_project.1 = (bf16[1024,768]{1,0:T(8,128)(2,1)}, bf16[1024,768]{1,0:T(8,128)(2,1)}, bf16[768,1024]{1,0:T(8,128)(2,1)}) custom-call(s32[17]{0:T(128)} %pad_add_fusion.order_ref, f32[8,768]{1,0:T(8,128)} %get-tuple-element.110.vec_ref, bf16[384,1024]{1,0:T(8,128)(2,1)} %get-tuple-element.118.rest_0_.o_ref, ...), custom_call_target="tpu_custom_call" | custom-call | flops 8800000000 | bytes 65536 | tf_op jit(solution)/shard_map/out_project/pallas_call | solution.py:960
  110.1 23.7 %mlp_half.2 = (bf16[1024,768]{1,0:T(8,128)(2,1)}, bf16[1024,768]{1,0:T(8,128)(2,1)}, bf16[16,192,768]{2,1,0:T(8,128)(2,1)}, f32[1,1536]{1,0:T(1,128)}) custom-call(s32[17]{0:T(128)} %pad_add_fusion.order_ref, bf16[1024,768]{1,0:T(8,128)(2,1)} %get-tuple-element.132.c_in, bf16[768,1024]{1,0:T(8,128)(2,1)} %get-tuple-element.133.ct_in, ...), custom_call_target="tpu_custom_call" | custom-call | flops 25300000768 | bytes 65536 | tf_op jit(solution)/shard_map/mlp_half/pallas_call | solution.py:1084
  133.8 23.7 %mlp_half.3 = (bf16[1024,768]{1,0:T(8,128)(2,1)}, bf16[1024,768]{1,0:T(8,128)(2,1)}, bf16[2,8,96,768]{3,2,1,0:T(8,128)(2,1)}, bf16[2,8,96,768]{3,2,1,0:T(8,128)(2,1)}, f32[1,1536]{1,0:T(1,128)}) custom-call(s32[17]{0:T(128)} %pad_add_fusion.order_ref, bf16[1024,768]{1,0:T(8,128)(2,1)} %get-tuple-element.132.c_in, ...), custom_call_target="tpu_custom_call" | custom-call | flops 25300000768 | bytes 65536 | tf_op jit(solution)/shard_map/mlp_half/pallas_call | solution.py:1084
  157.8 12.2 %out_back.1 = (bf16[1024,768]{1,0:T(8,128)(2,1)}, bf16[768,1024]{1,0:T(8,128)(2,1)}, bf16[8,240,384]{2,1,0:T(8,128)(2,1)}, bf16[8,240,384]{2,1,0:T(8,128)(2,1)}, f32[8,768]{1,0:T(8,128)}) custom-call(s32[17]{0:T(128)} %pad_add_fusion.order_ref, bf16[1024,768]{1,0:T(8,128)(2,1)} %get-tuple-element.141.dc_ref, ...), custom_call_target="tpu_custom_call" | custom-call | flops 13200000000 | bytes 65536 | tf_op jit(solution)/shard_map/out_back/pallas_call | solution.py:1165
  174.7 12.1 %heads_back.2 = (bf16[384,1024]{1,0:T(8,128)(2,1)S(1)}, bf16[384,1024]{1,0:T(8,128)(2,1)S(1)}, bf16[384,1024]{1,0:T(8,128)(2,1)S(1)}, bf16[192,1024]{1,0:T(8,128)(2,1)S(1)}) custom-call(s32[3]{0:T(128)S(1)} %bitcast.54, bf16[384,1024]{1,0:T(8,128)(2,1)S(1)} %copy-done.71, bf16[384,1024]{1,0:T(8,128)(2,1)S(1)} %copy-done.72, ...), custom_call_target="tpu_custom_call" | custom-call | flops 14300000256 | bytes 65536 | tf_op jit(solution)/shard_map/heads_back/pallas_call | solution.py:1260
  186.9 6.3 %qkv_grad.2 = (bf16[8,240,384]{2,1,0:T(8,128)(2,1)S(1)}, bf16[8,240,384]{2,1,0:T(8,128)(2,1)S(1)}, f32[16,1152]{1,0:T(8,128)S(1)}, f32[16,192]{1,0:T(8,128)S(1)}) custom-call(s32[17]{0:T(128)S(1)} %copy-done.67, bf16[768,1024]{1,0:T(8,128)(2,1)S(1)} %copy-done.68, bf16[16,1024]{1,0:T(8,128)(2,1)S(1)} %copy-done.82, ...), custom_call_target="tpu_custom_call", output_to_operand_aliasing={{0}: (7, {}), {1}: (8, {})} | custom-call | flops 6600000000 | bytes 65536 | tf_op jit(solution)/shard_map/qkv_grad/pallas_call | solution.py:1297
  193.4 6.4 %collective-permute-done.31 = bf16[8,96,768]{2,1,0:T(8,128)(2,1)S(1)} collective-permute-done((bf16[8,96,768]{2,1,0:T(8,128)(2,1)S(1)}, bf16[8,96,768]{2,1,0:T(8,128)(2,1)S(1)}, u32[]{:S(2)}, u32[]{:S(2)}) %collective-permute-start.31) | collective-permute-done | bytes 1179680 | tf_op jit(solution)/shard_map/ppermute | solution.py:640
  201.7 11.7 %heads_back.3 = (bf16[384,1024]{1,0:T(8,128)(2,1)S(1)}, bf16[384,1024]{1,0:T(8,128)(2,1)S(1)}, bf16[384,1024]{1,0:T(8,128)(2,1)S(1)}, bf16[192,1024]{1,0:T(8,128)(2,1)S(1)}) custom-call(s32[3]{0:T(128)S(1)} %bitcast.55, bf16[384,1024]{1,0:T(8,128)(2,1)S(1)} %copy-done.75, bf16[384,1024]{1,0:T(8,128)(2,1)S(1)} %copy-done.76, ...), custom_call_target="tpu_custom_call" | custom-call | flops 14300000256 | bytes 65536 | tf_op jit(solution)/shard_map/heads_back/pallas_call | solution.py:1260
  218.0 6.3 %qkv_grad.3 = (bf16[8,144,384]{2,1,0:T(8,128)(2,1)S(1)}, bf16[8,144,384]{2,1,0:T(8,128)(2,1)S(1)}, f32[16,1152]{1,0:T(8,128)S(1)}, f32[16,192]{1,0:T(8,128)S(1)}) custom-call(s32[17]{0:T(128)S(1)} %copy-done.67, bf16[768,1024]{1,0:T(8,128)(2,1)S(1)} %copy-done.68, bf16[16,1024]{1,0:T(8,128)(2,1)S(1)} %copy-done.82, ...), custom_call_target="tpu_custom_call" | custom-call | flops 6600000000 | bytes 65536 | tf_op jit(solution)/shard_map/qkv_grad/pallas_call | solution.py:1297
  224.5 6.4 %input_part.1.da_ref = f32[768,1024]{1,0:T(8,128)S(1)} custom-call(s32[17]{0:T(128)S(1)} %copy-done.67, bf16[384,1024]{1,0:T(8,128)(2,1)S(1)} %get-tuple-element.167.dq_ref.rest_0_, bf16[384,1024]{1,0:T(8,128)(2,1)S(1)} %get-tuple-element.168.dk_ref.rest_1_, bf16[384,1024]{1,0:T(8,128)(2,1)S(1)} %get-tuple-element.169.dv_ref.rest_2_, ...), custom_call_target="tpu_custom_call" | custom-call | flops 6600000000 | bytes 65536 | tf_op jit(solution)/shard_map/input_part/pallas_call | solution.py:1347
  237.3 9.5 %input_back.1 = (bf16[1024,768]{1,0:T(8,128)(2,1)}, f32[8,768]{1,0:T(8,128)S(1)}) custom-call(s32[17]{0:T(128)S(1)} %copy-done.67, bf16[1024,768]{1,0:T(8,128)(2,1)S(1)} %bitcast.49, bf16[1024,768]{1,0:T(8,128)(2,1)S(1)} %copy-done.74, f32[8,768]{1,0:T(8,128)S(1)} %copy-done.85, f32[768,1024]{1,0:T(8,128)S(1)} %input_part.1.da_ref, ...), custom_call_target="tpu_custom_call" | custom-call | flops 11000000512 | bytes 65536 | tf_op jit(solution)/shard_map/input_back/pallas_call | solution.py:1380
  255.9 4.1 %all-to-all-start = ((f32[16,1,672]{2,1,0:T(1,128)}), f32[16,1,672]{2,1,0:T(1,128)}, u32[]{:S(2)}, u32[]{:S(2)}) async-start(f32[16,1,672]{2,1,0:T(1,128)} %pack.1), calls=%async_computation | async-start | bytes 98304 | tf_op jit(solution)/shard_map/all_to_all | solution.py:1478
  260.0 3.0 %collective-permute-done.40 = bf16[2,144,384]{2,1,0:T(8,128)(2,1)} collective-permute-done((bf16[2,144,384]{2,1,0:T(8,128)(2,1)}, bf16[2,144,384]{2,1,0:T(8,128)(2,1)}, u32[]{:S(2)}, u32[]{:S(2)}) %collective-permute-start.40) | collective-permute-done | bytes 221216 | tf_op jit(solution)/shard_map/ppermute | solution.py:564
  280.0 4.1 %collective-permute-done.44.c_other_ref = bf16[192,768]{1,0:T(8,128)(2,1)S(1)} collective-permute-done((bf16[192,768]{1,0:T(8,128)(2,1)}, bf16[192,768]{1,0:T(8,128)(2,1)S(1)}, u32[]{:S(2)}, u32[]{:S(2)}) %collective-permute-start.44) | collective-permute-done | bytes 294944 | tf_op jit(solution)/shard_map/ppermute | solution.py:640
  (346 shorter events, 79.7 us)
Async XLA Ops:
  7.3 102.8 %all-gather.5.cloned.1.call-start = ((), (), s32[]{:S(2)}) async-start(), calls=%async_computation.3 | async-start | bytes 5013504 | tf_op jit(solution)/shard_map/all_gather | solution.py:1414
  9.4 124.5 %all-gather.7.cloned.1.call-start = ((), (), s32[]{:S(2)}) async-start(), calls=%async_computation.4 | async-start | bytes 5013504 | tf_op jit(solution)/shard_map/all_gather | solution.py:1415
  10.1 265.6 %reduce-scatter.2.cloned.1.call-start = ((), (), s32[]{:S(2)}) async-start(), calls=%async_computation.2 | async-start | bytes 5013504 | tf_op jit(solution)/shard_map/reduce_scatter | solution.py:1439
  37.9 45.1 %collective-permute-start.15 = (bf16[240,384]{1,0:T(8,128)(2,1)}, bf16[240,384]{1,0:T(8,128)(2,1)S(1)}, u32[]{:S(2)}, u32[]{:S(2)}) collective-permute-start(bf16[240,384]{1,0:T(8,128)(2,1)} %get-tuple-element.120.rest_0_.rest_3_.rest_2_), channel_id=1, source_target_pairs={{0,1},{1,0},{2,3},{3,2},{4,5},{5,4},{6,7},{7,6},{8,9},{9,8},{10,11... | collective-permute-start | bytes 552968 | tf_op jit(solution)/shard_map/ppermute | solution.py:564
  38.4 18.7 %collective-permute-start.22 = (bf16[240,384]{1,0:T(8,128)(2,1)}, bf16[240,384]{1,0:T(8,128)(2,1)S(1)}, u32[]{:S(2)}, u32[]{:S(2)}) collective-permute-start(bf16[240,384]{1,0:T(8,128)(2,1)} %get-tuple-element.120.rest_0_.rest_3_.rest_2_), channel_id=1, source_target_pairs={{0,8},{1,9},{2,10},{3,11},{4,12},{5,13},{6,14},{7,15},{8,0},{9,1},... | collective-permute-start | bytes 552968 | tf_op jit(solution)/shard_map/ppermute | solution.py:564
  39.7 26.1 %collective-permute-start.18 = (bf16[240,384]{1,0:T(8,128)(2,1)}, bf16[240,384]{1,0:T(8,128)(2,1)S(1)}, u32[]{:S(2)}, u32[]{:S(2)}) collective-permute-start(bf16[240,384]{1,0:T(8,128)(2,1)} %get-tuple-element.120.rest_0_.rest_3_.rest_2_), channel_id=1, source_target_pairs={{0,4},{1,5},{2,6},{3,7},{4,0},{5,1},{6,2},{7,3},{8,12},{9,13},{10,... | collective-permute-start | bytes 552968 | tf_op jit(solution)/shard_map/ppermute | solution.py:564
  42.6 29.2 %collective-permute-start.16 = (bf16[240,384]{1,0:T(8,128)(2,1)}, bf16[240,384]{1,0:T(8,128)(2,1)S(1)}, u32[]{:S(2)}, u32[]{:S(2)}) collective-permute-start(bf16[240,384]{1,0:T(8,128)(2,1)} %get-tuple-element.120.rest_0_.rest_3_.rest_2_), channel_id=1, source_target_pairs={{0,2},{1,3},{2,0},{3,1},{4,6},{5,7},{6,4},{7,5},{8,10},{9,11},{10,... | collective-permute-start | bytes 552968 | tf_op jit(solution)/shard_map/ppermute | solution.py:564
  57.1 14.6 %collective-permute-start.26 = (bf16[240,384]{1,0:T(8,128)(2,1)S(1)}, bf16[240,384]{1,0:T(8,128)(2,1)S(1)}, u32[]{:S(2)}, u32[]{:S(2)}) collective-permute-start(bf16[240,384]{1,0:T(8,128)(2,1)S(1)} %collective-permute-done.22.rest_8_.rest_11_.rest_10_), channel_id=1, source_target_pairs={{0,4},{1,5},{2,6},{3,7},{4,0},{5,1},{6,2},{7,3},{8,12},{9,13},{10,... | collective-permute-start | bytes 552968 | tf_op jit(solution)/shard_map/ppermute | solution.py:564
  57.1 16.4 %collective-permute-start.24 = (bf16[240,384]{1,0:T(8,128)(2,1)S(1)}, bf16[240,384]{1,0:T(8,128)(2,1)S(1)}, u32[]{:S(2)}, u32[]{:S(2)}) collective-permute-start(bf16[240,384]{1,0:T(8,128)(2,1)S(1)} %collective-permute-done.22.rest_8_.rest_11_.rest_10_), channel_id=1, source_target_pairs={{0,2},{1,3},{2,0},{3,1},{4,6},{5,7},{6,4},{7,5},{8,10},{9,11},{10,... | collective-permute-start | bytes 552968 | tf_op jit(solution)/shard_map/ppermute | solution.py:564
  65.9 17.4 %collective-permute-start.23 = (bf16[240,384]{1,0:T(8,128)(2,1)S(1)}, bf16[240,384]{1,0:T(8,128)(2,1)S(1)}, u32[]{:S(2)}, u32[]{:S(2)}) collective-permute-start(bf16[240,384]{1,0:T(8,128)(2,1)S(1)} %collective-permute-done.22.rest_8_.rest_11_.rest_10_), channel_id=1, source_target_pairs={{0,1},{1,0},{2,3},{3,2},{4,5},{5,4},{6,7},{7,6},{8,9},{9,8},{10,11... | collective-permute-start | bytes 552968 | tf_op jit(solution)/shard_map/ppermute | solution.py:564
  157.5 12.5 %collective-permute-start.30 = (bf16[2,8,96,768]{3,2,1,0:T(8,128)(2,1)}, bf16[2,8,96,768]{3,2,1,0:T(8,128)(2,1)S(1)}, u32[]{:S(2)}, u32[]{:S(2)}) collective-permute-start(bf16[2,8,96,768]{3,2,1,0:T(8,128)(2,1)} %get-tuple-element.145), channel_id=1, source_target_pairs={{0,1},{1,0},{2,3},{3,2},{4,5},{5,4},{6,7},{7,6},{8,9},{9,8},{10,11... | collective-permute-start | bytes 7077896 | tf_op jit(solution)/shard_map/ppermute | solution.py:564
  171.5 28.2 %collective-permute-start.31 = (bf16[8,96,768]{2,1,0:T(8,128)(2,1)S(1)}, bf16[8,96,768]{2,1,0:T(8,128)(2,1)S(1)}, u32[]{:S(2)}, u32[]{:S(2)}) collective-permute-start(bf16[8,96,768]{2,1,0:T(8,128)(2,1)S(1)} %fusion), channel_id=1, source_target_pairs={{0,16},{16,0},{1,17},{17,1},{2,18},{18,2},{3,19},{19,3},{4,20},{20... | collective-permute-start | bytes 3538952 | tf_op jit(solution)/shard_map/ppermute | solution.py:640
  193.2 20.2 %collective-permute-start.33 = (bf16[8,240,384]{2,1,0:T(8,128)(2,1)S(1)}, bf16[8,240,384]{2,1,0:T(8,128)(2,1)S(1)}, u32[]{:S(2)}, u32[]{:S(2)}) collective-permute-start(bf16[8,240,384]{2,1,0:T(8,128)(2,1)S(1)} %get-tuple-element.160), channel_id=1, source_target_pairs={{0,1},{1,0},{2,3},{3,2},{4,5},{5,4},{6,7},{7,6},{8,9},{9,8},{10,11... | collective-permute-start | bytes 4423688 | tf_op jit(solution)/shard_map/ppermute | solution.py:564
  200.0 15.8 %collective-permute-start.32 = (bf16[4,96,768]{2,1,0:T(8,128)(2,1)S(1)}, bf16[4,96,768]{2,1,0:T(8,128)(2,1)S(1)}, u32[]{:S(2)}, u32[]{:S(2)}) collective-permute-start(bf16[4,96,768]{2,1,0:T(8,128)(2,1)S(1)} %fusion.1), channel_id=1, source_target_pairs={{0,2},{1,3},{2,0},{3,1},{4,6},{5,7},{6,4},{7,5},{8,10},{9,11},{10,... | collective-permute-start | bytes 1769480 | tf_op jit(solution)/shard_map/ppermute | solution.py:564
  213.6 21.1 %collective-permute-start.35 = (bf16[4,240,384]{2,1,0:T(8,128)(2,1)S(1)}, bf16[4,240,384]{2,1,0:T(8,128)(2,1)S(1)}, u32[]{:S(2)}, u32[]{:S(2)}) collective-permute-start(bf16[4,240,384]{2,1,0:T(8,128)(2,1)S(1)} %add_convert_fusion.1), channel_id=1, source_target_pairs={{0,2},{1,3},{2,0},{3,1},{4,6},{5,7},{6,4},{7,5},{8,10},{9,11},{10,... | collective-permute-start | bytes 2211848 | tf_op jit(solution)/shard_map/ppermute | solution.py:564
  215.9 15.1 %collective-permute-start.36 = (bf16[2,96,768]{2,1,0:T(8,128)(2,1)S(1)}, bf16[2,96,768]{2,1,0:T(8,128)(2,1)S(1)}, u32[]{:S(2)}, u32[]{:S(2)}) collective-permute-start(bf16[2,96,768]{2,1,0:T(8,128)(2,1)S(1)} %fusion.3), channel_id=1, source_target_pairs={{0,4},{1,5},{2,6},{3,7},{4,0},{5,1},{6,2},{7,3},{8,12},{9,13},{10,... | collective-permute-start | bytes 884744 | tf_op jit(solution)/shard_map/ppermute | solution.py:564
  224.3 12.1 %collective-permute-start.34 = (bf16[8,144,384]{2,1,0:T(8,128)(2,1)S(1)}, bf16[8,144,384]{2,1,0:T(8,128)(2,1)S(1)}, u32[]{:S(2)}, u32[]{:S(2)}) collective-permute-start(bf16[8,144,384]{2,1,0:T(8,128)(2,1)S(1)} %get-tuple-element.170), channel_id=1, source_target_pairs={{0,1},{1,0},{2,3},{3,2},{4,5},{5,4},{6,7},{7,6},{8,9},{9,8},{10,11... | collective-permute-start | bytes 2654216 | tf_op jit(solution)/shard_map/ppermute | solution.py:564
  231.3 15.6 %collective-permute-start.39 = (bf16[1,96,768]{2,1,0:T(8,128)(2,1)S(1)}, bf16[1,96,768]{2,1,0:T(8,128)(2,1)S(1)}, u32[]{:S(2)}, u32[]{:S(2)}) collective-permute-start(bf16[1,96,768]{2,1,0:T(8,128)(2,1)S(1)} %fusion.10), channel_id=1, source_target_pairs={{0,8},{1,9},{2,10},{3,11},{4,12},{5,13},{6,14},{7,15},{8,0},{9,1},... | collective-permute-start | bytes 442376 | tf_op jit(solution)/shard_map/ppermute | solution.py:564
  234.8 14.3 %collective-permute-start.38 = (bf16[2,240,384]{2,1,0:T(8,128)(2,1)S(1)}, bf16[2,240,384]{2,1,0:T(8,128)(2,1)S(1)}, u32[]{:S(2)}, u32[]{:S(2)}) collective-permute-start(bf16[2,240,384]{2,1,0:T(8,128)(2,1)S(1)} %add_convert_fusion.3), channel_id=1, source_target_pairs={{0,4},{1,5},{2,6},{3,7},{4,0},{5,1},{6,2},{7,3},{8,12},{9,13},{10,... | collective-permute-start | bytes 1105928 | tf_op jit(solution)/shard_map/ppermute | solution.py:564
  236.5 12.6 %collective-permute-start.37 = (bf16[4,144,384]{2,1,0:T(8,128)(2,1)S(1)}, bf16[4,144,384]{2,1,0:T(8,128)(2,1)S(1)}, u32[]{:S(2)}, u32[]{:S(2)}) collective-permute-start(bf16[4,144,384]{2,1,0:T(8,128)(2,1)S(1)} %add_convert_fusion.2), channel_id=1, source_target_pairs={{0,2},{1,3},{2,0},{3,1},{4,6},{5,7},{6,4},{7,5},{8,10},{9,11},{10,... | collective-permute-start | bytes 1327112 | tf_op jit(solution)/shard_map/ppermute | solution.py:564
  250.8 14.0 %collective-permute-start.46 = (bf16[1,240,384]{2,1,0:T(8,128)(2,1)}, bf16[1,240,384]{2,1,0:T(8,128)(2,1)}, u32[]{:S(2)}, u32[]{:S(2)}) collective-permute-start(bf16[1,240,384]{2,1,0:T(8,128)(2,1)} %add_convert_fusion.6), channel_id=1, source_target_pairs={{0,8},{1,9},{2,10},{3,11},{4,12},{5,13},{6,14},{7,15},{8,0},{9,1},... | collective-permute-start | bytes 552968 | tf_op jit(solution)/shard_map/ppermute | solution.py:564
  253.6 26.4 %collective-permute-start.45 = (bf16[96,768]{1,0:T(8,128)(2,1)S(1)}, bf16[96,768]{1,0:T(8,128)(2,1)S(1)}, u32[]{:S(2)}, u32[]{:S(2)}) collective-permute-start(bf16[96,768]{1,0:T(8,128)(2,1)S(1)} %fusion.12.d_ref), channel_id=1, source_target_pairs={{0,16},{16,0},{1,17},{17,1},{2,18},{18,2},{3,19},{19,3},{4,20},{20... | collective-permute-start | bytes 442376 | tf_op jit(solution)/shard_map/ppermute | solution.py:640
  266.8 12.2 %collective-permute-start.47 = (bf16[240,384]{1,0:T(8,128)(2,1)}, bf16[240,384]{1,0:T(8,128)(2,1)S(1)}, u32[]{:S(2)}, u32[]{:S(2)}) collective-permute-start(bf16[240,384]{1,0:T(8,128)(2,1)} %fusion.11), channel_id=1, source_target_pairs={{0,16},{16,0},{1,17},{17,1},{2,18},{18,2},{3,19},{19,3},{4,20},{20... | collective-permute-start | bytes 552968 | tf_op jit(solution)/shard_map/ppermute | solution.py:640
  274.6 12.3 %collective-permute-start.43 = (bf16[144,384]{1,0:T(8,128)(2,1)S(1)}, bf16[144,384]{1,0:T(8,128)(2,1)S(1)}, u32[]{:S(2)}, u32[]{:S(2)}) collective-permute-start(bf16[144,384]{1,0:T(8,128)(2,1)S(1)} %fusion.13), channel_id=1, source_target_pairs={{0,16},{16,0},{1,17},{17,1},{2,18},{18,2},{3,19},{19,3},{4,20},{20... | collective-permute-start | bytes 331784 | tf_op jit(solution)/shard_map/ppermute | solution.py:640
  (134 other events, 987.2 us)
Sparse Core Ops, SparseCore 0:
  11.0 64.0 all-gather.4
  77.9 53.5 all-gather.6
  157.9 85.9 reduce-scatter.1
